TPU v7x, 32 devices: a whole 2x2x4 slice. The times are simulated.
32 devices in a mesh: head: 2 (over core), dp: 16 (over z, y, x).
Axes of the slice: x: 2, y: 2, z: 4, core: 2. Of those that a mesh axis runs over, the one named last changes fastest.
Arguments:
- tokens: bfloat16 [16384, 768], P(('dp', 'head')), may hold values from -6 to 6
- segment_ids: int32 [16384], P('dp'), may hold values from 0 to 7, as said below
- routes: int32 [16384, 1], P('dp'), may hold values from 0 to 15; in each aligned block of 512 rows (0 to 511, 512 to 1023, ...) at most 64 rows name the same one
- norm_gains: bfloat16 [4, 768], replicated, may hold values from 0.5 to 1.5
- qkv_one: bfloat16 [3, 768, 768], P(None, None, 'head'), may hold values from -0.21875 to 0.21875
- out_one: bfloat16 [768, 768], P('head'), may hold values from -0.625 to 0.625
- up_one: bfloat16 [768, 3072], P(None, 'head'), may hold values from -0.21875 to 0.21875
- down_one: bfloat16 [3072, 768], P('head'), may hold values from -0.21875 to 0.21875
- qkv_two: bfloat16 [3, 768, 768], P(None, None, 'head'), may hold values from -0.21875 to 0.21875
- out_two: bfloat16 [768, 768], P('head'), may hold values from -0.625 to 0.625
- expert_up: bfloat16 [16, 768, 3072], P('dp', None, 'head'), may hold values from -0.21875 to 0.21875
- expert_down: bfloat16 [16, 3072, 768], P('dp', 'head'), may hold values from -0.21875 to 0.21875
- centroids: bfloat16 [16, 768], P('dp'), may hold values from -0.15625 to 0.15625
- cotangent: bfloat16 [16384, 768], P(('dp', 'head')), may hold values from -6 to 6
Outputs:
- first_out: bfloat16 [16384, 768], P(('dp', 'head'))
- second_out: bfloat16 [16384, 768], P(('dp', 'head'))
- input_grad: float32 [16384, 768], P(('dp', 'head'))
- gains_grad: float32 [4, 768], replicated
- qkv_one_grad: float32 [3, 768, 768], P(None, None, 'head')
- out_one_grad: float32 [768, 768], P('head')
- up_one_grad: float32 [768, 3072], P(None, 'head')
- down_one_grad: float32 [3072, 768], P('head')
- qkv_two_grad: float32 [3, 768, 768], P(None, None, 'head')
- out_two_grad: float32 [768, 768], P('head')
- expert_up_grad: float32 [16, 768, 3072], P('dp', None, 'head')
- expert_down_grad: float32 [16, 3072, 768], P('dp', 'head')
- centroids_grad: float32 [16, 768], P('dp')
Inputs may be any that keep to these rules, and one draw needn't show every extreme that they name: `segment_ids`: within each 1024-token row the ids start at 0 and rise by one at each of 7 document starts; no document starts at positions 385 to 640. `routes`: in each aligned block of 512 rows (the rows of one device) no expert is named by more than 64 rows, a bound that some block reaches; every expert is named somewhere.
All inputs are finite; a program needn't handle non-finite values.
Results may differ from a plain program's by a relative error of at most 0.025.
Values may be sent and summed in bfloat16 or wider, within the bound.
No kernel may reach another device: no remote copies, remote signals or barrier semaphores. Data moves between devices by JAX's collectives and lax.ppermute only.
A program may use at most 256 MiB of HBM per device.

v0:
```python
import math

import jax
import jax.numpy as jnp
from jax import lax
from jax.sharding import PartitionSpec as P

HEAD_DIM = 64


norm_epsilon = 1e-05
masked_score = -1e30


def layer_norm(residual, gain_row):
    centered = residual - jnp.mean(residual, axis=-1, keepdims=True)
    variance = jnp.mean(centered * centered, axis=-1, keepdims=True)
    return centered * lax.rsqrt(variance + norm_epsilon) * gain_row


def gelu_exact(values):
    return jax.nn.gelu(values, approximate=False)


def gather_rows(pieces):
    return lax.all_gather(pieces, "head", axis=0, tiled=True)


def sum_rows(term_fn, row_count):
    return lax.psum_scatter(
        term_fn(jnp.int32(0), row_count * lax.axis_size("head")).astype(jnp.bfloat16),
        "head",
        scatter_dimension=0,
        tiled=True,
    ).astype(jnp.float32)


def row_slicer(gathered):

    def term_fn(first_row, row_count):
        return gathered

    return term_fn


def masked_scores(queries, key_rows, segments, first_row):
    block_rows = queries.shape[0]
    raw_scores = jnp.einsum("qhd,khd->hqk", queries, key_rows, preferred_element_type=jnp.float32)
    scaled = raw_scores * (1.0 / math.sqrt(queries.shape[2]))
    query_place = first_row + jnp.arange(block_rows, dtype=jnp.int32)
    key_place = jnp.arange(key_rows.shape[0], dtype=jnp.int32)
    query_segments = lax.dynamic_slice_in_dim(segments, first_row, block_rows, 0)
    allowed = (key_place[None, :] <= query_place[:, None]) & (
        segments[None, :] == query_segments[:, None]
    )
    return jnp.where(allowed[None], scaled, masked_score)


def attention_forward(residual, gain_row, qkv_weight, out_weight, segments):
    row_count = residual.shape[0]
    normed = layer_norm(residual, gain_row).astype(jnp.bfloat16)
    gathered = gather_rows(normed)
    length = gathered.shape[0]
    head_count = qkv_weight.shape[2] // HEAD_DIM
    projected = jnp.einsum(
        "td,cde->cte", gathered, qkv_weight, preferred_element_type=jnp.float32
    ).astype(jnp.bfloat16)
    qkv_heads = projected.reshape(3, length, head_count, HEAD_DIM)
    block_rows = min(512, length)
    block_starts = jnp.arange(length // block_rows, dtype=jnp.int32) * block_rows

    def one_block(first_row):
        queries = lax.dynamic_slice_in_dim(qkv_heads[0], first_row, block_rows, 0)
        scores = masked_scores(queries, qkv_heads[1], segments, first_row)
        row_max = jnp.max(scores, axis=-1, keepdims=True)
        weights = jnp.exp(scores - row_max)
        row_total = jnp.sum(weights, axis=-1, keepdims=True)
        rounded = (weights / row_total).astype(jnp.bfloat16)
        mixture = jnp.einsum(
            "hqk,khd->qhd", rounded, qkv_heads[2], preferred_element_type=jnp.float32
        )
        return (mixture.astype(jnp.bfloat16), row_max + jnp.log(row_total))

    mixture, log_totals = lax.map(one_block, block_starts)
    mixture = mixture.reshape(length, head_count * HEAD_DIM)

    def attention_project(first_row, count_rows):
        return jnp.dot(mixture, out_weight, preferred_element_type=jnp.float32)

    branch = sum_rows(attention_project, row_count)
    return (residual + branch, (gathered, qkv_heads, mixture, log_totals))


def attention_backward(grad_resid, residual, gain_row, qkv_weight, out_weight, segments, stored):
    gathered, qkv_heads, mixture, log_totals = stored
    row_count = residual.shape[0]
    length = qkv_heads.shape[1]
    head_count = qkv_heads.shape[2]
    head_size = qkv_heads.shape[3]
    score_scale = 1.0 / math.sqrt(head_size)
    grad_branch = gather_rows(grad_resid.astype(jnp.bfloat16))
    grad_out = jnp.einsum("te,td->ed", mixture, grad_branch, preferred_element_type=jnp.float32)
    grad_mixture = jnp.einsum(
        "td,ed->te", grad_branch, out_weight, preferred_element_type=jnp.float32
    ).astype(jnp.bfloat16)
    grad_heads = grad_mixture.reshape(length, head_count, head_size)
    block_rows = min(512, length)

    def back_block(carried, block_index):
        grad_keys, grad_values = carried
        first_row = block_index * block_rows
        queries = lax.dynamic_slice_in_dim(qkv_heads[0], first_row, block_rows, 0)
        grad_part = lax.dynamic_slice_in_dim(grad_heads, first_row, block_rows, 0)
        scores = masked_scores(queries, qkv_heads[1], segments, first_row)
        weights = jnp.exp(scores - log_totals[block_index])
        grad_weights = jnp.einsum(
            "qhd,khd->hqk", grad_part, qkv_heads[2], preferred_element_type=jnp.float32
        )
        row_delta = jnp.sum(weights * grad_weights, axis=-1, keepdims=True)
        grad_scores = (weights * (grad_weights - row_delta)).astype(jnp.bfloat16)
        grad_queries = (
            jnp.einsum(
                "hqk,khd->qhd", grad_scores, qkv_heads[1], preferred_element_type=jnp.float32
            )
            * score_scale
        )
        grad_keys = (
            grad_keys
            + jnp.einsum("hqk,qhd->khd", grad_scores, queries, preferred_element_type=jnp.float32)
            * score_scale
        )
        grad_values = grad_values + jnp.einsum(
            "hqk,qhd->khd",
            weights.astype(jnp.bfloat16),
            grad_part,
            preferred_element_type=jnp.float32,
        )
        return ((grad_keys, grad_values), grad_queries.astype(jnp.bfloat16))

    zero_grads = jnp.zeros((length, head_count, head_size), jnp.float32)
    (grad_keys, grad_values), grad_queries = lax.scan(
        back_block, (zero_grads, zero_grads), jnp.arange(length // block_rows, dtype=jnp.int32)
    )
    columns = head_count * head_size
    grad_qkv = jnp.stack(
        [
            grad_queries.reshape(length, columns),
            grad_keys.astype(jnp.bfloat16).reshape(length, columns),
            grad_values.astype(jnp.bfloat16).reshape(length, columns),
        ]
    )
    grad_weight = jnp.einsum("td,cte->cde", gathered, grad_qkv, preferred_element_type=jnp.float32)

    def attention_back_project(first_row, count_rows):
        return jnp.einsum("cte,cde->td", grad_qkv, qkv_weight, preferred_element_type=jnp.float32)

    grad_normed = sum_rows(attention_back_project, row_count)
    unused, pullback = jax.vjp(layer_norm, residual, gain_row)
    grad_input, grad_gain = pullback(grad_normed)
    return (grad_resid + grad_input, grad_gain, grad_weight, grad_out)


def dense_forward(residual, gain_row, up_weight, down_weight):
    row_count = residual.shape[0]
    gathered = gather_rows(layer_norm(residual, gain_row).astype(jnp.bfloat16))
    hidden = jnp.dot(gathered, up_weight, preferred_element_type=jnp.float32)
    active = gelu_exact(hidden).astype(jnp.bfloat16)

    def dense_project(first_row, count_rows):
        return jnp.dot(active, down_weight, preferred_element_type=jnp.float32)

    return (residual + sum_rows(dense_project, row_count), (gathered, hidden, active))


def dense_backward(grad_resid, residual, gain_row, up_weight, down_weight, stored):
    gathered, hidden, active = stored
    row_count = residual.shape[0]
    grad_branch = gather_rows(grad_resid.astype(jnp.bfloat16))
    grad_down = jnp.einsum("tf,td->fd", active, grad_branch, preferred_element_type=jnp.float32)
    grad_active = jnp.einsum(
        "td,fd->tf", grad_branch, down_weight, preferred_element_type=jnp.float32
    )
    unused, pullback = jax.vjp(gelu_exact, hidden)
    grad_hidden = pullback(grad_active)[0].astype(jnp.bfloat16)
    grad_up = jnp.einsum("td,tf->df", gathered, grad_hidden, preferred_element_type=jnp.float32)

    def dense_back_project(first_row, count_rows):
        return jnp.einsum("tf,df->td", grad_hidden, up_weight, preferred_element_type=jnp.float32)

    grad_normed = sum_rows(dense_back_project, row_count)
    unused, norm_pull = jax.vjp(layer_norm, residual, gain_row)
    grad_input, grad_gain = norm_pull(grad_normed)
    return (grad_resid + grad_input, grad_gain, grad_up, grad_down)


def slot_index(chosen, capacity, expert_total):
    blocks, row_count = chosen.shape
    matches = chosen[:, :, None] == jnp.arange(expert_total, dtype=jnp.int32)[None, None, :]
    position = jnp.arange(row_count, dtype=jnp.int32)
    earlier = (position[None, :] < position[:, None]).astype(jnp.bfloat16)
    before = jnp.einsum(
        "rs,bse->bre", earlier, matches.astype(jnp.bfloat16), preferred_element_type=jnp.float32
    )
    slot_rank = jnp.sum(jnp.where(matches, before, 0.0), axis=2).astype(jnp.int32)
    block_number = jnp.arange(blocks, dtype=jnp.int32)[:, None]
    flat_slots = chosen * (blocks * capacity) + block_number * capacity + slot_rank
    return flat_slots.reshape(blocks * row_count)


def fill_slots(row_values, flat_slots, layout):
    buffer = jnp.zeros((layout[0] * layout[1] * layout[2], row_values.shape[1]), row_values.dtype)
    return (
        buffer.at[flat_slots]
        .set(row_values)
        .reshape(layout[0], layout[1], layout[2], row_values.shape[1])
    )


def read_slots(buffer, flat_slots):
    return buffer.reshape(-1, buffer.shape[3])[flat_slots]


def expert_forward(slot_rows, centroid_rows, up_weight, down_weight):
    scores = jnp.einsum(
        "nesd,ed->nes", slot_rows, centroid_rows, preferred_element_type=jnp.float32
    )
    gating = jax.nn.sigmoid(scores)
    hidden = jnp.einsum("nesd,edf->nesf", slot_rows, up_weight, preferred_element_type=jnp.float32)
    active = gelu_exact(hidden).astype(jnp.bfloat16)
    partial_value = jnp.einsum(
        "nesf,efd->nesd", active, down_weight, preferred_element_type=jnp.float32
    )
    return (gating[..., None] * partial_value, (gating, hidden, active, partial_value))


def expert_backward(slot_rows, grad_gated, centroid_rows, up_weight, down_weight, stored):
    gating, hidden, active, partial_value = stored
    grad_float = grad_gated.astype(jnp.float32)
    grad_score = jnp.sum(grad_float * partial_value, axis=-1) * gating * (1.0 - gating)
    grad_output = (gating[..., None] * grad_float).astype(jnp.bfloat16)
    grad_down = jnp.einsum(
        "nesf,nesd->efd", active, grad_output, preferred_element_type=jnp.float32
    )
    grad_active = jnp.einsum(
        "nesd,efd->nesf", grad_output, down_weight, preferred_element_type=jnp.float32
    )
    unused, pullback = jax.vjp(gelu_exact, hidden)
    grad_hidden = pullback(grad_active)[0].astype(jnp.bfloat16)
    grad_up = jnp.einsum(
        "nesd,nesf->edf", slot_rows, grad_hidden, preferred_element_type=jnp.float32
    )
    grad_centroid = jnp.einsum("nes,nesd->ed", grad_score, slot_rows.astype(jnp.float32))
    grad_slots = jnp.einsum(
        "nesf,edf->nesd", grad_hidden, up_weight, preferred_element_type=jnp.float32
    )
    grad_slots = (
        grad_slots + grad_score[..., None] * centroid_rows.astype(jnp.float32)[None, :, None, :]
    )
    return (grad_slots, grad_up, grad_down, grad_centroid)


def body(
    tokens,
    segment_ids,
    routes,
    norm_gains,
    qkv_one,
    out_one,
    up_one,
    down_one,
    qkv_two,
    out_two,
    expert_up,
    expert_down,
    centroids,
    cotangent,
):
    residual = tokens.astype(jnp.float32)
    gain_rows = norm_gains.astype(jnp.float32)
    first_mid, saved_one = attention_forward(residual, gain_rows[0], qkv_one, out_one, segment_ids)
    first, saved_two = dense_forward(first_mid, gain_rows[1], up_one, down_one)
    second_mid, saved_three = attention_forward(first, gain_rows[2], qkv_two, out_two, segment_ids)
    row_count = tokens.shape[0]
    dp_size = lax.axis_size("dp")
    pair_size = lax.axis_size("head")
    local_experts = expert_up.shape[0]
    expert_total = dp_size * local_experts
    capacity = 2 * row_count // expert_total
    normed = layer_norm(second_mid, gain_rows[3]).astype(jnp.bfloat16)
    chosen = routes[:, 0]

    def send_all(buffer):
        return lax.all_to_all(buffer, "dp", split_axis=0, concat_axis=0, tiled=True)

    def return_all(buffer):
        return lax.all_to_all(
            buffer.astype(jnp.bfloat16), "dp", split_axis=0, concat_axis=0, tiled=True
        ).astype(buffer.dtype)

    layout = (dp_size, local_experts, pair_size * capacity)
    flat_slots = slot_index(chosen.reshape(pair_size, row_count), capacity, expert_total)
    slot_rows = send_all(fill_slots(gather_rows(normed), flat_slots, layout))
    gated, stored = expert_forward(slot_rows, centroids, expert_up, expert_down)
    branch = sum_rows(row_slicer(read_slots(return_all(gated), flat_slots)), row_count)
    grad_table = send_all(fill_slots(gather_rows(cotangent), flat_slots, layout))
    grad_slots, upward_grad, downward_grad, centroid_grad = expert_backward(
        slot_rows, grad_table, centroids, expert_up, expert_down, stored
    )
    grad_normed = sum_rows(row_slicer(read_slots(return_all(grad_slots), flat_slots)), row_count)
    second = second_mid + branch
    unused, pullback = jax.vjp(layer_norm, second_mid, gain_rows[3])
    grad_input, gain_three = pullback(grad_normed)
    grad_resid = cotangent.astype(jnp.float32) + grad_input
    grad_resid, gain_two, qkv_second, out_second = attention_backward(
        grad_resid, first, gain_rows[2], qkv_two, out_two, segment_ids, saved_three
    )
    qkv_second, out_second = lax.psum((qkv_second, out_second), "dp")
    grad_resid, gain_one, up_first, down_first = dense_backward(
        grad_resid, first_mid, gain_rows[1], up_one, down_one, saved_two
    )
    grad_resid, gain_zero, qkv_first, out_first = attention_backward(
        grad_resid, residual, gain_rows[0], qkv_one, out_one, segment_ids, saved_one
    )
    gain_grads = jnp.stack([gain_zero, gain_one, gain_two, gain_three])
    qkv_first, out_first, up_first, down_first, gain_grads = lax.psum(
        (qkv_first, out_first, up_first, down_first, gain_grads), "dp"
    )
    gain_grads, centroid_grad = lax.psum((gain_grads, centroid_grad), "head")
    return (
        first.astype(jnp.bfloat16),
        second.astype(jnp.bfloat16),
        grad_resid,
        gain_grads,
        qkv_first,
        out_first,
        up_first,
        down_first,
        qkv_second,
        out_second,
        upward_grad,
        downward_grad,
        centroid_grad,
    )


def solution(mesh):
    in_specs = (
        P(("dp", "head"), None),
        P("dp"),
        P("dp", None),
        P(),
        P(None, None, "head"),
        P("head", None),
        P(None, "head"),
        P("head", None),
        P(None, None, "head"),
        P("head", None),
        P("dp", None, "head"),
        P("dp", "head", None),
        P("dp", None),
        P(("dp", "head"), None),
    )
    out_specs = (
        P(("dp", "head"), None),
        P(("dp", "head"), None),
        P(("dp", "head"), None),
        P(),
        P(None, None, "head"),
        P("head", None),
        P(None, "head"),
        P("head", None),
        P(None, None, "head"),
        P("head", None),
        P("dp", None, "head"),
        P("dp", "head", None),
        P("dp", None),
    )
    return jax.shard_map(body, mesh=mesh, in_specs=in_specs, out_specs=out_specs, check_vma=False)
```

profile of v0, /device:TPU:0, one launch (start us, length us, event | category | flops | bytes accessed | tf_op | source)
XLA Modules:
  0.0 1455.1 jit_solution(16861746661135706177)
XLA Ops:
  14.6 12.6 all-gather.9.cloned.1.call-done
  27.2 5.4 convolution_convert_fusion.1
  34.1 37.9 %while.54 = (s32[]{:T(128)}, bf16[2,512,6,64]{1,3,2,0:T(8,128)(2,1)}, f32[2,6,512,1]{2,1,3,0:T(8,128)}, s32[2]{0:T(128)S(1)}, s32[1024]{0:T(1024)S(1)}, /*index=...) while((s32[]{:T(128)}, bf16[2,512,6,64]{1,3,2,0:T(8,128)(2,1)}, ...), condition=%wide.region_5.6_spmd, body=%wide.region_2.5_spmd.sunk | while | flops 844822016 | bytes 43894948 | solution.py:84
  46.8 5.7 fusion.289
  65.7 5.7 fusion.289
  78.7 10.1 reduce-scatter.9.cloned.1.call-done
  95.4 11.1 all-gather.11.cloned.1.call-done
  106.5 18.1 %multiply_convert_fusion.2 = (bf16[1024,1536]{1,0:T(8,128)(2,1)S(1)}, f32[1024,1536]{1,0:T(8,128)}, f32[1024,1536]{1,0:T(8,128)}) fusion(bf16[1024,768]{1,0:T(8,128)(2,1)} %all-gather.11.cloned.1.call-done, bf16[768,1536]{1,0:T(8,128)(2,1)S(1)} %copy-done), kind=kOutput, calls=%fused_computation.165 | convolution fusion | flops 2518155264 | bytes 19660800 | tf_op jit(solution)/shard_map/dot_general | solution.py:166
  130.0 10.3 reduce-scatter.11.cloned.1.call-done
  145.0 11.1 all-gather.13.cloned.1.call-done
  156.1 5.4 convolution_convert_fusion
  161.6 36.0 %while.55 = (s32[]{:T(128)}, bf16[2,512,6,64]{1,3,2,0:T(8,128)(2,1)S(1)}, f32[2,6,512,1]{2,1,3,0:T(8,128)S(1)}, s32[2]{0:T(128)S(1)}, s32[1024]{0:T(1024)S(1)}, ...) while((s32[]{:T(128)}, bf16[2,512,6,64]{1,3,2,0:T(8,128)(2,1)S(1)}, ...), condition=%wide.region_15.16_spmd, body=%wide.region_12.15_spmd.sunk | while | flops 844822016 | bytes 43911332 | solution.py:84
  174.7 5.1 fusion.294
  192.5 5.1 fusion.294
  202.8 10.3 reduce-scatter.13.cloned.1.call-done
  219.4 9.6 all-gather.15.cloned.1.call-done
  229.0 8.1 scatter_custom_fusion
  237.1 6.8 all-to-all-start
  244.7 12.8 all-gather.17.cloned.1.call-done
  257.5 7.9 scatter_custom_fusion.1
  265.3 39.9 %all-to-all-done = bf16[16,1,128,768]{3,2,1,0:T(8,128)(2,1)} async-done(((bf16[16,1,128,768]{3,2,1,0:T(8,128)(2,1)}), bf16[16,1,128,768]{3,2,1,0:T(8,128)(2,1)}, u32[]{:S(2)}, u32[]{:S(2)}) %all-to-all-start) | async-done | bytes 3145760 | tf_op jit(solution)/shard_map/all_to_all | solution.py:293
  305.2 16.5 %all-to-all-start.2 = ((bf16[16,1,128,768]{3,2,1,0:T(8,128)(2,1)}), bf16[16,1,128,768]{3,2,1,0:T(8,128)(2,1)}, u32[]{:S(2)}, u32[]{:S(2)}) async-start(bf16[16,1,128,768]{3,2,1,0:T(8,128)(2,1)} %bitcast.475), calls=%async_computation.6 | async-start | bytes 6291456 | tf_op jit(solution)/shard_map/all_to_all | solution.py:293
  325.2 10.0 fusion.136
  335.2 47.2 %all-to-all-done.2 = bf16[16,1,128,768]{3,2,1,0:T(8,128)(2,1)} async-done(((bf16[16,1,128,768]{3,2,1,0:T(8,128)(2,1)}), bf16[16,1,128,768]{3,2,1,0:T(8,128)(2,1)}, u32[]{:S(2)}, u32[]{:S(2)}) %all-to-all-start.2) | async-done | bytes 3145760 | tf_op jit(solution)/shard_map/all_to_all | solution.py:293
  382.4 36.7 %fusion.113 = (f32[16,128]{1,0:T(8,128)S(1)}, bf16[16,1,128,768]{3,2,1,0:T(8,128)(2,1)}) fusion(bf16[16,1,128,768]{3,2,1,0:T(8,128)(2,1)} %all-to-all-done.2, f32[16,128]{1,0:T(8,128)S(1)} %add_divide_fusion, bf16[1,1536,768]{2,1,0:T(8,128)(2,1)} %param.33, f32[16,128,1536]{2,1,0:T(8,128)} %fusion.136), kind=kOutput, calls=%fused_computation.153 | convolution fusion | flops 5044172800 | bytes 21250048 | tf_op jit(solution)/shard_map/nesf,efd->nesd/dot_general | solution.py:230
  419.2 34.0 %fusion.100 = bf16[16,1,128,1536]{3,2,0,1:T(8,128)(2,1)S(1)} fusion(f32[16,128,1536]{2,1,0:T(8,128)S(1)} %copy-done.108, bf16[16,1,128,768]{3,2,1,0:T(8,128)(2,1)} %all-to-all-done.2, f32[16,128]{1,0:T(8,128)S(1)} %add_divide_fusion, bf16[1,1536,768]{2,1,0:T(8,128)(2,1)S(1)} %copy-done.98), kind=kOutput, calls=%fused_computation.131 | convolution fusion | flops 5063049216 | bytes 24387584 | tf_op jit(solution)/shard_map/nesd,efd->nesf/dot_general | solution.py:244
  453.2 5.3 fusion.131
  458.6 84.7 %all_to_all.20 = bf16[16,1,128,768]{3,2,1,0:T(8,128)(2,1)} all-to-all(bf16[16,1,128,768]{3,2,1,0:T(8,128)(2,1)S(1)} %fusion.131), channel_id=1, replica_groups=mesh['head'=2,'dp'=16] {'dp'}, dimensions={0} | all-to-all | bytes 6291456 | tf_op jit(solution)/shard_map/all_to_all | solution.py:296
  543.3 4.9 all-to-all-start.1
  548.3 7.9 gather_fusion.1
  556.3 52.1 %all-to-all-done.1 = bf16[16,1,128,768]{3,2,1,0:T(8,128)(2,1)} async-done(((bf16[16,1,128,768]{3,2,1,0:T(8,128)(2,1)}), bf16[16,1,128,768]{3,2,1,0:T(8,128)(2,1)}, u32[]{:S(2)}, u32[]{:S(2)}) %all-to-all-start.1) | async-done | bytes 3145760 | tf_op jit(solution)/shard_map/all_to_all | solution.py:296
  608.4 7.9 gather_fusion
  619.4 14.5 reduce-scatter.15.cloned.1.call-done
  639.7 11.1 all-gather.19.cloned.1.call-done
  654.1 63.6 %while.56 = (s32[]{:T(128)}, f32[1024,6,64]{0,2,1:T(8,128)}, f32[1024,6,64]{0,2,1:T(8,128)}, bf16[2,512,6,64]{1,3,2,0:T(8,128)(2,1)}, bf16[3,1024,6,64]{1,3,2,0:...) while((s32[]{:T(128)}, f32[1024,6,64]{0,2,1:T(8,128)}, ...), condition=%wide.region_29.30_spmd.clone, body=%wide.region_27.29_spmd.clone.sunk | while | flops 2064381440 | bytes 137079200 | solution.py:141
  662.1 4.6 bitcast_add_fusion.10
  666.7 7.2 multiply_reduce_fusion.7
  673.8 7.0 multiply_convert_fusion.8
  693.1 5.8 bitcast_add_fusion.10
  699.0 7.2 multiply_reduce_fusion.7
  706.2 7.0 multiply_convert_fusion.8
  728.7 5.6 bitcast_convert_fusion.3
  734.4 10.3 reduce-scatter.19.cloned.1.call-done
  752.6 11.1 all-gather.21.cloned.1.call-done
  763.7 9.8 add_convert_fusion
  779.0 10.3 reduce-scatter.21.cloned.1.call-done
  796.5 10.7 all-gather.23.cloned.1.call-done
  810.5 65.0 %while.57 = (s32[]{:T(128)}, f32[1024,6,64]{0,2,1:T(8,128)}, f32[1024,6,64]{0,2,1:T(8,128)}, bf16[2,512,6,64]{1,3,2,0:T(8,128)(2,1)}, bf16[3,1024,6,64]{1,3,2,0:...) while((s32[]{:T(128)}, f32[1024,6,64]{0,2,1:T(8,128)}, ...), condition=%wide.region_38.39_spmd.clone, body=%wide.region_36.38_spmd.clone.sunk | while | flops 2064381440 | bytes 137079200 | solution.py:141
  819.2 4.6 bitcast_add_fusion.12
  823.8 7.2 multiply_reduce_fusion.8
  831.0 7.0 multiply_convert_fusion.9
  851.0 5.8 bitcast_add_fusion.12
  856.8 7.2 multiply_reduce_fusion.8
  864.0 7.0 multiply_convert_fusion.9
  886.7 5.7 bitcast_convert_fusion.2
  899.8 4.4 fusion.218
  904.2 4.4 fusion.217
  918.3 9.8 fusion.127
  928.3 34.8 %convolution_bitcast_fusion = f32[1,1536,768]{2,1,0:T(8,128)} fusion(bf16[16,1,128,768]{3,2,1,0:T(8,128)(2,1)} %all-to-all-done.2, f32[16,128]{1,0:T(8,128)S(1)} %copy-done.96, f32[16,128,1536]{2,1,0:T(8,128)S(1)} %bitcast.499), kind=kOutput, calls=%fused_computation.180 | convolution fusion | flops 5041029120 | bytes 20455424 | tf_op jit(solution)/shard_map/nesf,nesd->efd/dot_general | solution.py:241
  967.0 81.5 %psum.63 = f32[4,768]{1,0:T(4,128)S(1)} all-reduce(f32[4,768]{1,0:T(4,128)S(1)} %pad_maximum_fusion.6), channel_id=1, replica_groups=mesh['head'=2,'dp'=16] {'dp'}, use_global_device_ids=true, to_apply=%region_46.47 | all-reduce | flops 3072 | bytes 24576 | tf_op jit(solution)/shard_map/psum | solution.py:325
  1056.1 371.8 %all-reduce.4.cloned.1.call-done = (f32[3,768,384]{1,2,0:T(8,128)}, f32[384,768]{1,0:T(8,128)}, f32[768,1536]{1,0:T(8,128)}, f32[1536,768]{1,0:T(8,128)}, f32[3,768,384]{1,2,0:T(8,128)}, /*index=5*/f32[384,768]{1,0:T(8,128)}) async-done(((f32[3,768,384]{1,2,0:T(8,128)}, f32[384,768]{1,0:T(8,128)}, f32[768,1536]{1,0:T(8,128)}, f32[1536,768]{1,0:T(8,128)}, f32[3,768,384]{1,2,0:T(8,128)}, ...) | async-done | bytes 18874384 | tf_op jit(solution)/shard_map/psum | solution.py:325
  1427.9 5.2 copy.80
  1433.1 5.2 copy.81
  1439.4 5.5 copy.151
  (463 shorter events, 222.4 us)
Async XLA Ops:
  7.2 99.3 %copy-start = (bf16[768,1536]{1,0:T(8,128)(2,1)S(1)}, bf16[768,1536]{1,0:T(8,128)(2,1)}, u32[]{:S(2)}) copy-start(bf16[768,1536]{1,0:T(8,128)(2,1)} %param.28) | copy-start | bytes 7077892
  7.2 20.0 %all-gather.9.cloned.1.call-start = ((), (), s32[]{:S(2)}) async-start(), calls=%async_computation.12 | async-start | bytes 2359296 | tf_op jit(solution)/shard_map/all_gather | solution.py:26
  11.6 80.8 %copy-start.45 = (f32[768]{0:T(1024)}, f32[768]{0:T(1024)S(1)}, u32[]{:S(2)}) copy-start(f32[768]{0:T(1024)S(1)} %get-tuple-element.296) | copy-start | bytes 9220
  14.5 74.3 %reduce-scatter.9.cloned.1.call-start = ((), (), s32[]{:S(2)}) async-start(), calls=%async_computation.13 | async-start | bytes 2359296 | tf_op jit(solution)/shard_map/reduce_scatter | solution.py:30
  14.6 19.6 %copy-start.21 = (s32[1024]{0:T(1024)S(1)}, s32[1024]{0:T(1024)}, u32[]{:S(2)}) copy-start(s32[1024]{0:T(1024)} %param.23) | copy-start | bytes 12292
  72.1 16.7 %copy-start.3 = (bf16[512,768]{1,0:T(8,128)(2,1)S(1)}, bf16[512,768]{1,0:T(8,128)(2,1)}, u32[]{:S(2)}) copy-start(bf16[512,768]{1,0:T(8,128)(2,1)} %param.22) | copy-start | bytes 2359300
  78.4 28.1 %all-gather.11.cloned.1.call-start = ((), (), s32[]{:S(2)}) async-start(), calls=%async_computation.14 | async-start | bytes 2359296 | tf_op jit(solution)/shard_map/all_gather | solution.py:26
  95.3 45.0 %reduce-scatter.11.cloned.1.call-start = ((), (), s32[]{:S(2)}) async-start(), calls=%async_computation.15 | async-start | bytes 2359296 | tf_op jit(solution)/shard_map/reduce_scatter | solution.py:30
  106.5 19.8 %copy-start.100 = (bf16[1536,768]{1,0:T(8,128)(2,1)S(1)}, bf16[1536,768]{1,0:T(8,128)(2,1)}, u32[]{:S(2)}) copy-start(bf16[1536,768]{1,0:T(8,128)(2,1)} %param.29) | copy-start | bytes 7077892
  130.0 26.2 %all-gather.13.cloned.1.call-start = ((), (), s32[]{:S(2)}) async-start(), calls=%async_computation.16 | async-start | bytes 2359296 | tf_op jit(solution)/shard_map/all_gather | solution.py:26
  145.0 68.1 %reduce-scatter.13.cloned.1.call-start = ((), (), s32[]{:S(2)}) async-start(), calls=%async_computation.17 | async-start | bytes 2359296 | tf_op jit(solution)/shard_map/reduce_scatter | solution.py:30
  197.6 17.3 %copy-start.22 = (s32[1024]{0:T(1024)}, s32[1024]{0:T(1024)S(1)}, u32[]{:S(2)}) copy-start(s32[1024]{0:T(1024)S(1)} %get-tuple-element.791) | copy-start | bytes 12292
  197.6 17.3 %copy-start.43 = (f32[2,6,512,1]{2,1,3,0:T(8,128)}, f32[2,6,512,1]{2,1,3,0:T(8,128)S(1)}, u32[]{:S(2)}) copy-start(f32[2,6,512,1]{2,1,3,0:T(8,128)S(1)} %get-tuple-element.650) | copy-start | bytes 73732
  199.5 17.2 %copy-start.59 = (f32[768]{0:T(1024)S(1)}, f32[768]{0:T(1024)}, u32[]{:S(2)}) copy-start(f32[768]{0:T(1024)} %get-tuple-element.294) | copy-start | bytes 9220
  202.7 15.7 %copy-start.91 = (s32[1024,1]{0,1:T(1,128)S(1)}, s32[1024,1]{0,1:T(1,128)}, u32[]{:S(2)}) copy-start(s32[1024,1]{0,1:T(1,128)} %param.24) | copy-start | bytes 12292
  202.8 26.2 %all-gather.15.cloned.1.call-start = ((), (), s32[]{:S(2)}) async-start(), calls=%async_computation.18 | async-start | bytes 2359296 | tf_op jit(solution)/shard_map/all_gather | solution.py:26
  219.4 38.0 %copy-start.92 = (s32[1024,1]{0,1:T(1,128)}, s32[1024,1]{0,1:T(1,128)S(1)}, u32[]{:S(2)}) copy-start(s32[1024,1]{0,1:T(1,128)S(1)} %compare_select_fusion) | copy-start | bytes 12292
  237.1 68.2 %all-to-all-start = ((bf16[16,1,128,768]{3,2,1,0:T(8,128)(2,1)}), bf16[16,1,128,768]{3,2,1,0:T(8,128)(2,1)}, u32[]{:S(2)}, u32[]{:S(2)}) async-start(bf16[16,1,128,768]{3,2,1,0:T(8,128)(2,1)} %bitcast.474), calls=%async_computation.3 | async-start | bytes 6291456 | tf_op jit(solution)/shard_map/all_to_all | solution.py:293
  243.9 13.5 all-gather.17.cloned.1.call-start
  244.7 77.1 %copy-start.94 = (bf16[1,768]{1,0:T(2,128)(2,1)S(1)}, bf16[1,768]{1,0:T(2,128)(2,1)}, u32[]{:S(2)}) copy-start(bf16[1,768]{1,0:T(2,128)(2,1)} %param.34) | copy-start | bytes 4612
  305.2 77.2 %all-to-all-start.2 = ((bf16[16,1,128,768]{3,2,1,0:T(8,128)(2,1)}), bf16[16,1,128,768]{3,2,1,0:T(8,128)(2,1)}, u32[]{:S(2)}, u32[]{:S(2)}) async-start(bf16[16,1,128,768]{3,2,1,0:T(8,128)(2,1)} %bitcast.475), calls=%async_computation.6 | async-start | bytes 6291456 | tf_op jit(solution)/shard_map/all_to_all | solution.py:293
  325.2 93.9 %copy-start.95 = (f32[16,128]{1,0:T(8,128)}, f32[16,128]{1,0:T(8,128)S(1)}, u32[]{:S(2)}) copy-start(f32[16,128]{1,0:T(8,128)S(1)} %add_divide_fusion) | copy-start | bytes 24580
  382.4 36.7 %copy-start.98 = (bf16[1,1536,768]{2,1,0:T(8,128)(2,1)S(1)}, bf16[1,1536,768]{2,1,0:T(8,128)(2,1)}, u32[]{:S(2)}) copy-start(bf16[1,1536,768]{2,1,0:T(8,128)(2,1)} %param.33) | copy-start | bytes 7077892
  382.4 36.7 %copy-start.108 = (f32[16,128,1536]{2,1,0:T(8,128)S(1)}, f32[16,128,1536]{2,1,0:T(8,128)}, u32[]{:S(2)}) copy-start(f32[16,128,1536]{2,1,0:T(8,128)} %fusion.136) | copy-start | bytes 37748740
  419.1 34.1 %copy-start.72 = (f32[16,128]{1,0:T(8,128)}, f32[16,128]{1,0:T(8,128)S(1)}, u32[]{:S(2)}) copy-start(f32[16,128]{1,0:T(8,128)S(1)} %subtract_multiply_fusion) | copy-start | bytes 24580
  419.1 34.1 %copy-start.97 = (f32[768]{0:T(1024)S(1)}, f32[768]{0:T(1024)}, u32[]{:S(2)}) copy-start(f32[768]{0:T(1024)} %mul.496) | copy-start | bytes 9220
  419.1 34.1 %copy-start.99 = (bf16[1,768,1536]{2,1,0:T(8,128)(2,1)S(1)}, bf16[1,768,1536]{2,1,0:T(8,128)(2,1)}, u32[]{:S(2)}) copy-start(bf16[1,768,1536]{2,1,0:T(8,128)(2,1)} %param.32) | copy-start | bytes 7077892
  543.3 65.1 %all-to-all-start.1 = ((bf16[16,1,128,768]{3,2,1,0:T(8,128)(2,1)}), bf16[16,1,128,768]{3,2,1,0:T(8,128)(2,1)}, u32[]{:S(2)}, u32[]{:S(2)}) async-start(bf16[16,1,128,768]{3,2,1,0:T(8,128)(2,1)} %get-tuple-element.385), calls=%async_computation.4 | async-start | bytes 6291456 | tf_op jit(solution)/shard_map/all_to_all | solution.py:296
  548.3 68.1 %reduce-scatter.17.cloned.1.call-start = ((), (), s32[]{:S(2)}) async-start(), calls=%async_computation.21 | async-start | bytes 2359296 | tf_op jit(solution)/shard_map/reduce_scatter | solution.py:30
  556.2 77.7 %reduce-scatter.15.cloned.1.call-start = ((), (), s32[]{:S(2)}) async-start(), calls=%async_computation.19 | async-start | bytes 2359296 | tf_op jit(solution)/shard_map/reduce_scatter | solution.py:30
  616.3 22.2 %copy-start.18 = (bf16[512,768]{1,0:T(8,128)(2,1)S(1)}, bf16[512,768]{1,0:T(8,128)(2,1)}, u32[]{:S(2)}) copy-start(bf16[512,768]{1,0:T(8,128)(2,1)} %param.35) | copy-start | bytes 2359300
  616.3 34.5 %all-gather.19.cloned.1.call-start = ((), (), s32[]{:S(2)}) async-start(), calls=%async_computation.22 | async-start | bytes 2359296 | tf_op jit(solution)/shard_map/all_gather | solution.py:26
  637.3 16.8 %copy-start.23 = (s32[1024]{0:T(1024)S(1)}, s32[1024]{0:T(1024)}, u32[]{:S(2)}) copy-start(s32[1024]{0:T(1024)} %copy-done.22) | copy-start | bytes 12292
  637.3 16.8 %copy-start.44 = (f32[2,6,512,1]{2,1,3,0:T(8,128)S(1)}, f32[2,6,512,1]{2,1,3,0:T(8,128)}, u32[]{:S(2)}) copy-start(f32[2,6,512,1]{2,1,3,0:T(8,128)} %copy-done.43) | copy-start | bytes 73732
  637.4 16.8 %copy-start.86 = (f32[512]{0:T(512)}, f32[512]{0:T(512)S(1)}, u32[]{:S(2)}) copy-start(f32[512]{0:T(512)S(1)} %negate_multiply_fusion.5) | copy-start | bytes 6148
  639.7 105.1 %reduce-scatter.19.cloned.1.call-start = ((), (), s32[]{:S(2)}) async-start(), calls=%async_computation.23 | async-start | bytes 2359296 | tf_op jit(solution)/shard_map/reduce_scatter | solution.py:30
  728.7 16.0 %copy-start.51 = (f32[768]{0:T(1024)S(1)}, f32[768]{0:T(1024)}, u32[]{:S(2)}) copy-start(f32[768]{0:T(1024)} %get-tuple-element.295) | copy-start | bytes 9220
  728.7 16.0 %copy-start.58 = (f32[512]{0:T(512)S(1)}, f32[512]{0:T(512)}, u32[]{:S(2)}) copy-start(f32[512]{0:T(512)} %copy-done.57) | copy-start | bytes 6148
  728.7 18.2 %copy-start.83 = (f32[512]{0:T(512)S(1)}, f32[512]{0:T(512)}, u32[]{:S(2)}) copy-start(f32[512]{0:T(512)} %copy-done.82) | copy-start | bytes 6148
  728.7 18.3 %copy-start.71 = (f32[512]{0:T(512)S(1)}, f32[512]{0:T(512)}, u32[]{:S(2)}) copy-start(f32[512]{0:T(512)} %copy-done.70) | copy-start | bytes 6148
  734.3 15.8 %copy-start.19 = (bf16[512,768]{1,0:T(8,128)(2,1)S(1)}, bf16[512,768]{1,0:T(8,128)(2,1)}, u32[]{:S(2)}) copy-start(bf16[512,768]{1,0:T(8,128)(2,1)} %param.35) | copy-start | bytes 2359300
  734.4 15.8 %copy-start.87 = (f32[512]{0:T(512)S(1)}, f32[512]{0:T(512)}, u32[]{:S(2)}) copy-start(f32[512]{0:T(512)} %copy-done.86) | copy-start | bytes 6148
  734.4 29.3 %all-gather.21.cloned.1.call-start = ((), (), s32[]{:S(2)}) async-start(), calls=%async_computation.24 | async-start | bytes 2359296 | tf_op jit(solution)/shard_map/all_gather | solution.py:26
  752.5 36.8 %reduce-scatter.21.cloned.1.call-start = ((), (), s32[]{:S(2)}) async-start(), calls=%async_computation.25 | async-start | bytes 2359296 | tf_op jit(solution)/shard_map/reduce_scatter | solution.py:30
  775.2 14.2 copy-start.46
  775.2 14.2 copy-start.53
  775.2 16.2 %copy-start.81 = (f32[512]{0:T(512)S(1)}, f32[512]{0:T(512)}, u32[]{:S(2)}) copy-start(f32[512]{0:T(512)} %copy-done.80) | copy-start | bytes 6148
  775.2 16.3 %copy-start.62 = (f32[512]{0:T(512)S(1)}, f32[512]{0:T(512)}, u32[]{:S(2)}) copy-start(f32[512]{0:T(512)} %copy-done.61) | copy-start | bytes 6148
  778.9 28.3 %all-gather.23.cloned.1.call-start = ((), (), s32[]{:S(2)}) async-start(), calls=%async_computation.26 | async-start | bytes 2359296 | tf_op jit(solution)/shard_map/all_gather | solution.py:26
  796.1 167.1 %reduce-scatter.23.cloned.1.call-start = ((), (), s32[]{:S(2)}) async-start(), calls=%async_computation.27 | async-start | bytes 2359296 | tf_op jit(solution)/shard_map/reduce_scatter | solution.py:30
  892.4 535.6 %all-reduce.4.cloned.1.call-start = ((), (), s32[]{:S(2)}) async-start(), calls=%async_computation.28 | async-start | bytes 37748736 | tf_op jit(solution)/shard_map/psum | solution.py:325
  928.1 34.9 %copy-start.88 = (f32[768]{0:T(1024)S(1)}, f32[768]{0:T(1024)}, u32[]{:S(2)}) copy-start(f32[768]{0:T(1024)} %get-tuple-element.290) | copy-start | bytes 9220
  928.1 35.0 %copy-start.89 = (f32[768]{0:T(1024)S(1)}, f32[768]{0:T(1024)}, u32[]{:S(2)}) copy-start(f32[768]{0:T(1024)} %get-tuple-element.288) | copy-start | bytes 9220
  928.1 35.0 %copy-start.90 = (f32[768]{0:T(1024)S(1)}, f32[768]{0:T(1024)}, u32[]{:S(2)}) copy-start(f32[768]{0:T(1024)} %get-tuple-element.286) | copy-start | bytes 9220
  928.2 35.0 %copy-start.5 = (bf16[512,768]{1,0:T(8,128)(2,1)S(1)}, bf16[512,768]{1,0:T(8,128)(2,1)}, u32[]{:S(2)}) copy-start(bf16[512,768]{1,0:T(8,128)(2,1)} %param.22) | copy-start | bytes 2359300
  928.2 35.0 %copy-start.49 = (f32[768]{0:T(1024)S(1)}, f32[768]{0:T(1024)}, u32[]{:S(2)}) copy-start(f32[768]{0:T(1024)} %copy-done.48) | copy-start | bytes 9220
  928.2 35.0 %copy-start.56 = (f32[512]{0:T(512)S(1)}, f32[512]{0:T(512)}, u32[]{:S(2)}) copy-start(f32[512]{0:T(512)} %copy-done.55) | copy-start | bytes 6148
  928.2 36.6 %copy-start.79 = (f32[512]{0:T(512)S(1)}, f32[512]{0:T(512)}, u32[]{:S(2)}) copy-start(f32[512]{0:T(512)} %copy-done.78) | copy-start | bytes 6148
  928.2 36.6 %copy-start.69 = (f32[512]{0:T(512)S(1)}, f32[512]{0:T(512)}, u32[]{:S(2)}) copy-start(f32[512]{0:T(512)} %copy-done.68) | copy-start | bytes 6148
  928.2 124.2 %copy-start.47 = (f32[768]{0:T(1024)S(1)}, f32[768]{0:T(1024)}, u32[]{:S(2)}) copy-start(f32[768]{0:T(1024)} %copy-done.45) | copy-start | bytes 9220
  928.2 124.2 %copy-start.54 = (f32[512]{0:T(512)S(1)}, f32[512]{0:T(512)}, u32[]{:S(2)}) copy-start(f32[512]{0:T(512)} %copy-done.52) | copy-start | bytes 6148
  928.2 124.2 %copy-start.63 = (f32[512]{0:T(512)S(1)}, f32[512]{0:T(512)}, u32[]{:S(2)}) copy-start(f32[512]{0:T(512)} %copy-done.61) | copy-start | bytes 6148
  928.2 124.2 %copy-start.67 = (f32[512]{0:T(512)S(1)}, f32[512]{0:T(512)}, u32[]{:S(2)}) copy-start(f32[512]{0:T(512)} %copy-done.66) | copy-start | bytes 6148
  928.2 124.2 %copy-start.77 = (f32[512]{0:T(512)S(1)}, f32[512]{0:T(512)}, u32[]{:S(2)}) copy-start(f32[512]{0:T(512)} %copy-done.76) | copy-start | bytes 6148
  (80 other events, 315.7 us)
Sparse Core Ops, SparseCore 0:
  14.6 12.4 all-gather.8
  78.5 10.2 reduce-scatter.8
  95.4 10.9 all-gather.10
  130.1 10.2 reduce-scatter.10
  145.1 10.9 all-gather.12
  202.9 10.1 reduce-scatter.12
  217.9 11.0 all-gather.14
  246.4 11.0 all-gather.16
  556.3 10.2 reduce-scatter.16
  616.4 17.4 reduce-scatter.14
  639.8 10.9 all-gather.18
  734.5 10.2 reduce-scatter.18
  752.7 10.9 all-gather.20
  779.1 10.2 reduce-scatter.20
  796.2 11.0 all-gather.22
  892.5 10.2 reduce-scatter.22
  915.2 512.6 all-reduce.3
where the time goes:
time: 1470 us; the launch traced here: 1460 us
  waiting for transfers between devices  668 us (45%)
  matrix products  339 us (23%)
  blocking collectives  170 us (12%)
  local copies, waits for them, and re-layouts  108 us (7%)
  other arithmetic  105 us (7%)
  starting transfers between devices  29.6 us (2%)
  loops' own time  19.4 us (1%)
  between operations  15.7 us (1%)
    psum x1, waiting for transfers between devices, body(): lax.psum((qkv_first, out_first, up_first, down_first, gain_grads), 'dp')  372 us
    all_gather x8, waiting for transfers between devices, gather_rows(): return lax.all_gather(pieces, 'head', axis=0, tiled=True)  90 us
    all_to_all x2, waiting for transfers between devices, send_all(): return lax.all_to_all(buffer, 'dp', split_axis=0, concat_axis=0, tiled=True)  87.1 us
    all_to_all x1, blocking collectives, return_all(): lax.all_to_all(buffer.astype(jnp.bfloat16), 'dp', split_axis=0, concat_ax...  84.7 us
    psum x1, blocking collectives, body(): lax.psum((qkv_first, out_first, up_first, down_first, gain_grads), 'dp')  81.5 us
    reduce_scatter x8, waiting for transfers between devices, sum_rows(): lax.psum_scatter(term_fn(jnp.int32(0), row_count * lax.axis_size('head'))...  66 us
    all_to_all x1, waiting for transfers between devices, return_all(): lax.all_to_all(buffer.astype(jnp.bfloat16), 'dp', split_axis=0, concat_ax...  52.1 us
    dot_general x1, matrix products, expert_forward(): jnp.einsum('nesf,efd->nesd', active, down_weight, preferred_element_type=...  36.7 us
  transfers between devices with their start and end apart: 20, of which 18 were waited for; matrix products, arithmetic and copies ran while one was open for 8% of the time, Pallas kernels for 0%

commit v1 on v0

v1 whole, which is shorter than its diff:
```python
import functools

import jax
import jax.numpy as jnp
from jax import lax
from jax.experimental import pallas as pl
from jax.experimental.pallas import tpu as pltpu
from jax.sharding import PartitionSpec as P

BF = jnp.bfloat16
F32 = jnp.float32
EPS = 1e-05
MASKED = -1e30
BLK = 256
HEAD_DIM = 64
SWAP = [(0, 1), (1, 0)]
VLIM = 56 * 1024 * 1024


def mm(a, b):
    return lax.dot_general(a, b, (((1,), (0,)), ((), ())), preferred_element_type=F32)


def mm_nt(a, b):
    return lax.dot_general(a, b, (((1,), (1,)), ((), ())), preferred_element_type=F32)


def mm_tn(a, b):
    return lax.dot_general(a, b, (((0,), (0,)), ((), ())), preferred_element_type=F32)


def norm_stats(x):
    c = x - jnp.mean(x, axis=-1, keepdims=True)
    r = lax.rsqrt(jnp.mean(c * c, axis=-1, keepdims=True) + EPS)
    return c * r, r


def norm_back(x, gain, dn):
    xh, r = norm_stats(x)
    dxh = dn * gain
    a = jnp.mean(dxh, axis=-1, keepdims=True)
    b = jnp.mean(dxh * xh, axis=-1, keepdims=True)
    return r * (dxh - a - xh * b), jnp.sum(dn * xh, axis=0, keepdims=True)


def gelu_pair(u):
    z = jnp.abs(u) * 0.7071067811865476
    t = 1.0 / (1.0 + 0.3275911 * z)
    ex = jnp.exp(-(z * z))
    poly = t * (
        0.254829592
        + t * (-0.284496736 + t * (1.421413741 + t * (-1.453152027 + t * 1.061405429)))
    )
    tail = 0.5 * poly * ex
    phi = jnp.where(u >= 0.0, 1.0 - tail, tail)
    return u * phi, phi + u * (ex * 0.3989422804014327)


def mask_bias(segc, segr, b, keys):
    row = lax.broadcasted_iota(jnp.int32, (BLK, keys), 0) + b * BLK
    col = lax.broadcasted_iota(jnp.int32, (BLK, keys), 1)
    return jnp.where((segc == segr[:, :keys]) & (col <= row), 0.0, MASKED)


def half_lane(hh):
    lane = lax.broadcasted_iota(jnp.int32, (BLK, 128), 1)
    return (lane >= 64) if hh else (lane < 64)


def attn_fwd_kernel(blocks, split, h_ref, *refs):
    if split:
        own, peer, g, wqkv, wo, segc, segr = refs[:7]
        outs = refs[7:]
    else:
        xr, pa, pb, g, wqkv, wo, segc, segr = refs[:8]
        outs = refs[8:]
    x_out, n_out, qkv_out, o_out, lse_out, p_out, ks, vs = outs
    i = pl.program_id(0)
    if split:
        mine = (i // (blocks // 2)) == h_ref[0]
        x = jnp.where(mine, own[...].astype(F32), peer[...].astype(F32))
    else:
        x = xr[...] + pa[...].astype(F32) + pb[...].astype(F32)
    x_out[...] = x
    xh, _ = norm_stats(x)
    n = (xh * g[...]).astype(BF)
    n_out[...] = n
    q = (mm(n, wqkv[0]).astype(BF).astype(F32) * 0.125).astype(BF)
    k = mm(n, wqkv[1]).astype(BF)
    v = mm(n, wqkv[2]).astype(BF)
    qkv_out[0] = q
    qkv_out[1] = k
    qkv_out[2] = v
    rows = pl.ds(pl.multiple_of(i * BLK, BLK), BLK)
    ks[rows, :] = k
    vs[rows, :] = v
    pairs = q.shape[1] // 128
    for b in range(blocks):

        @pl.when(i == b)
        def _(b=b):
            keys = BLK * (b + 1)
            bias = mask_bias(segc[...], segr[...], b, keys)
            lse = jnp.zeros((BLK, 128), F32)
            lanes = lax.broadcasted_iota(jnp.int32, (BLK, 128), 1)
            total = jnp.zeros((BLK, wo.shape[1]), F32)
            for pr in range(pairs):
                cols = slice(pr * 128, pr * 128 + 128)
                qp = qkv_out[0, :, cols]
                kp = ks[0:keys, cols]
                vp = vs[0:keys, cols]
                res = []
                for hh in range(2):
                    qh = jnp.where(half_lane(hh), qp, jnp.zeros_like(qp))
                    s = mm_nt(qh, kp) + bias
                    m = jnp.max(s, axis=-1, keepdims=True)
                    e = jnp.exp(s - m)
                    l = jnp.sum(e, axis=-1, keepdims=True)
                    res.append(mm(e.astype(BF), vp) * (1.0 / l))
                    lse = jnp.where(lanes == pr * 2 + hh, m + jnp.log(l), lse)
                ob = jnp.where(half_lane(0), res[0], res[1]).astype(BF)
                o_out[:, cols] = ob
                total = total + mm(ob, wo[cols, :])
            lse_out[...] = lse
            p_out[...] = total.astype(BF)


def attn_bwd_kernel(blocks, split, h_ref, *refs):
    if split:
        dro, drp, dno, dnp_ = refs[:4]
    else:
        drr, dna, dnb = refs[:3]
    rest = refs[4 if split else 3 :]
    xn, gn, qr, kf, vf, orf, lser, wqkv, wo, segc, segr = rest[:11]
    dr_out, da_out, dqkv_out, dn_out, dg_out, dks, dvs = rest[11:]
    i = pl.program_id(0)
    blk = blocks - 1 - i
    if split:
        mine = (blk // (blocks // 2)) == h_ref[0]
        dr = jnp.where(mine, dro[...].astype(F32), drp[...].astype(F32))
        dn = jnp.where(mine, dno[...].astype(F32), dnp_[...].astype(F32))
    else:
        dr = drr[...]
        dn = dna[...].astype(F32) + dnb[...].astype(F32)
    dx, dg = norm_back(xn[...], gn[...], dn)
    dr = dr + dx
    dr_out[...] = dr
    da = dr.astype(BF)
    da_out[...] = da

    @pl.when(i == 0)
    def _():
        dks[...] = jnp.zeros_like(dks)
        dvs[...] = jnp.zeros_like(dvs)
        dg_out[...] = jnp.zeros_like(dg_out)

    dg_out[...] += jnp.broadcast_to(dg, dg_out.shape)
    do = mm_nt(da, wo[...]).astype(BF)
    pairs = wo.shape[0] // 128
    for b in range(blocks):

        @pl.when(blk == b)
        def _(b=b):
            keys = BLK * (b + 1)
            here = slice(b * BLK, b * BLK + BLK)
            bias = mask_bias(segc[...], segr[...], b, keys)
            lse = lser[...]
            for pr in range(pairs):
                cols = slice(pr * 128, pr * 128 + 128)
                qp = qr[0, :, cols]
                kp = kf[0, 0:keys, cols]
                vp = vf[0, 0:keys, cols]
                dop = do[:, cols]
                prod = dop.astype(F32) * orf[:, cols].astype(F32)
                dqs, dss, ps, qs, dos = [], [], [], [], []
                for hh in range(2):
                    hm = half_lane(hh)
                    qh = jnp.where(hm, qp, jnp.zeros_like(qp))
                    doh = jnp.where(hm, dop, jnp.zeros_like(dop))
                    delta = jnp.sum(jnp.where(hm, prod, 0.0), axis=-1, keepdims=True)
                    h = pr * 2 + hh
                    p = jnp.exp(mm_nt(qh, kp) + bias - lse[:, h : h + 1])
                    dp = mm_nt(doh, vp)
                    ds = (p * (dp - delta)).astype(BF)
                    dqs.append(mm(ds, kp))
                    dks[0:keys, cols] += mm_tn(ds, qh)
                    dvs[0:keys, cols] += mm_tn(p.astype(BF), doh)
                dq = jnp.where(half_lane(0), dqs[0], dqs[1]) * 0.125
                dqkv_out[0, :, cols] = dq.astype(BF)
            dqkv_out[1] = dks[here, :].astype(BF)
            dqkv_out[2] = dvs[here, :].astype(BF)

    dn_out[...] = (
        mm_nt(dqkv_out[0], wqkv[0]) + mm_nt(dqkv_out[1], wqkv[1]) + mm_nt(dqkv_out[2], wqkv[2])
    ).astype(BF)


def dense_fwd_kernel(xr, pa, pb, g, up, down, x_out, n_out, act_out, gp_out, p_out):
    x = xr[...] + pa[...].astype(F32) + pb[...].astype(F32)
    x_out[...] = x
    xh, _ = norm_stats(x)
    n = (xh * g[...]).astype(BF)
    n_out[...] = n
    act, gp = gelu_pair(mm(n, up[...]))
    act = act.astype(BF)
    act_out[...] = act
    gp_out[...] = gp.astype(BF)
    p_out[...] = mm(act, down[...]).astype(BF)


def dense_bwd_kernel(drr, dna, dnb, xn, gn, gp, up, down, dr_out, df_out, du_out, dn_out, dg_out):
    dx, dg = norm_back(xn[...], gn[...], dna[...].astype(F32) + dnb[...].astype(F32))
    dr = drr[...] + dx
    dr_out[...] = dr
    df = dr.astype(BF)
    df_out[...] = df

    @pl.when(pl.program_id(0) == 0)
    def _():
        dg_out[...] = jnp.zeros_like(dg_out)

    dg_out[...] += jnp.broadcast_to(dg, dg_out.shape)
    du = (mm_nt(df, down[...]) * gp[...].astype(F32)).astype(BF)
    du_out[...] = du
    dn_out[...] = mm_nt(du, up[...]).astype(BF)


def final_kernel(h_ref, drr, dna, dnb, xo, xp, gn, dr_out, dg_out):
    i = pl.program_id(0)
    mine = i >= 2
    x = jnp.where(mine, xo[...].astype(F32), xp[...].astype(F32))
    dx, dg = norm_back(x, gn[...], dna[...].astype(F32) + dnb[...].astype(F32))
    dr_out[...] = drr[...] + dx

    @pl.when(i == 0)
    def _():
        dg_out[...] = jnp.zeros_like(dg_out)

    dg_out[...] += jnp.broadcast_to(dg, dg_out.shape)


def spread_kernel(rows_ref, slot_ref, out_ref):
    count = out_ref.shape[0]
    place = lax.broadcasted_iota(jnp.int32, (count, rows_ref.shape[0]), 0)
    place = place + pl.program_id(0) * count
    hot = (place == slot_ref[...]).astype(F32).astype(BF)
    out_ref[...] = mm(hot, rows_ref[...]).astype(BF)


def route_kernel(h_ref, xr, pa, pb, g, slot_ref, x_out, send_out, ms):
    i = pl.program_id(0)
    x = xr[...] + pa[...].astype(F32) + pb[...].astype(F32)
    x_out[...] = x

    @pl.when(i >= 2)
    def _():
        xh, _ = norm_stats(x)
        rows = pl.ds(pl.multiple_of((i - 2) * BLK, BLK), BLK)
        ms[rows, :] = (xh * g[...]).astype(BF)

    @pl.when(i == 3)
    def _():
        count = send_out.shape[0]
        place = lax.broadcasted_iota(jnp.int32, (count, ms.shape[0]), 0)
        hot = (place == slot_ref[...]).astype(F32).astype(BF)
        send_out[...] = mm(hot, ms[...]).astype(BF)


def collect_kernel(table, slot_ref, out_ref):
    count = table.shape[0]
    place = lax.broadcasted_iota(jnp.int32, (out_ref.shape[0], count), 1)
    hot = (place == slot_ref[...]).astype(F32).astype(BF)
    out_ref[...] = mm(hot, table[...]).astype(BF)


def collect_add_kernel(h_ref, table, slot_ref, x_ref, out_ref):
    count = table.shape[0]
    place = lax.broadcasted_iota(jnp.int32, (out_ref.shape[0], count), 1)
    hot = (place == slot_ref[...]).astype(F32).astype(BF)
    out_ref[...] = (x_ref[...] + mm(hot, table[...])).astype(BF)


def expert_kernel(
    half, mo, mp, go, gp_, cen, up, down,
    yo, yp, dmo, dmp, m_all, dy_all, ae_all, due_all, dc_out,
):
    i = pl.program_id(0)
    first = i < half
    m = jnp.where(first, mo[...], mp[...])
    gb = jnp.where(first, go[...], gp_[...]).astype(F32)
    mf = m.astype(F32)
    cf = cen[...].astype(F32)
    gate = jax.nn.sigmoid(jnp.sum(mf * cf, axis=-1, keepdims=True))
    act, gd = gelu_pair(mm(m, up[0]))
    act = act.astype(BF)
    y = mm(act, down[0])
    dscore = jnp.sum(gb * y, axis=-1, keepdims=True) * gate * (1.0 - gate)
    dy = (gate * gb).astype(BF)
    due = (mm_nt(dy, down[0]) * gd).astype(BF)
    dm = (mm_nt(due, up[0]) + dscore * cf).astype(BF)
    gy = (gate * y).astype(BF)
    m_all[...] = m
    dy_all[...] = dy
    ae_all[...] = act
    due_all[...] = due

    @pl.when(i == 0)
    def _():
        dc_out[...] = jnp.zeros_like(dc_out)

    dc_out[...] += jnp.broadcast_to(jnp.sum(dscore * mf, axis=0, keepdims=True), dc_out.shape)

    @pl.when(first)
    def _():
        yo[...] = gy
        dmo[...] = dm

    @pl.when(jnp.logical_not(first))
    def _():
        yp[...] = gy
        dmp[...] = dm


def shape(dims, kind):
    return jax.ShapeDtypeStruct(dims, kind)


def fixed(dims):
    zero = (0,) * len(dims)
    return pl.BlockSpec(dims, lambda *a: zero, pipeline_mode=pl.Buffered(1))


def rows_spec(width, index=lambda i: i):
    return pl.BlockSpec((BLK, width), lambda i, *a: (index(i), 0))


PARAMS = pltpu.CompilerParams(vmem_limit_bytes=VLIM, dimension_semantics=("arbitrary",))


def call(kernel, grid, in_specs, out_specs, outs, scratch, flops, moved, args, prefetch=None):
    cost = pl.CostEstimate(flops=int(flops), bytes_accessed=int(moved), transcendentals=0)
    if prefetch is None:
        spec = pl.GridSpec(
            grid=grid, in_specs=in_specs, out_specs=out_specs, scratch_shapes=scratch
        )
    else:
        spec = pltpu.PrefetchScalarGridSpec(
            num_scalar_prefetch=1,
            grid=grid,
            in_specs=in_specs,
            out_specs=out_specs,
            scratch_shapes=scratch,
        )
        args = (prefetch,) + tuple(args)
    return pl.pallas_call(
        kernel, grid_spec=spec, out_shape=outs, compiler_params=PARAMS, cost_estimate=cost
    )(*args)


def attention_forward(h, inputs, split, gain, wqkv, wo, segc, segr):
    length, d = segc.shape[0], wqkv.shape[1]
    c = wqkv.shape[2]
    blocks = length // BLK
    if split:
        ins = [rows_spec(d, lambda i: i % (blocks // 2))] * 2
    else:
        ins = [rows_spec(d)] * 3
    ins += [
        fixed((1, d)),
        fixed((3, d, c)),
        fixed((c, d)),
        pl.BlockSpec((BLK, 1), lambda i, *a: (i, 0)),
        fixed((1, length)),
    ]
    outs = [
        (rows_spec(d), shape((length, d), F32)),
        (rows_spec(d), shape((length, d), BF)),
        (pl.BlockSpec((3, BLK, c), lambda i, *a: (0, i, 0)), shape((3, length, c), BF)),
        (rows_spec(c), shape((length, c), BF)),
        (rows_spec(128), shape((length, 128), F32)),
        (rows_spec(d), shape((length, d), BF)),
    ]
    scratch = [pltpu.VMEM((length, c), BF), pltpu.VMEM((length, c), BF)]
    flops = 2 * length * d * c * 4 + 4 * length * length * c
    return call(
        functools.partial(attn_fwd_kernel, blocks, split),
        (blocks,),
        ins,
        [o[0] for o in outs],
        [o[1] for o in outs],
        scratch,
        flops * 2,
        length * d * 20,
        (*inputs, gain, wqkv, wo, segc, segr),
        prefetch=h,
    )


def attention_backward(h, inputs, split, xn, gn, saved, wqkv, wo, segc, segr):
    qkv, o, lse = saved
    length, d = segc.shape[0], wqkv.shape[1]
    c = wqkv.shape[2]
    blocks = length // BLK
    back = lambda i: blocks - 1 - i
    if split:
        ins = [rows_spec(d, lambda i: back(i) % (blocks // 2))] * 4
    else:
        ins = [rows_spec(d, back)] * 3
    part = lambda n: pl.BlockSpec(
        (1, length, c), lambda i, *a: (n, 0, 0), pipeline_mode=pl.Buffered(1)
    )
    ins += [
        rows_spec(d, back),
        fixed((1, d)),
        pl.BlockSpec((1, BLK, c), lambda i, *a: (0, back(i), 0)),
        part(1),
        part(2),
        rows_spec(c, back),
        rows_spec(128, back),
        fixed((3, d, c)),
        fixed((c, d)),
        pl.BlockSpec((BLK, 1), lambda i, *a: (back(i), 0)),
        fixed((1, length)),
    ]
    outs = [
        (rows_spec(d, back), shape((length, d), F32)),
        (rows_spec(d, back), shape((length, d), BF)),
        (pl.BlockSpec((3, BLK, c), lambda i, *a: (0, back(i), 0)), shape((3, length, c), BF)),
        (rows_spec(d, back), shape((length, d), BF)),
        (fixed((8, d)), shape((8, d), F32)),
    ]
    scratch = [pltpu.VMEM((length, c), F32), pltpu.VMEM((length, c), F32)]
    flops = 2 * length * d * c * 4 + 10 * length * length * c
    return call(
        functools.partial(attn_bwd_kernel, blocks, split),
        (blocks,),
        ins,
        [s[0] for s in outs],
        [s[1] for s in outs],
        scratch,
        flops * 2,
        length * d * 20,
        (*inputs, xn, gn, qkv, qkv, qkv, o, lse, wqkv, wo, segc, segr),
        prefetch=h,
    )


def dense_forward(x, pa, pb, gain, up, down):
    length, d = x.shape
    f = up.shape[1]
    return call(
        dense_fwd_kernel,
        (length // BLK,),
        [rows_spec(d)] * 3 + [fixed((1, d)), fixed((d, f)), fixed((f, d))],
        [rows_spec(d), rows_spec(d), rows_spec(f), rows_spec(f), rows_spec(d)],
        [
            shape((length, d), F32),
            shape((length, d), BF),
            shape((length, f), BF),
            shape((length, f), BF),
            shape((length, d), BF),
        ],
        [],
        4 * length * d * f,
        length * d * 20 + 4 * d * f,
        (x, pa, pb, gain, up, down),
    )


def dense_backward(dr, dna, dnb, xn, gn, gp, up, down):
    length, d = dr.shape
    f = up.shape[1]
    return call(
        dense_bwd_kernel,
        (length // BLK,),
        [rows_spec(d)] * 4
        + [fixed((1, d)), rows_spec(f), fixed((d, f)), fixed((f, d))],
        [rows_spec(d), rows_spec(d), rows_spec(f), rows_spec(d), fixed((8, d))],
        [
            shape((length, d), F32),
            shape((length, d), BF),
            shape((length, f), BF),
            shape((length, d), BF),
            shape((8, d), F32),
        ],
        [],
        4 * length * d * f,
        length * d * 20 + 4 * d * f,
        (dr, dna, dnb, xn, gn, gp, up, down),
    )


def own_last(blocks):
    return lambda i, h: lax.rem(i + (blocks // 2) * (1 - h[0]), blocks)


def final_step(h, dr, dna, dnb, xo, xp, gn):
    length, d = dr.shape
    blocks = length // BLK
    place = own_last(blocks)
    spec = pl.BlockSpec((BLK, d), lambda i, h: (place(i, h), 0))
    late = lambda i, h: (jnp.maximum(i - blocks // 2, 0), 0)
    return call(
        final_kernel,
        (blocks,),
        [spec] * 3
        + [pl.BlockSpec((BLK, d), late)]
        + [pl.BlockSpec((BLK, d), lambda i, h: (lax.rem(i, blocks // 2), 0)), fixed((1, d))],
        [pl.BlockSpec((BLK, d), late), fixed((8, d))],
        [shape((length // 2, d), F32), shape((8, d), F32)],
        [],
        length * d * 40,
        length * d * 14,
        (dr, dna, dnb, xo, xp, gn),
        prefetch=h,
    )


def route_step(h, x, pa, pb, gain, slot_row, slots):
    length, d = x.shape
    blocks = length // BLK
    place = own_last(blocks)
    spec = pl.BlockSpec((BLK, d), lambda i, h: (place(i, h), 0))
    return call(
        route_kernel,
        (blocks,),
        [spec] * 3 + [fixed((1, d)), fixed((1, length // 2))],
        [spec, fixed((slots, d))],
        [shape((length, d), F32), shape((slots, d), BF)],
        [pltpu.VMEM((length // 2, d), BF)],
        length * slots * d,
        length * d * 14,
        (x, pa, pb, gain, slot_row),
        prefetch=h,
    )


def spread(rows, slot_row, slots):
    count, d = rows.shape
    return call(
        spread_kernel,
        (slots // BLK,),
        [fixed((count, d)), fixed((1, count))],
        [rows_spec(d)],
        [shape((slots, d), BF)],
        [],
        2 * count * slots * d,
        4 * slots * d,
        (rows, slot_row),
    )[0]


def collect(table, slot_col):
    slots, d = table.shape
    count = slot_col.shape[0]
    return call(
        collect_kernel,
        (count // BLK,),
        [fixed((slots, d)), pl.BlockSpec((BLK, 1), lambda i, *a: (i, 0))],
        [rows_spec(d)],
        [shape((count, d), BF)],
        [],
        2 * count * slots * d,
        4 * slots * d,
        (table, slot_col),
    )[0]


def collect_add(h, table, slot_col, x):
    slots, d = table.shape
    count = slot_col.shape[0]
    per = count // BLK
    return call(
        collect_add_kernel,
        (per,),
        [
            fixed((slots, d)),
            pl.BlockSpec((BLK, 1), lambda i, *a: (i, 0)),
            pl.BlockSpec((BLK, d), lambda i, h: (h[0] * per + i, 0)),
        ],
        [rows_spec(d)],
        [shape((count, d), BF)],
        [],
        2 * count * slots * d,
        8 * slots * d,
        (table, slot_col, x),
        prefetch=h,
    )[0]


def expert_step(mo, mp, go, gp, cen, up, down):
    rows, d = mo.shape
    f = up.shape[2]
    half = rows // BLK
    lo = lambda i: jnp.minimum(i, half - 1)
    hi = lambda i: jnp.maximum(i - half, 0)
    return call(
        functools.partial(expert_kernel, half),
        (2 * half,),
        [rows_spec(d, lo), rows_spec(d, hi), rows_spec(d, lo), rows_spec(d, hi)]
        + [fixed((1, d)), fixed((1, d, f)), fixed((1, f, d))],
        [rows_spec(d, lo), rows_spec(d, hi), rows_spec(d, lo), rows_spec(d, hi)]
        + [rows_spec(d), rows_spec(d), rows_spec(f), rows_spec(f), fixed((8, d))],
        [shape((rows, d), BF)] * 4
        + [shape((2 * rows, d), BF)] * 2
        + [shape((2 * rows, f), BF)] * 2
        + [shape((8, d), F32)],
        [],
        16 * rows * d * f,
        rows * d * 24 + rows * f * 8,
        (mo, mp, go, gp, cen, up, down),
    )


def slot_index(chosen, capacity, experts):
    rows = chosen.shape[0]
    matches = chosen[:, None] == jnp.arange(experts, dtype=jnp.int32)[None, :]
    position = jnp.arange(rows, dtype=jnp.int32)
    earlier = (position[None, :] < position[:, None]).astype(BF)
    before = jnp.dot(earlier, matches.astype(BF), preferred_element_type=F32)
    rank = jnp.sum(jnp.where(matches, before, 0.0), axis=1).astype(jnp.int32)
    return chosen * capacity + rank


def swap(v):
    return lax.ppermute(v, "head", SWAP)


def exchange_half(v, bit, pairs):
    half = v.shape[0] // 2
    out = lax.dynamic_slice_in_dim(v, (1 - bit) * half, half, 0)
    return lax.dynamic_slice_in_dim(v, bit * half, half, 0) + lax.ppermute(out, "dp", pairs)


def regather(v, bit, pairs):
    other = lax.ppermute(v, "dp", pairs)
    both = jnp.concatenate([v, v], axis=0)
    return lax.dynamic_update_slice_in_dim(both, other, (1 - bit) * v.shape[0], 0)


def reduce_all(v, steps):
    if steps is None:
        return lax.psum(v, "dp")
    me = lax.axis_index("dp")
    half = v.shape[0] // 2
    pairs = {s: [(i, i ^ s) for i in range(16)] for s in (1, 2, 4, 8)}
    bits = {s: (me // s) % 2 for s in (1, 2, 4, 8)}
    a, b = v[:half], v[half:]
    a, b = exchange_half(a, bits[1], pairs[1]), exchange_half(b, bits[2], pairs[2])
    a, b = exchange_half(a, bits[2], pairs[2]), exchange_half(b, bits[1], pairs[1])
    c = jnp.concatenate([a, b], axis=0)
    c = exchange_half(c, bits[4], pairs[4])
    c = exchange_half(c, bits[8], pairs[8])
    c = regather(c, bits[8], pairs[8])
    c = regather(c, bits[4], pairs[4])
    quarter = c.shape[0] // 2
    a, b = c[:quarter], c[quarter:]
    a, b = regather(a, bits[2], pairs[2]), regather(b, bits[1], pairs[1])
    a, b = regather(a, bits[1], pairs[1]), regather(b, bits[2], pairs[2])
    return jnp.concatenate([a, b], axis=0)


def body(
    steps,
    tokens,
    segment_ids,
    routes,
    norm_gains,
    qkv_one,
    out_one,
    up_one,
    down_one,
    qkv_two,
    out_two,
    expert_up,
    expert_down,
    centroids,
    cotangent,
):
    count, d = tokens.shape
    side = lax.axis_index("head")
    h = side.astype(jnp.int32).reshape(1)
    experts = lax.axis_size("dp") * expert_up.shape[0]
    capacity = 2 * count // experts
    slots = experts * capacity
    gains = norm_gains.astype(F32)
    gain = [gains[j : j + 1] for j in range(4)]
    segc, segr = segment_ids[:, None], segment_ids[None, :]

    chosen = lax.dynamic_slice_in_dim(routes[:, 0], side * count, count, 0)
    flat = slot_index(chosen, capacity, experts)
    slot_row, slot_col = flat[None, :], flat[:, None]

    def travel(v):
        box = v.reshape(experts, capacity, d)
        return lax.all_to_all(box, "dp", 0, 0, tiled=True).reshape(slots, d)

    tokens_peer = swap(tokens)
    x0, n1, qkv1, o1, lse1, p1 = attention_forward(
        h, (tokens, tokens_peer), True, gain[0], qkv_one, out_one, segc, segr
    )
    p1r = swap(p1)
    cot_peer = swap(cotangent)
    grad_own = travel(spread(cotangent, slot_row, slots))
    grad_peer = swap(grad_own)
    x1, n2, act, gp, p2 = dense_forward(x0, p1, p1r, gain[1], up_one, down_one)
    p2r = swap(p2)
    first, n3, qkv2, o2, lse2, p3 = attention_forward(
        h, (x1, p2, p2r), False, gain[2], qkv_two, out_two, segc, segr
    )
    p3r = swap(p3)
    x2, sent = route_step(h, first, p3, p3r, gain[3], slot_row, slots)
    m_own = travel(sent)
    m_peer = swap(m_own)
    yo, yp, dmo, dmp, m_all, dy_all, ae_all, due_all, dc = expert_step(
        m_own, m_peer, grad_own, grad_peer, centroids, expert_up, expert_down
    )
    dm_sum = (dmo.astype(F32) + swap(dmp).astype(F32)).astype(BF)
    dm_own = collect(travel(dm_sum), slot_col)
    dm_peer = swap(dm_own)
    up_grad = mm_tn(m_all, due_all)[None]
    down_grad = mm_tn(ae_all, dy_all)[None]
    dc = dc[:1]
    cen_grad = dc + swap(dc)

    dr2, da2, dqkv2, dn2, dg3 = attention_backward(
        h,
        (cotangent, cot_peer, dm_own, dm_peer),
        True,
        x2,
        gain[3],
        (qkv2, o2, lse2),
        qkv_two,
        out_two,
        segc,
        segr,
    )
    dn2r = swap(dn2)

    def attention_grads(n, dqkv, o, da):
        w = [mm_tn(n, dqkv[j]).astype(BF) for j in range(3)]
        wo = mm_tn(o, da).astype(BF)
        c = wo.shape[0]
        return jnp.concatenate([*w, wo[:, :c], wo[:, c:]], axis=0)

    def split_grads(total):
        total = total.astype(F32)
        c = total.shape[1]
        wo = jnp.concatenate([total[3 * d : 3 * d + c], total[3 * d + c :]], axis=1)
        return total[: 3 * d].reshape(3, d, c), wo

    qkv_second, out_second = split_grads(reduce_all(attention_grads(n3, dqkv2, o2, da2), steps))
    y_sum = (yo.astype(F32) + swap(yp).astype(F32)).astype(BF)
    second = collect_add(h, travel(y_sum), slot_col, x2)

    dr1, df, du, dnd, dg2 = dense_backward(dr2, dn2, dn2r, first, gain[2], gp, up_one, down_one)
    dndr = swap(dnd)
    f = du.shape[1]
    w_up = mm_tn(n2, du).astype(BF)
    w_down = mm_tn(act, df).astype(BF)
    dense_total = jnp.concatenate([w_up[:, : f // 2], w_up[:, f // 2 :], w_down], axis=0)
    dense_total = reduce_all(dense_total, steps).astype(F32)
    up_first = jnp.concatenate([dense_total[:d], dense_total[d : 2 * d]], axis=1)
    down_first = dense_total[2 * d :]

    dr0, da1, dqkv1, dn1, dg1 = attention_backward(
        h,
        (dr1, dnd, dndr),
        False,
        x1,
        gain[1],
        (qkv1, o1, lse1),
        qkv_one,
        out_one,
        segc,
        segr,
    )
    dn1r = swap(dn1)
    input_grad, dg0 = final_step(h, dr0, dn1, dn1r, tokens, tokens_peer, gain[0])
    qkv_first, out_first = split_grads(reduce_all(attention_grads(n1, dqkv1, o1, da1), steps))
    gain_grads = jnp.concatenate([dg0[:1], dg1[:1], dg2[:1], dg3[:1]], axis=0)
    gain_grads = lax.psum(gain_grads, "dp")
    first_own = lax.dynamic_slice_in_dim(first, side * count, count, 0).astype(BF)
    return (
        first_own,
        second,
        input_grad,
        gain_grads,
        qkv_first,
        out_first,
        up_first,
        down_first,
        qkv_second,
        out_second,
        up_grad,
        down_grad,
        cen_grad,
    )


def solution(mesh):
    rows = P(("dp", "head"), None)
    shared = (
        P(None, None, "head"),
        P("head", None),
        P(None, "head"),
        P("head", None),
        P(None, None, "head"),
        P("head", None),
        P("dp", None, "head"),
        P("dp", "head", None),
        P("dp", None),
    )
    steps = 16 if mesh.shape["dp"] == 16 else None
    return jax.shard_map(
        functools.partial(body, steps),
        mesh=mesh,
        in_specs=(rows, P("dp"), P("dp", None), P(), *shared, rows),
        out_specs=(rows, rows, rows, P(), *shared),
        check_vma=False,
    )
```

time: 1470 us -> 675 us (0.46)
  waiting for transfers between devices: 668 us -> 217 us
  matrix products: 339 us -> 35.1 us
  Pallas kernels: 0 us -> 190 us
  blocking collectives: 170 us -> 75.1 us
  local copies, waits for them, and re-layouts: 108 us -> 31.4 us
  other arithmetic: 105 us -> 34.7 us
  starting transfers between devices: 29.6 us -> 78.7 us
  loops' own time: 19.4 us -> 0 us
    psum x1 -> x0, waiting for transfers between devices: 372 us -> none  [body(): lax.psum((qkv_first, out_first, up_first, down_first, gain_grads), 'dp')]
    dot_general x55 -> x13, matrix products: 339 us -> 35.1 us  [the longest x12 34.8 us: mm_tn(): lax.dot_general(a, b, (((0,), (0,)), ((), ())), preferred_element_type=F32)]
    pallas_call x0 -> x12, Pallas kernels: none -> 190 us  [call(): pl.pallas_call(kernel, grid_spec=spec, out_shape=outs, compiler_params=PA...]
    ppermute x0 -> x50, waiting for transfers between devices: none -> 147 us  [the longest x18 68 us: regather(): other = lax.ppermute(v, 'dp', pairs)]
    all_gather x8 -> x0, waiting for transfers between devices: 90 us -> none  [gather_rows(): return lax.all_gather(pieces, 'head', axis=0, tiled=True)]
    all_to_all x1 -> x0, blocking collectives: 84.7 us -> none  [return_all(): lax.all_to_all(buffer.astype(jnp.bfloat16), 'dp', split_axis=0, concat_ax...]
    all_to_all x3 -> x4, waiting for transfers between devices: 139 us -> 69.8 us  [travel(): return lax.all_to_all(box, 'dp', 0, 0, tiled=True).reshape(slots, d)]
    reduce_scatter x8 -> x0, waiting for transfers between devices: 66 us -> none  [sum_rows(): lax.psum_scatter(term_fn(jnp.int32(0), row_count * lax.axis_size('head'))...]
  transfers between devices with their start and end apart: 20 -> 54, of which waited for: 18 -> 31; matrix products, arithmetic and copies ran while one was open for 8% -> 12% of each run, Pallas kernels for 0% -> 18%
where the time goes in v1:
time: 675 us; the launch traced here: 664 us
  waiting for transfers between devices  217 us (32%)
  Pallas kernels  190 us (28%)
  starting transfers between devices  78.7 us (12%)
  blocking collectives  75.1 us (11%)
  matrix products  35.1 us (5%)
  other arithmetic  34.7 us (5%)
  local copies, waits for them, and re-layouts  31.4 us (5%)
    pallas_call x12, Pallas kernels, call(): pl.pallas_call(kernel, grid_spec=spec, out_shape=outs, compiler_params=PA...  190 us
    psum x1, blocking collectives, body(): gain_grads = lax.psum(gain_grads, 'dp')  75.1 us
    all_to_all x4, waiting for transfers between devices, travel(): return lax.all_to_all(box, 'dp', 0, 0, tiled=True).reshape(slots, d)  69.8 us
    ppermute x18, waiting for transfers between devices, regather(): other = lax.ppermute(v, 'dp', pairs)  68 us
    ppermute x18, waiting for transfers between devices, exchange_half(): lax.ppermute(out, 'dp', pairs)  65 us
    dot_general x12, matrix products, mm_tn(): lax.dot_general(a, b, (((0,), (0,)), ((), ())), preferred_element_type=F32)  34.8 us
    all_to_all x4, starting transfers between devices, travel(): return lax.all_to_all(box, 'dp', 0, 0, tiled=True).reshape(slots, d)  29.9 us
    ppermute x18, starting transfers between devices, exchange_half(): lax.ppermute(out, 'dp', pairs)  29.9 us
  transfers between devices with their start and end apart: 54, of which 31 were waited for; matrix products, arithmetic and copies ran while one was open for 12% of the time, Pallas kernels for 18%

profile of v1, /device:TPU:0, one launch (start us, length us, event | category | flops | bytes accessed | tf_op | source)
XLA Modules:
  0.0 664.3 jit_solution(16119363856628111609)
XLA Ops:
  5.2 19.0 %shard_map.237 = (f32[1024,768]{1,0:T(8,128)}, bf16[1024,768]{1,0:T(8,128)(2,1)}, bf16[3,1024,384]{2,1,0:T(8,128)(2,1)}, bf16[1024,384]{1,0:T(8,128)(2,1)}, f32[...) custom-call(s32[1]{0:T(128)} %bitcast.h_ref, bf16[512,768]{1,0:T(8,128)(2,1)} %xo.1, bf16[512,768]{1,0:T(8,128)(2,1)} %copy-done.13, ...), custom_call_target="tpu_custom_call" | custom-call | flops 8053063680 | bytes 15728640 | tf_op jit(solution)/shard_map/pallas_call | solution.py:355
  24.3 3.6 collective-permute-done.1.pb
  29.0 15.3 %shard_map.238 = (f32[1024,768]{1,0:T(8,128)}, bf16[1024,768]{1,0:T(8,128)(2,1)}, bf16[1024,1536]{1,0:T(8,128)(2,1)}, bf16[1024,1536]{1,0:T(8,128)(2,1)}, bf16[1024,768]{1,0:T(8,128)(2,1)}) custom-call(f32[1024,768]{1,0:T(8,128)} %get-tuple-element.58.xr, bf16[1024,768]{1,0:T(8,128)(2,1)} %get-tuple-element.59.pa, bf16[1024,768]{1,0:T(8,128)(2,1)} %copy-done.21, ...), custom_call_target="tpu_custom_call" | custom-call | flops 4831838208 | bytes 20447232 | tf_op jit(solution)/shard_map/pallas_call | solution.py:355
  46.4 3.8 shard_map.241
  50.2 8.2 %all-to-all-start.1 = ((bf16[16,64,768]{2,1,0:T(8,128)(2,1)}), bf16[16,64,768]{2,1,0:T(8,128)(2,1)S(1)}, u32[]{:S(2)}, u32[]{:S(2)}) async-start(bf16[16,64,768]{2,1,0:T(8,128)(2,1)} %bitcast.64), calls=%async_computation.1 | async-start | bytes 3145728 | tf_op jit(solution)/shard_map/all_to_all | solution.py:696
  59.6 19.3 %shard_map.239 = (f32[1024,768]{1,0:T(8,128)}, bf16[1024,768]{1,0:T(8,128)(2,1)}, bf16[3,1024,384]{2,1,0:T(8,128)(2,1)}, bf16[1024,384]{1,0:T(8,128)(2,1)}, f32[...) custom-call(s32[1]{0:T(128)} %bitcast.h_ref, f32[1024,768]{1,0:T(8,128)} %get-tuple-element.60.refs_0_.refs_3_, ...), custom_call_target="tpu_custom_call" | custom-call | flops 8053063680 | bytes 15728640 | tf_op jit(solution)/shard_map/pallas_call | solution.py:355
  79.0 3.6 collective-permute-done.3.pb
  83.7 6.8 %shard_map.240 = (f32[1024,768]{1,0:T(8,128)}, bf16[1024,768]{1,0:T(8,128)(2,1)}) custom-call(s32[1]{0:T(128)} %bitcast.h_ref, f32[1024,768]{1,0:T(8,128)} %get-tuple-element.62.xr.xn, bf16[1024,768]{1,0:T(8,128)(2,1)} %get-tuple-element.63.pa, bf16[1024,768]{1,0:T(8,128)(2,1)} %copy-done.12, f32[1,768]{1,0:T(1,128)} %get-tuple-element.123.g.refs_5_, ...), custom_call_target="tpu_custom_call" | custom-call | flops 805306368 | bytes 11010048 | tf_op jit(solution)/shard_map/pallas_call | solution.py:355
  90.5 2.2 all-to-all-done.1
  92.7 8.0 %all-to-all-start = ((bf16[16,64,768]{2,1,0:T(8,128)(2,1)}), bf16[16,64,768]{2,1,0:T(8,128)(2,1)S(1)}, u32[]{:S(2)}, u32[]{:S(2)}) async-start(bf16[16,64,768]{2,1,0:T(8,128)(2,1)} %bitcast.65), calls=%async_computation | async-start | bytes 3145728 | tf_op jit(solution)/shard_map/all_to_all | solution.py:696
  100.8 33.4 %all-to-all-done = bf16[16,64,768]{2,1,0:T(8,128)(2,1)S(1)} async-done(((bf16[16,64,768]{2,1,0:T(8,128)(2,1)}), bf16[16,64,768]{2,1,0:T(8,128)(2,1)S(1)}, u32[]{:S(2)}, u32[]{:S(2)}) %all-to-all-start) | async-done | bytes 1572896 | tf_op jit(solution)/shard_map/all_to_all | solution.py:696
  134.2 3.4 collective-permute-done.4.mp
  138.8 35.5 %shard_map.242 = (bf16[1024,768]{1,0:T(8,128)(2,1)}, bf16[1024,768]{1,0:T(8,128)(2,1)}, bf16[1024,768]{1,0:T(8,128)(2,1)}, bf16[1024,768]{1,0:T(8,128)(2,1)}, bf...) custom-call(bf16[1024,768]{1,0:T(8,128)(2,1)} %bitcast.63, ...), custom_call_target="tpu_custom_call" | custom-call | flops 19327352832 | bytes 31457280 | tf_op jit(solution)/shard_map/pallas_call | solution.py:355
  174.5 3.5 collective-permute-done.8
  177.9 3.0 add_convert_fusion
  180.9 7.4 %all-to-all-start.3 = ((bf16[16,64,768]{2,1,0:T(8,128)(2,1)}), bf16[16,64,768]{2,1,0:T(8,128)(2,1)S(1)}, u32[]{:S(2)}, u32[]{:S(2)}) async-start(bf16[16,64,768]{2,1,0:T(8,128)(2,1)} %bitcast.11), calls=%async_computation.3 | async-start | bytes 3145728 | tf_op jit(solution)/shard_map/all_to_all | solution.py:696
  188.4 34.2 %all-to-all-done.3 = bf16[16,64,768]{2,1,0:T(8,128)(2,1)S(1)} async-done(((bf16[16,64,768]{2,1,0:T(8,128)(2,1)}), bf16[16,64,768]{2,1,0:T(8,128)(2,1)S(1)}, u32[]{:S(2)}, u32[]{:S(2)}) %all-to-all-start.3) | async-done | bytes 1572896 | tf_op jit(solution)/shard_map/all_to_all | solution.py:696
  223.8 3.6 shard_map.244.refs_2_
  227.4 2.5 dynamic-slice_convert_fusion
  232.0 36.9 %shard_map.245 = (f32[1024,768]{1,0:T(8,128)}, bf16[1024,768]{1,0:T(8,128)(2,1)}, bf16[3,1024,384]{2,1,0:T(8,128)(2,1)}, bf16[1024,768]{1,0:T(8,128)(2,1)}, f32[8,768]{1,0:T(8,128)}) custom-call(s32[1]{0:T(128)} %bitcast.h_ref, bf16[512,768]{1,0:T(8,128)(2,1)} %refs_0_.3, bf16[512,768]{1,0:T(8,128)(2,1)} %copy-done.23, bf16[512,768]{1,0:T(8,128)(2,1)} %shard_map.244.refs_2_, ...), custom_call_target="tpu_custom_call" | custom-call | flops 12884901888 | bytes 15728640 | tf_op jit(solution)/shard_map/pallas_call | solution.py:355
  269.0 2.8 convolution_convert_fusion.4
  272.9 1.9 fusion.17
  278.8 2.7 collective-permute-start.39
  283.1 6.2 all-to-all-start.2
  290.7 2.1 fusion.19
  292.9 2.8 collective-permute-start.38
  295.7 6.5 collective-permute-done.39
  304.4 9.7 %convolution_bitcast_fusion.1 = f32[1,768,1536]{2,1,0:T(8,128)} fusion(bf16[2048,768]{1,0:T(8,128)(2,1)S(1)} %copy-done.32, bf16[2048,1536]{1,0:T(8,128)(2,1)} %get-tuple-element.99), kind=kOutput, calls=%fused_computation.2 | convolution fusion | flops 4831838208 | bytes 14155776 | tf_op jit(solution)/shard_map/dot_general | solution.py:29
  315.6 2.1 collective-permute-done.40
  318.3 3.1 collective-permute-start.41
  321.5 6.9 %convolution_bitcast_fusion = f32[1,1536,768]{2,1,0:T(8,128)} fusion(bf16[2048,1536]{1,0:T(8,128)(2,1)S(1)} %bitcast.77, bf16[2048,768]{1,0:T(8,128)(2,1)S(1)} %copy-done.28), kind=kOutput, calls=%fused_computation.1 | convolution fusion | flops 4831838208 | bytes 14155776 | tf_op jit(solution)/shard_map/dot_general | solution.py:29
  329.4 8.0 %collective-permute-start.42 = (bf16[192,384]{1,0:T(8,128)(2,1)S(1)}, bf16[192,384]{1,0:T(8,128)(2,1)S(1)}, u32[]{:S(2)}, u32[]{:S(2)}) collective-permute-start(bf16[192,384]{1,0:T(8,128)(2,1)S(1)} %constant_dynamic-slice_fusion), channel_id=1, source_target_pairs={{0,8},{1,9},{2,10},{3,11},{4,12},{5,13},{6,14},{7,15},{8,0},{9,1},... | collective-permute-start | bytes 442376 | tf_op jit(solution)/shard_map/ppermute | solution.py:632
  338.8 3.9 collective-permute-done.42
  344.9 3.8 shard_map.243
  352.9 13.4 %shard_map.246 = (f32[1024,768]{1,0:T(8,128)}, bf16[1024,768]{1,0:T(8,128)(2,1)}, bf16[1024,1536]{1,0:T(8,128)(2,1)}, bf16[1024,768]{1,0:T(8,128)(2,1)}, f32[8,768]{1,0:T(8,128)}) custom-call(f32[1024,768]{1,0:T(8,128)} %get-tuple-element.73.drr, bf16[1024,768]{1,0:T(8,128)(2,1)} %get-tuple-element.74.dna, bf16[1024,768]{1,0:T(8,128)(2,1)} %collective-permute-done.10.dnb, ...), custom_call_target="tpu_custom_call" | custom-call | flops 4831838208 | bytes 20447232 | tf_op jit(solution)/shard_map/pallas_call | solution.py:355
  367.1 4.5 convolution_convert_fusion
  373.0 3.1 convolution_convert_fusion.1
  381.2 5.2 collective-permute-done.47
  387.4 19.5 %collective-permute-done.45 = bf16[384,384]{1,0:T(8,128)(2,1)S(1)} collective-permute-done((bf16[384,384]{1,0:T(8,128)(2,1)S(1)}, bf16[384,384]{1,0:T(8,128)(2,1)S(1)}, u32[]{:S(2)}, u32[]{:S(2)}) %collective-permute-start.45) | collective-permute-done | bytes 294944 | tf_op jit(solution)/shard_map/ppermute | solution.py:636
  409.2 7.9 %collective-permute-done.48 = bf16[768,384]{1,0:T(8,128)(2,1)S(1)} collective-permute-done((bf16[768,384]{1,0:T(8,128)(2,1)S(1)}, bf16[768,384]{1,0:T(8,128)(2,1)S(1)}, u32[]{:S(2)}, u32[]{:S(2)}) %collective-permute-start.48) | collective-permute-done | bytes 589856 | tf_op jit(solution)/shard_map/ppermute | solution.py:636
  417.1 5.5 collective-permute-done.46
  423.1 2.0 slice.169
  430.8 26.8 %shard_map.247 = (f32[1024,768]{1,0:T(8,128)}, bf16[1024,768]{1,0:T(8,128)(2,1)}, bf16[3,1024,384]{2,1,0:T(8,128)(2,1)}, bf16[1024,768]{1,0:T(8,128)(2,1)}, f32[8,768]{1,0:T(8,128)}) custom-call(s32[1]{0:T(128)} %bitcast.h_ref, f32[1024,768]{1,0:T(8,128)} %get-tuple-element.76.refs_0_, bf16[1024,768]{1,0:T(8,128)(2,1)} %get-tuple-element.77.refs_1_, ...), custom_call_target="tpu_custom_call" | custom-call | flops 12884901888 | bytes 15728640 | tf_op jit(solution)/shard_map/pallas_call | solution.py:355
  457.7 2.3 convolution_convert_fusion.8
  467.9 10.3 %collective-permute-done.13 = bf16[768,384]{1,0:T(8,128)(2,1)S(1)} collective-permute-done((bf16[768,384]{1,0:T(8,128)(2,1)S(1)}, bf16[768,384]{1,0:T(8,128)(2,1)S(1)}, u32[]{:S(2)}, u32[]{:S(2)}) %collective-permute-start.13) | collective-permute-done | bytes 589856 | tf_op jit(solution)/shard_map/ppermute | solution.py:632
  482.7 3.5 collective-permute-done.14
  488.9 11.7 %collective-permute-done.29 = bf16[384,768]{1,0:T(8,128)(2,1)S(1)} collective-permute-done((bf16[384,768]{1,0:T(8,128)(2,1)S(1)}, bf16[384,768]{1,0:T(8,128)(2,1)S(1)}, u32[]{:S(2)}, u32[]{:S(2)}) %collective-permute-start.29) | collective-permute-done | bytes 589856 | tf_op jit(solution)/shard_map/ppermute | solution.py:632
  501.9 2.3 collective-permute-done.17
  504.7 2.9 collective-permute-start.18
  507.7 14.7 %collective-permute-done.30 = bf16[192,768]{1,0:T(8,128)(2,1)S(1)} collective-permute-done((bf16[192,768]{1,0:T(8,128)(2,1)S(1)}, bf16[192,768]{1,0:T(8,128)(2,1)S(1)}, u32[]{:S(2)}, u32[]{:S(2)}) %collective-permute-start.30) | collective-permute-done | bytes 294944 | tf_op jit(solution)/shard_map/ppermute | solution.py:632
  522.6 4.7 collective-permute-done.18
  528.2 5.6 collective-permute-done.31
  539.0 6.3 shard_map.248
  546.0 75.1 %psum.7 = f32[4,768]{1,0:T(4,128)} all-reduce(f32[4,768]{1,0:T(4,128)S(1)} %pad_maximum_fusion.24), channel_id=1, replica_groups=mesh['head'=2,'dp'=16] {'dp'}, use_global_device_ids=true, to_apply=%region_1.2 | all-reduce | flops 3072 | bytes 24576 | tf_op jit(solution)/shard_map/psum | solution.py:782
  623.7 2.0 collective-permute-start.33
  625.8 2.1 collective-permute-start.35
  628.0 4.4 collective-permute-done.23
  632.4 2.0 collective-permute-start.24
  634.7 4.4 collective-permute-done.35
  641.7 3.7 collective-permute-done.24
  645.9 2.0 slice.160
  649.6 8.4 %collective-permute-done.36 = bf16[768,768]{1,0:T(8,128)(2,1)S(1)} collective-permute-done((bf16[768,768]{1,0:T(8,128)(2,1)S(1)}, bf16[768,768]{1,0:T(8,128)(2,1)S(1)}, u32[]{:S(2)}, u32[]{:S(2)}) %collective-permute-start.36) | collective-permute-done | bytes 1179680 | tf_op jit(solution)/shard_map/ppermute | solution.py:636
  658.3 2.5 fusion
  661.2 2.9 pad_maximum_fusion
  (251 shorter events, 84.9 us)
Async XLA Ops:
  0.6 43.8 %copy-start = (s32[1024,1]{0,1:T(1,128)S(1)}, s32[1024,1]{0,1:T(1,128)}, u32[]{:S(2)}) copy-start(s32[1024,1]{0,1:T(1,128)} %param.16) | copy-start | bytes 12292
  0.7 3.7 collective-permute-start
  24.3 3.6 collective-permute-start.1
  44.3 14.2 %collective-permute-start.2 = (bf16[1024,768]{1,0:T(8,128)(2,1)}, bf16[1024,768]{1,0:T(8,128)(2,1)S(1)}, u32[]{:S(2)}, u32[]{:S(2)}) collective-permute-start(bf16[1024,768]{1,0:T(8,128)(2,1)} %get-tuple-element.61.refs_1_), channel_id=1, source_target_pairs={{0,16},{16,0},{1,17},{17,1},{2,18},{18,2},{3,19},{19,3},{4,20},{20... | collective-permute-start | bytes 4718600 | tf_op jit(solution)/shard_map/ppermute | solution.py:626
  50.2 42.5 %all-to-all-start.1 = ((bf16[16,64,768]{2,1,0:T(8,128)(2,1)}), bf16[16,64,768]{2,1,0:T(8,128)(2,1)S(1)}, u32[]{:S(2)}, u32[]{:S(2)}) async-start(bf16[16,64,768]{2,1,0:T(8,128)(2,1)} %bitcast.64), calls=%async_computation.1 | async-start | bytes 3145728 | tf_op jit(solution)/shard_map/all_to_all | solution.py:696
  78.9 3.7 collective-permute-start.3
  92.7 8.0 %copy-start.4 = (bf16[16,64,768]{2,1,0:T(8,128)(2,1)}, bf16[16,64,768]{2,1,0:T(8,128)(2,1)S(1)}, u32[]{:S(2)}) copy-start(bf16[16,64,768]{2,1,0:T(8,128)(2,1)S(1)} %all-to-all-done.1) | copy-start | bytes 4718596
  92.7 41.5 %all-to-all-start = ((bf16[16,64,768]{2,1,0:T(8,128)(2,1)}), bf16[16,64,768]{2,1,0:T(8,128)(2,1)S(1)}, u32[]{:S(2)}, u32[]{:S(2)}) async-start(bf16[16,64,768]{2,1,0:T(8,128)(2,1)} %bitcast.65), calls=%async_computation | async-start | bytes 3145728 | tf_op jit(solution)/shard_map/all_to_all | solution.py:696
  100.8 33.5 %collective-permute-start.5 = (bf16[1024,768]{1,0:T(8,128)(2,1)S(1)}, bf16[1024,768]{1,0:T(8,128)(2,1)}, u32[]{:S(2)}, u32[]{:S(2)}) collective-permute-start(bf16[1024,768]{1,0:T(8,128)(2,1)S(1)} %bitcast.60), channel_id=1, source_target_pairs={{0,16},{16,0},{1,17},{17,1},{2,18},{18,2},{3,19},{19,3},{4,20},{20... | collective-permute-start | bytes 4718600 | tf_op jit(solution)/shard_map/ppermute | solution.py:626
  134.2 3.4 collective-permute-start.4
  174.3 3.7 collective-permute-start.8
  180.9 7.4 %copy-start.22 = (bf16[512,768]{1,0:T(8,128)(2,1)S(1)}, bf16[512,768]{1,0:T(8,128)(2,1)}, u32[]{:S(2)}) copy-start(bf16[512,768]{1,0:T(8,128)(2,1)} %refs_0_.3) | copy-start | bytes 2359300
  180.9 41.7 %all-to-all-start.3 = ((bf16[16,64,768]{2,1,0:T(8,128)(2,1)}), bf16[16,64,768]{2,1,0:T(8,128)(2,1)S(1)}, u32[]{:S(2)}, u32[]{:S(2)}) async-start(bf16[16,64,768]{2,1,0:T(8,128)(2,1)} %bitcast.11), calls=%async_computation.3 | async-start | bytes 3145728 | tf_op jit(solution)/shard_map/all_to_all | solution.py:696
  188.4 42.7 %collective-permute-start.7 = (bf16[512,768]{1,0:T(8,128)(2,1)S(1)}, bf16[512,768]{1,0:T(8,128)(2,1)S(1)}, u32[]{:S(2)}, u32[]{:S(2)}) collective-permute-start(bf16[512,768]{1,0:T(8,128)(2,1)S(1)} %copy-done.22), channel_id=1, source_target_pairs={{0,16},{16,0},{1,17},{17,1},{2,18},{18,2},{3,19},{19,3},{4,20},{20... | collective-permute-start | bytes 2359304 | tf_op jit(solution)/shard_map/ppermute | solution.py:626
  227.4 3.7 collective-permute-start.9
  230.6 106.8 %collective-permute-start.49 = (f32[1,768]{1,0:T(1,128)S(1)}, f32[1,768]{1,0:T(1,128)S(1)}, u32[]{:S(2)}, u32[]{:S(2)}) collective-permute-start(f32[1,768]{1,0:T(1,128)S(1)} %slice.151), channel_id=1, source_target_pairs={{0,16},{16,0},{1,17},{17,1},{2,18},{18,2},{3,19},{19,3},{4,20},{20... | collective-permute-start | bytes 9224 | tf_op jit(solution)/shard_map/ppermute | solution.py:626
  231.0 50.5 %collective-permute-start.6 = (bf16[1024,768]{1,0:T(8,128)(2,1)S(1)}, bf16[1024,768]{1,0:T(8,128)(2,1)S(1)}, u32[]{:S(2)}, u32[]{:S(2)}) collective-permute-start(bf16[1024,768]{1,0:T(8,128)(2,1)S(1)} %copy-done.16), channel_id=1, source_target_pairs={{0,16},{16,0},{1,17},{17,1},{2,18},{18,2},{3,19},{19,3},{4,20},{20... | collective-permute-start | bytes 4718600 | tf_op jit(solution)/shard_map/ppermute | solution.py:626
  274.8 15.9 %collective-permute-start.37 = (bf16[768,384]{1,0:T(8,128)(2,1)}, bf16[768,384]{1,0:T(8,128)(2,1)}, u32[]{:S(2)}, u32[]{:S(2)}) collective-permute-start(bf16[768,384]{1,0:T(8,128)(2,1)} %fusion.17), channel_id=1, source_target_pairs={{0,1},{1,0},{2,3},{3,2},{4,5},{5,4},{6,7},{7,6},{8,9},{9,8},{10,11... | collective-permute-start | bytes 1769480 | tf_op jit(solution)/shard_map/ppermute | solution.py:632
  278.8 23.3 %collective-permute-start.39 = (bf16[768,384]{1,0:T(8,128)(2,1)}, bf16[768,384]{1,0:T(8,128)(2,1)}, u32[]{:S(2)}, u32[]{:S(2)}) collective-permute-start(bf16[768,384]{1,0:T(8,128)(2,1)} %constant_dynamic-slice_fusion.2), channel_id=1, source_target_pairs={{0,2},{1,3},{2,0},{3,1},{4,6},{5,7},{6,4},{7,5},{8,10},{9,11},{10,... | collective-permute-start | bytes 1769480 | tf_op jit(solution)/shard_map/ppermute | solution.py:632
  283.1 60.6 %all-to-all-start.2 = ((bf16[16,64,768]{2,1,0:T(8,128)(2,1)}), bf16[16,64,768]{2,1,0:T(8,128)(2,1)S(1)}, u32[]{:S(2)}, u32[]{:S(2)}) async-start(bf16[16,64,768]{2,1,0:T(8,128)(2,1)} %bitcast.8), calls=%async_computation.2 | async-start | bytes 3145728 | tf_op jit(solution)/shard_map/all_to_all | solution.py:696
  290.7 13.7 %copy-start.32 = (bf16[2048,768]{1,0:T(8,128)(2,1)S(1)}, bf16[2048,768]{1,0:T(8,128)(2,1)}, u32[]{:S(2)}) copy-start(bf16[2048,768]{1,0:T(8,128)(2,1)} %get-tuple-element.98) | copy-start | bytes 9437188
  292.9 22.7 %collective-permute-start.38 = (bf16[384,384]{1,0:T(8,128)(2,1)S(1)}, bf16[384,384]{1,0:T(8,128)(2,1)S(1)}, u32[]{:S(2)}, u32[]{:S(2)}) collective-permute-start(bf16[384,384]{1,0:T(8,128)(2,1)S(1)} %constant_dynamic-slice_fusion.3), channel_id=1, source_target_pairs={{0,2},{1,3},{2,0},{3,1},{4,6},{5,7},{6,4},{7,5},{8,10},{9,11},{10,... | collective-permute-start | bytes 884744 | tf_op jit(solution)/shard_map/ppermute | solution.py:632
  303.4 14.3 %collective-permute-start.40 = (bf16[384,384]{1,0:T(8,128)(2,1)S(1)}, bf16[384,384]{1,0:T(8,128)(2,1)S(1)}, u32[]{:S(2)}, u32[]{:S(2)}) collective-permute-start(bf16[384,384]{1,0:T(8,128)(2,1)S(1)} %constant_dynamic-slice_fusion.1), channel_id=1, source_target_pairs={{0,1},{1,0},{2,3},{3,2},{4,5},{5,4},{6,7},{7,6},{8,9},{9,8},{10,11... | collective-permute-start | bytes 884744 | tf_op jit(solution)/shard_map/ppermute | solution.py:632
  304.4 17.1 %slice-start = ((s8[6291456]{0:T(1024)(128)(4,1)}), s8[4194304]{0:T(1024)(128)(4,1)S(1)}, s32[]{:S(2)}) async-start(s8[6291456]{0:T(1024)(128)(4,1)} %bitcast.76), calls=%async_computation.4 | async-start | bytes 8388608
  304.4 17.1 %slice-start.1 = ((s8[6291456]{0:T(1024)(128)(4,1)}), s8[2097152]{0:T(1024)(128)(4,1)S(1)}, s32[]{:S(2)}) async-start(s8[6291456]{0:T(1024)(128)(4,1)} %bitcast.76), calls=%async_computation.5 | async-start | bytes 4194304
  304.4 17.1 %copy-start.28 = (bf16[2048,768]{1,0:T(8,128)(2,1)S(1)}, bf16[2048,768]{1,0:T(8,128)(2,1)}, u32[]{:S(2)}) copy-start(bf16[2048,768]{1,0:T(8,128)(2,1)} %get-tuple-element.101) | copy-start | bytes 9437188
  314.1 38.8 %collective-permute-start.10 = (bf16[1024,768]{1,0:T(8,128)(2,1)}, bf16[1024,768]{1,0:T(8,128)(2,1)}, u32[]{:S(2)}, u32[]{:S(2)}) collective-permute-start(bf16[1024,768]{1,0:T(8,128)(2,1)} %get-tuple-element.74.dna), channel_id=1, source_target_pairs={{0,16},{16,0},{1,17},{17,1},{2,18},{18,2},{3,19},{19,3},{4,20},{20... | collective-permute-start | bytes 4718600 | tf_op jit(solution)/shard_map/ppermute | solution.py:626
  318.3 10.5 %collective-permute-start.41 = (bf16[384,384]{1,0:T(8,128)(2,1)S(1)}, bf16[384,384]{1,0:T(8,128)(2,1)S(1)}, u32[]{:S(2)}, u32[]{:S(2)}) collective-permute-start(bf16[384,384]{1,0:T(8,128)(2,1)S(1)} %fusion.26), channel_id=1, source_target_pairs={{0,4},{1,5},{2,6},{3,7},{4,0},{5,1},{6,2},{7,3},{8,12},{9,13},{10,... | collective-permute-start | bytes 884744 | tf_op jit(solution)/shard_map/ppermute | solution.py:632
  329.4 13.2 %collective-permute-start.42 = (bf16[192,384]{1,0:T(8,128)(2,1)S(1)}, bf16[192,384]{1,0:T(8,128)(2,1)S(1)}, u32[]{:S(2)}, u32[]{:S(2)}) collective-permute-start(bf16[192,384]{1,0:T(8,128)(2,1)S(1)} %constant_dynamic-slice_fusion), channel_id=1, source_target_pairs={{0,8},{1,9},{2,10},{3,11},{4,12},{5,13},{6,14},{7,15},{8,0},{9,1},... | collective-permute-start | bytes 442376 | tf_op jit(solution)/shard_map/ppermute | solution.py:632
  342.7 8.7 %collective-permute-start.43 = (bf16[192,384]{1,0:T(8,128)(2,1)S(1)}, bf16[192,384]{1,0:T(8,128)(2,1)S(1)}, u32[]{:S(2)}, u32[]{:S(2)}) collective-permute-start(bf16[192,384]{1,0:T(8,128)(2,1)S(1)} %dynamic-slice_add_fusion.10), channel_id=1, source_target_pairs={{0,8},{1,9},{2,10},{3,11},{4,12},{5,13},{6,14},{7,15},{8,0},{9,1},... | collective-permute-start | bytes 442376 | tf_op jit(solution)/shard_map/ppermute | solution.py:636
  351.4 24.8 %collective-permute-start.44 = (bf16[384,384]{1,0:T(8,128)(2,1)S(1)}, bf16[384,384]{1,0:T(8,128)(2,1)S(1)}, u32[]{:S(2)}, u32[]{:S(2)}) collective-permute-start(bf16[384,384]{1,0:T(8,128)(2,1)S(1)} %constant_dynamic-update-slice_fusion.5), channel_id=1, source_target_pairs={{0,4},{1,5},{2,6},{3,7},{4,0},{5,1},{6,2},{7,3},{8,12},{9,13},{10,... | collective-permute-start | bytes 884744 | tf_op jit(solution)/shard_map/ppermute | solution.py:636
  352.9 14.2 %copy-start.33 = (bf16[1024,1536]{1,0:T(8,128)(2,1)S(1)}, bf16[1024,1536]{1,0:T(8,128)(2,1)}, u32[]{:S(2)}) copy-start(bf16[1024,1536]{1,0:T(8,128)(2,1)} %get-tuple-element.93) | copy-start | bytes 9437188
  367.1 5.6 copy-start.24
  371.7 53.5 %collective-permute-start.27 = (bf16[768,768]{1,0:T(8,128)(2,1)S(1)}, bf16[768,768]{1,0:T(8,128)(2,1)S(1)}, u32[]{:S(2)}, u32[]{:S(2)}) collective-permute-start(bf16[768,768]{1,0:T(8,128)(2,1)S(1)} %constant_dynamic-slice_fusion.6), channel_id=1, source_target_pairs={{0,2},{1,3},{2,0},{3,1},{4,6},{5,7},{6,4},{7,5},{8,10},{9,11},{10,... | collective-permute-start | bytes 3538952 | tf_op jit(solution)/shard_map/ppermute | solution.py:632
  376.4 10.0 %collective-permute-start.47 = (bf16[384,384]{1,0:T(8,128)(2,1)S(1)}, bf16[384,384]{1,0:T(8,128)(2,1)S(1)}, u32[]{:S(2)}, u32[]{:S(2)}) collective-permute-start(bf16[384,384]{1,0:T(8,128)(2,1)S(1)} %get-tuple-element.114), channel_id=1, source_target_pairs={{0,1},{1,0},{2,3},{3,2},{4,5},{5,4},{6,7},{7,6},{8,9},{9,8},{10,11... | collective-permute-start | bytes 884744 | tf_op jit(solution)/shard_map/ppermute | solution.py:636
  379.9 47.4 %collective-permute-start.25 = (bf16[768,768]{1,0:T(8,128)(2,1)S(1)}, bf16[768,768]{1,0:T(8,128)(2,1)S(1)}, u32[]{:S(2)}, u32[]{:S(2)}) collective-permute-start(bf16[768,768]{1,0:T(8,128)(2,1)S(1)} %fusion.1), channel_id=1, source_target_pairs={{0,1},{1,0},{2,3},{3,2},{4,5},{5,4},{6,7},{7,6},{8,9},{9,8},{10,11... | collective-permute-start | bytes 3538952 | tf_op jit(solution)/shard_map/ppermute | solution.py:632
  380.2 49.5 %collective-permute-start.11 = (bf16[1024,768]{1,0:T(8,128)(2,1)S(1)}, bf16[1024,768]{1,0:T(8,128)(2,1)S(1)}, u32[]{:S(2)}, u32[]{:S(2)}) collective-permute-start(bf16[1024,768]{1,0:T(8,128)(2,1)S(1)} %copy-done.17), channel_id=1, source_target_pairs={{0,16},{16,0},{1,17},{17,1},{2,18},{18,2},{3,19},{19,3},{4,20},{20... | collective-permute-start | bytes 4718600 | tf_op jit(solution)/shard_map/ppermute | solution.py:626
  380.2 26.8 %collective-permute-start.45 = (bf16[384,384]{1,0:T(8,128)(2,1)S(1)}, bf16[384,384]{1,0:T(8,128)(2,1)S(1)}, u32[]{:S(2)}, u32[]{:S(2)}) collective-permute-start(bf16[384,384]{1,0:T(8,128)(2,1)S(1)} %get-tuple-element.113), channel_id=1, source_target_pairs={{0,2},{1,3},{2,0},{3,1},{4,6},{5,7},{6,4},{7,5},{8,10},{9,11},{10,... | collective-permute-start | bytes 884744 | tf_op jit(solution)/shard_map/ppermute | solution.py:636
  386.4 30.6 %collective-permute-start.48 = (bf16[768,384]{1,0:T(8,128)(2,1)S(1)}, bf16[768,384]{1,0:T(8,128)(2,1)S(1)}, u32[]{:S(2)}, u32[]{:S(2)}) collective-permute-start(bf16[768,384]{1,0:T(8,128)(2,1)S(1)} %constant_dynamic-update-slice_fusion.1), channel_id=1, source_target_pairs={{0,2},{1,3},{2,0},{3,1},{4,6},{5,7},{6,4},{7,5},{8,10},{9,11},{10,... | collective-permute-start | bytes 1769480 | tf_op jit(solution)/shard_map/ppermute | solution.py:636
  407.0 15.6 %collective-permute-start.46 = (bf16[768,384]{1,0:T(8,128)(2,1)S(1)}, bf16[768,384]{1,0:T(8,128)(2,1)S(1)}, u32[]{:S(2)}, u32[]{:S(2)}) collective-permute-start(bf16[768,384]{1,0:T(8,128)(2,1)S(1)} %constant_dynamic-update-slice_fusion.3), channel_id=1, source_target_pairs={{0,1},{1,0},{2,3},{3,2},{4,5},{5,4},{6,7},{7,6},{8,9},{9,8},{10,11... | collective-permute-start | bytes 1769480 | tf_op jit(solution)/shard_map/ppermute | solution.py:636
  425.6 42.0 %collective-permute-start.28 = (bf16[384,768]{1,0:T(8,128)(2,1)S(1)}, bf16[384,768]{1,0:T(8,128)(2,1)S(1)}, u32[]{:S(2)}, u32[]{:S(2)}) collective-permute-start(bf16[384,768]{1,0:T(8,128)(2,1)S(1)} %constant_dynamic-slice_fusion.5), channel_id=1, source_target_pairs={{0,1},{1,0},{2,3},{3,2},{4,5},{5,4},{6,7},{7,6},{8,9},{9,8},{10,11... | collective-permute-start | bytes 1769480 | tf_op jit(solution)/shard_map/ppermute | solution.py:632
  429.1 38.6 %collective-permute-start.26 = (bf16[384,768]{1,0:T(8,128)(2,1)S(1)}, bf16[384,768]{1,0:T(8,128)(2,1)S(1)}, u32[]{:S(2)}, u32[]{:S(2)}) collective-permute-start(bf16[384,768]{1,0:T(8,128)(2,1)S(1)} %constant_dynamic-slice_fusion.7), channel_id=1, source_target_pairs={{0,2},{1,3},{2,0},{3,1},{4,6},{5,7},{6,4},{7,5},{8,10},{9,11},{10,... | collective-permute-start | bytes 1769480 | tf_op jit(solution)/shard_map/ppermute | solution.py:632
  430.8 26.8 %copy-start.29 = (bf16[1024,768]{1,0:T(8,128)(2,1)S(1)}, bf16[1024,768]{1,0:T(8,128)(2,1)}, u32[]{:S(2)}) copy-start(bf16[1024,768]{1,0:T(8,128)(2,1)} %get-tuple-element.88) | copy-start | bytes 4718596
  465.3 12.9 %collective-permute-start.13 = (bf16[768,384]{1,0:T(8,128)(2,1)S(1)}, bf16[768,384]{1,0:T(8,128)(2,1)S(1)}, u32[]{:S(2)}, u32[]{:S(2)}) collective-permute-start(bf16[768,384]{1,0:T(8,128)(2,1)S(1)} %fusion.23), channel_id=1, source_target_pairs={{0,1},{1,0},{2,3},{3,2},{4,5},{5,4},{6,7},{7,6},{8,9},{9,8},{10,11... | collective-permute-start | bytes 1769480 | tf_op jit(solution)/shard_map/ppermute | solution.py:632
  466.2 15.0 %collective-permute-start.15 = (bf16[768,384]{1,0:T(8,128)(2,1)S(1)}, bf16[768,384]{1,0:T(8,128)(2,1)S(1)}, u32[]{:S(2)}, u32[]{:S(2)}) collective-permute-start(bf16[768,384]{1,0:T(8,128)(2,1)S(1)} %constant_dynamic-slice_fusion.10), channel_id=1, source_target_pairs={{0,2},{1,3},{2,0},{3,1},{4,6},{5,7},{6,4},{7,5},{8,10},{9,11},{10,... | collective-permute-start | bytes 1769480 | tf_op jit(solution)/shard_map/ppermute | solution.py:632
  467.5 70.3 %collective-permute-start.12 = (bf16[1024,768]{1,0:T(8,128)(2,1)S(1)}, bf16[1024,768]{1,0:T(8,128)(2,1)S(1)}, u32[]{:S(2)}, u32[]{:S(2)}) collective-permute-start(bf16[1024,768]{1,0:T(8,128)(2,1)S(1)} %copy-done.10), channel_id=1, source_target_pairs={{0,16},{16,0},{1,17},{17,1},{2,18},{18,2},{3,19},{19,3},{4,20},{20... | collective-permute-start | bytes 4718600 | tf_op jit(solution)/shard_map/ppermute | solution.py:626
  479.4 6.8 %collective-permute-start.14 = (bf16[384,384]{1,0:T(8,128)(2,1)S(1)}, bf16[384,384]{1,0:T(8,128)(2,1)S(1)}, u32[]{:S(2)}, u32[]{:S(2)}) collective-permute-start(bf16[384,384]{1,0:T(8,128)(2,1)S(1)} %constant_dynamic-slice_fusion.11), channel_id=1, source_target_pairs={{0,2},{1,3},{2,0},{3,1},{4,6},{5,7},{6,4},{7,5},{8,10},{9,11},{10,... | collective-permute-start | bytes 884744 | tf_op jit(solution)/shard_map/ppermute | solution.py:632
  481.4 6.8 %collective-permute-start.16 = (bf16[384,384]{1,0:T(8,128)(2,1)S(1)}, bf16[384,384]{1,0:T(8,128)(2,1)S(1)}, u32[]{:S(2)}, u32[]{:S(2)}) collective-permute-start(bf16[384,384]{1,0:T(8,128)(2,1)S(1)} %constant_dynamic-slice_fusion.9), channel_id=1, source_target_pairs={{0,1},{1,0},{2,3},{3,2},{4,5},{5,4},{6,7},{7,6},{8,9},{9,8},{10,11... | collective-permute-start | bytes 884744 | tf_op jit(solution)/shard_map/ppermute | solution.py:632
  482.6 18.0 %collective-permute-start.29 = (bf16[384,768]{1,0:T(8,128)(2,1)S(1)}, bf16[384,768]{1,0:T(8,128)(2,1)S(1)}, u32[]{:S(2)}, u32[]{:S(2)}) collective-permute-start(bf16[384,768]{1,0:T(8,128)(2,1)S(1)} %fusion.20), channel_id=1, source_target_pairs={{0,4},{1,5},{2,6},{3,7},{4,0},{5,1},{6,2},{7,3},{8,12},{9,13},{10,... | collective-permute-start | bytes 1769480 | tf_op jit(solution)/shard_map/ppermute | solution.py:632
  488.8 15.3 %collective-permute-start.17 = (bf16[384,384]{1,0:T(8,128)(2,1)S(1)}, bf16[384,384]{1,0:T(8,128)(2,1)S(1)}, u32[]{:S(2)}, u32[]{:S(2)}) collective-permute-start(bf16[384,384]{1,0:T(8,128)(2,1)S(1)} %fusion.29), channel_id=1, source_target_pairs={{0,4},{1,5},{2,6},{3,7},{4,0},{5,1},{6,2},{7,3},{8,12},{9,13},{10,... | collective-permute-start | bytes 884744 | tf_op jit(solution)/shard_map/ppermute | solution.py:632
  501.5 21.0 %collective-permute-start.30 = (bf16[192,768]{1,0:T(8,128)(2,1)S(1)}, bf16[192,768]{1,0:T(8,128)(2,1)S(1)}, u32[]{:S(2)}, u32[]{:S(2)}) collective-permute-start(bf16[192,768]{1,0:T(8,128)(2,1)S(1)} %constant_dynamic-slice_fusion.4), channel_id=1, source_target_pairs={{0,8},{1,9},{2,10},{3,11},{4,12},{5,13},{6,14},{7,15},{8,0},{9,1},... | collective-permute-start | bytes 884744 | tf_op jit(solution)/shard_map/ppermute | solution.py:632
  504.7 22.6 %collective-permute-start.18 = (bf16[192,384]{1,0:T(8,128)(2,1)S(1)}, bf16[192,384]{1,0:T(8,128)(2,1)S(1)}, u32[]{:S(2)}, u32[]{:S(2)}) collective-permute-start(bf16[192,384]{1,0:T(8,128)(2,1)S(1)} %constant_dynamic-slice_fusion.8), channel_id=1, source_target_pairs={{0,8},{1,9},{2,10},{3,11},{4,12},{5,13},{6,14},{7,15},{8,0},{9,1},... | collective-permute-start | bytes 442376 | tf_op jit(solution)/shard_map/ppermute | solution.py:632
  522.5 11.3 %collective-permute-start.31 = (bf16[192,768]{1,0:T(8,128)(2,1)S(1)}, bf16[192,768]{1,0:T(8,128)(2,1)S(1)}, u32[]{:S(2)}, u32[]{:S(2)}) collective-permute-start(bf16[192,768]{1,0:T(8,128)(2,1)S(1)} %dynamic-slice_add_fusion.7), channel_id=1, source_target_pairs={{0,8},{1,9},{2,10},{3,11},{4,12},{5,13},{6,14},{7,15},{8,0},{9,1},... | collective-permute-start | bytes 884744 | tf_op jit(solution)/shard_map/ppermute | solution.py:636
  527.4 8.0 %collective-permute-start.19 = (bf16[192,384]{1,0:T(8,128)(2,1)S(1)}, bf16[192,384]{1,0:T(8,128)(2,1)S(1)}, u32[]{:S(2)}, u32[]{:S(2)}) collective-permute-start(bf16[192,384]{1,0:T(8,128)(2,1)S(1)} %dynamic-slice_add_fusion.11), channel_id=1, source_target_pairs={{0,8},{1,9},{2,10},{3,11},{4,12},{5,13},{6,14},{7,15},{8,0},{9,1},... | collective-permute-start | bytes 442376 | tf_op jit(solution)/shard_map/ppermute | solution.py:636
  533.9 88.6 %collective-permute-start.32 = (bf16[384,768]{1,0:T(8,128)(2,1)S(1)}, bf16[384,768]{1,0:T(8,128)(2,1)}, u32[]{:S(2)}, u32[]{:S(2)}) collective-permute-start(bf16[384,768]{1,0:T(8,128)(2,1)S(1)} %constant_dynamic-update-slice_fusion.11), channel_id=1, source_target_pairs={{0,4},{1,5},{2,6},{3,7},{4,0},{5,1},{6,2},{7,3},{8,12},{9,13},{10,... | collective-permute-start | bytes 1769480 | tf_op jit(solution)/shard_map/ppermute | solution.py:636
  536.1 85.0 %collective-permute-start.20 = (bf16[384,384]{1,0:T(8,128)(2,1)}, bf16[384,384]{1,0:T(8,128)(2,1)}, u32[]{:S(2)}, u32[]{:S(2)}) collective-permute-start(bf16[384,384]{1,0:T(8,128)(2,1)} %constant_dynamic-update-slice_fusion.17), channel_id=1, source_target_pairs={{0,4},{1,5},{2,6},{3,7},{4,0},{5,1},{6,2},{7,3},{8,12},{9,13},{10,... | collective-permute-start | bytes 884744 | tf_op jit(solution)/shard_map/ppermute | solution.py:636
  622.2 12.2 %collective-permute-start.21 = (bf16[384,384]{1,0:T(8,128)(2,1)S(1)}, bf16[384,384]{1,0:T(8,128)(2,1)S(1)}, u32[]{:S(2)}, u32[]{:S(2)}) collective-permute-start(bf16[384,384]{1,0:T(8,128)(2,1)S(1)} %get-tuple-element.117), channel_id=1, source_target_pairs={{0,2},{1,3},{2,0},{3,1},{4,6},{5,7},{6,4},{7,5},{8,10},{9,11},{10,... | collective-permute-start | bytes 884744 | tf_op jit(solution)/shard_map/ppermute | solution.py:636
  622.3 10.0 %collective-permute-start.23 = (bf16[384,384]{1,0:T(8,128)(2,1)S(1)}, bf16[384,384]{1,0:T(8,128)(2,1)S(1)}, u32[]{:S(2)}, u32[]{:S(2)}) collective-permute-start(bf16[384,384]{1,0:T(8,128)(2,1)S(1)} %get-tuple-element.118), channel_id=1, source_target_pairs={{0,1},{1,0},{2,3},{3,2},{4,5},{5,4},{6,7},{7,6},{8,9},{9,8},{10,11... | collective-permute-start | bytes 884744 | tf_op jit(solution)/shard_map/ppermute | solution.py:636
  623.7 17.3 %collective-permute-start.33 = (bf16[384,768]{1,0:T(8,128)(2,1)S(1)}, bf16[384,768]{1,0:T(8,128)(2,1)S(1)}, u32[]{:S(2)}, u32[]{:S(2)}) collective-permute-start(bf16[384,768]{1,0:T(8,128)(2,1)S(1)} %get-tuple-element.111), channel_id=1, source_target_pairs={{0,2},{1,3},{2,0},{3,1},{4,6},{5,7},{6,4},{7,5},{8,10},{9,11},{10,... | collective-permute-start | bytes 1769480 | tf_op jit(solution)/shard_map/ppermute | solution.py:636
  625.8 13.3 %collective-permute-start.35 = (bf16[384,768]{1,0:T(8,128)(2,1)S(1)}, bf16[384,768]{1,0:T(8,128)(2,1)S(1)}, u32[]{:S(2)}, u32[]{:S(2)}) collective-permute-start(bf16[384,768]{1,0:T(8,128)(2,1)S(1)} %get-tuple-element.112), channel_id=1, source_target_pairs={{0,1},{1,0},{2,3},{3,2},{4,5},{5,4},{6,7},{7,6},{8,9},{9,8},{10,11... | collective-permute-start | bytes 1769480 | tf_op jit(solution)/shard_map/ppermute | solution.py:636
  632.4 13.0 %collective-permute-start.24 = (bf16[768,384]{1,0:T(8,128)(2,1)S(1)}, bf16[768,384]{1,0:T(8,128)(2,1)S(1)}, u32[]{:S(2)}, u32[]{:S(2)}) collective-permute-start(bf16[768,384]{1,0:T(8,128)(2,1)S(1)} %constant_dynamic-update-slice_fusion.13), channel_id=1, source_target_pairs={{0,2},{1,3},{2,0},{3,1},{4,6},{5,7},{6,4},{7,5},{8,10},{9,11},{10,... | collective-permute-start | bytes 1769480 | tf_op jit(solution)/shard_map/ppermute | solution.py:636
  634.4 11.0 %collective-permute-start.22 = (bf16[768,384]{1,0:T(8,128)(2,1)S(1)}, bf16[768,384]{1,0:T(8,128)(2,1)S(1)}, u32[]{:S(2)}, u32[]{:S(2)}) collective-permute-start(bf16[768,384]{1,0:T(8,128)(2,1)S(1)} %constant_dynamic-update-slice_fusion.15), channel_id=1, source_target_pairs={{0,1},{1,0},{2,3},{3,2},{4,5},{5,4},{6,7},{7,6},{8,9},{9,8},{10,11... | collective-permute-start | bytes 1769480 | tf_op jit(solution)/shard_map/ppermute | solution.py:636
  639.2 18.8 %collective-permute-start.36 = (bf16[768,768]{1,0:T(8,128)(2,1)S(1)}, bf16[768,768]{1,0:T(8,128)(2,1)S(1)}, u32[]{:S(2)}, u32[]{:S(2)}) collective-permute-start(bf16[768,768]{1,0:T(8,128)(2,1)S(1)} %constant_dynamic-update-slice_fusion.7), channel_id=1, source_target_pairs={{0,2},{1,3},{2,0},{3,1},{4,6},{5,7},{6,4},{7,5},{8,10},{9,11},{10,... | collective-permute-start | bytes 3538952 | tf_op jit(solution)/shard_map/ppermute | solution.py:636
  641.1 17.1 %collective-permute-start.34 = (bf16[768,768]{1,0:T(8,128)(2,1)S(1)}, bf16[768,768]{1,0:T(8,128)(2,1)S(1)}, u32[]{:S(2)}, u32[]{:S(2)}) collective-permute-start(bf16[768,768]{1,0:T(8,128)(2,1)S(1)} %constant_dynamic-update-slice_fusion.9), channel_id=1, source_target_pairs={{0,1},{1,0},{2,3},{3,2},{4,5},{5,4},{6,7},{7,6},{8,9},{9,8},{10,11... | collective-permute-start | bytes 3538952 | tf_op jit(solution)/shard_map/ppermute | solution.py:636
  (26 other events, 53.7 us)

commit v2 on v1

--- a/solution.py
+++ b/solution.py
@@ -80,7 +80,7 @@
         mine = (i // (blocks // 2)) == h_ref[0]
         x = jnp.where(mine, own[...].astype(F32), peer[...].astype(F32))
     else:
-        x = xr[...] + pa[...].astype(F32) + pb[...].astype(F32)
+        x = xr[...] + (pa[...].astype(F32) + pb[...].astype(F32))
     x_out[...] = x
     xh, _ = norm_stats(x)
     n = (xh * g[...]).astype(BF)
@@ -132,7 +132,7 @@
         drr, dna, dnb = refs[:3]
     rest = refs[4 if split else 3 :]
     xn, gn, qr, kf, vf, orf, lser, wqkv, wo, segc, segr = rest[:11]
-    dr_out, da_out, dqkv_out, dn_out, dg_out, dks, dvs = rest[11:]
+    dr_out, da_out, dqk_out, dv_out, dn_out, dg_out, dks, dvs = rest[11:]
     i = pl.program_id(0)
     blk = blocks - 1 - i
     if split:
@@ -186,17 +186,18 @@
                     dks[0:keys, cols] += mm_tn(ds, qh)
                     dvs[0:keys, cols] += mm_tn(p.astype(BF), doh)
                 dq = jnp.where(half_lane(0), dqs[0], dqs[1]) * 0.125
-                dqkv_out[0, :, cols] = dq.astype(BF)
-            dqkv_out[1] = dks[here, :].astype(BF)
-            dqkv_out[2] = dvs[here, :].astype(BF)
-
+                dqk_out[:, cols] = dq.astype(BF)
+            dqk_out[:, pairs * 128 :] = dks[here, :].astype(BF)
+            dv_out[...] = dvs[here, :].astype(BF)
+
+    c = pairs * 128
     dn_out[...] = (
-        mm_nt(dqkv_out[0], wqkv[0]) + mm_nt(dqkv_out[1], wqkv[1]) + mm_nt(dqkv_out[2], wqkv[2])
+        mm_nt(dqk_out[:, :c], wqkv[0]) + mm_nt(dqk_out[:, c:], wqkv[1]) + mm_nt(dv_out[...], wqkv[2])
     ).astype(BF)
 
 
 def dense_fwd_kernel(xr, pa, pb, g, up, down, x_out, n_out, act_out, gp_out, p_out):
-    x = xr[...] + pa[...].astype(F32) + pb[...].astype(F32)
+    x = xr[...] + (pa[...].astype(F32) + pb[...].astype(F32))
     x_out[...] = x
     xh, _ = norm_stats(x)
     n = (xh * g[...]).astype(BF)
@@ -249,7 +250,7 @@
 
 def route_kernel(h_ref, xr, pa, pb, g, slot_ref, x_out, send_out, ms):
     i = pl.program_id(0)
-    x = xr[...] + pa[...].astype(F32) + pb[...].astype(F32)
+    x = xr[...] + (pa[...].astype(F32) + pb[...].astype(F32))
     x_out[...] = x
 
     @pl.when(i >= 2)
@@ -425,7 +426,8 @@
     outs = [
         (rows_spec(d, back), shape((length, d), F32)),
         (rows_spec(d, back), shape((length, d), BF)),
-        (pl.BlockSpec((3, BLK, c), lambda i, *a: (0, back(i), 0)), shape((3, length, c), BF)),
+        (rows_spec(2 * c, back), shape((length, 2 * c), BF)),
+        (rows_spec(c, back), shape((length, c), BF)),
         (rows_spec(d, back), shape((length, d), BF)),
         (fixed((8, d)), shape((8, d), F32)),
     ]
@@ -626,38 +628,203 @@
     return lax.ppermute(v, "head", SWAP)
 
 
-def exchange_half(v, bit, pairs):
-    half = v.shape[0] // 2
-    out = lax.dynamic_slice_in_dim(v, (1 - bit) * half, half, 0)
-    return lax.dynamic_slice_in_dim(v, bit * half, half, 0) + lax.ppermute(out, "dp", pairs)
-
-
-def regather(v, bit, pairs):
-    other = lax.ppermute(v, "dp", pairs)
-    both = jnp.concatenate([v, v], axis=0)
-    return lax.dynamic_update_slice_in_dim(both, other, (1 - bit) * v.shape[0], 0)
-
-
-def reduce_all(v, steps):
-    if steps is None:
-        return lax.psum(v, "dp")
-    me = lax.axis_index("dp")
-    half = v.shape[0] // 2
-    pairs = {s: [(i, i ^ s) for i in range(16)] for s in (1, 2, 4, 8)}
-    bits = {s: (me // s) % 2 for s in (1, 2, 4, 8)}
-    a, b = v[:half], v[half:]
-    a, b = exchange_half(a, bits[1], pairs[1]), exchange_half(b, bits[2], pairs[2])
-    a, b = exchange_half(a, bits[2], pairs[2]), exchange_half(b, bits[1], pairs[1])
-    c = jnp.concatenate([a, b], axis=0)
-    c = exchange_half(c, bits[4], pairs[4])
-    c = exchange_half(c, bits[8], pairs[8])
-    c = regather(c, bits[8], pairs[8])
-    c = regather(c, bits[4], pairs[4])
-    quarter = c.shape[0] // 2
-    a, b = c[:quarter], c[quarter:]
-    a, b = regather(a, bits[2], pairs[2]), regather(b, bits[1], pairs[1])
-    a, b = regather(a, bits[1], pairs[1]), regather(b, bits[2], pairs[2])
-    return jnp.concatenate([a, b], axis=0)
+def hop(sends, during=None, inputs=()):
+    flat = [v for v, _ in sends]
+    flat, inputs = lax.optimization_barrier((flat, inputs))
+    got = [
+        lax.ppermute(v, "dp", [(i, i ^ s) for i in range(16)])
+        for v, (_, s) in zip(flat, sends)
+    ]
+    result = during(*inputs) if during else inputs
+    return lax.optimization_barrier((got, result))
+
+
+def pick(bit, a, b):
+    return jnp.where(bit == 1, a, b)
+
+
+def total_of(a, b):
+    return (a.astype(F32) + b.astype(F32)).astype(BF)
+
+
+def fold_kernel(plan, bits, *refs):
+    at = 0
+    outs = refs[sum(n for _, n, _, _ in plan) :]
+    for kind, n, place, count in plan:
+        ins = refs[at : at + n]
+        at += n
+        bit = bits[place]
+        if kind == "sum":
+            outs[0][...] = total_of(ins[0][...], ins[1][...])
+            outs = outs[1:]
+        elif kind == "cut":
+            half = ins[0].shape[0] // 2
+            lo, hi = ins[0][:half, :], ins[0][half:, :]
+            outs[0][...] = pick(bit, lo, hi)
+            outs[1][...] = pick(bit, hi, lo)
+            outs = outs[2:]
+        elif kind == "split":
+            for j in range(n // 2):
+                k, g = ins[2 * j], ins[2 * j + 1]
+                q = k.shape[0] // 2
+                rows = slice(j * q, j * q + q)
+                lo = total_of(k[:q, :], g[:q, :])
+                hi = total_of(k[q:, :], g[q:, :])
+                outs[0][rows, :] = pick(bit, lo, hi)
+                outs[1][rows, :] = pick(bit, hi, lo)
+            outs = outs[2:]
+        else:
+            q = ins[0].shape[0] // count
+            for j in range(count):
+                p, g = ins[0][j * q : j * q + q, :], ins[1][j * q : j * q + q, :]
+                outs[j][:q, :] = pick(bit, g, p)
+                outs[j][q:, :] = pick(bit, p, g)
+            outs = outs[count:]
+
+
+PLACE = {1: 0, 2: 1, 4: 2, 8: 3}
+
+
+def whole(arrays):
+    return [pl.BlockSpec(a.shape, lambda i, *r, n=len(a.shape): (0,) * n) for a in arrays]
+
+
+def one_step(kernel, bits, args, outs):
+    moved = sum(a.size * a.dtype.itemsize for a in (*args, *outs))
+    return call(kernel, (1,), whole(args), whole(outs), outs, [], moved, moved, args, prefetch=bits)
+
+
+def fold(bits, items):
+    plan, args, outs, sizes = [], [], [], []
+    for kind, arrays, step, count in items:
+        plan.append((kind, len(arrays), PLACE[step], count))
+        args += arrays
+        rows, width = arrays[0].shape
+        if kind == "sum":
+            made = [rows]
+        elif kind == "cut":
+            made = [rows // 2] * 2
+        elif kind == "split":
+            made = [sum(a.shape[0] for a in arrays) // 4] * 2
+        else:
+            made = [2 * rows // count] * count
+        outs += [shape((r, width), BF) for r in made]
+        sizes.append(len(made))
+    flat = one_step(functools.partial(fold_kernel, tuple(plan)), bits, args, outs)
+    result = []
+    for n in sizes:
+        result.append(flat[:n])
+        flat = flat[n:]
+    return result
+
+
+def grad_rounds(sends, keeps):
+    one, two = (1, 2, 4, 8), (2, 1, 8, 4)
+    got = yield list(zip(sends, one))
+    out = yield [("split", [k, g], s, 1) for k, g, s in zip(keeps, got, two)]
+    got = yield [(o[0], s) for o, s in zip(out, two)]
+    keeps = [o[1] for o in out]
+    out = yield [
+        ("split", [keeps[0], got[0], keeps[1], got[1]], 4, 1),
+        ("split", [keeps[2], got[2], keeps[3], got[3]], 1, 1),
+    ]
+    got = yield [(out[0][0], 4), (out[1][0], 1)]
+    out = yield [("split", [out[0][1], got[0]], 8, 1), ("split", [out[1][1], got[1]], 2, 1)]
+    got = yield [(out[0][0], 8), (out[1][0], 2)]
+    out = yield [("sum", [out[0][1], got[0]], 8, 1), ("sum", [out[1][1], got[1]], 2, 1)]
+    got = yield [(out[0][0], 8), (out[1][0], 2)]
+    out = yield [("raise", [out[0][0], got[0]], 8, 1), ("raise", [out[1][0], got[1]], 2, 1)]
+    got = yield [(out[0][0], 4), (out[1][0], 1)]
+    out = yield [("raise", [out[0][0], got[0]], 4, 2), ("raise", [out[1][0], got[1]], 1, 2)]
+    parts = [*out[0], *out[1]]
+    got = yield list(zip(parts, two))
+    out = yield [("raise", [p, g], s, 1) for p, g, s in zip(parts, got, two)]
+    parts = [o[0] for o in out]
+    got = yield list(zip(parts, one))
+    return [x for pair in zip(parts, got) for x in pair]
+
+
+def small_rounds(v):
+    for s in (1, 2, 4, 8):
+        got = yield [(v, s)]
+        v = v + got[0]
+        yield []
+    return v
+
+
+class Lane:
+    def __init__(self, rounds):
+        self.rounds = rounds
+        self.value = None
+        self.sends = next(rounds)
+
+    def push(self, value):
+        try:
+            return self.rounds.send(value)
+        except StopIteration as stop:
+            self.value, self.sends = stop.value, []
+            return []
+
+
+def advance(bits, lanes, during=None, inputs=()):
+    got, result = hop([x for lane in lanes for x in lane.sends], during, inputs)
+    asked = []
+    for lane in lanes:
+        count = len(lane.sends)
+        asked.append((lane, lane.push(got[:count]) if count else []))
+        got = got[count:]
+    items = [item for _, group in asked for item in group]
+    done = fold(bits, items) if items else []
+    for lane, group in asked:
+        if lane.value is None:
+            lane.sends = lane.push(done[: len(group)]) or []
+        done = done[len(group) :]
+    return result
+
+
+def wide(ref_a, ref_b, bit):
+    a, b = ref_a[...].astype(F32), ref_b[...].astype(F32)
+    return pick(bit, b, a), pick(bit, a, b)
+
+
+def finish_wide_kernel(bits, xp, xg, yp, yg, ap, ag, bp, bg, up, down, qkv, out):
+    lo, hi = wide(xp, xg, bits[0])
+    f = lo.shape[1]
+    up[:, :f] = lo
+    up[:, f:] = hi
+    lo, hi = wide(yp, yg, bits[1])
+    f = lo.shape[0]
+    down[:f, :] = lo
+    down[f:, :] = hi
+    c = qkv.shape[2]
+    for j, block in enumerate(wide(ap, ag, bits[2])):
+        n = block.shape[0]
+        qkv[0, j * n : j * n + n, :] = block[:, :c]
+        qkv[1, j * n : j * n + n, :] = block[:, c:]
+    v, o = wide(bp, bg, bits[3])
+    n = v.shape[0]
+    qkv[2, :n, :] = v[:, :c]
+    qkv[2, n:, :] = v[:, c:]
+    out[...] = o
+
+
+def finish_narrow_kernel(bits, xp, xg, yp, yg, ap, ag, bp, bg, qkv, out):
+    xl, xh = wide(xp, xg, bits[0])
+    yl, yh = wide(yp, yg, bits[1])
+    al, ah = wide(ap, ag, bits[2])
+    bl, bh = wide(bp, bg, bits[3])
+    n = xl.shape[0]
+    c = qkv.shape[2]
+    for j, block in enumerate((xl, xh, yl, yh)):
+        at = slice(j * n, j * n + n)
+        qkv[0, at, :] = block[:, :c]
+        qkv[1, at, :] = block[:, c:]
+    half = qkv.shape[1] // 2
+    for j, block in enumerate((al, ah)):
+        qkv[2, j * n : j * n + n, :] = block[:, :c]
+        qkv[2, half + j * n : half + j * n + n, :] = block[:, c:]
+    out[:n, :] = bl
+    out[n:, :] = bh
 
 
 def body(
@@ -716,14 +883,17 @@
         m_own, m_peer, grad_own, grad_peer, centroids, expert_up, expert_down
     )
     dm_sum = (dmo.astype(F32) + swap(dmp).astype(F32)).astype(BF)
-    dm_own = collect(travel(dm_sum), slot_col)
-    dm_peer = swap(dm_own)
     up_grad = mm_tn(m_all, due_all)[None]
     down_grad = mm_tn(ae_all, dy_all)[None]
+    dm_back, up_grad, down_grad = lax.optimization_barrier((travel(dm_sum), up_grad, down_grad))
+    dm_own = collect(dm_back, slot_col)
+    dm_peer = swap(dm_own)
+    y_sum = (yo.astype(F32) + swap(yp).astype(F32)).astype(BF)
+    y_back = travel(y_sum)
     dc = dc[:1]
     cen_grad = dc + swap(dc)
 
-    dr2, da2, dqkv2, dn2, dg3 = attention_backward(
+    dr2, da2, dqk2, dv2, dn2, dg3 = attention_backward(
         h,
         (cotangent, cot_peer, dm_own, dm_peer),
         True,
@@ -736,50 +906,127 @@
         segr,
     )
     dn2r = swap(dn2)
-
-    def attention_grads(n, dqkv, o, da):
-        w = [mm_tn(n, dqkv[j]).astype(BF) for j in range(3)]
-        wo = mm_tn(o, da).astype(BF)
-        c = wo.shape[0]
-        return jnp.concatenate([*w, wo[:, :c], wo[:, c:]], axis=0)
-
-    def split_grads(total):
-        total = total.astype(F32)
-        c = total.shape[1]
-        wo = jnp.concatenate([total[3 * d : 3 * d + c], total[3 * d + c :]], axis=1)
-        return total[: 3 * d].reshape(3, d, c), wo
-
-    qkv_second, out_second = split_grads(reduce_all(attention_grads(n3, dqkv2, o2, da2), steps))
-    y_sum = (yo.astype(F32) + swap(yp).astype(F32)).astype(BF)
-    second = collect_add(h, travel(y_sum), slot_col, x2)
-
-    dr1, df, du, dnd, dg2 = dense_backward(dr2, dn2, dn2r, first, gain[2], gp, up_one, down_one)
-    dndr = swap(dnd)
-    f = du.shape[1]
-    w_up = mm_tn(n2, du).astype(BF)
-    w_down = mm_tn(act, df).astype(BF)
-    dense_total = jnp.concatenate([w_up[:, : f // 2], w_up[:, f // 2 :], w_down], axis=0)
-    dense_total = reduce_all(dense_total, steps).astype(F32)
-    up_first = jnp.concatenate([dense_total[:d], dense_total[d : 2 * d]], axis=1)
-    down_first = dense_total[2 * d :]
-
-    dr0, da1, dqkv1, dn1, dg1 = attention_backward(
-        h,
-        (dr1, dnd, dndr),
-        False,
-        x1,
-        gain[1],
-        (qkv1, o1, lse1),
-        qkv_one,
-        out_one,
-        segc,
-        segr,
-    )
-    dn1r = swap(dn1)
-    input_grad, dg0 = final_step(h, dr0, dn1, dn1r, tokens, tokens_peer, gain[0])
-    qkv_first, out_first = split_grads(reduce_all(attention_grads(n1, dqkv1, o1, da1), steps))
-    gain_grads = jnp.concatenate([dg0[:1], dg1[:1], dg2[:1], dg3[:1]], axis=0)
-    gain_grads = lax.psum(gain_grads, "dp")
+    f = up_one.shape[1]
+    c = qkv_one.shape[2]
+
+    def grad(a, b):
+        return mm_tn(a, b).astype(BF)
+
+    def value_sides(n, dv):
+        w = grad(n, dv)
+        return jnp.concatenate([w[: d // 2], w[d // 2 :]], axis=1)
+
+    def finish(dr, dna, dnb):
+        return final_step(h, dr, dna, dnb, tokens, tokens_peer, gain[0])
+
+    def gather_y(y):
+        return collect_add(h, y, slot_col, x2)
+
+    def stack_gains(dg0):
+        return jnp.concatenate([dg0[:1], dg1[:1], dg2[:1], dg3[:1]], axis=0)
+
+    def last_attention(dr, dna, dnb):
+        return attention_backward(
+            h, (dr, dna, dnb), False, x1, gain[1], (qkv1, o1, lse1), qkv_one, out_one, segc, segr
+        )
+
+    qk_two = grad(n3, dqk2)
+    vo_two = jnp.concatenate([value_sides(n3, dv2), grad(o2, da2)], axis=0)
+    if steps is None:
+        dr1, df, du, dnd, dg2 = dense_backward(
+            dr2, dn2, dn2r, first, gain[2], gp, up_one, down_one
+        )
+        dr0, da1, dqk1, dv1, dn1, dg1 = last_attention(dr1, dnd, swap(dnd))
+        input_grad, dg0 = finish(dr0, dn1, swap(dn1))
+        second = gather_y(y_back)
+        qk_one = grad(n1, dqk1)
+        vo_one = jnp.concatenate([value_sides(n1, dv1), grad(o1, da1)], axis=0)
+        up_first, down_first, qk_two, vo_two, qk_one, vo_one, gain_grads = lax.psum(
+            (grad(n2, du), grad(act, df), qk_two, vo_two, qk_one, vo_one, stack_gains(dg0)), "dp"
+        )
+
+        def unpack(qk, vo):
+            v, wo = vo[: d // 2], vo[d // 2 :]
+            v = jnp.concatenate([v[:, :c], v[:, c:]], axis=0)
+            return jnp.stack([qk[:, :c], qk[:, c:], v]).astype(F32), wo.astype(F32)
+
+        up_first, down_first = up_first.astype(F32), down_first.astype(F32)
+        qkv_second, out_second = unpack(qk_two, vo_two)
+        qkv_first, out_first = unpack(qk_one, vo_one)
+    else:
+        me = lax.axis_index("dp")
+        bits = jnp.stack([(me // s) % 2 for s in (1, 2, 4, 8)]).astype(jnp.int32)
+        cut_two = fold(bits, [("cut", [qk_two], 4, 1), ("cut", [vo_two], 8, 1)])
+        cut_two, dr2, dn2, dn2r, y_back = lax.optimization_barrier(
+            (cut_two, dr2, dn2, dn2r, y_back)
+        )
+        dr1, df, du, dnd, dg2 = dense_backward(
+            dr2, dn2, dn2r, first, gain[2], gp, up_one, down_one
+        )
+        dndr = swap(dnd)
+
+        def up_part(bit):
+            return grad(n2, lax.dynamic_slice_in_dim(du, bit * (f // 2), f // 2, 1))
+
+        def down_part(bit):
+            return grad(lax.dynamic_slice_in_dim(act, bit * (f // 2), f // 2, 1), df)
+
+        sends = [up_part(1 - bits[0]), down_part(1 - bits[1]), cut_two[0][0], cut_two[1][0]]
+        keeps = [None, None, cut_two[0][1], cut_two[1][1]]
+
+        def heavy(dr, dna, dnb):
+            return last_attention(dr, dna, dnb), up_part(bits[0]), down_part(bits[1])
+
+        got, (last, keeps[0], keeps[1]) = hop(
+            list(zip(sends, (1, 2, 4, 8))), heavy, (dr1, dnd, dndr)
+        )
+        dr0, da1, dqk1, dv1, dn1, dg1 = last
+        dn1r = swap(dn1)
+        wide_lane = Lane(grad_rounds(sends, keeps))
+        cut = fold(bits, wide_lane.push(got))
+        wide_lane.sends = wide_lane.push(cut)
+
+        def narrow_grads(n, dqk, dv, o, da):
+            half = d // 2
+            return (
+                grad(n[:, :half], dqk),
+                grad(n[:, half:], dqk),
+                value_sides(n, dv),
+                grad(o, da),
+            )
+
+        raw = advance(bits, [wide_lane], narrow_grads, (n1, dqk1, dv1, o1, da1))
+        cut = fold(bits, [("cut", [w], s, 1) for w, s in zip(raw, (1, 2, 4, 8))])
+        lane = Lane(grad_rounds([x[0] for x in cut], [x[1] for x in cut]))
+        input_grad, dg0 = advance(bits, [wide_lane, lane], finish, (dr0, dn1, dn1r))
+        gain_lane = Lane(small_rounds(stack_gains(dg0)))
+        lanes = [wide_lane, lane, gain_lane]
+        second = advance(bits, lanes, gather_y, (y_back,))
+        while wide_lane.sends:
+            advance(bits, lanes)
+
+        def finish_wide(*parts):
+            return one_step(
+                finish_wide_kernel,
+                bits,
+                parts,
+                [
+                    shape((d, f), F32),
+                    shape((f, d), F32),
+                    shape((3, d, c), F32),
+                    shape((c, d), F32),
+                ],
+            )
+
+        up_first, down_first, qkv_second, out_second = advance(
+            bits, lanes, finish_wide, wide_lane.value
+        )
+        while lane.sends:
+            advance(bits, lanes)
+        gain_grads = gain_lane.value
+        qkv_first, out_first = one_step(
+            finish_narrow_kernel, bits, lane.value, [shape((3, d, c), F32), shape((c, d), F32)]
+        )
     first_own = lax.dynamic_slice_in_dim(first, side * count, count, 0).astype(BF)
     return (
         first_own,

time: 675 us -> 596 us (0.88)
  blocking collectives: 75.1 us -> 0 us
  Pallas kernels: 190 us -> 236 us
  waiting for transfers between devices: 217 us -> 176 us
  other arithmetic: 34.7 us -> 11.8 us
  starting transfers between devices: 78.7 us -> 90.2 us
    psum x1 -> x0, blocking collectives: 75.1 us -> none  [body(): gain_grads = lax.psum(gain_grads, 'dp')]
    pallas_call x12 -> x25, Pallas kernels: 190 us -> 236 us  [call(): pl.pallas_call(kernel, grid_spec=spec, out_shape=outs, compiler_params=PA...]
    ppermute x36 -> x52, waiting for transfers between devices: 133 us -> 112 us  [hop(): lax.ppermute(v, 'dp', [(i, i ^ s) for i in range(16)])]
    all_to_all x4, waiting for transfers between devices: 69.8 us -> 49.9 us  [travel(): return lax.all_to_all(box, 'dp', 0, 0, tiled=True).reshape(slots, d)]
    concatenate x29 -> x3, other arithmetic: 14.3 us -> 1.98 us  [the longest x1 1.1 us: body(): vo_two = jnp.concatenate([value_sides(n3, dv2), grad(o2, da2)], axis=0)]
    ppermute x36 -> x52, starting transfers between devices: 47.2 us -> 56.1 us  [hop(): lax.ppermute(v, 'dp', [(i, i ^ s) for i in range(16)])]
    add x18 -> x4, other arithmetic: 9.39 us -> 0.65 us  [small_rounds(): v = v + got[0]]
    unnamed x73 -> x163, local copies, waits for them, and re-layouts: 12.3 us -> 19.4 us
  transfers between devices with their start and end apart: 54 -> 70, of which waited for: 31 -> 25; matrix products, arithmetic and copies ran while one was open for 12% -> 10% of each run, Pallas kernels for 18% -> 22%
where the time goes in v2:
time: 596 us; the launch traced here: 586 us
  Pallas kernels  236 us (40%)
  waiting for transfers between devices  176 us (30%)
  starting transfers between devices  90.2 us (15%)
  matrix products  41.3 us (7%)
  local copies, waits for them, and re-layouts  29 us (5%)
  other arithmetic  11.8 us (2%)
    pallas_call x25, Pallas kernels, call(): pl.pallas_call(kernel, grid_spec=spec, out_shape=outs, compiler_params=PA...  236 us
    ppermute x52, waiting for transfers between devices, hop(): lax.ppermute(v, 'dp', [(i, i ^ s) for i in range(16)])  112 us
    ppermute x52, starting transfers between devices, hop(): lax.ppermute(v, 'dp', [(i, i ^ s) for i in range(16)])  56.1 us
    all_to_all x4, waiting for transfers between devices, travel(): return lax.all_to_all(box, 'dp', 0, 0, tiled=True).reshape(slots, d)  49.9 us
    dot_general x13, matrix products, mm_tn(): lax.dot_general(a, b, (((0,), (0,)), ((), ())), preferred_element_type=F32)  41 us
    all_to_all x4, starting transfers between devices, travel(): return lax.all_to_all(box, 'dp', 0, 0, tiled=True).reshape(slots, d)  31.7 us
    unnamed x163, local copies, waits for them, and re-layouts  19.4 us
    ppermute x14, waiting for transfers between devices, swap(): return lax.ppermute(v, 'head', SWAP)  14.1 us
  transfers between devices with their start and end apart: 70, of which 25 were waited for; matrix products, arithmetic and copies ran while one was open for 10% of the time, Pallas kernels for 22%

profile of v2, /device:TPU:0, one launch (start us, length us, event | category | flops | bytes accessed | tf_op | source)
XLA Modules:
  0.0 586.5 jit_solution(9849750239066417317)
XLA Ops:
  5.2 19.0 %shard_map.237 = (f32[1024,768]{1,0:T(8,128)}, bf16[1024,768]{1,0:T(8,128)(2,1)}, bf16[3,1024,384]{2,1,0:T(8,128)(2,1)}, bf16[1024,384]{1,0:T(8,128)(2,1)}, f32[...) custom-call(s32[1]{0:T(128)} %bitcast.h_ref, bf16[512,768]{1,0:T(8,128)(2,1)} %xo.1, bf16[512,768]{1,0:T(8,128)(2,1)} %copy-done.15, ...), custom_call_target="tpu_custom_call" | custom-call | flops 8053063680 | bytes 15728640 | tf_op jit(solution)/shard_map/pallas_call | solution.py:356
  24.3 3.6 collective-permute-done.1.pb
  29.0 15.4 %shard_map.238 = (f32[1024,768]{1,0:T(8,128)}, bf16[1024,768]{1,0:T(8,128)(2,1)}, bf16[1024,1536]{1,0:T(8,128)(2,1)}, bf16[1024,1536]{1,0:T(8,128)(2,1)}, bf16[1024,768]{1,0:T(8,128)(2,1)}) custom-call(f32[1024,768]{1,0:T(8,128)} %get-tuple-element.288.xr, bf16[1024,768]{1,0:T(8,128)(2,1)} %get-tuple-element.289.pa, bf16[1024,768]{1,0:T(8,128)(2,1)} %copy-done.66, ...), custom_call_target="tpu_custom_call" | custom-call | flops 4831838208 | bytes 20447232 | tf_op jit(solution)/shard_map/pallas_call | solution.py:356
  46.5 3.8 shard_map.241
  50.3 8.2 %all-to-all-start.1 = ((bf16[16,64,768]{2,1,0:T(8,128)(2,1)}), bf16[16,64,768]{2,1,0:T(8,128)(2,1)S(1)}, u32[]{:S(2)}, u32[]{:S(2)}) async-start(bf16[16,64,768]{2,1,0:T(8,128)(2,1)} %bitcast.48), calls=%async_computation.1 | async-start | bytes 3145728 | tf_op jit(solution)/shard_map/all_to_all | solution.py:863
  59.7 19.3 %shard_map.239 = (f32[1024,768]{1,0:T(8,128)}, bf16[1024,768]{1,0:T(8,128)(2,1)}, bf16[3,1024,384]{2,1,0:T(8,128)(2,1)}, bf16[1024,384]{1,0:T(8,128)(2,1)}, f32[...) custom-call(s32[1]{0:T(128)} %bitcast.h_ref, f32[1024,768]{1,0:T(8,128)} %get-tuple-element.290.refs_0_.refs_3_, ...), custom_call_target="tpu_custom_call" | custom-call | flops 8053063680 | bytes 15728640 | tf_op jit(solution)/shard_map/pallas_call | solution.py:356
  79.1 3.6 collective-permute-done.4.pb
  83.8 6.7 %shard_map.240 = (f32[1024,768]{1,0:T(8,128)}, bf16[1024,768]{1,0:T(8,128)(2,1)}) custom-call(s32[1]{0:T(128)} %bitcast.h_ref, f32[1024,768]{1,0:T(8,128)} %get-tuple-element.292.xr.xn, bf16[1024,768]{1,0:T(8,128)(2,1)} %get-tuple-element.295.pa, bf16[1024,768]{1,0:T(8,128)(2,1)} %copy-done.10, f32[1,768]{1,0:T(1,128)} %get-tuple-element.569.g.refs_5_, ...), custom_call_target="tpu_custom_call" | custom-call | flops 805306368 | bytes 11010048 | tf_op jit(solution)/shard_map/pallas_call | solution.py:356
  90.5 2.3 all-to-all-done.1
  92.8 8.2 %all-to-all-start = ((bf16[16,64,768]{2,1,0:T(8,128)(2,1)}), bf16[16,64,768]{2,1,0:T(8,128)(2,1)S(1)}, u32[]{:S(2)}, u32[]{:S(2)}) async-start(bf16[16,64,768]{2,1,0:T(8,128)(2,1)} %bitcast.50), calls=%async_computation | async-start | bytes 3145728 | tf_op jit(solution)/shard_map/all_to_all | solution.py:863
  101.1 33.2 %all-to-all-done = bf16[16,64,768]{2,1,0:T(8,128)(2,1)S(1)} async-done(((bf16[16,64,768]{2,1,0:T(8,128)(2,1)}), bf16[16,64,768]{2,1,0:T(8,128)(2,1)S(1)}, u32[]{:S(2)}, u32[]{:S(2)}) %all-to-all-start) | async-done | bytes 1572896 | tf_op jit(solution)/shard_map/all_to_all | solution.py:863
  134.3 3.4 collective-permute-done.5.mp
  138.9 35.5 %shard_map.242 = (bf16[1024,768]{1,0:T(8,128)(2,1)}, bf16[1024,768]{1,0:T(8,128)(2,1)}, bf16[1024,768]{1,0:T(8,128)(2,1)}, bf16[1024,768]{1,0:T(8,128)(2,1)}, bf...) custom-call(bf16[1024,768]{1,0:T(8,128)(2,1)} %bitcast.47, ...), custom_call_target="tpu_custom_call" | custom-call | flops 19327352832 | bytes 31457280 | tf_op jit(solution)/shard_map/pallas_call | solution.py:356
  174.6 3.5 collective-permute-done.7
  178.1 3.0 add_convert_fusion.1
  181.0 7.3 %all-to-all-start.2 = ((bf16[16,64,768]{2,1,0:T(8,128)(2,1)}), bf16[16,64,768]{2,1,0:T(8,128)(2,1)S(1)}, u32[]{:S(2)}, u32[]{:S(2)}) async-start(bf16[16,64,768]{2,1,0:T(8,128)(2,1)} %bitcast.12), calls=%async_computation.2 | async-start | bytes 3145728 | tf_op jit(solution)/shard_map/all_to_all | solution.py:863
  188.9 9.7 %convolution_bitcast_fusion = f32[1,1536,768]{2,1,0:T(8,128)} fusion(bf16[2048,1536]{1,0:T(8,128)(2,1)} %get-tuple-element.301, bf16[2048,768]{1,0:T(8,128)(2,1)} %get-tuple-element.302), kind=kOutput, calls=%fused_computation | convolution fusion | flops 4831838208 | bytes 14155776 | tf_op jit(solution)/shard_map/dot_general | solution.py:29
  198.7 9.5 %convolution_bitcast_fusion.1 = f32[1,768,1536]{2,1,0:T(8,128)} fusion(bf16[2048,768]{1,0:T(8,128)(2,1)S(1)} %copy-done.78, bf16[2048,1536]{1,0:T(8,128)(2,1)} %get-tuple-element.300), kind=kOutput, calls=%fused_computation.1 | convolution fusion | flops 4831838208 | bytes 14155776 | tf_op jit(solution)/shard_map/dot_general | solution.py:29
  208.2 14.4 %all-to-all-done.2 = bf16[16,64,768]{2,1,0:T(8,128)(2,1)S(1)} async-done(((bf16[16,64,768]{2,1,0:T(8,128)(2,1)}), bf16[16,64,768]{2,1,0:T(8,128)(2,1)S(1)}, u32[]{:S(2)}, u32[]{:S(2)}) %all-to-all-start.2) | async-done | bytes 1572896 | tf_op jit(solution)/shard_map/all_to_all | solution.py:863
  223.7 3.6 shard_map.243.refs_2_
  227.3 2.9 add_convert_fusion
  230.3 8.0 %all-to-all-start.3 = ((bf16[16,64,768]{2,1,0:T(8,128)(2,1)}), bf16[16,64,768]{2,1,0:T(8,128)(2,1)S(1)}, u32[]{:S(2)}, u32[]{:S(2)}) async-start(bf16[16,64,768]{2,1,0:T(8,128)(2,1)} %bitcast.17), calls=%async_computation.3 | async-start | bytes 3145728 | tf_op jit(solution)/shard_map/all_to_all | solution.py:863
  238.3 26.7 %shard_map.244 = (f32[1024,768]{1,0:T(8,128)}, bf16[1024,768]{1,0:T(8,128)(2,1)}, bf16[1024,768]{1,0:T(8,128)(2,1)}, bf16[1024,384]{1,0:T(8,128)(2,1)}, bf16[1024,768]{1,0:T(8,128)(2,1)}, /*index=5*/f32[8,768]{1,0:T(8,128)}) custom-call(s32[1]{0:T(128)} %bitcast.h_ref, bf16[512,768]{1,0:T(8,128)(2,1)} %refs_0_.3, ...), custom_call_target="tpu_custom_call" | custom-call | flops 12884901888 | bytes 15728640 | tf_op jit(solution)/shard_map/pallas_call | solution.py:356
  265.9 2.7 convolution_convert_fusion.6
  272.6 2.5 convolution_convert_fusion.refs_0_
  275.0 3.8 shard_map.245
  280.0 13.4 %shard_map.246 = (f32[1024,768]{1,0:T(8,128)}, bf16[1024,768]{1,0:T(8,128)(2,1)}, bf16[1024,1536]{1,0:T(8,128)(2,1)}, bf16[1024,768]{1,0:T(8,128)(2,1)}, f32[8,768]{1,0:T(8,128)}) custom-call(f32[1024,768]{1,0:T(8,128)} %get-tuple-element.319.drr, bf16[1024,768]{1,0:T(8,128)(2,1)} %get-tuple-element.320.dna, bf16[1024,768]{1,0:T(8,128)(2,1)} %copy-done.62, ...), custom_call_target="tpu_custom_call" | custom-call | flops 4831838208 | bytes 20447232 | tf_op jit(solution)/shard_map/pallas_call | solution.py:356
  293.7 4.5 fusion.17.refs_2_
  300.6 2.5 fusion.14.refs_0_
  309.4 2.4 collective-permute-start.15
  311.8 26.5 %shard_map.247 = (f32[1024,768]{1,0:T(8,128)}, bf16[1024,768]{1,0:T(8,128)(2,1)}, bf16[1024,768]{1,0:T(8,128)(2,1)}, bf16[1024,384]{1,0:T(8,128)(2,1)}, bf16[1024,768]{1,0:T(8,128)(2,1)}, /*index=5*/f32[8,768]{1,0:T(8,128)}) custom-call(s32[1]{0:T(128)} %bitcast.h_ref, f32[1024,768]{1,0:T(8,128)} %get-tuple-element.334.refs_0_, ...), custom_call_target="tpu_custom_call" | custom-call | flops 12884901888 | bytes 15728640 | tf_op jit(solution)/shard_map/pallas_call | solution.py:356
  340.1 6.1 %shard_map.248 = (bf16[384,768]{1,0:T(8,128)(2,1)}, bf16[384,768]{1,0:T(8,128)(2,1)}, bf16[384,768]{1,0:T(8,128)(2,1)}, bf16[384,768]{1,0:T(8,128)(2,1)}, bf16[1...) custom-call(s32[4]{0:T(128)} %pad_add_fusion.bits, ...), custom_call_target="tpu_custom_call" | custom-call | flops 10616832 | bytes 10616832 | tf_op jit(solution)/shard_map/pallas_call | solution.py:356
  357.0 5.0 collective-permute-done.18.refs_5_
  362.1 3.8 shard_map.250
  365.9 4.2 shard_map.249
  375.7 4.6 collective-permute-done.22.refs_3_
  383.2 6.3 %shard_map.251 = (f32[512,768]{1,0:T(8,128)}, f32[8,768]{1,0:T(8,128)}) custom-call(s32[1]{0:T(128)} %bitcast.h_ref, f32[1024,768]{1,0:T(8,128)} %get-tuple-element.398.drr, bf16[1024,768]{1,0:T(8,128)(2,1)} %get-tuple-element.399.dna, bf16[1024,768]{1,0:T(8,128)(2,1)} %copy-done.8, bf16[512,768]{1,0:T(8,128)(2,1)} %xo.1, bf16[512,768]{1,0:T(8,128)(2,1)} %copy-done.15, ...), custom_call_target="tpu_custom_call" | custom-call | flops 31457280 | bytes 11010048 | tf_op jit(solution)/shard_map/pallas_call | solution.py:356
  389.5 10.0 %collective-permute-done.25.refs_9_ = bf16[192,768]{1,0:T(8,128)(2,1)S(1)} collective-permute-done((bf16[192,768]{1,0:T(8,128)(2,1)S(1)}, bf16[192,768]{1,0:T(8,128)(2,1)S(1)}, u32[]{:S(2)}, u32[]{:S(2)}) %collective-permute-start.25) | collective-permute-done | bytes 294944 | tf_op jit(solution)/shard_map/ppermute | solution.py:635
  400.5 4.3 shard_map.252
  413.2 4.0 shard_map.253
  417.2 9.8 %collective-permute-done.31.refs_9_ = bf16[96,768]{1,0:T(8,128)(2,1)S(1)} collective-permute-done((bf16[96,768]{1,0:T(8,128)(2,1)}, bf16[96,768]{1,0:T(8,128)(2,1)S(1)}, u32[]{:S(2)}, u32[]{:S(2)}) %collective-permute-start.31) | collective-permute-done | bytes 147488 | tf_op jit(solution)/shard_map/ppermute | solution.py:635
  427.9 3.3 shard_map.254
  431.8 2.2 collective-permute-start.36
  436.1 2.2 collective-permute-done.38
  438.3 3.0 collective-permute-done.36.refs_5_
  441.3 4.2 collective-permute-done.34.refs_1_
  446.3 3.0 shard_map.255
  449.9 3.1 collective-permute-start.41
  453.7 12.9 %collective-permute-done.43 = f32[4,768]{1,0:T(4,128)S(1)} collective-permute-done((f32[4,768]{1,0:T(4,128)S(1)}, f32[4,768]{1,0:T(4,128)S(1)}, u32[]{:S(2)}, u32[]{:S(2)}) %collective-permute-start.43) | collective-permute-done | bytes 12320 | tf_op jit(solution)/shard_map/ppermute | solution.py:635
  467.6 3.4 shard_map.256
  475.9 11.5 %collective-permute-done.50 = f32[4,768]{1,0:T(4,128)S(1)} collective-permute-done((f32[4,768]{1,0:T(4,128)S(1)}, f32[4,768]{1,0:T(4,128)S(1)}, u32[]{:S(2)}, u32[]{:S(2)}) %collective-permute-start.50) | collective-permute-done | bytes 12320 | tf_op jit(solution)/shard_map/ppermute | solution.py:635
  488.6 4.9 collective-permute-done.48.refs_9_
  494.9 3.1 collective-permute-done.49.refs_11_
  499.9 4.6 shard_map.257
  507.5 2.5 collective-permute-start.54
  510.2 25.0 %collective-permute-done.55.refs_1_ = bf16[96,768]{1,0:T(8,128)(2,1)S(1)} collective-permute-done((bf16[96,768]{1,0:T(8,128)(2,1)}, bf16[96,768]{1,0:T(8,128)(2,1)S(1)}, u32[]{:S(2)}, u32[]{:S(2)}) %collective-permute-start.55) | collective-permute-done | bytes 147488 | tf_op jit(solution)/shard_map/ppermute | solution.py:635
  535.7 4.8 collective-permute-done.56.refs_3_
  541.2 2.6 shard_map.258
  548.3 9.3 %shard_map.259 = (f32[768,1536]{1,0:T(8,128)}, f32[1536,768]{1,0:T(8,128)}, f32[3,768,384]{2,1,0:T(8,128)}, f32[384,768]{1,0:T(8,128)}) custom-call(s32[4]{0:T(128)} %pad_add_fusion.bits, bf16[768,768]{1,0:T(8,128)(2,1)} %get-tuple-element.526.xp, bf16[768,768]{1,0:T(8,128)(2,1)} %copy-done.11, bf16[768,768]{1,0:T(8,128)(2,1)} %get-tuple-element.528.yp, ...), custom_call_target="tpu_custom_call" | custom-call | flops 21233664 | bytes 21233664 | tf_op jit(solution)/shard_map/pallas_call | solution.py:356
  558.4 3.0 shard_map.260
  564.7 2.1 collective-permute-start.64
  566.8 2.4 dynamic-slice_convert_fusion
  572.2 6.8 %collective-permute-done.63.ag = bf16[192,768]{1,0:T(8,128)(2,1)S(1)} collective-permute-done((bf16[192,768]{1,0:T(8,128)(2,1)}, bf16[192,768]{1,0:T(8,128)(2,1)S(1)}, u32[]{:S(2)}, u32[]{:S(2)}) %collective-permute-start.63) | collective-permute-done | bytes 294944 | tf_op jit(solution)/shard_map/ppermute | solution.py:635
  581.5 4.8 shard_map.261
  (304 shorter events, 92.8 us)
Async XLA Ops:
  44.5 14.1 %collective-permute-start.2 = (bf16[1024,768]{1,0:T(8,128)(2,1)}, bf16[1024,768]{1,0:T(8,128)(2,1)S(1)}, u32[]{:S(2)}, u32[]{:S(2)}) collective-permute-start(bf16[1024,768]{1,0:T(8,128)(2,1)} %get-tuple-element.291.refs_1_), channel_id=1, source_target_pairs={{0,16},{16,0},{1,17},{17,1},{2,18},{18,2},{3,19},{19,3},{4,20},{20... | collective-permute-start | bytes 4718600 | tf_op jit(solution)/shard_map/ppermute | solution.py:628
  50.3 42.5 %all-to-all-start.1 = ((bf16[16,64,768]{2,1,0:T(8,128)(2,1)}), bf16[16,64,768]{2,1,0:T(8,128)(2,1)S(1)}, u32[]{:S(2)}, u32[]{:S(2)}) async-start(bf16[16,64,768]{2,1,0:T(8,128)(2,1)} %bitcast.48), calls=%async_computation.1 | async-start | bytes 3145728 | tf_op jit(solution)/shard_map/all_to_all | solution.py:863
  92.8 41.5 %all-to-all-start = ((bf16[16,64,768]{2,1,0:T(8,128)(2,1)}), bf16[16,64,768]{2,1,0:T(8,128)(2,1)S(1)}, u32[]{:S(2)}, u32[]{:S(2)}) async-start(bf16[16,64,768]{2,1,0:T(8,128)(2,1)} %bitcast.50), calls=%async_computation | async-start | bytes 3145728 | tf_op jit(solution)/shard_map/all_to_all | solution.py:863
  101.0 33.3 %collective-permute-start.6 = (bf16[1024,768]{1,0:T(8,128)(2,1)S(1)}, bf16[1024,768]{1,0:T(8,128)(2,1)}, u32[]{:S(2)}, u32[]{:S(2)}) collective-permute-start(bf16[1024,768]{1,0:T(8,128)(2,1)S(1)} %bitcast.44), channel_id=1, source_target_pairs={{0,16},{16,0},{1,17},{17,1},{2,18},{18,2},{3,19},{19,3},{4,20},{20... | collective-permute-start | bytes 4718600 | tf_op jit(solution)/shard_map/ppermute | solution.py:628
  181.0 41.6 %all-to-all-start.2 = ((bf16[16,64,768]{2,1,0:T(8,128)(2,1)}), bf16[16,64,768]{2,1,0:T(8,128)(2,1)S(1)}, u32[]{:S(2)}, u32[]{:S(2)}) async-start(bf16[16,64,768]{2,1,0:T(8,128)(2,1)} %bitcast.12), calls=%async_computation.2 | async-start | bytes 3145728 | tf_op jit(solution)/shard_map/all_to_all | solution.py:863
  188.3 49.9 %collective-permute-start.3 = (bf16[512,768]{1,0:T(8,128)(2,1)}, bf16[512,768]{1,0:T(8,128)(2,1)}, u32[]{:S(2)}, u32[]{:S(2)}) collective-permute-start(bf16[512,768]{1,0:T(8,128)(2,1)} %refs_0_.3), channel_id=1, source_target_pairs={{0,16},{16,0},{1,17},{17,1},{2,18},{18,2},{3,19},{19,3},{4,20},{20... | collective-permute-start | bytes 2359304 | tf_op jit(solution)/shard_map/ppermute | solution.py:628
  188.4 38.9 %collective-permute-start.10 = (bf16[1024,768]{1,0:T(8,128)(2,1)}, bf16[1024,768]{1,0:T(8,128)(2,1)}, u32[]{:S(2)}, u32[]{:S(2)}) collective-permute-start(bf16[1024,768]{1,0:T(8,128)(2,1)} %get-tuple-element.318), channel_id=1, source_target_pairs={{0,16},{16,0},{1,17},{17,1},{2,18},{18,2},{3,19},{19,3},{4,20},{20... | collective-permute-start | bytes 4718600 | tf_op jit(solution)/shard_map/ppermute | solution.py:628
  227.3 11.0 %collective-permute-start.8 = (bf16[512,768]{1,0:T(8,128)(2,1)}, bf16[512,768]{1,0:T(8,128)(2,1)}, u32[]{:S(2)}, u32[]{:S(2)}) collective-permute-start(bf16[512,768]{1,0:T(8,128)(2,1)} %shard_map.243.refs_2_), channel_id=1, source_target_pairs={{0,16},{16,0},{1,17},{17,1},{2,18},{18,2},{3,19},{19,3},{4,20},{20... | collective-permute-start | bytes 2359304 | tf_op jit(solution)/shard_map/ppermute | solution.py:628
  230.3 48.5 %all-to-all-start.3 = ((bf16[16,64,768]{2,1,0:T(8,128)(2,1)}), bf16[16,64,768]{2,1,0:T(8,128)(2,1)S(1)}, u32[]{:S(2)}, u32[]{:S(2)}) async-start(bf16[16,64,768]{2,1,0:T(8,128)(2,1)} %bitcast.17), calls=%async_computation.3 | async-start | bytes 3145728 | tf_op jit(solution)/shard_map/all_to_all | solution.py:863
  265.0 13.8 %collective-permute-start.9 = (bf16[1024,768]{1,0:T(8,128)(2,1)}, bf16[1024,768]{1,0:T(8,128)(2,1)S(1)}, u32[]{:S(2)}, u32[]{:S(2)}) collective-permute-start(bf16[1024,768]{1,0:T(8,128)(2,1)} %get-tuple-element.320.dna), channel_id=1, source_target_pairs={{0,16},{16,0},{1,17},{17,1},{2,18},{18,2},{3,19},{19,3},{4,20},{20... | collective-permute-start | bytes 4718600 | tf_op jit(solution)/shard_map/ppermute | solution.py:628
  293.3 11.1 %collective-permute-start.11 = (bf16[1024,768]{1,0:T(8,128)(2,1)}, bf16[1024,768]{1,0:T(8,128)(2,1)S(1)}, u32[]{:S(2)}, u32[]{:S(2)}) collective-permute-start(bf16[1024,768]{1,0:T(8,128)(2,1)} %get-tuple-element.335.refs_1_), channel_id=1, source_target_pairs={{0,16},{16,0},{1,17},{17,1},{2,18},{18,2},{3,19},{19,3},{4,20},{20... | collective-permute-start | bytes 4718600 | tf_op jit(solution)/shard_map/ppermute | solution.py:628
  304.5 33.8 %collective-permute-start.12 = (bf16[768,768]{1,0:T(8,128)(2,1)S(1)}, bf16[768,768]{1,0:T(8,128)(2,1)S(1)}, u32[]{:S(2)}, u32[]{:S(2)}) collective-permute-start(bf16[768,768]{1,0:T(8,128)(2,1)S(1)} %fusion.8), channel_id=1, source_target_pairs={{0,1},{1,0},{2,3},{3,2},{4,5},{5,4},{6,7},{7,6},{8,9},{9,8},{10,11... | collective-permute-start | bytes 3538952 | tf_op jit(solution)/shard_map/ppermute | solution.py:635
  306.5 31.9 %collective-permute-start.13 = (bf16[768,768]{1,0:T(8,128)(2,1)S(1)}, bf16[768,768]{1,0:T(8,128)(2,1)S(1)}, u32[]{:S(2)}, u32[]{:S(2)}) collective-permute-start(bf16[768,768]{1,0:T(8,128)(2,1)S(1)} %fusion.11), channel_id=1, source_target_pairs={{0,2},{1,3},{2,0},{3,1},{4,6},{5,7},{6,4},{7,5},{8,10},{9,11},{10,... | collective-permute-start | bytes 3538952 | tf_op jit(solution)/shard_map/ppermute | solution.py:635
  308.0 30.3 %collective-permute-start.14 = (bf16[384,768]{1,0:T(8,128)(2,1)}, bf16[384,768]{1,0:T(8,128)(2,1)S(1)}, u32[]{:S(2)}, u32[]{:S(2)}) collective-permute-start(bf16[384,768]{1,0:T(8,128)(2,1)} %get-tuple-element.332), channel_id=1, source_target_pairs={{0,4},{1,5},{2,6},{3,7},{4,0},{5,1},{6,2},{7,3},{8,12},{9,13},{10,... | collective-permute-start | bytes 1769480 | tf_op jit(solution)/shard_map/ppermute | solution.py:635
  309.4 28.9 %collective-permute-start.15 = (bf16[384,768]{1,0:T(8,128)(2,1)}, bf16[384,768]{1,0:T(8,128)(2,1)S(1)}, u32[]{:S(2)}, u32[]{:S(2)}) collective-permute-start(bf16[384,768]{1,0:T(8,128)(2,1)} %get-tuple-element.333), channel_id=1, source_target_pairs={{0,8},{1,9},{2,10},{3,11},{4,12},{5,13},{6,14},{7,15},{8,0},{9,1},... | collective-permute-start | bytes 1769480 | tf_op jit(solution)/shard_map/ppermute | solution.py:635
  338.4 31.7 %collective-permute-start.20 = (bf16[1024,768]{1,0:T(8,128)(2,1)}, bf16[1024,768]{1,0:T(8,128)(2,1)S(1)}, u32[]{:S(2)}, u32[]{:S(2)}) collective-permute-start(bf16[1024,768]{1,0:T(8,128)(2,1)} %get-tuple-element.399.dna), channel_id=1, source_target_pairs={{0,16},{16,0},{1,17},{17,1},{2,18},{18,2},{3,19},{19,3},{4,20},{20... | collective-permute-start | bytes 4718600 | tf_op jit(solution)/shard_map/ppermute | solution.py:628
  346.2 15.9 %collective-permute-start.16 = (bf16[384,768]{1,0:T(8,128)(2,1)}, bf16[384,768]{1,0:T(8,128)(2,1)S(1)}, u32[]{:S(2)}, u32[]{:S(2)}) collective-permute-start(bf16[384,768]{1,0:T(8,128)(2,1)} %get-tuple-element.363), channel_id=1, source_target_pairs={{0,2},{1,3},{2,0},{3,1},{4,6},{5,7},{6,4},{7,5},{8,10},{9,11},{10,... | collective-permute-start | bytes 1769480 | tf_op jit(solution)/shard_map/ppermute | solution.py:635
  346.7 15.3 %collective-permute-start.17 = (bf16[384,768]{1,0:T(8,128)(2,1)}, bf16[384,768]{1,0:T(8,128)(2,1)S(1)}, u32[]{:S(2)}, u32[]{:S(2)}) collective-permute-start(bf16[384,768]{1,0:T(8,128)(2,1)} %get-tuple-element.364), channel_id=1, source_target_pairs={{0,1},{1,0},{2,3},{3,2},{4,5},{5,4},{6,7},{7,6},{8,9},{9,8},{10,11... | collective-permute-start | bytes 1769480 | tf_op jit(solution)/shard_map/ppermute | solution.py:635
  347.3 14.7 %collective-permute-start.18 = (bf16[192,768]{1,0:T(8,128)(2,1)}, bf16[192,768]{1,0:T(8,128)(2,1)S(1)}, u32[]{:S(2)}, u32[]{:S(2)}) collective-permute-start(bf16[192,768]{1,0:T(8,128)(2,1)} %get-tuple-element.365), channel_id=1, source_target_pairs={{0,8},{1,9},{2,10},{3,11},{4,12},{5,13},{6,14},{7,15},{8,0},{9,1},... | collective-permute-start | bytes 884744 | tf_op jit(solution)/shard_map/ppermute | solution.py:635
  347.8 14.2 %collective-permute-start.19 = (bf16[192,768]{1,0:T(8,128)(2,1)}, bf16[192,768]{1,0:T(8,128)(2,1)S(1)}, u32[]{:S(2)}, u32[]{:S(2)}) collective-permute-start(bf16[192,768]{1,0:T(8,128)(2,1)} %get-tuple-element.366), channel_id=1, source_target_pairs={{0,4},{1,5},{2,6},{3,7},{4,0},{5,1},{6,2},{7,3},{8,12},{9,13},{10,... | collective-permute-start | bytes 884744 | tf_op jit(solution)/shard_map/ppermute | solution.py:635
  370.1 10.1 %collective-permute-start.22 = (bf16[192,768]{1,0:T(8,128)(2,1)}, bf16[192,768]{1,0:T(8,128)(2,1)S(1)}, u32[]{:S(2)}, u32[]{:S(2)}) collective-permute-start(bf16[192,768]{1,0:T(8,128)(2,1)} %get-tuple-element.393), channel_id=1, source_target_pairs={{0,1},{1,0},{2,3},{3,2},{4,5},{5,4},{6,7},{7,6},{8,9},{9,8},{10,11... | collective-permute-start | bytes 884744 | tf_op jit(solution)/shard_map/ppermute | solution.py:635
  371.7 27.8 %collective-permute-start.21 = (bf16[384,768]{1,0:T(8,128)(2,1)}, bf16[384,768]{1,0:T(8,128)(2,1)S(1)}, u32[]{:S(2)}, u32[]{:S(2)}) collective-permute-start(bf16[384,768]{1,0:T(8,128)(2,1)} %get-tuple-element.392), channel_id=1, source_target_pairs={{0,4},{1,5},{2,6},{3,7},{4,0},{5,1},{6,2},{7,3},{8,12},{9,13},{10,... | collective-permute-start | bytes 1769480 | tf_op jit(solution)/shard_map/ppermute | solution.py:635
  371.7 17.8 %collective-permute-start.23 = (bf16[192,768]{1,0:T(8,128)(2,1)S(1)}, bf16[192,768]{1,0:T(8,128)(2,1)S(1)}, u32[]{:S(2)}, u32[]{:S(2)}) collective-permute-start(bf16[192,768]{1,0:T(8,128)(2,1)S(1)} %copy-done.70), channel_id=1, source_target_pairs={{0,1},{1,0},{2,3},{3,2},{4,5},{5,4},{6,7},{7,6},{8,9},{9,8},{10,11... | collective-permute-start | bytes 884744 | tf_op jit(solution)/shard_map/ppermute | solution.py:635
  372.2 17.2 %collective-permute-start.24 = (bf16[192,768]{1,0:T(8,128)(2,1)S(1)}, bf16[192,768]{1,0:T(8,128)(2,1)S(1)}, u32[]{:S(2)}, u32[]{:S(2)}) collective-permute-start(bf16[192,768]{1,0:T(8,128)(2,1)S(1)} %copy-done.69), channel_id=1, source_target_pairs={{0,2},{1,3},{2,0},{3,1},{4,6},{5,7},{6,4},{7,5},{8,10},{9,11},{10,... | collective-permute-start | bytes 884744 | tf_op jit(solution)/shard_map/ppermute | solution.py:635
  373.7 25.8 %collective-permute-start.25 = (bf16[192,768]{1,0:T(8,128)(2,1)S(1)}, bf16[192,768]{1,0:T(8,128)(2,1)S(1)}, u32[]{:S(2)}, u32[]{:S(2)}) collective-permute-start(bf16[192,768]{1,0:T(8,128)(2,1)S(1)} %copy-done.68), channel_id=1, source_target_pairs={{0,4},{1,5},{2,6},{3,7},{4,0},{5,1},{6,2},{7,3},{8,12},{9,13},{10,... | collective-permute-start | bytes 884744 | tf_op jit(solution)/shard_map/ppermute | solution.py:635
  380.3 19.2 %collective-permute-start.26 = (bf16[192,768]{1,0:T(8,128)(2,1)S(1)}, bf16[192,768]{1,0:T(8,128)(2,1)S(1)}, u32[]{:S(2)}, u32[]{:S(2)}) collective-permute-start(bf16[192,768]{1,0:T(8,128)(2,1)S(1)} %copy-done.67), channel_id=1, source_target_pairs={{0,8},{1,9},{2,10},{3,11},{4,12},{5,13},{6,14},{7,15},{8,0},{9,1},... | collective-permute-start | bytes 884744 | tf_op jit(solution)/shard_map/ppermute | solution.py:635
  404.8 8.1 %collective-permute-start.28 = (bf16[96,768]{1,0:T(8,128)(2,1)}, bf16[96,768]{1,0:T(8,128)(2,1)S(1)}, u32[]{:S(2)}, u32[]{:S(2)}) collective-permute-start(bf16[96,768]{1,0:T(8,128)(2,1)} %get-tuple-element.426), channel_id=1, source_target_pairs={{0,2},{1,3},{2,0},{3,1},{4,6},{5,7},{6,4},{7,5},{8,10},{9,11},{10,... | collective-permute-start | bytes 442376 | tf_op jit(solution)/shard_map/ppermute | solution.py:635
  406.3 20.8 %collective-permute-start.27 = (bf16[192,768]{1,0:T(8,128)(2,1)}, bf16[192,768]{1,0:T(8,128)(2,1)S(1)}, u32[]{:S(2)}, u32[]{:S(2)}) collective-permute-start(bf16[192,768]{1,0:T(8,128)(2,1)} %get-tuple-element.425), channel_id=1, source_target_pairs={{0,8},{1,9},{2,10},{3,11},{4,12},{5,13},{6,14},{7,15},{8,0},{9,1},... | collective-permute-start | bytes 884744 | tf_op jit(solution)/shard_map/ppermute | solution.py:635
  407.9 9.2 %collective-permute-start.29 = (bf16[96,768]{1,0:T(8,128)(2,1)}, bf16[96,768]{1,0:T(8,128)(2,1)S(1)}, u32[]{:S(2)}, u32[]{:S(2)}) collective-permute-start(bf16[96,768]{1,0:T(8,128)(2,1)} %get-tuple-element.427), channel_id=1, source_target_pairs={{0,2},{1,3},{2,0},{3,1},{4,6},{5,7},{6,4},{7,5},{8,10},{9,11},{10,... | collective-permute-start | bytes 442376 | tf_op jit(solution)/shard_map/ppermute | solution.py:635
  408.5 8.7 %collective-permute-start.30 = (bf16[96,768]{1,0:T(8,128)(2,1)}, bf16[96,768]{1,0:T(8,128)(2,1)S(1)}, u32[]{:S(2)}, u32[]{:S(2)}) collective-permute-start(bf16[96,768]{1,0:T(8,128)(2,1)} %get-tuple-element.428), channel_id=1, source_target_pairs={{0,1},{1,0},{2,3},{3,2},{4,5},{5,4},{6,7},{7,6},{8,9},{9,8},{10,11... | collective-permute-start | bytes 442376 | tf_op jit(solution)/shard_map/ppermute | solution.py:635
  411.1 15.9 %collective-permute-start.31 = (bf16[96,768]{1,0:T(8,128)(2,1)}, bf16[96,768]{1,0:T(8,128)(2,1)S(1)}, u32[]{:S(2)}, u32[]{:S(2)}) collective-permute-start(bf16[96,768]{1,0:T(8,128)(2,1)} %get-tuple-element.429), channel_id=1, source_target_pairs={{0,8},{1,9},{2,10},{3,11},{4,12},{5,13},{6,14},{7,15},{8,0},{9,1},... | collective-permute-start | bytes 442376 | tf_op jit(solution)/shard_map/ppermute | solution.py:635
  412.9 14.2 %collective-permute-start.32 = (bf16[96,768]{1,0:T(8,128)(2,1)}, bf16[96,768]{1,0:T(8,128)(2,1)S(1)}, u32[]{:S(2)}, u32[]{:S(2)}) collective-permute-start(bf16[96,768]{1,0:T(8,128)(2,1)} %get-tuple-element.430), channel_id=1, source_target_pairs={{0,4},{1,5},{2,6},{3,7},{4,0},{5,1},{6,2},{7,3},{8,12},{9,13},{10,... | collective-permute-start | bytes 442376 | tf_op jit(solution)/shard_map/ppermute | solution.py:635
  431.2 14.4 %collective-permute-start.34 = (bf16[192,768]{1,0:T(8,128)(2,1)}, bf16[192,768]{1,0:T(8,128)(2,1)S(1)}, u32[]{:S(2)}, u32[]{:S(2)}) collective-permute-start(bf16[192,768]{1,0:T(8,128)(2,1)} %get-tuple-element.452.refs_0_), channel_id=1, source_target_pairs={{0,8},{1,9},{2,10},{3,11},{4,12},{5,13},{6,14},{7,15},{8,0},{9,1},... | collective-permute-start | bytes 884744 | tf_op jit(solution)/shard_map/ppermute | solution.py:635
  431.2 7.1 %collective-permute-start.35 = (bf16[96,768]{1,0:T(8,128)(2,1)}, bf16[96,768]{1,0:T(8,128)(2,1)S(1)}, u32[]{:S(2)}, u32[]{:S(2)}) collective-permute-start(bf16[96,768]{1,0:T(8,128)(2,1)} %get-tuple-element.453.refs_2_), channel_id=1, source_target_pairs={{0,2},{1,3},{2,0},{3,1},{4,6},{5,7},{6,4},{7,5},{8,10},{9,11},{10,... | collective-permute-start | bytes 442376 | tf_op jit(solution)/shard_map/ppermute | solution.py:635
  431.8 9.5 %collective-permute-start.36 = (bf16[96,768]{1,0:T(8,128)(2,1)}, bf16[96,768]{1,0:T(8,128)(2,1)S(1)}, u32[]{:S(2)}, u32[]{:S(2)}) collective-permute-start(bf16[96,768]{1,0:T(8,128)(2,1)} %get-tuple-element.454), channel_id=1, source_target_pairs={{0,4},{1,5},{2,6},{3,7},{4,0},{5,1},{6,2},{7,3},{8,12},{9,13},{10,... | collective-permute-start | bytes 442376 | tf_op jit(solution)/shard_map/ppermute | solution.py:635
  434.0 7.3 %collective-permute-start.37 = (bf16[96,768]{1,0:T(8,128)(2,1)}, bf16[96,768]{1,0:T(8,128)(2,1)S(1)}, u32[]{:S(2)}, u32[]{:S(2)}) collective-permute-start(bf16[96,768]{1,0:T(8,128)(2,1)} %get-tuple-element.455), channel_id=1, source_target_pairs={{0,1},{1,0},{2,3},{3,2},{4,5},{5,4},{6,7},{7,6},{8,9},{9,8},{10,11... | collective-permute-start | bytes 442376 | tf_op jit(solution)/shard_map/ppermute | solution.py:635
  434.6 3.7 collective-permute-start.38
  449.3 17.4 %collective-permute-start.39 = (bf16[384,768]{1,0:T(8,128)(2,1)}, bf16[384,768]{1,0:T(8,128)(2,1)S(1)}, u32[]{:S(2)}, u32[]{:S(2)}) collective-permute-start(bf16[384,768]{1,0:T(8,128)(2,1)} %get-tuple-element.468.refs_0_), channel_id=1, source_target_pairs={{0,4},{1,5},{2,6},{3,7},{4,0},{5,1},{6,2},{7,3},{8,12},{9,13},{10,... | collective-permute-start | bytes 1769480 | tf_op jit(solution)/shard_map/ppermute | solution.py:635
  449.3 17.3 %collective-permute-start.40 = (bf16[192,768]{1,0:T(8,128)(2,1)}, bf16[192,768]{1,0:T(8,128)(2,1)S(1)}, u32[]{:S(2)}, u32[]{:S(2)}) collective-permute-start(bf16[192,768]{1,0:T(8,128)(2,1)} %get-tuple-element.469.refs_2_), channel_id=1, source_target_pairs={{0,1},{1,0},{2,3},{3,2},{4,5},{5,4},{6,7},{7,6},{8,9},{9,8},{10,11... | collective-permute-start | bytes 884744 | tf_op jit(solution)/shard_map/ppermute | solution.py:635
  449.9 16.7 %collective-permute-start.41 = (bf16[48,768]{1,0:T(8,128)(2,1)}, bf16[48,768]{1,0:T(8,128)(2,1)S(1)}, u32[]{:S(2)}, u32[]{:S(2)}) collective-permute-start(bf16[48,768]{1,0:T(8,128)(2,1)} %get-tuple-element.470), channel_id=1, source_target_pairs={{0,8},{1,9},{2,10},{3,11},{4,12},{5,13},{6,14},{7,15},{8,0},{9,1},... | collective-permute-start | bytes 221192 | tf_op jit(solution)/shard_map/ppermute | solution.py:635
  453.1 13.6 %collective-permute-start.42 = (bf16[48,768]{1,0:T(8,128)(2,1)}, bf16[48,768]{1,0:T(8,128)(2,1)S(1)}, u32[]{:S(2)}, u32[]{:S(2)}) collective-permute-start(bf16[48,768]{1,0:T(8,128)(2,1)} %get-tuple-element.471), channel_id=1, source_target_pairs={{0,2},{1,3},{2,0},{3,1},{4,6},{5,7},{6,4},{7,5},{8,10},{9,11},{10,... | collective-permute-start | bytes 221192 | tf_op jit(solution)/shard_map/ppermute | solution.py:635
  453.6 13.0 %collective-permute-start.43 = (f32[4,768]{1,0:T(4,128)S(1)}, f32[4,768]{1,0:T(4,128)S(1)}, u32[]{:S(2)}, u32[]{:S(2)}) collective-permute-start(f32[4,768]{1,0:T(4,128)S(1)} %fusion.52), channel_id=1, source_target_pairs={{0,4},{1,5},{2,6},{3,7},{4,0},{5,1},{6,2},{7,3},{8,12},{9,13},{10,... | collective-permute-start | bytes 36872 | tf_op jit(solution)/shard_map/ppermute | solution.py:635
  471.0 27.1 %collective-permute-start.44 = (bf16[384,768]{1,0:T(8,128)(2,1)}, bf16[384,768]{1,0:T(8,128)(2,1)S(1)}, u32[]{:S(2)}, u32[]{:S(2)}) collective-permute-start(bf16[384,768]{1,0:T(8,128)(2,1)} %get-tuple-element.486.refs_0_), channel_id=1, source_target_pairs={{0,2},{1,3},{2,0},{3,1},{4,6},{5,7},{6,4},{7,5},{8,10},{9,11},{10,... | collective-permute-start | bytes 1769480 | tf_op jit(solution)/shard_map/ppermute | solution.py:635
  471.6 26.5 %collective-permute-start.45 = (bf16[384,768]{1,0:T(8,128)(2,1)}, bf16[384,768]{1,0:T(8,128)(2,1)S(1)}, u32[]{:S(2)}, u32[]{:S(2)}) collective-permute-start(bf16[384,768]{1,0:T(8,128)(2,1)} %get-tuple-element.487.refs_2_), channel_id=1, source_target_pairs={{0,1},{1,0},{2,3},{3,2},{4,5},{5,4},{6,7},{7,6},{8,9},{9,8},{10,11... | collective-permute-start | bytes 1769480 | tf_op jit(solution)/shard_map/ppermute | solution.py:635
  472.1 25.9 %collective-permute-start.46 = (bf16[192,768]{1,0:T(8,128)(2,1)}, bf16[192,768]{1,0:T(8,128)(2,1)S(1)}, u32[]{:S(2)}, u32[]{:S(2)}) collective-permute-start(bf16[192,768]{1,0:T(8,128)(2,1)} %get-tuple-element.488.refs_4_), channel_id=1, source_target_pairs={{0,8},{1,9},{2,10},{3,11},{4,12},{5,13},{6,14},{7,15},{8,0},{9,1},... | collective-permute-start | bytes 884744 | tf_op jit(solution)/shard_map/ppermute | solution.py:635
  473.2 24.9 %collective-permute-start.47 = (bf16[192,768]{1,0:T(8,128)(2,1)}, bf16[192,768]{1,0:T(8,128)(2,1)S(1)}, u32[]{:S(2)}, u32[]{:S(2)}) collective-permute-start(bf16[192,768]{1,0:T(8,128)(2,1)} %get-tuple-element.489.refs_6_), channel_id=1, source_target_pairs={{0,4},{1,5},{2,6},{3,7},{4,0},{5,1},{6,2},{7,3},{8,12},{9,13},{10,... | collective-permute-start | bytes 884744 | tf_op jit(solution)/shard_map/ppermute | solution.py:635
  474.8 12.5 %collective-permute-start.50 = (f32[4,768]{1,0:T(4,128)S(1)}, f32[4,768]{1,0:T(4,128)S(1)}, u32[]{:S(2)}, u32[]{:S(2)}) collective-permute-start(f32[4,768]{1,0:T(4,128)S(1)} %add.82), channel_id=1, source_target_pairs={{0,8},{1,9},{2,10},{3,11},{4,12},{5,13},{6,14},{7,15},{8,0},{9,1},... | collective-permute-start | bytes 36872 | tf_op jit(solution)/shard_map/ppermute | solution.py:635
  487.3 6.1 %collective-permute-start.48 = (bf16[48,768]{1,0:T(8,128)(2,1)}, bf16[48,768]{1,0:T(8,128)(2,1)S(1)}, u32[]{:S(2)}, u32[]{:S(2)}) collective-permute-start(bf16[48,768]{1,0:T(8,128)(2,1)} %get-tuple-element.490.refs_8_), channel_id=1, source_target_pairs={{0,8},{1,9},{2,10},{3,11},{4,12},{5,13},{6,14},{7,15},{8,0},{9,1},... | collective-permute-start | bytes 221192 | tf_op jit(solution)/shard_map/ppermute | solution.py:635
  493.5 4.6 collective-permute-start.49
  504.5 36.1 %collective-permute-start.51 = (bf16[768,768]{1,0:T(8,128)(2,1)}, bf16[768,768]{1,0:T(8,128)(2,1)S(1)}, u32[]{:S(2)}, u32[]{:S(2)}) collective-permute-start(bf16[768,768]{1,0:T(8,128)(2,1)} %get-tuple-element.526.xp), channel_id=1, source_target_pairs={{0,1},{1,0},{2,3},{3,2},{4,5},{5,4},{6,7},{7,6},{8,9},{9,8},{10,11... | collective-permute-start | bytes 3538952 | tf_op jit(solution)/shard_map/ppermute | solution.py:635
  506.0 34.6 %collective-permute-start.52 = (bf16[768,768]{1,0:T(8,128)(2,1)}, bf16[768,768]{1,0:T(8,128)(2,1)S(1)}, u32[]{:S(2)}, u32[]{:S(2)}) collective-permute-start(bf16[768,768]{1,0:T(8,128)(2,1)} %get-tuple-element.528.yp), channel_id=1, source_target_pairs={{0,2},{1,3},{2,0},{3,1},{4,6},{5,7},{6,4},{7,5},{8,10},{9,11},{10,... | collective-permute-start | bytes 3538952 | tf_op jit(solution)/shard_map/ppermute | solution.py:635
  507.5 33.1 %collective-permute-start.53 = (bf16[384,768]{1,0:T(8,128)(2,1)}, bf16[384,768]{1,0:T(8,128)(2,1)S(1)}, u32[]{:S(2)}, u32[]{:S(2)}) collective-permute-start(bf16[384,768]{1,0:T(8,128)(2,1)} %get-tuple-element.530.ap), channel_id=1, source_target_pairs={{0,4},{1,5},{2,6},{3,7},{4,0},{5,1},{6,2},{7,3},{8,12},{9,13},{10,... | collective-permute-start | bytes 1769480 | tf_op jit(solution)/shard_map/ppermute | solution.py:635
  507.5 33.1 %collective-permute-start.54 = (bf16[384,768]{1,0:T(8,128)(2,1)}, bf16[384,768]{1,0:T(8,128)(2,1)S(1)}, u32[]{:S(2)}, u32[]{:S(2)}) collective-permute-start(bf16[384,768]{1,0:T(8,128)(2,1)} %get-tuple-element.532.bp), channel_id=1, source_target_pairs={{0,8},{1,9},{2,10},{3,11},{4,12},{5,13},{6,14},{7,15},{8,0},{9,1},... | collective-permute-start | bytes 1769480 | tf_op jit(solution)/shard_map/ppermute | solution.py:635
  510.0 25.2 %collective-permute-start.55 = (bf16[96,768]{1,0:T(8,128)(2,1)}, bf16[96,768]{1,0:T(8,128)(2,1)S(1)}, u32[]{:S(2)}, u32[]{:S(2)}) collective-permute-start(bf16[96,768]{1,0:T(8,128)(2,1)} %get-tuple-element.500.refs_0_), channel_id=1, source_target_pairs={{0,4},{1,5},{2,6},{3,7},{4,0},{5,1},{6,2},{7,3},{8,12},{9,13},{10,... | collective-permute-start | bytes 442376 | tf_op jit(solution)/shard_map/ppermute | solution.py:635
  535.2 5.4 collective-permute-start.56
  543.8 13.7 %collective-permute-start.57 = (bf16[96,768]{1,0:T(8,128)(2,1)}, bf16[96,768]{1,0:T(8,128)(2,1)S(1)}, u32[]{:S(2)}, u32[]{:S(2)}) collective-permute-start(bf16[96,768]{1,0:T(8,128)(2,1)} %get-tuple-element.522.refs_0_), channel_id=1, source_target_pairs={{0,2},{1,3},{2,0},{3,1},{4,6},{5,7},{6,4},{7,5},{8,10},{9,11},{10,... | collective-permute-start | bytes 442376 | tf_op jit(solution)/shard_map/ppermute | solution.py:635
  544.4 13.2 %collective-permute-start.58 = (bf16[96,768]{1,0:T(8,128)(2,1)}, bf16[96,768]{1,0:T(8,128)(2,1)S(1)}, u32[]{:S(2)}, u32[]{:S(2)}) collective-permute-start(bf16[96,768]{1,0:T(8,128)(2,1)} %get-tuple-element.523.refs_2_), channel_id=1, source_target_pairs={{0,1},{1,0},{2,3},{3,2},{4,5},{5,4},{6,7},{7,6},{8,9},{9,8},{10,11... | collective-permute-start | bytes 442376 | tf_op jit(solution)/shard_map/ppermute | solution.py:635
  544.9 12.6 %collective-permute-start.59 = (bf16[96,768]{1,0:T(8,128)(2,1)}, bf16[96,768]{1,0:T(8,128)(2,1)S(1)}, u32[]{:S(2)}, u32[]{:S(2)}) collective-permute-start(bf16[96,768]{1,0:T(8,128)(2,1)} %get-tuple-element.524.refs_4_), channel_id=1, source_target_pairs={{0,8},{1,9},{2,10},{3,11},{4,12},{5,13},{6,14},{7,15},{8,0},{9,1},... | collective-permute-start | bytes 442376 | tf_op jit(solution)/shard_map/ppermute | solution.py:635
  545.8 11.8 %collective-permute-start.60 = (bf16[96,768]{1,0:T(8,128)(2,1)}, bf16[96,768]{1,0:T(8,128)(2,1)S(1)}, u32[]{:S(2)}, u32[]{:S(2)}) collective-permute-start(bf16[96,768]{1,0:T(8,128)(2,1)} %get-tuple-element.525.refs_6_), channel_id=1, source_target_pairs={{0,4},{1,5},{2,6},{3,7},{4,0},{5,1},{6,2},{7,3},{8,12},{9,13},{10,... | collective-permute-start | bytes 442376 | tf_op jit(solution)/shard_map/ppermute | solution.py:635
  548.2 20.9 %collective-permute-start.65 = (f32[1,768]{1,0:T(1,128)S(1)}, f32[1,768]{1,0:T(1,128)S(1)}, u32[]{:S(2)}, u32[]{:S(2)}) collective-permute-start(f32[1,768]{1,0:T(1,128)S(1)} %slice.59), channel_id=1, source_target_pairs={{0,16},{16,0},{1,17},{17,1},{2,18},{18,2},{3,19},{19,3},{4,20},{20... | collective-permute-start | bytes 9224 | tf_op jit(solution)/shard_map/ppermute | solution.py:628
  561.4 9.7 %collective-permute-start.61 = (bf16[192,768]{1,0:T(8,128)(2,1)}, bf16[192,768]{1,0:T(8,128)(2,1)S(1)}, u32[]{:S(2)}, u32[]{:S(2)}) collective-permute-start(bf16[192,768]{1,0:T(8,128)(2,1)} %get-tuple-element.542.xp), channel_id=1, source_target_pairs={{0,1},{1,0},{2,3},{3,2},{4,5},{5,4},{6,7},{7,6},{8,9},{9,8},{10,11... | collective-permute-start | bytes 884744 | tf_op jit(solution)/shard_map/ppermute | solution.py:635
  562.9 9.3 %collective-permute-start.62 = (bf16[192,768]{1,0:T(8,128)(2,1)}, bf16[192,768]{1,0:T(8,128)(2,1)S(1)}, u32[]{:S(2)}, u32[]{:S(2)}) collective-permute-start(bf16[192,768]{1,0:T(8,128)(2,1)} %get-tuple-element.548.yp), channel_id=1, source_target_pairs={{0,2},{1,3},{2,0},{3,1},{4,6},{5,7},{6,4},{7,5},{8,10},{9,11},{10,... | collective-permute-start | bytes 884744 | tf_op jit(solution)/shard_map/ppermute | solution.py:635
  564.3 14.6 %collective-permute-start.63 = (bf16[192,768]{1,0:T(8,128)(2,1)}, bf16[192,768]{1,0:T(8,128)(2,1)S(1)}, u32[]{:S(2)}, u32[]{:S(2)}) collective-permute-start(bf16[192,768]{1,0:T(8,128)(2,1)} %get-tuple-element.550.ap), channel_id=1, source_target_pairs={{0,4},{1,5},{2,6},{3,7},{4,0},{5,1},{6,2},{7,3},{8,12},{9,13},{10,... | collective-permute-start | bytes 884744 | tf_op jit(solution)/shard_map/ppermute | solution.py:635
  564.7 16.0 %collective-permute-start.64 = (bf16[192,768]{1,0:T(8,128)(2,1)}, bf16[192,768]{1,0:T(8,128)(2,1)S(1)}, u32[]{:S(2)}, u32[]{:S(2)}) collective-permute-start(bf16[192,768]{1,0:T(8,128)(2,1)} %get-tuple-element.546), channel_id=1, source_target_pairs={{0,8},{1,9},{2,10},{3,11},{4,12},{5,13},{6,14},{7,15},{8,0},{9,1},... | collective-permute-start | bytes 884744 | tf_op jit(solution)/shard_map/ppermute | solution.py:635
  (87 other events, 419.3 us)

commit v3 on v1

--- a/solution.py
+++ b/solution.py
@@ -80,7 +80,7 @@
         mine = (i // (blocks // 2)) == h_ref[0]
         x = jnp.where(mine, own[...].astype(F32), peer[...].astype(F32))
     else:
-        x = xr[...] + pa[...].astype(F32) + pb[...].astype(F32)
+        x = xr[...] + (pa[...].astype(F32) + pb[...].astype(F32))
     x_out[...] = x
     xh, _ = norm_stats(x)
     n = (xh * g[...]).astype(BF)
@@ -132,7 +132,7 @@
         drr, dna, dnb = refs[:3]
     rest = refs[4 if split else 3 :]
     xn, gn, qr, kf, vf, orf, lser, wqkv, wo, segc, segr = rest[:11]
-    dr_out, da_out, dqkv_out, dn_out, dg_out, dks, dvs = rest[11:]
+    dr_out, da_out, dqk_out, dv_out, dn_out, dg_out, dks, dvs = rest[11:]
     i = pl.program_id(0)
     blk = blocks - 1 - i
     if split:
@@ -186,17 +186,18 @@
                     dks[0:keys, cols] += mm_tn(ds, qh)
                     dvs[0:keys, cols] += mm_tn(p.astype(BF), doh)
                 dq = jnp.where(half_lane(0), dqs[0], dqs[1]) * 0.125
-                dqkv_out[0, :, cols] = dq.astype(BF)
-            dqkv_out[1] = dks[here, :].astype(BF)
-            dqkv_out[2] = dvs[here, :].astype(BF)
-
+                dqk_out[:, cols] = dq.astype(BF)
+            dqk_out[:, pairs * 128 :] = dks[here, :].astype(BF)
+            dv_out[...] = dvs[here, :].astype(BF)
+
+    c = pairs * 128
     dn_out[...] = (
-        mm_nt(dqkv_out[0], wqkv[0]) + mm_nt(dqkv_out[1], wqkv[1]) + mm_nt(dqkv_out[2], wqkv[2])
+        mm_nt(dqk_out[:, :c], wqkv[0]) + mm_nt(dqk_out[:, c:], wqkv[1]) + mm_nt(dv_out[...], wqkv[2])
     ).astype(BF)
 
 
 def dense_fwd_kernel(xr, pa, pb, g, up, down, x_out, n_out, act_out, gp_out, p_out):
-    x = xr[...] + pa[...].astype(F32) + pb[...].astype(F32)
+    x = xr[...] + (pa[...].astype(F32) + pb[...].astype(F32))
     x_out[...] = x
     xh, _ = norm_stats(x)
     n = (xh * g[...]).astype(BF)
@@ -249,7 +250,7 @@
 
 def route_kernel(h_ref, xr, pa, pb, g, slot_ref, x_out, send_out, ms):
     i = pl.program_id(0)
-    x = xr[...] + pa[...].astype(F32) + pb[...].astype(F32)
+    x = xr[...] + (pa[...].astype(F32) + pb[...].astype(F32))
     x_out[...] = x
 
     @pl.when(i >= 2)
@@ -334,10 +335,12 @@
     return pl.BlockSpec((BLK, width), lambda i, *a: (index(i), 0))
 
 
-PARAMS = pltpu.CompilerParams(vmem_limit_bytes=VLIM, dimension_semantics=("arbitrary",))
-
-
-def call(kernel, grid, in_specs, out_specs, outs, scratch, flops, moved, args, prefetch=None):
+def call(
+    kernel, grid, in_specs, out_specs, outs, scratch, flops, moved, args, prefetch=None, limit=VLIM
+):
+    params = pltpu.CompilerParams(
+        vmem_limit_bytes=int(limit), dimension_semantics=("arbitrary",)
+    )
     cost = pl.CostEstimate(flops=int(flops), bytes_accessed=int(moved), transcendentals=0)
     if prefetch is None:
         spec = pl.GridSpec(
@@ -353,7 +356,7 @@
         )
         args = (prefetch,) + tuple(args)
     return pl.pallas_call(
-        kernel, grid_spec=spec, out_shape=outs, compiler_params=PARAMS, cost_estimate=cost
+        kernel, grid_spec=spec, out_shape=outs, compiler_params=params, cost_estimate=cost
     )(*args)
 
 
@@ -425,7 +428,8 @@
     outs = [
         (rows_spec(d, back), shape((length, d), F32)),
         (rows_spec(d, back), shape((length, d), BF)),
-        (pl.BlockSpec((3, BLK, c), lambda i, *a: (0, back(i), 0)), shape((3, length, c), BF)),
+        (rows_spec(2 * c, back), shape((length, 2 * c), BF)),
+        (rows_spec(c, back), shape((length, c), BF)),
         (rows_spec(d, back), shape((length, d), BF)),
         (fixed((8, d)), shape((8, d), F32)),
     ]
@@ -626,38 +630,206 @@
     return lax.ppermute(v, "head", SWAP)
 
 
-def exchange_half(v, bit, pairs):
-    half = v.shape[0] // 2
-    out = lax.dynamic_slice_in_dim(v, (1 - bit) * half, half, 0)
-    return lax.dynamic_slice_in_dim(v, bit * half, half, 0) + lax.ppermute(out, "dp", pairs)
-
-
-def regather(v, bit, pairs):
-    other = lax.ppermute(v, "dp", pairs)
-    both = jnp.concatenate([v, v], axis=0)
-    return lax.dynamic_update_slice_in_dim(both, other, (1 - bit) * v.shape[0], 0)
-
-
-def reduce_all(v, steps):
-    if steps is None:
-        return lax.psum(v, "dp")
-    me = lax.axis_index("dp")
-    half = v.shape[0] // 2
-    pairs = {s: [(i, i ^ s) for i in range(16)] for s in (1, 2, 4, 8)}
-    bits = {s: (me // s) % 2 for s in (1, 2, 4, 8)}
-    a, b = v[:half], v[half:]
-    a, b = exchange_half(a, bits[1], pairs[1]), exchange_half(b, bits[2], pairs[2])
-    a, b = exchange_half(a, bits[2], pairs[2]), exchange_half(b, bits[1], pairs[1])
-    c = jnp.concatenate([a, b], axis=0)
-    c = exchange_half(c, bits[4], pairs[4])
-    c = exchange_half(c, bits[8], pairs[8])
-    c = regather(c, bits[8], pairs[8])
-    c = regather(c, bits[4], pairs[4])
-    quarter = c.shape[0] // 2
-    a, b = c[:quarter], c[quarter:]
-    a, b = regather(a, bits[2], pairs[2]), regather(b, bits[1], pairs[1])
-    a, b = regather(a, bits[1], pairs[1]), regather(b, bits[2], pairs[2])
-    return jnp.concatenate([a, b], axis=0)
+def pick(bit, a, b):
+    return jnp.where(bit == 1, a, b)
+
+
+def total_of(a, b):
+    return (a.astype(F32) + b.astype(F32)).astype(BF)
+
+
+def whole(arrays):
+    return [pl.BlockSpec(a.shape, lambda i, *r, n=len(a.shape): (0,) * n) for a in arrays]
+
+
+def one_step(kernel, bits, args, outs):
+    moved = sum(a.size * a.dtype.itemsize for a in (*args, *outs))
+    return call(
+        kernel,
+        (1,),
+        whole(args),
+        whole(outs),
+        outs,
+        [],
+        moved,
+        moved,
+        args,
+        prefetch=bits,
+        limit=2 * moved + 8 * 1024 * 1024,
+    )
+
+
+PLACE = {1: 0, 2: 1, 4: 2, 8: 3}
+
+
+def fold_kernel(plan, n_in, bits, *refs):
+    def get(piece):
+        at, lo, n = piece
+        return refs[at][lo : lo + n, :]
+
+    def put(piece, value):
+        at, lo, n = piece
+        refs[n_in + at][lo : lo + n, :] = value
+
+    for kind, ins, outs, place in plan:
+        if kind == "copy":
+            put(outs[0], get(ins[0]))
+        elif kind == "sum":
+            put(outs[0], total_of(get(ins[0]), get(ins[1])))
+        elif kind == "split":
+            (ka, kl, n), (ga, gl, _) = ins
+            q = n // 2
+            lo = total_of(get((ka, kl, q)), get((ga, gl, q)))
+            hi = total_of(get((ka, kl + q, q)), get((ga, gl + q, q)))
+            put(outs[0], pick(bits[place], lo, hi))
+            put(outs[1], pick(bits[place], hi, lo))
+        else:
+            p, g = get(ins[0]), get(ins[1])
+            at, lo, n = outs[0]
+            put((at, lo, n // 2), pick(bits[place], g, p))
+            put((at, lo + n // 2, n // 2), pick(bits[place], p, g))
+
+
+class Part:
+    def __init__(self, order, send, keep=None):
+        self.order, self.phase = order, 0
+        self.sent = (send, 0, send.shape[0])
+        self.kept = None if keep is None else (keep, 0, keep.shape[0])
+        self.got = None
+        self.fresh = True
+
+    @property
+    def live(self):
+        return self.phase < len(self.order)
+
+
+def halving(order):
+    return order + order[::-1]
+
+
+def advance(bits, parts, during=None, inputs=()):
+    parts = [p for p in parts if p.live]
+    width = parts[0].sent[0].shape[1]
+    buffers = {}
+    for p in parts:
+        buffers.setdefault(p.order[p.phase], p.sent[0])
+    steps = sorted(buffers)
+    flat, inputs = lax.optimization_barrier(([buffers[s] for s in steps], inputs))
+    got = [lax.ppermute(v, "dp", [(i, i ^ s) for i in range(16)]) for v, s in zip(flat, steps)]
+    result = during(*inputs) if during else inputs
+    (flat, got), result = lax.optimization_barrier(((flat, got), result))
+    for p in parts:
+        at = steps.index(p.order[p.phase])
+        p.sent = (flat[at],) + p.sent[1:]
+        p.got = (got[at],) + p.sent[1:]
+        p.phase += 1
+    return result
+
+
+def fold(bits, parts):
+    args, plan, rows, moved = [], [], {}, []
+
+    def source(piece):
+        for j, a in enumerate(args):
+            if a is piece[0]:
+                return (j,) + piece[1:]
+        args.append(piece[0])
+        return (len(args) - 1,) + piece[1:]
+
+    def room(name, n):
+        lo = rows.get(name, 0)
+        rows[name] = lo + n
+        return (name, lo, n)
+
+    for p in parts:
+        if not p.live:
+            continue
+        step = p.order[p.phase]
+        half = len(p.order) // 2
+        if p.phase == 0:
+            ins, kind, place = [source(p.sent)], "copy", 0
+            outs = [room(step, p.sent[2])]
+        elif p.kept is not None and p.kept[0] is None:
+            ins, kind, place = [source(p.sent), source(p.got)], "sum", 0
+            outs = [room(step, p.sent[2])]
+        elif p.phase < half:
+            ins, kind, place = [source(p.kept), source(p.got)], "split", PLACE[step]
+            n = p.kept[2] // 2
+            outs = [room(step, n), room("keep", n)]
+        elif p.phase == half:
+            ins, kind, place = [source(p.kept), source(p.got)], "sum", 0
+            outs = [room(step, p.kept[2])]
+        else:
+            ins, kind, place = [source(p.sent), source(p.got)], "raise", PLACE[p.order[p.phase - 1]]
+            outs = [room(step, 2 * p.sent[2])]
+        plan.append((kind, ins, outs, place))
+        moved.append(p)
+    names = list(rows)
+    width = args[0].shape[1]
+    shapes = [shape((rows[n], width), BF) for n in names]
+    fixed_plan = tuple(
+        (kind, tuple(ins), tuple((names.index(o[0]),) + o[1:] for o in outs), place)
+        for kind, ins, outs, place in plan
+    )
+    made = one_step(functools.partial(fold_kernel, fixed_plan, len(args)), bits, args, shapes)
+    for p, (_, _, outs, _) in zip(moved, plan):
+        p.sent = (made[names.index(outs[0][0])],) + outs[0][1:]
+        if len(outs) > 1:
+            p.kept = (made[names.index(outs[1][0])],) + outs[1][1:]
+
+
+def ends(bits, ref_s, ref_g, piece, place):
+    lo, n = piece
+    a, b = ref_s[lo : lo + n, :].astype(F32), ref_g[lo : lo + n, :].astype(F32)
+    return pick(bits[place], b, a), pick(bits[place], a, b)
+
+
+def put_query_key(qkv, blocks):
+    c = qkv.shape[2]
+    n = blocks[0].shape[0]
+    for j, block in enumerate(blocks):
+        qkv[0, j * n : j * n + n, :] = block[:, :c]
+        qkv[1, j * n : j * n + n, :] = block[:, c:]
+
+
+def put_value_out(qkv, out, v, o):
+    c = qkv.shape[2]
+    n = v.shape[0]
+    qkv[2, :n, :] = v[:, :c]
+    qkv[2, n:, :] = v[:, c:]
+    out[...] = o
+
+
+def finish_wide_kernel(at, bits, xp, xg, yp, yg, ap, ag, bp, bg, up, down, qkv, out):
+    lo, hi = ends(bits, xp, xg, at[0], 0)
+    f = lo.shape[1]
+    up[:, :f] = lo
+    up[:, f:] = hi
+    lo, hi = ends(bits, yp, yg, at[1], 1)
+    f = lo.shape[0]
+    down[:f, :] = lo
+    down[f:, :] = hi
+    put_query_key(qkv, ends(bits, ap, ag, at[2], 2))
+    put_value_out(qkv, out, *ends(bits, bp, bg, at[3], 3))
+
+
+def finish_narrow_kernel(at, bits, xp, xg, yp, yg, qkv, out):
+    put_query_key(qkv, ends(bits, xp, xg, at[0], 0))
+    put_value_out(qkv, out, *ends(bits, yp, yg, at[1], 1))
+
+
+def stack_kernel(bits, *refs):
+    out = refs[-1]
+    row = lax.broadcasted_iota(jnp.int32, out.shape, 0)
+    total = jnp.zeros(out.shape, F32)
+    for j, ref in enumerate(refs[:-1]):
+        total = jnp.where(row == j, ref[0:1, :], total)
+    out[...] = total.astype(BF)
+
+
+def finish(kernel, bits, parts, arrays, outs):
+    at = tuple((p.sent[1], p.sent[2]) for p in parts)
+    return one_step(functools.partial(kernel, at), bits, arrays, outs)
 
 
 def body(
@@ -716,14 +888,17 @@
         m_own, m_peer, grad_own, grad_peer, centroids, expert_up, expert_down
     )
     dm_sum = (dmo.astype(F32) + swap(dmp).astype(F32)).astype(BF)
-    dm_own = collect(travel(dm_sum), slot_col)
-    dm_peer = swap(dm_own)
     up_grad = mm_tn(m_all, due_all)[None]
     down_grad = mm_tn(ae_all, dy_all)[None]
+    dm_back, up_grad, down_grad = lax.optimization_barrier((travel(dm_sum), up_grad, down_grad))
+    dm_own = collect(dm_back, slot_col)
+    dm_peer = swap(dm_own)
+    y_sum = (yo.astype(F32) + swap(yp).astype(F32)).astype(BF)
+    y_back = travel(y_sum)
     dc = dc[:1]
     cen_grad = dc + swap(dc)
 
-    dr2, da2, dqkv2, dn2, dg3 = attention_backward(
+    dr2, da2, dqk2, dv2, dn2, dg3 = attention_backward(
         h,
         (cotangent, cot_peer, dm_own, dm_peer),
         True,
@@ -736,50 +911,159 @@
         segr,
     )
     dn2r = swap(dn2)
-
-    def attention_grads(n, dqkv, o, da):
-        w = [mm_tn(n, dqkv[j]).astype(BF) for j in range(3)]
-        wo = mm_tn(o, da).astype(BF)
-        c = wo.shape[0]
-        return jnp.concatenate([*w, wo[:, :c], wo[:, c:]], axis=0)
-
-    def split_grads(total):
-        total = total.astype(F32)
-        c = total.shape[1]
-        wo = jnp.concatenate([total[3 * d : 3 * d + c], total[3 * d + c :]], axis=1)
-        return total[: 3 * d].reshape(3, d, c), wo
-
-    qkv_second, out_second = split_grads(reduce_all(attention_grads(n3, dqkv2, o2, da2), steps))
-    y_sum = (yo.astype(F32) + swap(yp).astype(F32)).astype(BF)
-    second = collect_add(h, travel(y_sum), slot_col, x2)
-
-    dr1, df, du, dnd, dg2 = dense_backward(dr2, dn2, dn2r, first, gain[2], gp, up_one, down_one)
-    dndr = swap(dnd)
-    f = du.shape[1]
-    w_up = mm_tn(n2, du).astype(BF)
-    w_down = mm_tn(act, df).astype(BF)
-    dense_total = jnp.concatenate([w_up[:, : f // 2], w_up[:, f // 2 :], w_down], axis=0)
-    dense_total = reduce_all(dense_total, steps).astype(F32)
-    up_first = jnp.concatenate([dense_total[:d], dense_total[d : 2 * d]], axis=1)
-    down_first = dense_total[2 * d :]
-
-    dr0, da1, dqkv1, dn1, dg1 = attention_backward(
-        h,
-        (dr1, dnd, dndr),
-        False,
-        x1,
-        gain[1],
-        (qkv1, o1, lse1),
-        qkv_one,
-        out_one,
-        segc,
-        segr,
-    )
-    dn1r = swap(dn1)
-    input_grad, dg0 = final_step(h, dr0, dn1, dn1r, tokens, tokens_peer, gain[0])
-    qkv_first, out_first = split_grads(reduce_all(attention_grads(n1, dqkv1, o1, da1), steps))
-    gain_grads = jnp.concatenate([dg0[:1], dg1[:1], dg2[:1], dg3[:1]], axis=0)
-    gain_grads = lax.psum(gain_grads, "dp")
+    f = up_one.shape[1]
+    c = qkv_one.shape[2]
+
+    def grad(a, b):
+        return mm_tn(a, b).astype(BF)
+
+    def value_sides(n, dv):
+        w = grad(n, dv)
+        return jnp.concatenate([w[: d // 2], w[d // 2 :]], axis=1)
+
+    def last_step(dr, dna, dnb):
+        return final_step(h, dr, dna, dnb, tokens, tokens_peer, gain[0])
+
+    def gather_y(y):
+        return collect_add(h, y, slot_col, x2)
+
+    def stack_gains(dg0):
+        return jnp.concatenate([dg0[:1], dg1[:1], dg2[:1], dg3[:1]], axis=0)
+
+    def last_attention(dr, dna, dnb):
+        return attention_backward(
+            h, (dr, dna, dnb), False, x1, gain[1], (qkv1, o1, lse1), qkv_one, out_one, segc, segr
+        )
+
+    if steps is None:
+        dr1, df, du, dnd, dg2 = dense_backward(
+            dr2, dn2, dn2r, first, gain[2], gp, up_one, down_one
+        )
+        dr0, da1, dqk1, dv1, dn1, dg1 = last_attention(dr1, dnd, swap(dnd))
+        input_grad, dg0 = last_step(dr0, dn1, swap(dn1))
+        second = gather_y(y_back)
+        up_first, down_first, qk_two, v_two, wo_two, qk_one, v_one, wo_one, gain_grads = lax.psum(
+            (
+                grad(n2, du),
+                grad(act, df),
+                grad(n3, dqk2),
+                grad(n3, dv2),
+                grad(o2, da2),
+                grad(n1, dqk1),
+                grad(n1, dv1),
+                grad(o1, da1),
+                stack_gains(dg0),
+            ),
+            "dp",
+        )
+
+        def unpack(qk, v):
+            return jnp.stack([qk[:, :c], qk[:, c:], v]).astype(F32)
+
+        up_first, down_first = up_first.astype(F32), down_first.astype(F32)
+        qkv_second, out_second = unpack(qk_two, v_two), wo_two.astype(F32)
+        qkv_first, out_first = unpack(qk_one, v_one), wo_one.astype(F32)
+    else:
+        me = lax.axis_index("dp")
+        bits = jnp.stack([(me // s) % 2 for s in (1, 2, 4, 8)]).astype(jnp.int32)
+
+        def columns(v, bit):
+            half = v.shape[1] // 2
+            return lax.dynamic_slice_in_dim(v, bit * half, half, 1)
+
+        def query_key(n, dqk, bit):
+            return grad(columns(n, bit), dqk)
+
+        def value_out(n, dv, o, da, bit):
+            v, wo = value_sides(n, dv), grad(o, da)
+            return jnp.where(bit == 1, v, wo), jnp.where(bit == 1, wo, v)
+
+        qk_send = query_key(n3, dqk2, 1 - bits[2])
+        qk_keep = query_key(n3, dqk2, bits[2])
+        vo_send, vo_keep = value_out(n3, dv2, o2, da2, bits[3])
+        (qk_send, qk_keep, vo_send, vo_keep), dr2, dn2, dn2r, y_back = lax.optimization_barrier(
+            ((qk_send, qk_keep, vo_send, vo_keep), dr2, dn2, dn2r, y_back)
+        )
+        dr1, df, du, dnd, dg2 = dense_backward(
+            dr2, dn2, dn2r, first, gain[2], gp, up_one, down_one
+        )
+        dndr = swap(dnd)
+
+        def gather_all(y, *dgs):
+            stacked = one_step(stack_kernel, bits, dgs, [shape((16, d), BF)])[0]
+            return gather_y(y), stacked
+
+        def heavy(dr, dna, dnb, n, g, a, b):
+            kept = grad(n, columns(g, bits[0])), grad(columns(a, bits[1]), b)
+            kept, dr, dna, dnb = lax.optimization_barrier((kept, dr, dna, dnb))
+            return last_attention(dr, dna, dnb), *kept
+
+        orders = [halving(o) for o in ((1, 2, 4, 8), (2, 1, 8, 4), (4, 8, 1, 2), (8, 4, 2, 1))]
+        big = [
+            Part(orders[0], grad(n2, columns(du, 1 - bits[0]))),
+            Part(orders[1], grad(columns(act, 1 - bits[1]), df)),
+            Part(orders[2], qk_send, qk_keep),
+            Part(orders[3], vo_send, vo_keep),
+        ]
+        last, up_keep, down_keep = advance(bits, big, heavy, (dr1, dnd, dndr, n2, du, act, df))
+        dr0, da1, dqk1, dv1, dn1, dg1 = last
+        dn1r = swap(dn1)
+        big[0].kept, big[1].kept = (up_keep, 0, up_keep.shape[0]), (down_keep, 0, down_keep.shape[0])
+        fold(bits, big)
+
+        def narrow_grads(n, dqk, dv, o, da):
+            return (
+                query_key(n, dqk, 1 - bits[0]),
+                query_key(n, dqk, bits[0]),
+                value_out(n, dv, o, da, bits[1]),
+            )
+
+        qk_send, qk_keep, (vo_send, vo_keep) = advance(
+            bits, big, narrow_grads, (n1, dqk1, dv1, o1, da1)
+        )
+        small = [Part(orders[0], qk_send, qk_keep), Part(orders[1], vo_send, vo_keep)]
+        parts = big + small
+        fold(bits, parts)
+        input_grad, dg0 = advance(bits, parts, last_step, (dr0, dn1, dn1r))
+        fold(bits, parts)
+        second, gains_own = advance(bits, parts, gather_all, (y_back, dg0, dg1, dg2, dg3))
+        tail = Part((1, 2, 4, 8), gains_own)
+        tail.kept = (None, 0, 0)
+        parts.append(tail)
+        while big[0].live:
+            fold(bits, parts)
+            advance(bits, parts)
+        fold(bits, parts)
+        arrays = [x for p in big for x in (p.sent[0], p.got[0])]
+
+        def finish_wide(*arrays):
+            return finish(
+                finish_wide_kernel,
+                bits,
+                big,
+                arrays,
+                [
+                    shape((d, f), F32),
+                    shape((f, d), F32),
+                    shape((3, d, c), F32),
+                    shape((c, d), F32),
+                ],
+            )
+
+        up_first, down_first, qkv_second, out_second = advance(bits, small, finish_wide, arrays)
+        while small[0].live:
+            fold(bits, small)
+            advance(bits, small)
+        gain_grads = (tail.sent[0], tail.got[0])
+        lo = tail.sent[1]
+        gain_grads = sum(v[lo : lo + 4].astype(F32) for v in gain_grads)
+        qkv_first, out_first = finish(
+            finish_narrow_kernel,
+            bits,
+            small,
+            [x for p in small for x in (p.sent[0], p.got[0])],
+            [shape((3, d, c), F32), shape((c, d), F32)],
+        )
     first_own = lax.dynamic_slice_in_dim(first, side * count, count, 0).astype(BF)
     return (
         first_own,

time: 675 us -> 514 us (0.76)
  blocking collectives: 75.1 us -> 0 us
  waiting for transfers between devices: 217 us -> 152 us
  other arithmetic: 34.7 us -> 9.26 us
  Pallas kernels: 190 us -> 201 us
  local copies, waits for them, and re-layouts: 31.4 us -> 24.5 us
    psum x1 -> x0, blocking collectives: 75.1 us -> none  [body(): gain_grads = lax.psum(gain_grads, 'dp')]
    ppermute x36, waiting for transfers between devices: 133 us -> 87.7 us  [advance(): lax.ppermute(v, 'dp', [(i, i ^ s) for i in range(16)])]
    all_to_all x4, waiting for transfers between devices: 69.8 us -> 50 us  [travel(): return lax.all_to_all(box, 'dp', 0, 0, tiled=True).reshape(slots, d)]
    concatenate x29 -> x0, other arithmetic: 14.3 us -> none  [the longest x4 3.32 us: attention_grads(): return jnp.concatenate([*w, wo[:, :c], wo[:, c:]], axis=0)]
    pallas_call x12 -> x24, Pallas kernels: 190 us -> 201 us  [call(): pl.pallas_call(kernel, grid_spec=spec, out_shape=outs, compiler_params=pa...]
    add x18 -> x1, other arithmetic: 9.39 us -> 0.6 us  [body(): gain_grads = sum((v[lo:lo + 4].astype(F32) for v in gain_grads))]
    slice x12 -> x2, local copies, waits for them, and re-layouts: 7.48 us -> 0.12 us  [value_sides(): return jnp.concatenate([w[:d // 2], w[d // 2:]], axis=1)]
    unnamed x73 -> x87, local copies, waits for them, and re-layouts: 12.3 us -> 17.9 us
  transfers between devices with their start and end apart: 54 -> 54, of which waited for: 31 -> 26; matrix products, arithmetic and copies ran while one was open for 12% -> 10% of each run, Pallas kernels for 18% -> 22%
where the time goes in v3:
time: 514 us; the launch traced here: 505 us
  Pallas kernels  201 us (39%)
  waiting for transfers between devices  152 us (30%)
  starting transfers between devices  78.9 us (15%)
  matrix products  38.8 us (8%)
  local copies, waits for them, and re-layouts  24.5 us (5%)
  other arithmetic  9.26 us (2%)
    pallas_call x24, Pallas kernels, call(): pl.pallas_call(kernel, grid_spec=spec, out_shape=outs, compiler_params=pa...  201 us
    ppermute x36, waiting for transfers between devices, advance(): lax.ppermute(v, 'dp', [(i, i ^ s) for i in range(16)])  87.7 us
    all_to_all x4, waiting for transfers between devices, travel(): return lax.all_to_all(box, 'dp', 0, 0, tiled=True).reshape(slots, d)  50 us
    ppermute x36, starting transfers between devices, advance(): lax.ppermute(v, 'dp', [(i, i ^ s) for i in range(16)])  44.8 us
    dot_general x14, matrix products, mm_tn(): lax.dot_general(a, b, (((0,), (0,)), ((), ())), preferred_element_type=F32)  38.5 us
    all_to_all x4, starting transfers between devices, travel(): return lax.all_to_all(box, 'dp', 0, 0, tiled=True).reshape(slots, d)  31.7 us
    unnamed x87, local copies, waits for them, and re-layouts  17.9 us
    ppermute x14, waiting for transfers between devices, swap(): return lax.ppermute(v, 'head', SWAP)  14.1 us
  transfers between devices with their start and end apart: 54, of which 26 were waited for; matrix products, arithmetic and copies ran while one was open for 10% of the time, Pallas kernels for 22%

profile of v3, /device:TPU:0, one launch (start us, length us, event | category | flops | bytes accessed | tf_op | source)
XLA Modules:
  0.0 505.4 jit_solution(8339196214285471118)
XLA Ops:
  1.2 1.7 copy.30.refs_5_.refs_6_.refs_13_.refs_12_
  5.2 19.0 %shard_map.237 = (f32[1024,768]{1,0:T(8,128)}, bf16[1024,768]{1,0:T(8,128)(2,1)}, bf16[3,1024,384]{2,1,0:T(8,128)(2,1)}, bf16[1024,384]{1,0:T(8,128)(2,1)}, f32[...) custom-call(s32[1]{0:T(128)} %bitcast.h_ref, bf16[512,768]{1,0:T(8,128)(2,1)} %xo.1, bf16[512,768]{1,0:T(8,128)(2,1)} %copy-done.23, ...), custom_call_target="tpu_custom_call" | custom-call | flops 8053063680 | bytes 15728640 | tf_op jit(solution)/shard_map/pallas_call | solution.py:358
  24.4 3.5 collective-permute-done.1.pb
  29.0 15.3 %shard_map.238 = (f32[1024,768]{1,0:T(8,128)}, bf16[1024,768]{1,0:T(8,128)(2,1)}, bf16[1024,1536]{1,0:T(8,128)(2,1)}, bf16[1024,1536]{1,0:T(8,128)(2,1)}, bf16[1024,768]{1,0:T(8,128)(2,1)}) custom-call(f32[1024,768]{1,0:T(8,128)} %get-tuple-element.253.xr, bf16[1024,768]{1,0:T(8,128)(2,1)} %get-tuple-element.254.pa, bf16[1024,768]{1,0:T(8,128)(2,1)} %copy-done.28, ...), custom_call_target="tpu_custom_call" | custom-call | flops 4831838208 | bytes 20447232 | tf_op jit(solution)/shard_map/pallas_call | solution.py:358
  46.4 3.8 shard_map.241
  50.2 8.2 %all-to-all-start.1 = ((bf16[16,64,768]{2,1,0:T(8,128)(2,1)}), bf16[16,64,768]{2,1,0:T(8,128)(2,1)S(1)}, u32[]{:S(2)}, u32[]{:S(2)}) async-start(bf16[16,64,768]{2,1,0:T(8,128)(2,1)} %bitcast.48), calls=%async_computation.1 | async-start | bytes 3145728 | tf_op jit(solution)/shard_map/all_to_all | solution.py:868
  59.6 19.3 %shard_map.239 = (f32[1024,768]{1,0:T(8,128)}, bf16[1024,768]{1,0:T(8,128)(2,1)}, bf16[3,1024,384]{2,1,0:T(8,128)(2,1)}, bf16[1024,384]{1,0:T(8,128)(2,1)}, f32[...) custom-call(s32[1]{0:T(128)} %bitcast.h_ref, f32[1024,768]{1,0:T(8,128)} %get-tuple-element.255.refs_0_.refs_3_, ...), custom_call_target="tpu_custom_call" | custom-call | flops 8053063680 | bytes 15728640 | tf_op jit(solution)/shard_map/pallas_call | solution.py:358
  78.9 3.6 collective-permute-done.4.pb
  83.7 6.7 %shard_map.240 = (f32[1024,768]{1,0:T(8,128)}, bf16[1024,768]{1,0:T(8,128)(2,1)}) custom-call(s32[1]{0:T(128)} %bitcast.h_ref, f32[1024,768]{1,0:T(8,128)} %get-tuple-element.257.xr.xn, bf16[1024,768]{1,0:T(8,128)(2,1)} %get-tuple-element.260.pa, bf16[1024,768]{1,0:T(8,128)(2,1)} %copy-done.20, f32[1,768]{1,0:T(1,128)} %get-tuple-element.503.g.refs_5_, ...), custom_call_target="tpu_custom_call" | custom-call | flops 805306368 | bytes 11010048 | tf_op jit(solution)/shard_map/pallas_call | solution.py:358
  90.4 2.3 all-to-all-done.1
  92.7 8.2 %all-to-all-start = ((bf16[16,64,768]{2,1,0:T(8,128)(2,1)}), bf16[16,64,768]{2,1,0:T(8,128)(2,1)S(1)}, u32[]{:S(2)}, u32[]{:S(2)}) async-start(bf16[16,64,768]{2,1,0:T(8,128)(2,1)} %bitcast.50), calls=%async_computation | async-start | bytes 3145728 | tf_op jit(solution)/shard_map/all_to_all | solution.py:868
  101.0 33.2 %all-to-all-done = bf16[16,64,768]{2,1,0:T(8,128)(2,1)S(1)} async-done(((bf16[16,64,768]{2,1,0:T(8,128)(2,1)}), bf16[16,64,768]{2,1,0:T(8,128)(2,1)S(1)}, u32[]{:S(2)}, u32[]{:S(2)}) %all-to-all-start) | async-done | bytes 1572896 | tf_op jit(solution)/shard_map/all_to_all | solution.py:868
  134.2 3.4 collective-permute-done.5.mp
  138.8 35.5 %shard_map.242 = (bf16[1024,768]{1,0:T(8,128)(2,1)}, bf16[1024,768]{1,0:T(8,128)(2,1)}, bf16[1024,768]{1,0:T(8,128)(2,1)}, bf16[1024,768]{1,0:T(8,128)(2,1)}, bf...) custom-call(bf16[1024,768]{1,0:T(8,128)(2,1)} %bitcast.47, ...), custom_call_target="tpu_custom_call" | custom-call | flops 19327352832 | bytes 31457280 | tf_op jit(solution)/shard_map/pallas_call | solution.py:358
  174.5 3.5 collective-permute-done.7
  178.0 3.0 add_convert_fusion.1
  180.9 7.3 %all-to-all-start.2 = ((bf16[16,64,768]{2,1,0:T(8,128)(2,1)}), bf16[16,64,768]{2,1,0:T(8,128)(2,1)S(1)}, u32[]{:S(2)}, u32[]{:S(2)}) async-start(bf16[16,64,768]{2,1,0:T(8,128)(2,1)} %bitcast.12), calls=%async_computation.2 | async-start | bytes 3145728 | tf_op jit(solution)/shard_map/all_to_all | solution.py:868
  188.8 9.7 %convolution_bitcast_fusion = f32[1,1536,768]{2,1,0:T(8,128)} fusion(bf16[2048,1536]{1,0:T(8,128)(2,1)} %get-tuple-element.266, bf16[2048,768]{1,0:T(8,128)(2,1)} %get-tuple-element.267), kind=kOutput, calls=%fused_computation | convolution fusion | flops 4831838208 | bytes 14155776 | tf_op jit(solution)/shard_map/dot_general | solution.py:29
  198.6 9.5 %convolution_bitcast_fusion.1 = f32[1,768,1536]{2,1,0:T(8,128)} fusion(bf16[2048,768]{1,0:T(8,128)(2,1)S(1)} %copy-done.39, bf16[2048,1536]{1,0:T(8,128)(2,1)} %get-tuple-element.265), kind=kOutput, calls=%fused_computation.1 | convolution fusion | flops 4831838208 | bytes 14155776 | tf_op jit(solution)/shard_map/dot_general | solution.py:29
  208.1 14.4 %all-to-all-done.2 = bf16[16,64,768]{2,1,0:T(8,128)(2,1)S(1)} async-done(((bf16[16,64,768]{2,1,0:T(8,128)(2,1)}), bf16[16,64,768]{2,1,0:T(8,128)(2,1)S(1)}, u32[]{:S(2)}, u32[]{:S(2)}) %all-to-all-start.2) | async-done | bytes 1572896 | tf_op jit(solution)/shard_map/all_to_all | solution.py:868
  223.7 3.6 shard_map.243.refs_2_
  227.3 3.0 add_convert_fusion
  230.2 8.0 %all-to-all-start.3 = ((bf16[16,64,768]{2,1,0:T(8,128)(2,1)}), bf16[16,64,768]{2,1,0:T(8,128)(2,1)S(1)}, u32[]{:S(2)}, u32[]{:S(2)}) async-start(bf16[16,64,768]{2,1,0:T(8,128)(2,1)} %bitcast.17), calls=%async_computation.3 | async-start | bytes 3145728 | tf_op jit(solution)/shard_map/all_to_all | solution.py:868
  238.3 26.8 %shard_map.244 = (f32[1024,768]{1,0:T(8,128)}, bf16[1024,768]{1,0:T(8,128)(2,1)}, bf16[1024,768]{1,0:T(8,128)(2,1)}, bf16[1024,384]{1,0:T(8,128)(2,1)}, bf16[1024,768]{1,0:T(8,128)(2,1)}, /*index=5*/f32[8,768]{1,0:T(8,128)}) custom-call(s32[1]{0:T(128)} %bitcast.h_ref, bf16[512,768]{1,0:T(8,128)(2,1)} %refs_0_.3, ...), custom_call_target="tpu_custom_call" | custom-call | flops 12884901888 | bytes 15728640 | tf_op jit(solution)/shard_map/pallas_call | solution.py:358
  265.4 2.8 convolution_convert_fusion.5
  268.3 1.7 convolution_convert_fusion.6.refs_4_
  270.0 1.7 convolution_convert_fusion.7
  271.6 1.9 broadcast_select_fusion.2
  274.7 13.2 %shard_map.245 = (f32[1024,768]{1,0:T(8,128)}, bf16[1024,768]{1,0:T(8,128)(2,1)}, bf16[1024,1536]{1,0:T(8,128)(2,1)}, bf16[1024,768]{1,0:T(8,128)(2,1)}, f32[8,768]{1,0:T(8,128)}) custom-call(f32[1024,768]{1,0:T(8,128)} %get-tuple-element.280.drr, bf16[1024,768]{1,0:T(8,128)(2,1)} %get-tuple-element.281.dna, bf16[1024,768]{1,0:T(8,128)(2,1)} %copy-done.24, ...), custom_call_target="tpu_custom_call" | custom-call | flops 4831838208 | bytes 20447232 | tf_op jit(solution)/shard_map/pallas_call | solution.py:358
  288.3 3.5 fusion.11
  297.4 2.0 collective-permute-start.12
  300.8 3.3 collective-permute-start.14
  305.0 26.3 %shard_map.246 = (f32[1024,768]{1,0:T(8,128)}, bf16[1024,768]{1,0:T(8,128)(2,1)}, bf16[1024,768]{1,0:T(8,128)(2,1)}, bf16[1024,384]{1,0:T(8,128)(2,1)}, bf16[1024,768]{1,0:T(8,128)(2,1)}, /*index=5*/f32[8,768]{1,0:T(8,128)}) custom-call(s32[1]{0:T(128)} %bitcast.h_ref, f32[1024,768]{1,0:T(8,128)} %get-tuple-element.302.refs_0_, ...), custom_call_target="tpu_custom_call" | custom-call | flops 12884901888 | bytes 15728640 | tf_op jit(solution)/shard_map/pallas_call | solution.py:358
  340.2 1.6 shard_map.247
  342.9 2.0 collective-permute-start.18
  344.9 1.5 collective-permute-start.19
  350.6 6.4 %collective-permute-done.18.refs_4_ = bf16[192,768]{1,0:T(8,128)(2,1)S(1)} collective-permute-done((bf16[192,768]{1,0:T(8,128)(2,1)S(1)}, bf16[192,768]{1,0:T(8,128)(2,1)S(1)}, u32[]{:S(2)}, u32[]{:S(2)}) %collective-permute-start.18) | collective-permute-done | bytes 294944 | tf_op jit(solution)/shard_map/ppermute | solution.py:718
  357.0 3.8 collective-permute-done.19.refs_3_
  363.9 2.6 collective-permute-start.24
  366.5 6.3 %shard_map.249 = (f32[512,768]{1,0:T(8,128)}, f32[8,768]{1,0:T(8,128)}) custom-call(s32[1]{0:T(128)} %bitcast.h_ref, f32[1024,768]{1,0:T(8,128)} %get-tuple-element.359.drr, bf16[1024,768]{1,0:T(8,128)(2,1)} %get-tuple-element.360.dna, bf16[1024,768]{1,0:T(8,128)(2,1)} %collective-permute-done.20.dnb, bf16[512,768]{1,0:T(8,128)(2,1)} %xo.1, ...), custom_call_target="tpu_custom_call" | custom-call | flops 31457280 | bytes 11010048 | tf_op jit(solution)/shard_map/pallas_call | solution.py:358
  372.8 2.9 collective-permute-done.23.refs_1_
  375.7 2.6 collective-permute-done.24.refs_2_
  380.4 1.7 collective-permute-start.25
  383.1 1.9 collective-permute-start.28
  385.6 4.1 shard_map.251
  391.7 2.1 collective-permute-start.32
  396.1 3.5 collective-permute-done.30.refs_5_
  399.6 2.9 collective-permute-done.31.refs_3_
  402.5 1.6 collective-permute-done.32.refs_1_
  404.9 2.3 collective-permute-start.36
  409.5 3.9 collective-permute-done.33.refs_5_
  413.4 5.9 %collective-permute-done.35.refs_1_ = bf16[240,768]{1,0:T(8,128)(2,1)S(1)} collective-permute-done((bf16[240,768]{1,0:T(8,128)(2,1)S(1)}, bf16[240,768]{1,0:T(8,128)(2,1)S(1)}, u32[]{:S(2)}, u32[]{:S(2)}) %collective-permute-start.35) | collective-permute-done | bytes 368672 | tf_op jit(solution)/shard_map/ppermute | solution.py:718
  421.3 1.6 collective-permute-start.37
  424.0 1.9 collective-permute-start.40
  425.9 13.1 %collective-permute-done.40.refs_5_ = bf16[240,768]{1,0:T(8,128)(2,1)S(1)} collective-permute-done((bf16[240,768]{1,0:T(8,128)(2,1)S(1)}, bf16[240,768]{1,0:T(8,128)(2,1)S(1)}, u32[]{:S(2)}, u32[]{:S(2)}) %collective-permute-start.40) | collective-permute-done | bytes 368672 | tf_op jit(solution)/shard_map/ppermute | solution.py:718
  441.3 1.7 collective-permute-start.42
  443.9 1.5 collective-permute-start.43
  445.4 26.9 %collective-permute-done.43.refs_1_.ag = bf16[480,768]{1,0:T(8,128)(2,1)S(1)} collective-permute-done((bf16[480,768]{1,0:T(8,128)(2,1)S(1)}, bf16[480,768]{1,0:T(8,128)(2,1)S(1)}, u32[]{:S(2)}, u32[]{:S(2)}) %collective-permute-start.43) | collective-permute-done | bytes 737312 | tf_op jit(solution)/shard_map/ppermute | solution.py:718
  472.3 2.6 collective-permute-done.44.refs_3_.bg
  477.3 8.7 %shard_map.258 = (f32[768,1536]{1,0:T(8,128)}, f32[1536,768]{1,0:T(8,128)}, f32[3,768,384]{2,1,0:T(8,128)}, f32[384,768]{1,0:T(8,128)}) custom-call(s32[4]{0:T(128)S(1)} %pad_add_fusion.bits, bf16[768,768]{1,0:T(8,128)(2,1)S(1)} %get-tuple-element.462.xp, bf16[768,768]{1,0:T(8,128)(2,1)} %copy-done.21, bf16[768,768]{1,0:T(8,128)(2,1)} %copy-done.4, ...), custom_call_target="tpu_custom_call" | custom-call | flops 21872640 | bytes 21872640 | tf_op jit(solution)/shard_map/pallas_call | solution.py:358
  487.3 1.7 collective-permute-start.48
  489.8 2.4 dynamic-slice_convert_fusion
  494.1 7.4 %collective-permute-done.47.xg = bf16[384,768]{1,0:T(8,128)(2,1)S(1)} collective-permute-done((bf16[384,768]{1,0:T(8,128)(2,1)S(1)}, bf16[384,768]{1,0:T(8,128)(2,1)S(1)}, u32[]{:S(2)}, u32[]{:S(2)}) %collective-permute-start.47) | collective-permute-done | bytes 589856 | tf_op jit(solution)/shard_map/ppermute | solution.py:718
  501.7 3.2 shard_map.260
  (186 shorter events, 62.6 us)
Async XLA Ops:
  0.6 43.8 %copy-start = (s32[1024,1]{0,1:T(1,128)S(1)}, s32[1024,1]{0,1:T(1,128)}, u32[]{:S(2)}) copy-start(s32[1024,1]{0,1:T(1,128)} %param.16) | copy-start | bytes 12292
  0.7 3.7 collective-permute-start
  24.3 3.6 collective-permute-start.1
  44.3 14.1 %collective-permute-start.2 = (bf16[1024,768]{1,0:T(8,128)(2,1)}, bf16[1024,768]{1,0:T(8,128)(2,1)S(1)}, u32[]{:S(2)}, u32[]{:S(2)}) collective-permute-start(bf16[1024,768]{1,0:T(8,128)(2,1)} %get-tuple-element.256.refs_1_), channel_id=1, source_target_pairs={{0,16},{16,0},{1,17},{17,1},{2,18},{18,2},{3,19},{19,3},{4,20},{20... | collective-permute-start | bytes 4718600 | tf_op jit(solution)/shard_map/ppermute | solution.py:630
  50.2 42.5 %all-to-all-start.1 = ((bf16[16,64,768]{2,1,0:T(8,128)(2,1)}), bf16[16,64,768]{2,1,0:T(8,128)(2,1)S(1)}, u32[]{:S(2)}, u32[]{:S(2)}) async-start(bf16[16,64,768]{2,1,0:T(8,128)(2,1)} %bitcast.48), calls=%async_computation.1 | async-start | bytes 3145728 | tf_op jit(solution)/shard_map/all_to_all | solution.py:868
  78.9 3.7 collective-permute-start.4
  92.7 8.2 %copy-start.16 = (bf16[16,64,768]{2,1,0:T(8,128)(2,1)}, bf16[16,64,768]{2,1,0:T(8,128)(2,1)S(1)}, u32[]{:S(2)}) copy-start(bf16[16,64,768]{2,1,0:T(8,128)(2,1)S(1)} %all-to-all-done.1) | copy-start | bytes 4718596
  92.7 41.5 %all-to-all-start = ((bf16[16,64,768]{2,1,0:T(8,128)(2,1)}), bf16[16,64,768]{2,1,0:T(8,128)(2,1)S(1)}, u32[]{:S(2)}, u32[]{:S(2)}) async-start(bf16[16,64,768]{2,1,0:T(8,128)(2,1)} %bitcast.50), calls=%async_computation | async-start | bytes 3145728 | tf_op jit(solution)/shard_map/all_to_all | solution.py:868
  100.9 33.3 %collective-permute-start.6 = (bf16[1024,768]{1,0:T(8,128)(2,1)S(1)}, bf16[1024,768]{1,0:T(8,128)(2,1)}, u32[]{:S(2)}, u32[]{:S(2)}) collective-permute-start(bf16[1024,768]{1,0:T(8,128)(2,1)S(1)} %bitcast.44), channel_id=1, source_target_pairs={{0,16},{16,0},{1,17},{17,1},{2,18},{18,2},{3,19},{19,3},{4,20},{20... | collective-permute-start | bytes 4718600 | tf_op jit(solution)/shard_map/ppermute | solution.py:630
  134.2 3.4 collective-permute-start.5
  174.3 3.7 collective-permute-start.7
  180.9 41.6 %all-to-all-start.2 = ((bf16[16,64,768]{2,1,0:T(8,128)(2,1)}), bf16[16,64,768]{2,1,0:T(8,128)(2,1)S(1)}, u32[]{:S(2)}, u32[]{:S(2)}) async-start(bf16[16,64,768]{2,1,0:T(8,128)(2,1)} %bitcast.12), calls=%async_computation.2 | async-start | bytes 3145728 | tf_op jit(solution)/shard_map/all_to_all | solution.py:868
  188.2 50.0 %collective-permute-start.3 = (bf16[512,768]{1,0:T(8,128)(2,1)}, bf16[512,768]{1,0:T(8,128)(2,1)}, u32[]{:S(2)}, u32[]{:S(2)}) collective-permute-start(bf16[512,768]{1,0:T(8,128)(2,1)} %refs_0_.3), channel_id=1, source_target_pairs={{0,16},{16,0},{1,17},{17,1},{2,18},{18,2},{3,19},{19,3},{4,20},{20... | collective-permute-start | bytes 2359304 | tf_op jit(solution)/shard_map/ppermute | solution.py:630
  188.3 38.9 %collective-permute-start.10 = (bf16[1024,768]{1,0:T(8,128)(2,1)}, bf16[1024,768]{1,0:T(8,128)(2,1)}, u32[]{:S(2)}, u32[]{:S(2)}) collective-permute-start(bf16[1024,768]{1,0:T(8,128)(2,1)} %get-tuple-element.279), channel_id=1, source_target_pairs={{0,16},{16,0},{1,17},{17,1},{2,18},{18,2},{3,19},{19,3},{4,20},{20... | collective-permute-start | bytes 4718600 | tf_op jit(solution)/shard_map/ppermute | solution.py:630
  188.8 9.7 %copy-start.39 = (bf16[2048,768]{1,0:T(8,128)(2,1)S(1)}, bf16[2048,768]{1,0:T(8,128)(2,1)}, u32[]{:S(2)}) copy-start(bf16[2048,768]{1,0:T(8,128)(2,1)} %get-tuple-element.264) | copy-start | bytes 9437188
  208.1 19.2 %copy-start.19 = (bf16[1024,768]{1,0:T(8,128)(2,1)S(1)}, bf16[1024,768]{1,0:T(8,128)(2,1)}, u32[]{:S(2)}) copy-start(bf16[1024,768]{1,0:T(8,128)(2,1)} %get-tuple-element.278) | copy-start | bytes 4718596
  227.3 11.0 %collective-permute-start.8 = (bf16[512,768]{1,0:T(8,128)(2,1)}, bf16[512,768]{1,0:T(8,128)(2,1)}, u32[]{:S(2)}, u32[]{:S(2)}) collective-permute-start(bf16[512,768]{1,0:T(8,128)(2,1)} %shard_map.243.refs_2_), channel_id=1, source_target_pairs={{0,16},{16,0},{1,17},{17,1},{2,18},{18,2},{3,19},{19,3},{4,20},{20... | collective-permute-start | bytes 2359304 | tf_op jit(solution)/shard_map/ppermute | solution.py:630
  230.2 43.3 %all-to-all-start.3 = ((bf16[16,64,768]{2,1,0:T(8,128)(2,1)}), bf16[16,64,768]{2,1,0:T(8,128)(2,1)S(1)}, u32[]{:S(2)}, u32[]{:S(2)}) async-start(bf16[16,64,768]{2,1,0:T(8,128)(2,1)} %bitcast.17), calls=%async_computation.3 | async-start | bytes 3145728 | tf_op jit(solution)/shard_map/all_to_all | solution.py:868
  265.1 8.4 %collective-permute-start.9 = (bf16[1024,768]{1,0:T(8,128)(2,1)}, bf16[1024,768]{1,0:T(8,128)(2,1)S(1)}, u32[]{:S(2)}, u32[]{:S(2)}) collective-permute-start(bf16[1024,768]{1,0:T(8,128)(2,1)} %get-tuple-element.281.dna), channel_id=1, source_target_pairs={{0,16},{16,0},{1,17},{17,1},{2,18},{18,2},{3,19},{19,3},{4,20},{20... | collective-permute-start | bytes 4718600 | tf_op jit(solution)/shard_map/ppermute | solution.py:630
  273.5 14.4 %copy-start.15 = (bf16[16,64,768]{2,1,0:T(8,128)(2,1)}, bf16[16,64,768]{2,1,0:T(8,128)(2,1)S(1)}, u32[]{:S(2)}) copy-start(bf16[16,64,768]{2,1,0:T(8,128)(2,1)S(1)} %all-to-all-done.3) | copy-start | bytes 4718596
  287.9 5.3 %collective-permute-start.11 = (bf16[1024,768]{1,0:T(8,128)(2,1)}, bf16[1024,768]{1,0:T(8,128)(2,1)S(1)}, u32[]{:S(2)}, u32[]{:S(2)}) collective-permute-start(bf16[1024,768]{1,0:T(8,128)(2,1)} %get-tuple-element.303.refs_1_), channel_id=1, source_target_pairs={{0,16},{16,0},{1,17},{17,1},{2,18},{18,2},{3,19},{19,3},{4,20},{20... | collective-permute-start | bytes 4718600 | tf_op jit(solution)/shard_map/ppermute | solution.py:630
  297.4 36.2 %collective-permute-start.12 = (bf16[768,768]{1,0:T(8,128)(2,1)S(1)}, bf16[768,768]{1,0:T(8,128)(2,1)S(1)}, u32[]{:S(2)}, u32[]{:S(2)}) collective-permute-start(bf16[768,768]{1,0:T(8,128)(2,1)S(1)} %fusion.8), channel_id=1, source_target_pairs={{0,1},{1,0},{2,3},{3,2},{4,5},{5,4},{6,7},{7,6},{8,9},{9,8},{10,11... | collective-permute-start | bytes 3538952 | tf_op jit(solution)/shard_map/ppermute | solution.py:718
  299.4 34.2 %collective-permute-start.13 = (bf16[768,768]{1,0:T(8,128)(2,1)S(1)}, bf16[768,768]{1,0:T(8,128)(2,1)S(1)}, u32[]{:S(2)}, u32[]{:S(2)}) collective-permute-start(bf16[768,768]{1,0:T(8,128)(2,1)S(1)} %fusion.11), channel_id=1, source_target_pairs={{0,2},{1,3},{2,0},{3,1},{4,6},{5,7},{6,4},{7,5},{8,10},{9,11},{10,... | collective-permute-start | bytes 3538952 | tf_op jit(solution)/shard_map/ppermute | solution.py:718
  300.8 30.4 %collective-permute-start.14 = (bf16[384,768]{1,0:T(8,128)(2,1)}, bf16[384,768]{1,0:T(8,128)(2,1)S(1)}, u32[]{:S(2)}, u32[]{:S(2)}) collective-permute-start(bf16[384,768]{1,0:T(8,128)(2,1)} %convolution_convert_fusion.7), channel_id=1, source_target_pairs={{0,4},{1,5},{2,6},{3,7},{4,0},{5,1},{6,2},{7,3},{8,12},{9,13},{10,... | collective-permute-start | bytes 1769480 | tf_op jit(solution)/shard_map/ppermute | solution.py:718
  304.2 28.6 %collective-permute-start.15 = (bf16[384,768]{1,0:T(8,128)(2,1)}, bf16[384,768]{1,0:T(8,128)(2,1)S(1)}, u32[]{:S(2)}, u32[]{:S(2)}) collective-permute-start(bf16[384,768]{1,0:T(8,128)(2,1)} %get-tuple-element.294), channel_id=1, source_target_pairs={{0,8},{1,9},{2,10},{3,11},{4,12},{5,13},{6,14},{7,15},{8,0},{9,1},... | collective-permute-start | bytes 1769480 | tf_op jit(solution)/shard_map/ppermute | solution.py:718
  334.6 27.3 %collective-permute-start.20 = (bf16[1024,768]{1,0:T(8,128)(2,1)}, bf16[1024,768]{1,0:T(8,128)(2,1)}, u32[]{:S(2)}, u32[]{:S(2)}) collective-permute-start(bf16[1024,768]{1,0:T(8,128)(2,1)} %get-tuple-element.360.dna), channel_id=1, source_target_pairs={{0,16},{16,0},{1,17},{17,1},{2,18},{18,2},{3,19},{19,3},{4,20},{20... | collective-permute-start | bytes 4718600 | tf_op jit(solution)/shard_map/ppermute | solution.py:630
  340.2 6.2 %copy-start.31 = (bf16[1024,768]{1,0:T(8,128)(2,1)S(1)}, bf16[1024,768]{1,0:T(8,128)(2,1)}, u32[]{:S(2)}) copy-start(bf16[1024,768]{1,0:T(8,128)(2,1)} %get-tuple-element.337) | copy-start | bytes 4718596
  340.2 6.2 %copy-start.38 = (bf16[1024,384]{1,0:T(8,128)(2,1)S(1)}, bf16[1024,384]{1,0:T(8,128)(2,1)}, u32[]{:S(2)}) copy-start(bf16[1024,384]{1,0:T(8,128)(2,1)} %get-tuple-element.339) | copy-start | bytes 2359300
  341.9 18.8 %collective-permute-start.16 = (bf16[384,768]{1,0:T(8,128)(2,1)S(1)}, bf16[384,768]{1,0:T(8,128)(2,1)S(1)}, u32[]{:S(2)}, u32[]{:S(2)}) collective-permute-start(bf16[384,768]{1,0:T(8,128)(2,1)S(1)} %get-tuple-element.333), channel_id=1, source_target_pairs={{0,1},{1,0},{2,3},{3,2},{4,5},{5,4},{6,7},{7,6},{8,9},{9,8},{10,11... | collective-permute-start | bytes 1769480 | tf_op jit(solution)/shard_map/ppermute | solution.py:718
  342.8 17.9 %collective-permute-start.17 = (bf16[384,768]{1,0:T(8,128)(2,1)S(1)}, bf16[384,768]{1,0:T(8,128)(2,1)S(1)}, u32[]{:S(2)}, u32[]{:S(2)}) collective-permute-start(bf16[384,768]{1,0:T(8,128)(2,1)S(1)} %get-tuple-element.334), channel_id=1, source_target_pairs={{0,2},{1,3},{2,0},{3,1},{4,6},{5,7},{6,4},{7,5},{8,10},{9,11},{10,... | collective-permute-start | bytes 1769480 | tf_op jit(solution)/shard_map/ppermute | solution.py:718
  342.9 14.1 %collective-permute-start.18 = (bf16[192,768]{1,0:T(8,128)(2,1)S(1)}, bf16[192,768]{1,0:T(8,128)(2,1)S(1)}, u32[]{:S(2)}, u32[]{:S(2)}) collective-permute-start(bf16[192,768]{1,0:T(8,128)(2,1)S(1)} %get-tuple-element.335), channel_id=1, source_target_pairs={{0,4},{1,5},{2,6},{3,7},{4,0},{5,1},{6,2},{7,3},{8,12},{9,13},{10,... | collective-permute-start | bytes 884744 | tf_op jit(solution)/shard_map/ppermute | solution.py:718
  344.9 15.8 %collective-permute-start.19 = (bf16[192,768]{1,0:T(8,128)(2,1)S(1)}, bf16[192,768]{1,0:T(8,128)(2,1)S(1)}, u32[]{:S(2)}, u32[]{:S(2)}) collective-permute-start(bf16[192,768]{1,0:T(8,128)(2,1)S(1)} %get-tuple-element.336), channel_id=1, source_target_pairs={{0,8},{1,9},{2,10},{3,11},{4,12},{5,13},{6,14},{7,15},{8,0},{9,1},... | collective-permute-start | bytes 884744 | tf_op jit(solution)/shard_map/ppermute | solution.py:718
  361.9 17.3 %collective-permute-start.21 = (bf16[480,768]{1,0:T(8,128)(2,1)S(1)}, bf16[480,768]{1,0:T(8,128)(2,1)S(1)}, u32[]{:S(2)}, u32[]{:S(2)}) collective-permute-start(bf16[480,768]{1,0:T(8,128)(2,1)S(1)} %get-tuple-element.355), channel_id=1, source_target_pairs={{0,1},{1,0},{2,3},{3,2},{4,5},{5,4},{6,7},{7,6},{8,9},{9,8},{10,11... | collective-permute-start | bytes 2211848 | tf_op jit(solution)/shard_map/ppermute | solution.py:718
  362.7 16.5 %collective-permute-start.22 = (bf16[480,768]{1,0:T(8,128)(2,1)S(1)}, bf16[480,768]{1,0:T(8,128)(2,1)S(1)}, u32[]{:S(2)}, u32[]{:S(2)}) collective-permute-start(bf16[480,768]{1,0:T(8,128)(2,1)S(1)} %get-tuple-element.356), channel_id=1, source_target_pairs={{0,2},{1,3},{2,0},{3,1},{4,6},{5,7},{6,4},{7,5},{8,10},{9,11},{10,... | collective-permute-start | bytes 2211848 | tf_op jit(solution)/shard_map/ppermute | solution.py:718
  363.4 12.3 %collective-permute-start.23 = (bf16[192,768]{1,0:T(8,128)(2,1)S(1)}, bf16[192,768]{1,0:T(8,128)(2,1)S(1)}, u32[]{:S(2)}, u32[]{:S(2)}) collective-permute-start(bf16[192,768]{1,0:T(8,128)(2,1)S(1)} %get-tuple-element.357), channel_id=1, source_target_pairs={{0,4},{1,5},{2,6},{3,7},{4,0},{5,1},{6,2},{7,3},{8,12},{9,13},{10,... | collective-permute-start | bytes 884744 | tf_op jit(solution)/shard_map/ppermute | solution.py:718
  363.9 14.4 %collective-permute-start.24 = (bf16[192,768]{1,0:T(8,128)(2,1)S(1)}, bf16[192,768]{1,0:T(8,128)(2,1)S(1)}, u32[]{:S(2)}, u32[]{:S(2)}) collective-permute-start(bf16[192,768]{1,0:T(8,128)(2,1)S(1)} %get-tuple-element.358), channel_id=1, source_target_pairs={{0,8},{1,9},{2,10},{3,11},{4,12},{5,13},{6,14},{7,15},{8,0},{9,1},... | collective-permute-start | bytes 884744 | tf_op jit(solution)/shard_map/ppermute | solution.py:718
  379.2 5.8 %copy-start.14 = (f32[8,768]{1,0:T(8,128)S(1)}, f32[8,768]{1,0:T(8,128)}, u32[]{:S(2)}) copy-start(f32[8,768]{1,0:T(8,128)} %get-tuple-element.384.refs_0_) | copy-start | bytes 73732
  380.4 10.4 %collective-permute-start.25 = (bf16[240,768]{1,0:T(8,128)(2,1)S(1)}, bf16[240,768]{1,0:T(8,128)(2,1)S(1)}, u32[]{:S(2)}, u32[]{:S(2)}) collective-permute-start(bf16[240,768]{1,0:T(8,128)(2,1)S(1)} %get-tuple-element.379), channel_id=1, source_target_pairs={{0,1},{1,0},{2,3},{3,2},{4,5},{5,4},{6,7},{7,6},{8,9},{9,8},{10,11... | collective-permute-start | bytes 1105928 | tf_op jit(solution)/shard_map/ppermute | solution.py:718
  382.1 8.7 %collective-permute-start.26 = (bf16[240,768]{1,0:T(8,128)(2,1)S(1)}, bf16[240,768]{1,0:T(8,128)(2,1)S(1)}, u32[]{:S(2)}, u32[]{:S(2)}) collective-permute-start(bf16[240,768]{1,0:T(8,128)(2,1)S(1)} %get-tuple-element.380), channel_id=1, source_target_pairs={{0,2},{1,3},{2,0},{3,1},{4,6},{5,7},{6,4},{7,5},{8,10},{9,11},{10,... | collective-permute-start | bytes 1105928 | tf_op jit(solution)/shard_map/ppermute | solution.py:718
  382.4 7.3 %collective-permute-start.27 = (bf16[96,768]{1,0:T(8,128)(2,1)S(1)}, bf16[96,768]{1,0:T(8,128)(2,1)S(1)}, u32[]{:S(2)}, u32[]{:S(2)}) collective-permute-start(bf16[96,768]{1,0:T(8,128)(2,1)S(1)} %get-tuple-element.381), channel_id=1, source_target_pairs={{0,4},{1,5},{2,6},{3,7},{4,0},{5,1},{6,2},{7,3},{8,12},{9,13},{10,... | collective-permute-start | bytes 442376 | tf_op jit(solution)/shard_map/ppermute | solution.py:718
  383.1 7.7 %collective-permute-start.28 = (bf16[96,768]{1,0:T(8,128)(2,1)S(1)}, bf16[96,768]{1,0:T(8,128)(2,1)S(1)}, u32[]{:S(2)}, u32[]{:S(2)}) collective-permute-start(bf16[96,768]{1,0:T(8,128)(2,1)S(1)} %get-tuple-element.382), channel_id=1, source_target_pairs={{0,8},{1,9},{2,10},{3,11},{4,12},{5,13},{6,14},{7,15},{8,0},{9,1},... | collective-permute-start | bytes 442376 | tf_op jit(solution)/shard_map/ppermute | solution.py:718
  391.6 10.9 %collective-permute-start.31 = (bf16[192,768]{1,0:T(8,128)(2,1)S(1)}, bf16[192,768]{1,0:T(8,128)(2,1)S(1)}, u32[]{:S(2)}, u32[]{:S(2)}) collective-permute-start(bf16[192,768]{1,0:T(8,128)(2,1)S(1)} %get-tuple-element.406.refs_2_), channel_id=1, source_target_pairs={{0,4},{1,5},{2,6},{3,7},{4,0},{5,1},{6,2},{7,3},{8,12},{9,13},{10,... | collective-permute-start | bytes 884744 | tf_op jit(solution)/shard_map/ppermute | solution.py:718
  391.7 12.4 %collective-permute-start.32 = (bf16[192,768]{1,0:T(8,128)(2,1)S(1)}, bf16[192,768]{1,0:T(8,128)(2,1)S(1)}, u32[]{:S(2)}, u32[]{:S(2)}) collective-permute-start(bf16[192,768]{1,0:T(8,128)(2,1)S(1)} %get-tuple-element.404.refs_0_), channel_id=1, source_target_pairs={{0,8},{1,9},{2,10},{3,11},{4,12},{5,13},{6,14},{7,15},{8,0},{9,1},... | collective-permute-start | bytes 884744 | tf_op jit(solution)/shard_map/ppermute | solution.py:718
  393.9 5.7 %collective-permute-start.29 = (bf16[64,768]{1,0:T(8,128)(2,1)S(1)}, bf16[64,768]{1,0:T(8,128)(2,1)S(1)}, u32[]{:S(2)}, u32[]{:S(2)}) collective-permute-start(bf16[64,768]{1,0:T(8,128)(2,1)S(1)} %get-tuple-element.410.refs_6_), channel_id=1, source_target_pairs={{0,1},{1,0},{2,3},{3,2},{4,5},{5,4},{6,7},{7,6},{8,9},{9,8},{10,11... | collective-permute-start | bytes 294920 | tf_op jit(solution)/shard_map/ppermute | solution.py:718
  395.2 4.4 collective-permute-start.30
  404.8 14.5 %collective-permute-start.35 = (bf16[240,768]{1,0:T(8,128)(2,1)S(1)}, bf16[240,768]{1,0:T(8,128)(2,1)S(1)}, u32[]{:S(2)}, u32[]{:S(2)}) collective-permute-start(bf16[240,768]{1,0:T(8,128)(2,1)S(1)} %get-tuple-element.421.refs_0_), channel_id=1, source_target_pairs={{0,4},{1,5},{2,6},{3,7},{4,0},{5,1},{6,2},{7,3},{8,12},{9,13},{10,... | collective-permute-start | bytes 1105928 | tf_op jit(solution)/shard_map/ppermute | solution.py:718
  404.9 15.8 %collective-permute-start.36 = (bf16[240,768]{1,0:T(8,128)(2,1)S(1)}, bf16[240,768]{1,0:T(8,128)(2,1)S(1)}, u32[]{:S(2)}, u32[]{:S(2)}) collective-permute-start(bf16[240,768]{1,0:T(8,128)(2,1)S(1)} %get-tuple-element.423.refs_2_), channel_id=1, source_target_pairs={{0,8},{1,9},{2,10},{3,11},{4,12},{5,13},{6,14},{7,15},{8,0},{9,1},... | collective-permute-start | bytes 1105928 | tf_op jit(solution)/shard_map/ppermute | solution.py:718
  407.2 6.2 %collective-permute-start.34 = (bf16[112,768]{1,0:T(8,128)(2,1)S(1)}, bf16[112,768]{1,0:T(8,128)(2,1)S(1)}, u32[]{:S(2)}, u32[]{:S(2)}) collective-permute-start(bf16[112,768]{1,0:T(8,128)(2,1)S(1)} %get-tuple-element.427.refs_6_), channel_id=1, source_target_pairs={{0,2},{1,3},{2,0},{3,1},{4,6},{5,7},{6,4},{7,5},{8,10},{9,11},{10,... | collective-permute-start | bytes 516104 | tf_op jit(solution)/shard_map/ppermute | solution.py:718
  408.2 5.1 %collective-permute-start.33 = (bf16[96,768]{1,0:T(8,128)(2,1)S(1)}, bf16[96,768]{1,0:T(8,128)(2,1)S(1)}, u32[]{:S(2)}, u32[]{:S(2)}) collective-permute-start(bf16[96,768]{1,0:T(8,128)(2,1)S(1)} %get-tuple-element.425.refs_4_), channel_id=1, source_target_pairs={{0,1},{1,0},{2,3},{3,2},{4,5},{5,4},{6,7},{7,6},{8,9},{9,8},{10,11... | collective-permute-start | bytes 442376 | tf_op jit(solution)/shard_map/ppermute | solution.py:718
  421.3 17.7 %collective-permute-start.37 = (bf16[384,768]{1,0:T(8,128)(2,1)S(1)}, bf16[384,768]{1,0:T(8,128)(2,1)S(1)}, u32[]{:S(2)}, u32[]{:S(2)}) collective-permute-start(bf16[384,768]{1,0:T(8,128)(2,1)S(1)} %get-tuple-element.440.refs_2_), channel_id=1, source_target_pairs={{0,1},{1,0},{2,3},{3,2},{4,5},{5,4},{6,7},{7,6},{8,9},{9,8},{10,11... | collective-permute-start | bytes 1769480 | tf_op jit(solution)/shard_map/ppermute | solution.py:718
  422.9 16.1 %collective-permute-start.38 = (bf16[384,768]{1,0:T(8,128)(2,1)S(1)}, bf16[384,768]{1,0:T(8,128)(2,1)S(1)}, u32[]{:S(2)}, u32[]{:S(2)}) collective-permute-start(bf16[384,768]{1,0:T(8,128)(2,1)S(1)} %get-tuple-element.438.refs_0_), channel_id=1, source_target_pairs={{0,2},{1,3},{2,0},{3,1},{4,6},{5,7},{6,4},{7,5},{8,10},{9,11},{10,... | collective-permute-start | bytes 1769480 | tf_op jit(solution)/shard_map/ppermute | solution.py:718
  424.0 15.0 %collective-permute-start.39 = (bf16[256,768]{1,0:T(8,128)(2,1)S(1)}, bf16[256,768]{1,0:T(8,128)(2,1)S(1)}, u32[]{:S(2)}, u32[]{:S(2)}) collective-permute-start(bf16[256,768]{1,0:T(8,128)(2,1)S(1)} %get-tuple-element.444.refs_6_), channel_id=1, source_target_pairs={{0,4},{1,5},{2,6},{3,7},{4,0},{5,1},{6,2},{7,3},{8,12},{9,13},{10,... | collective-permute-start | bytes 1179656 | tf_op jit(solution)/shard_map/ppermute | solution.py:718
  424.0 15.0 %collective-permute-start.40 = (bf16[240,768]{1,0:T(8,128)(2,1)S(1)}, bf16[240,768]{1,0:T(8,128)(2,1)S(1)}, u32[]{:S(2)}, u32[]{:S(2)}) collective-permute-start(bf16[240,768]{1,0:T(8,128)(2,1)S(1)} %get-tuple-element.442.refs_4_), channel_id=1, source_target_pairs={{0,8},{1,9},{2,10},{3,11},{4,12},{5,13},{6,14},{7,15},{8,0},{9,1},... | collective-permute-start | bytes 1105928 | tf_op jit(solution)/shard_map/ppermute | solution.py:718
  439.8 37.5 %copy-start.4 = (bf16[768,768]{1,0:T(8,128)(2,1)}, bf16[768,768]{1,0:T(8,128)(2,1)S(1)}, u32[]{:S(2)}) copy-start(bf16[768,768]{1,0:T(8,128)(2,1)S(1)} %get-tuple-element.464.yp) | copy-start | bytes 3538948
  439.8 35.0 %collective-permute-start.41 = (bf16[768,768]{1,0:T(8,128)(2,1)S(1)}, bf16[768,768]{1,0:T(8,128)(2,1)S(1)}, u32[]{:S(2)}, u32[]{:S(2)}) collective-permute-start(bf16[768,768]{1,0:T(8,128)(2,1)S(1)} %get-tuple-element.462.xp), channel_id=1, source_target_pairs={{0,1},{1,0},{2,3},{3,2},{4,5},{5,4},{6,7},{7,6},{8,9},{9,8},{10,11... | collective-permute-start | bytes 3538952 | tf_op jit(solution)/shard_map/ppermute | solution.py:718
  441.3 33.5 %collective-permute-start.42 = (bf16[768,768]{1,0:T(8,128)(2,1)S(1)}, bf16[768,768]{1,0:T(8,128)(2,1)S(1)}, u32[]{:S(2)}, u32[]{:S(2)}) collective-permute-start(bf16[768,768]{1,0:T(8,128)(2,1)S(1)} %get-tuple-element.464.yp), channel_id=1, source_target_pairs={{0,2},{1,3},{2,0},{3,1},{4,6},{5,7},{6,4},{7,5},{8,10},{9,11},{10,... | collective-permute-start | bytes 3538952 | tf_op jit(solution)/shard_map/ppermute | solution.py:718
  443.0 31.8 %collective-permute-start.44 = (bf16[496,768]{1,0:T(8,128)(2,1)S(1)}, bf16[496,768]{1,0:T(8,128)(2,1)S(1)}, u32[]{:S(2)}, u32[]{:S(2)}) collective-permute-start(bf16[496,768]{1,0:T(8,128)(2,1)S(1)} %get-tuple-element.468.refs_2_.bp), channel_id=1, source_target_pairs={{0,8},{1,9},{2,10},{3,11},{4,12},{5,13},{6,14},{7,15},{8,0},{9,1},... | collective-permute-start | bytes 2285576 | tf_op jit(solution)/shard_map/ppermute | solution.py:718
  443.9 28.4 %collective-permute-start.43 = (bf16[480,768]{1,0:T(8,128)(2,1)S(1)}, bf16[480,768]{1,0:T(8,128)(2,1)S(1)}, u32[]{:S(2)}, u32[]{:S(2)}) collective-permute-start(bf16[480,768]{1,0:T(8,128)(2,1)S(1)} %get-tuple-element.466.refs_0_.ap), channel_id=1, source_target_pairs={{0,4},{1,5},{2,6},{3,7},{4,0},{5,1},{6,2},{7,3},{8,12},{9,13},{10,... | collective-permute-start | bytes 2211848 | tf_op jit(solution)/shard_map/ppermute | solution.py:718
  475.4 10.6 %collective-permute-start.45 = (bf16[192,768]{1,0:T(8,128)(2,1)S(1)}, bf16[192,768]{1,0:T(8,128)(2,1)S(1)}, u32[]{:S(2)}, u32[]{:S(2)}) collective-permute-start(bf16[192,768]{1,0:T(8,128)(2,1)S(1)} %get-tuple-element.476.refs_2_), channel_id=1, source_target_pairs={{0,1},{1,0},{2,3},{3,2},{4,5},{5,4},{6,7},{7,6},{8,9},{9,8},{10,11... | collective-permute-start | bytes 884744 | tf_op jit(solution)/shard_map/ppermute | solution.py:718
  475.9 10.2 %collective-permute-start.46 = (bf16[192,768]{1,0:T(8,128)(2,1)S(1)}, bf16[192,768]{1,0:T(8,128)(2,1)S(1)}, u32[]{:S(2)}, u32[]{:S(2)}) collective-permute-start(bf16[192,768]{1,0:T(8,128)(2,1)S(1)} %get-tuple-element.474.refs_0_), channel_id=1, source_target_pairs={{0,2},{1,3},{2,0},{3,1},{4,6},{5,7},{6,4},{7,5},{8,10},{9,11},{10,... | collective-permute-start | bytes 884744 | tf_op jit(solution)/shard_map/ppermute | solution.py:718
  486.7 14.8 %collective-permute-start.47 = (bf16[384,768]{1,0:T(8,128)(2,1)S(1)}, bf16[384,768]{1,0:T(8,128)(2,1)S(1)}, u32[]{:S(2)}, u32[]{:S(2)}) collective-permute-start(bf16[384,768]{1,0:T(8,128)(2,1)S(1)} %get-tuple-element.480.xp), channel_id=1, source_target_pairs={{0,1},{1,0},{2,3},{3,2},{4,5},{5,4},{6,7},{7,6},{8,9},{9,8},{10,11... | collective-permute-start | bytes 1769480 | tf_op jit(solution)/shard_map/ppermute | solution.py:718
  487.3 14.4 %collective-permute-start.48 = (bf16[384,768]{1,0:T(8,128)(2,1)S(1)}, bf16[384,768]{1,0:T(8,128)(2,1)S(1)}, u32[]{:S(2)}, u32[]{:S(2)}) collective-permute-start(bf16[384,768]{1,0:T(8,128)(2,1)S(1)} %get-tuple-element.482.yp), channel_id=1, source_target_pairs={{0,2},{1,3},{2,0},{3,1},{4,6},{5,7},{6,4},{7,5},{8,10},{9,11},{10,... | collective-permute-start | bytes 1769480 | tf_op jit(solution)/shard_map/ppermute | solution.py:718
  489.8 2.4 collective-permute-start.49
  489.8 15.1 %copy-start.1 = (s32[1024,1]{0,1:T(1,128)S(1)}, s32[1024,1]{0,1:T(1,128)}, u32[]{:S(2)}) copy-start(s32[1024,1]{0,1:T(1,128)} %param.16) | copy-start | bytes 12292
  (33 other events, 76.9 us)

commit v4 on v3

--- a/solution.py
+++ b/solution.py
@@ -15,6 +15,7 @@
 HEAD_DIM = 64
 SWAP = [(0, 1), (1, 0)]
 VLIM = 56 * 1024 * 1024
+SMALL = 16 * 1024 * 1024
 
 
 def mm(a, b):
@@ -67,6 +68,10 @@
     return (lane >= 64) if hh else (lane < 64)
 
 
+def residual_of(xr, pa, pb):
+    return xr[...].astype(F32) + (pa[...].astype(F32) + pb[...].astype(F32))
+
+
 def attn_fwd_kernel(blocks, split, h_ref, *refs):
     if split:
         own, peer, g, wqkv, wo, segc, segr = refs[:7]
@@ -74,14 +79,17 @@
     else:
         xr, pa, pb, g, wqkv, wo, segc, segr = refs[:8]
         outs = refs[8:]
-    x_out, n_out, qkv_out, o_out, lse_out, p_out, ks, vs = outs
+    x_out = None
+    if not split:
+        x_out, *outs = outs
+    n_out, qkv_out, o_out, lse_out, p_out, ks, vs = outs
     i = pl.program_id(0)
     if split:
         mine = (i // (blocks // 2)) == h_ref[0]
         x = jnp.where(mine, own[...].astype(F32), peer[...].astype(F32))
     else:
-        x = xr[...] + (pa[...].astype(F32) + pb[...].astype(F32))
-    x_out[...] = x
+        x = residual_of(xr, pa, pb)
+        x_out[...] = x.astype(BF)
     xh, _ = norm_stats(x)
     n = (xh * g[...]).astype(BF)
     n_out[...] = n
@@ -130,9 +138,15 @@
         dro, drp, dno, dnp_ = refs[:4]
     else:
         drr, dna, dnb = refs[:3]
-    rest = refs[4 if split else 3 :]
-    xn, gn, qr, kf, vf, orf, lser, wqkv, wo, segc, segr = rest[:11]
-    dr_out, da_out, dqk_out, dv_out, dn_out, dg_out, dks, dvs = rest[11:]
+    if split:
+        xr, pa, pb = refs[4:7]
+        xn = residual_of(xr, pa, pb)
+        rest = refs[7:]
+    else:
+        xn = refs[3][...].astype(F32)
+        rest = refs[4:]
+    gn, qr, kf, vf, orf, lser, wqkv, wo, segc, segr = rest[:10]
+    da_out, dqk_out, dv_out, dn_out, dg_out, dks, dvs = rest[10:]
     i = pl.program_id(0)
     blk = blocks - 1 - i
     if split:
@@ -140,12 +154,10 @@
         dr = jnp.where(mine, dro[...].astype(F32), drp[...].astype(F32))
         dn = jnp.where(mine, dno[...].astype(F32), dnp_[...].astype(F32))
     else:
-        dr = drr[...]
+        dr = drr[...].astype(F32)
         dn = dna[...].astype(F32) + dnb[...].astype(F32)
-    dx, dg = norm_back(xn[...], gn[...], dn)
-    dr = dr + dx
-    dr_out[...] = dr
-    da = dr.astype(BF)
+    dx, dg = norm_back(xn, gn[...], dn)
+    da = (dr + dx).astype(BF)
     da_out[...] = da
 
     @pl.when(i == 0)
@@ -196,9 +208,13 @@
     ).astype(BF)
 
 
-def dense_fwd_kernel(xr, pa, pb, g, up, down, x_out, n_out, act_out, gp_out, p_out):
-    x = xr[...] + (pa[...].astype(F32) + pb[...].astype(F32))
-    x_out[...] = x
+def dense_fwd_kernel(
+    blocks, h_ref, own, peer, pa, pb, g, up, down, x_out, n_out, act_out, gp_out, p_out
+):
+    mine = (pl.program_id(0) // (blocks // 2)) == h_ref[0]
+    x = jnp.where(mine, own[...].astype(F32), peer[...].astype(F32))
+    x = x + (pa[...].astype(F32) + pb[...].astype(F32))
+    x_out[...] = x.astype(BF)
     xh, _ = norm_stats(x)
     n = (xh * g[...]).astype(BF)
     n_out[...] = n
@@ -209,11 +225,9 @@
     p_out[...] = mm(act, down[...]).astype(BF)
 
 
-def dense_bwd_kernel(drr, dna, dnb, xn, gn, gp, up, down, dr_out, df_out, du_out, dn_out, dg_out):
-    dx, dg = norm_back(xn[...], gn[...], dna[...].astype(F32) + dnb[...].astype(F32))
-    dr = drr[...] + dx
-    dr_out[...] = dr
-    df = dr.astype(BF)
+def dense_bwd_kernel(drr, dna, dnb, xn, gn, gp, up, down, df_out, du_out, dn_out, dg_out):
+    dx, dg = norm_back(xn[...].astype(F32), gn[...], dna[...].astype(F32) + dnb[...].astype(F32))
+    df = (drr[...].astype(F32) + dx).astype(BF)
     df_out[...] = df
 
     @pl.when(pl.program_id(0) == 0)
@@ -231,7 +245,7 @@
     mine = i >= 2
     x = jnp.where(mine, xo[...].astype(F32), xp[...].astype(F32))
     dx, dg = norm_back(x, gn[...], dna[...].astype(F32) + dnb[...].astype(F32))
-    dr_out[...] = drr[...] + dx
+    dr_out[...] = drr[...].astype(F32) + dx
 
     @pl.when(i == 0)
     def _():
@@ -250,16 +264,13 @@
 
 def route_kernel(h_ref, xr, pa, pb, g, slot_ref, x_out, send_out, ms):
     i = pl.program_id(0)
-    x = xr[...] + (pa[...].astype(F32) + pb[...].astype(F32))
+    x = residual_of(xr, pa, pb)
     x_out[...] = x
-
-    @pl.when(i >= 2)
-    def _():
-        xh, _ = norm_stats(x)
-        rows = pl.ds(pl.multiple_of((i - 2) * BLK, BLK), BLK)
-        ms[rows, :] = (xh * g[...]).astype(BF)
-
-    @pl.when(i == 3)
+    xh, _ = norm_stats(x)
+    rows = pl.ds(pl.multiple_of(i * BLK, BLK), BLK)
+    ms[rows, :] = (xh * g[...]).astype(BF)
+
+    @pl.when(i == pl.num_programs(0) - 1)
     def _():
         count = send_out.shape[0]
         place = lax.broadcasted_iota(jnp.int32, (count, ms.shape[0]), 0)
@@ -292,12 +303,14 @@
     mf = m.astype(F32)
     cf = cen[...].astype(F32)
     gate = jax.nn.sigmoid(jnp.sum(mf * cf, axis=-1, keepdims=True))
-    act, gd = gelu_pair(mm(m, up[0]))
+    dy = (gate * gb).astype(BF)
+    u = mm(m, up[0])
+    dact = mm_nt(dy, down[0])
+    act, gd = gelu_pair(u)
     act = act.astype(BF)
     y = mm(act, down[0])
     dscore = jnp.sum(gb * y, axis=-1, keepdims=True) * gate * (1.0 - gate)
-    dy = (gate * gb).astype(BF)
-    due = (mm_nt(dy, down[0]) * gd).astype(BF)
+    due = (dact * gd).astype(BF)
     dm = (mm_nt(due, up[0]) + dscore * cf).astype(BF)
     gy = (gate * y).astype(BF)
     m_all[...] = m
@@ -375,8 +388,8 @@
         pl.BlockSpec((BLK, 1), lambda i, *a: (i, 0)),
         fixed((1, length)),
     ]
-    outs = [
-        (rows_spec(d), shape((length, d), F32)),
+    outs = [] if split else [(rows_spec(d), shape((length, d), BF))]
+    outs += [
         (rows_spec(d), shape((length, d), BF)),
         (pl.BlockSpec((3, BLK, c), lambda i, *a: (0, i, 0)), shape((3, length, c), BF)),
         (rows_spec(c), shape((length, c), BF)),
@@ -399,21 +412,20 @@
     )
 
 
-def attention_backward(h, inputs, split, xn, gn, saved, wqkv, wo, segc, segr):
+def attention_backward(h, inputs, split, gn, saved, wqkv, wo, segc, segr):
     qkv, o, lse = saved
     length, d = segc.shape[0], wqkv.shape[1]
     c = wqkv.shape[2]
     blocks = length // BLK
     back = lambda i: blocks - 1 - i
     if split:
-        ins = [rows_spec(d, lambda i: back(i) % (blocks // 2))] * 4
+        ins = [rows_spec(d, lambda i: back(i) % (blocks // 2))] * 4 + [rows_spec(d, back)] * 3
     else:
-        ins = [rows_spec(d, back)] * 3
+        ins = [rows_spec(d, back)] * 4
     part = lambda n: pl.BlockSpec(
         (1, length, c), lambda i, *a: (n, 0, 0), pipeline_mode=pl.Buffered(1)
     )
     ins += [
-        rows_spec(d, back),
         fixed((1, d)),
         pl.BlockSpec((1, BLK, c), lambda i, *a: (0, back(i), 0)),
         part(1),
@@ -426,7 +438,6 @@
         fixed((1, length)),
     ]
     outs = [
-        (rows_spec(d, back), shape((length, d), F32)),
         (rows_spec(d, back), shape((length, d), BF)),
         (rows_spec(2 * c, back), shape((length, 2 * c), BF)),
         (rows_spec(c, back), shape((length, c), BF)),
@@ -444,21 +455,23 @@
         scratch,
         flops * 2,
         length * d * 20,
-        (*inputs, xn, gn, qkv, qkv, qkv, o, lse, wqkv, wo, segc, segr),
+        (*inputs, gn, qkv, qkv, qkv, o, lse, wqkv, wo, segc, segr),
         prefetch=h,
     )
 
 
-def dense_forward(x, pa, pb, gain, up, down):
-    length, d = x.shape
+def dense_forward(h, own, peer, pa, pb, gain, up, down):
+    length, d = pa.shape
     f = up.shape[1]
+    blocks = length // BLK
+    half = rows_spec(d, lambda i: lax.rem(i, blocks // 2))
     return call(
-        dense_fwd_kernel,
-        (length // BLK,),
-        [rows_spec(d)] * 3 + [fixed((1, d)), fixed((d, f)), fixed((f, d))],
+        functools.partial(dense_fwd_kernel, blocks),
+        (blocks,),
+        [half] * 2 + [rows_spec(d)] * 2 + [fixed((1, d)), fixed((d, f)), fixed((f, d))],
         [rows_spec(d), rows_spec(d), rows_spec(f), rows_spec(f), rows_spec(d)],
         [
-            shape((length, d), F32),
+            shape((length, d), BF),
             shape((length, d), BF),
             shape((length, f), BF),
             shape((length, f), BF),
@@ -467,7 +480,8 @@
         [],
         4 * length * d * f,
         length * d * 20 + 4 * d * f,
-        (x, pa, pb, gain, up, down),
+        (own, peer, pa, pb, gain, up, down),
+        prefetch=h,
     )
 
 
@@ -479,9 +493,8 @@
         (length // BLK,),
         [rows_spec(d)] * 4
         + [fixed((1, d)), rows_spec(f), fixed((d, f)), fixed((f, d))],
-        [rows_spec(d), rows_spec(d), rows_spec(f), rows_spec(d), fixed((8, d))],
+        [rows_spec(d), rows_spec(f), rows_spec(d), fixed((8, d))],
         [
-            shape((length, d), F32),
             shape((length, d), BF),
             shape((length, f), BF),
             shape((length, d), BF),
@@ -517,25 +530,26 @@
         length * d * 14,
         (dr, dna, dnb, xo, xp, gn),
         prefetch=h,
+        limit=SMALL,
     )
 
 
 def route_step(h, x, pa, pb, gain, slot_row, slots):
     length, d = x.shape
-    blocks = length // BLK
-    place = own_last(blocks)
-    spec = pl.BlockSpec((BLK, d), lambda i, h: (place(i, h), 0))
+    per = length // 2 // BLK
+    spec = pl.BlockSpec((BLK, d), lambda i, h: (h[0] * per + i, 0))
     return call(
         route_kernel,
-        (blocks,),
+        (per,),
         [spec] * 3 + [fixed((1, d)), fixed((1, length // 2))],
-        [spec, fixed((slots, d))],
-        [shape((length, d), F32), shape((slots, d), BF)],
+        [rows_spec(d), fixed((slots, d))],
+        [shape((length // 2, d), F32), shape((slots, d), BF)],
         [pltpu.VMEM((length // 2, d), BF)],
         length * slots * d,
         length * d * 14,
         (x, pa, pb, gain, slot_row),
         prefetch=h,
+        limit=SMALL,
     )
 
 
@@ -551,6 +565,7 @@
         2 * count * slots * d,
         4 * slots * d,
         (rows, slot_row),
+        limit=SMALL,
     )[0]
 
 
@@ -567,6 +582,7 @@
         2 * count * slots * d,
         4 * slots * d,
         (table, slot_col),
+        limit=SMALL,
     )[0]
 
 
@@ -580,7 +596,7 @@
         [
             fixed((slots, d)),
             pl.BlockSpec((BLK, 1), lambda i, *a: (i, 0)),
-            pl.BlockSpec((BLK, d), lambda i, h: (h[0] * per + i, 0)),
+            rows_spec(d),
         ],
         [rows_spec(d)],
         [shape((count, d), BF)],
@@ -589,6 +605,7 @@
         8 * slots * d,
         (table, slot_col, x),
         prefetch=h,
+        limit=SMALL,
     )[0]
 
 
@@ -657,6 +674,10 @@
         prefetch=bits,
         limit=2 * moved + 8 * 1024 * 1024,
     )
+
+
+def sum_kernel(h_ref, a, b, out):
+    out[...] = total_of(a[...], b[...])
 
 
 PLACE = {1: 0, 2: 1, 4: 2, 8: 3}
@@ -867,15 +888,21 @@
         box = v.reshape(experts, capacity, d)
         return lax.all_to_all(box, "dp", 0, 0, tiled=True).reshape(slots, d)
 
+    def add(a, b):
+        return one_step(sum_kernel, h, (a, b), [shape(a.shape, BF)])[0]
+
     tokens_peer = swap(tokens)
-    x0, n1, qkv1, o1, lse1, p1 = attention_forward(
+    n1, qkv1, o1, lse1, p1 = attention_forward(
         h, (tokens, tokens_peer), True, gain[0], qkv_one, out_one, segc, segr
     )
     p1r = swap(p1)
     cot_peer = swap(cotangent)
-    grad_own = travel(spread(cotangent, slot_row, slots))
+    p1r, cot_table = lax.optimization_barrier((p1r, spread(cotangent, slot_row, slots)))
+    grad_own = travel(cot_table)
     grad_peer = swap(grad_own)
-    x1, n2, act, gp, p2 = dense_forward(x0, p1, p1r, gain[1], up_one, down_one)
+    x1, n2, act, gp, p2 = dense_forward(
+        h, tokens, tokens_peer, p1, p1r, gain[1], up_one, down_one
+    )
     p2r = swap(p2)
     first, n3, qkv2, o2, lse2, p3 = attention_forward(
         h, (x1, p2, p2r), False, gain[2], qkv_two, out_two, segc, segr
@@ -887,22 +914,23 @@
     yo, yp, dmo, dmp, m_all, dy_all, ae_all, due_all, dc = expert_step(
         m_own, m_peer, grad_own, grad_peer, centroids, expert_up, expert_down
     )
-    dm_sum = (dmo.astype(F32) + swap(dmp).astype(F32)).astype(BF)
+    dm_sum = add(dmo, swap(dmp))
+    y_sum = add(yo, swap(yp))
     up_grad = mm_tn(m_all, due_all)[None]
     down_grad = mm_tn(ae_all, dy_all)[None]
-    dm_back, up_grad, down_grad = lax.optimization_barrier((travel(dm_sum), up_grad, down_grad))
+    dm_back, up_grad, down_grad, y_sum = lax.optimization_barrier(
+        (travel(dm_sum), up_grad, down_grad, y_sum)
+    )
+    y_back = travel(y_sum)
     dm_own = collect(dm_back, slot_col)
     dm_peer = swap(dm_own)
-    y_sum = (yo.astype(F32) + swap(yp).astype(F32)).astype(BF)
-    y_back = travel(y_sum)
     dc = dc[:1]
     cen_grad = dc + swap(dc)
 
-    dr2, da2, dqk2, dv2, dn2, dg3 = attention_backward(
+    da2, dqk2, dv2, dn2, dg3 = attention_backward(
         h,
-        (cotangent, cot_peer, dm_own, dm_peer),
+        (cotangent, cot_peer, dm_own, dm_peer, first, p3, p3r),
         True,
-        x2,
         gain[3],
         (qkv2, o2, lse2),
         qkv_two,
@@ -932,15 +960,15 @@
 
     def last_attention(dr, dna, dnb):
         return attention_backward(
-            h, (dr, dna, dnb), False, x1, gain[1], (qkv1, o1, lse1), qkv_one, out_one, segc, segr
+            h, (dr, dna, dnb, x1), False, gain[1], (qkv1, o1, lse1), qkv_one, out_one, segc, segr
         )
 
     if steps is None:
-        dr1, df, du, dnd, dg2 = dense_backward(
-            dr2, dn2, dn2r, first, gain[2], gp, up_one, down_one
+        df, du, dnd, dg2 = dense_backward(
+            da2, dn2, dn2r, first, gain[2], gp, up_one, down_one
         )
-        dr0, da1, dqk1, dv1, dn1, dg1 = last_attention(dr1, dnd, swap(dnd))
-        input_grad, dg0 = last_step(dr0, dn1, swap(dn1))
+        da1, dqk1, dv1, dn1, dg1 = last_attention(df, dnd, swap(dnd))
+        input_grad, dg0 = last_step(da1, dn1, swap(dn1))
         second = gather_y(y_back)
         up_first, down_first, qk_two, v_two, wo_two, qk_one, v_one, wo_one, gain_grads = lax.psum(
             (
@@ -981,11 +1009,11 @@
         qk_send = query_key(n3, dqk2, 1 - bits[2])
         qk_keep = query_key(n3, dqk2, bits[2])
         vo_send, vo_keep = value_out(n3, dv2, o2, da2, bits[3])
-        (qk_send, qk_keep, vo_send, vo_keep), dr2, dn2, dn2r, y_back = lax.optimization_barrier(
-            ((qk_send, qk_keep, vo_send, vo_keep), dr2, dn2, dn2r, y_back)
+        (qk_send, qk_keep, vo_send, vo_keep), da2, dn2, dn2r, y_back = lax.optimization_barrier(
+            ((qk_send, qk_keep, vo_send, vo_keep), da2, dn2, dn2r, y_back)
         )
-        dr1, df, du, dnd, dg2 = dense_backward(
-            dr2, dn2, dn2r, first, gain[2], gp, up_one, down_one
+        df, du, dnd, dg2 = dense_backward(
+            da2, dn2, dn2r, first, gain[2], gp, up_one, down_one
         )
         dndr = swap(dnd)
 
@@ -1005,10 +1033,11 @@
             Part(orders[2], qk_send, qk_keep),
             Part(orders[3], vo_send, vo_keep),
         ]
-        last, up_keep, down_keep = advance(bits, big, heavy, (dr1, dnd, dndr, n2, du, act, df))
-        dr0, da1, dqk1, dv1, dn1, dg1 = last
+        last, up_keep, down_keep = advance(bits, big, heavy, (df, dnd, dndr, n2, du, act, df))
+        da1, dqk1, dv1, dn1, dg1 = last
         dn1r = swap(dn1)
-        big[0].kept, big[1].kept = (up_keep, 0, up_keep.shape[0]), (down_keep, 0, down_keep.shape[0])
+        big[0].kept = (up_keep, 0, up_keep.shape[0])
+        big[1].kept = (down_keep, 0, down_keep.shape[0])
         fold(bits, big)
 
         def narrow_grads(n, dqk, dv, o, da):
@@ -1024,7 +1053,7 @@
         small = [Part(orders[0], qk_send, qk_keep), Part(orders[1], vo_send, vo_keep)]
         parts = big + small
         fold(bits, parts)
-        input_grad, dg0 = advance(bits, parts, last_step, (dr0, dn1, dn1r))
+        input_grad, dg0 = advance(bits, parts, last_step, (da1, dn1, dn1r))
         fold(bits, parts)
         second, gains_own = advance(bits, parts, gather_all, (y_back, dg0, dg1, dg2, dg3))
         tail = Part((1, 2, 4, 8), gains_own)
@@ -1064,7 +1093,7 @@
             [x for p in small for x in (p.sent[0], p.got[0])],
             [shape((3, d, c), F32), shape((c, d), F32)],
         )
-    first_own = lax.dynamic_slice_in_dim(first, side * count, count, 0).astype(BF)
+    first_own = lax.dynamic_slice_in_dim(first, side * count, count, 0)
     return (
         first_own,
         second,

time: 514 us -> 507 us (0.986)
  Pallas kernels: 201 us -> 193 us
  other arithmetic: 9.26 us -> 2.17 us
    pallas_call x24 -> x26, Pallas kernels: 201 us -> 193 us  [call(): pl.pallas_call(kernel, grid_spec=spec, out_shape=outs, compiler_params=pa...]
    convert_element_type x2 -> x0, other arithmetic: 5.93 us -> none  [the longest x1 2.98 us: body(): y_sum = (yo.astype(F32) + swap(yp).astype(F32)).astype(BF)]
    ppermute x36, waiting for transfers between devices: 87.7 us -> 93.3 us  [advance(): lax.ppermute(v, 'dp', [(i, i ^ s) for i in range(16)])]
    unnamed x87 -> x101, local copies, waits for them, and re-layouts: 17.9 us -> 22.7 us
  transfers between devices with their start and end apart: 54 -> 54, of which waited for: 26 -> 26; matrix products, arithmetic and copies ran while one was open for 10% -> 9% of each run, Pallas kernels for 22% -> 20%
where the time goes in v4:
time: 507 us; the launch traced here: 498 us
  Pallas kernels  193 us (38%)
  waiting for transfers between devices  154 us (30%)
  starting transfers between devices  77.7 us (15%)
  matrix products  42 us (8%)
  local copies, waits for them, and re-layouts  27.8 us (5%)
    pallas_call x26, Pallas kernels, call(): pl.pallas_call(kernel, grid_spec=spec, out_shape=outs, compiler_params=pa...  193 us
    ppermute x36, waiting for transfers between devices, advance(): lax.ppermute(v, 'dp', [(i, i ^ s) for i in range(16)])  93.3 us
    all_to_all x4, waiting for transfers between devices, travel(): return lax.all_to_all(box, 'dp', 0, 0, tiled=True).reshape(slots, d)  49.6 us
    ppermute x36, starting transfers between devices, advance(): lax.ppermute(v, 'dp', [(i, i ^ s) for i in range(16)])  43.5 us
    dot_general x14, matrix products, mm_tn(): lax.dot_general(a, b, (((0,), (0,)), ((), ())), preferred_element_type=F32)  41.8 us
    all_to_all x4, starting transfers between devices, travel(): return lax.all_to_all(box, 'dp', 0, 0, tiled=True).reshape(slots, d)  31.8 us
    unnamed x101, local copies, waits for them, and re-layouts  22.7 us
    ppermute x14, waiting for transfers between devices, swap(): return lax.ppermute(v, 'head', SWAP)  10.8 us
  transfers between devices with their start and end apart: 54, of which 26 were waited for; matrix products, arithmetic and copies ran while one was open for 9% of the time, Pallas kernels for 20%

profile of v4, /device:TPU:0, one launch (start us, length us, event | category | flops | bytes accessed | tf_op | source)
XLA Modules:
  0.0 497.6 jit_solution(16492271016136737414)
XLA Ops:
  1.2 1.7 copy.30.refs_5_.refs_6_.refs_15_.refs_12_
  5.2 18.7 %shard_map.237 = (bf16[1024,768]{1,0:T(8,128)(2,1)}, bf16[3,1024,384]{2,1,0:T(8,128)(2,1)}, bf16[1024,384]{1,0:T(8,128)(2,1)}, f32[1024,128]{1,0:T(8,128)}, bf16[1024,768]{1,0:T(8,128)(2,1)}) custom-call(s32[1]{0:T(128)} %bitcast.h_ref, bf16[512,768]{1,0:T(8,128)(2,1)} %xo.1, bf16[512,768]{1,0:T(8,128)(2,1)} %copy-done.18, ...), custom_call_target="tpu_custom_call" | custom-call | flops 8053063680 | bytes 15728640 | tf_op jit(solution)/shard_map/pallas_call | solution.py:371
  25.1 2.6 shard_map.238
  27.8 15.7 %shard_map.239 = (bf16[1024,768]{1,0:T(8,128)(2,1)}, bf16[1024,768]{1,0:T(8,128)(2,1)}, bf16[1024,1536]{1,0:T(8,128)(2,1)}, bf16[1024,1536]{1,0:T(8,128)(2,1)}, bf16[1024,768]{1,0:T(8,128)(2,1)}) custom-call(s32[1]{0:T(128)} %bitcast.h_ref, bf16[512,768]{1,0:T(8,128)(2,1)} %xo.1, bf16[512,768]{1,0:T(8,128)(2,1)} %copy-done.18, ...), custom_call_target="tpu_custom_call" | custom-call | flops 4831838208 | bytes 20447232 | tf_op jit(solution)/shard_map/pallas_call | solution.py:371
  43.7 8.2 %all-to-all-start.1 = ((bf16[16,64,768]{2,1,0:T(8,128)(2,1)}), bf16[16,64,768]{2,1,0:T(8,128)(2,1)}, u32[]{:S(2)}, u32[]{:S(2)}) async-start(bf16[16,64,768]{2,1,0:T(8,128)(2,1)} %bitcast.10), calls=%async_computation.1 | async-start | bytes 3145728 | tf_op jit(solution)/shard_map/all_to_all | solution.py:889
  53.0 19.2 %shard_map.240 = (bf16[1024,768]{1,0:T(8,128)(2,1)}, bf16[1024,768]{1,0:T(8,128)(2,1)}, bf16[3,1024,384]{2,1,0:T(8,128)(2,1)}, bf16[1024,384]{1,0:T(8,128)(2,1)}...) custom-call(s32[1]{0:T(128)} %bitcast.h_ref, bf16[1024,768]{1,0:T(8,128)(2,1)} %get-tuple-element.253.refs_0_.refs_3_, ...), custom_call_target="tpu_custom_call" | custom-call | flops 8053063680 | bytes 15728640 | tf_op jit(solution)/shard_map/pallas_call | solution.py:371
  72.4 3.6 collective-permute-done.4.pb.refs_6_
  78.8 2.8 shard_map.241
  82.8 3.4 all-to-all-done.1
  86.2 8.3 %all-to-all-start = ((bf16[16,64,768]{2,1,0:T(8,128)(2,1)}), bf16[16,64,768]{2,1,0:T(8,128)(2,1)S(1)}, u32[]{:S(2)}, u32[]{:S(2)}) async-start(bf16[16,64,768]{2,1,0:T(8,128)(2,1)} %bitcast.8), calls=%async_computation | async-start | bytes 3145728 | tf_op jit(solution)/shard_map/all_to_all | solution.py:889
  94.5 33.4 %all-to-all-done = bf16[16,64,768]{2,1,0:T(8,128)(2,1)S(1)} async-done(((bf16[16,64,768]{2,1,0:T(8,128)(2,1)}), bf16[16,64,768]{2,1,0:T(8,128)(2,1)S(1)}, u32[]{:S(2)}, u32[]{:S(2)}) %all-to-all-start) | async-done | bytes 1572896 | tf_op jit(solution)/shard_map/all_to_all | solution.py:889
  127.9 3.4 collective-permute-done.5.mp
  132.5 34.1 %shard_map.242 = (bf16[1024,768]{1,0:T(8,128)(2,1)}, bf16[1024,768]{1,0:T(8,128)(2,1)}, bf16[1024,768]{1,0:T(8,128)(2,1)}, bf16[1024,768]{1,0:T(8,128)(2,1)}, bf...) custom-call(bf16[1024,768]{1,0:T(8,128)(2,1)} %bitcast.46, ...), custom_call_target="tpu_custom_call" | custom-call | flops 19327352832 | bytes 31457280 | tf_op jit(solution)/shard_map/pallas_call | solution.py:371
  166.8 3.5 collective-permute-done.7.b
  173.2 7.3 %all-to-all-start.2 = ((bf16[16,64,768]{2,1,0:T(8,128)(2,1)}), bf16[16,64,768]{2,1,0:T(8,128)(2,1)S(1)}, u32[]{:S(2)}, u32[]{:S(2)}) async-start(bf16[16,64,768]{2,1,0:T(8,128)(2,1)} %bitcast.12), calls=%async_computation.2 | async-start | bytes 3145728 | tf_op jit(solution)/shard_map/all_to_all | solution.py:889
  181.1 9.7 %convolution_bitcast_fusion = f32[1,1536,768]{2,1,0:T(8,128)} fusion(bf16[2048,1536]{1,0:T(8,128)(2,1)} %get-tuple-element.265, bf16[2048,768]{1,0:T(8,128)(2,1)} %get-tuple-element.266), kind=kOutput, calls=%fused_computation | convolution fusion | flops 4831838208 | bytes 14155776 | tf_op jit(solution)/shard_map/dot_general | solution.py:30
  190.8 9.6 %convolution_bitcast_fusion.1 = f32[1,768,1536]{2,1,0:T(8,128)} fusion(bf16[2048,768]{1,0:T(8,128)(2,1)S(1)} %copy-done.45, bf16[2048,1536]{1,0:T(8,128)(2,1)} %get-tuple-element.264), kind=kOutput, calls=%fused_computation.1 | convolution fusion | flops 4831838208 | bytes 14155776 | tf_op jit(solution)/shard_map/dot_general | solution.py:30
  201.9 12.8 %all-to-all-done.2 = bf16[16,64,768]{2,1,0:T(8,128)(2,1)S(1)} async-done(((bf16[16,64,768]{2,1,0:T(8,128)(2,1)}), bf16[16,64,768]{2,1,0:T(8,128)(2,1)S(1)}, u32[]{:S(2)}, u32[]{:S(2)}) %all-to-all-start.2) | async-done | bytes 1572896 | tf_op jit(solution)/shard_map/all_to_all | solution.py:889
  214.7 2.1 shard_map.245.refs_2_
  216.8 8.0 %all-to-all-start.3 = ((bf16[16,64,768]{2,1,0:T(8,128)(2,1)}), bf16[16,64,768]{2,1,0:T(8,128)(2,1)S(1)}, u32[]{:S(2)}, u32[]{:S(2)}) async-start(bf16[16,64,768]{2,1,0:T(8,128)(2,1)} %bitcast.17), calls=%async_computation.3 | async-start | bytes 3145728 | tf_op jit(solution)/shard_map/all_to_all | solution.py:889
  224.9 27.5 %shard_map.246 = (bf16[1024,768]{1,0:T(8,128)(2,1)}, bf16[1024,768]{1,0:T(8,128)(2,1)}, bf16[1024,384]{1,0:T(8,128)(2,1)}, bf16[1024,768]{1,0:T(8,128)(2,1)}, f32[8,768]{1,0:T(8,128)}) custom-call(s32[1]{0:T(128)} %bitcast.h_ref, bf16[512,768]{1,0:T(8,128)(2,1)} %refs_0_.3, bf16[512,768]{1,0:T(8,128)(2,1)} %collective-permute-done.3.refs_1_, ...), custom_call_target="tpu_custom_call" | custom-call | flops 12884901888 | bytes 15728640 | tf_op jit(solution)/shard_map/pallas_call | solution.py:371
  252.6 2.8 convolution_convert_fusion.5
  255.5 1.6 convolution_convert_fusion.6.refs_4_
  257.1 1.7 convolution_convert_fusion.7
  258.8 1.9 broadcast_select_fusion.2
  260.7 13.0 %shard_map.247 = (bf16[1024,768]{1,0:T(8,128)(2,1)}, bf16[1024,1536]{1,0:T(8,128)(2,1)}, bf16[1024,768]{1,0:T(8,128)(2,1)}, f32[8,768]{1,0:T(8,128)}) custom-call(bf16[1024,768]{1,0:T(8,128)(2,1)} %get-tuple-element.278.drr, bf16[1024,768]{1,0:T(8,128)(2,1)} %get-tuple-element.279.dna, bf16[1024,768]{1,0:T(8,128)(2,1)} %collective-permute-done.10.dnb, ...), custom_call_target="tpu_custom_call" | custom-call | flops 4831838208 | bytes 20447232 | tf_op jit(solution)/shard_map/pallas_call | solution.py:371
  274.0 3.5 fusion.11
  277.6 2.5 fusion.8
  280.0 2.5 fusion.17.refs_2_
  282.6 2.5 fusion.14.refs_0_
  285.0 1.9 collective-permute-start.12
  288.4 2.8 collective-permute-start.14
  292.2 26.0 %shard_map.248 = (bf16[1024,768]{1,0:T(8,128)(2,1)}, bf16[1024,768]{1,0:T(8,128)(2,1)}, bf16[1024,384]{1,0:T(8,128)(2,1)}, bf16[1024,768]{1,0:T(8,128)(2,1)}, f32[8,768]{1,0:T(8,128)}) custom-call(s32[1]{0:T(128)} %bitcast.h_ref, bf16[1024,768]{1,0:T(8,128)(2,1)} %get-tuple-element.299.refs_0_, bf16[1024,768]{1,0:T(8,128)(2,1)} %get-tuple-element.300.refs_1_, ...), custom_call_target="tpu_custom_call" | custom-call | flops 12884901888 | bytes 15728640 | tf_op jit(solution)/shard_map/pallas_call | solution.py:371
  332.0 1.6 shard_map.249
  334.6 1.9 collective-permute-start.18
  336.5 1.7 collective-permute-start.19
  342.4 6.5 %collective-permute-done.18.refs_4_ = bf16[192,768]{1,0:T(8,128)(2,1)S(1)} collective-permute-done((bf16[192,768]{1,0:T(8,128)(2,1)S(1)}, bf16[192,768]{1,0:T(8,128)(2,1)S(1)}, u32[]{:S(2)}, u32[]{:S(2)}) %collective-permute-start.18) | collective-permute-done | bytes 294944 | tf_op jit(solution)/shard_map/ppermute | solution.py:739
  348.9 3.5 collective-permute-done.19.refs_3_
  355.5 2.6 collective-permute-start.24
  358.1 5.0 shard_map.251
  363.1 3.9 collective-permute-done.23.refs_1_
  367.0 2.9 collective-permute-done.24.refs_2_
  376.2 2.3 shard_map.253
  378.9 3.5 collective-permute-done.28.refs_1_
  383.3 2.3 collective-permute-start.32
  387.8 3.4 collective-permute-done.30.refs_5_
  391.2 3.0 collective-permute-done.31.refs_3_
  394.2 1.8 collective-permute-done.32.refs_1_
  396.8 1.6 collective-permute-start.36
  398.4 1.5 collective-permute-start.34
  401.3 3.8 collective-permute-done.33.refs_5_
  405.1 5.6 %collective-permute-done.35.refs_1_ = bf16[240,768]{1,0:T(8,128)(2,1)S(1)} collective-permute-done((bf16[240,768]{1,0:T(8,128)(2,1)S(1)}, bf16[240,768]{1,0:T(8,128)(2,1)S(1)}, u32[]{:S(2)}, u32[]{:S(2)}) %collective-permute-start.35) | collective-permute-done | bytes 368672 | tf_op jit(solution)/shard_map/ppermute | solution.py:739
  410.6 1.6 collective-permute-done.36.refs_3_
  412.9 1.9 collective-permute-start.37
  415.9 1.9 collective-permute-start.40
  417.8 13.5 %collective-permute-done.40.refs_5_ = bf16[240,768]{1,0:T(8,128)(2,1)S(1)} collective-permute-done((bf16[240,768]{1,0:T(8,128)(2,1)S(1)}, bf16[240,768]{1,0:T(8,128)(2,1)S(1)}, u32[]{:S(2)}, u32[]{:S(2)}) %collective-permute-start.40) | collective-permute-done | bytes 368672 | tf_op jit(solution)/shard_map/ppermute | solution.py:739
  432.2 1.7 collective-permute-start.41
  434.9 1.8 collective-permute-start.43
  436.7 26.6 %collective-permute-done.43.refs_1_.ag = bf16[480,768]{1,0:T(8,128)(2,1)S(1)} collective-permute-done((bf16[480,768]{1,0:T(8,128)(2,1)S(1)}, bf16[480,768]{1,0:T(8,128)(2,1)S(1)}, u32[]{:S(2)}, u32[]{:S(2)}) %collective-permute-start.43) | collective-permute-done | bytes 737312 | tf_op jit(solution)/shard_map/ppermute | solution.py:739
  463.3 2.6 collective-permute-done.44.refs_3_.bg
  466.5 1.5 collective-permute-start.45
  469.0 8.7 %shard_map.260 = (f32[768,1536]{1,0:T(8,128)}, f32[1536,768]{1,0:T(8,128)}, f32[3,768,384]{2,1,0:T(8,128)}, f32[384,768]{1,0:T(8,128)}) custom-call(s32[4]{0:T(128)S(1)} %pad_add_fusion.bits, bf16[768,768]{1,0:T(8,128)(2,1)S(1)} %get-tuple-element.458.xp, bf16[768,768]{1,0:T(8,128)(2,1)} %copy-done.33, bf16[768,768]{1,0:T(8,128)(2,1)} %copy-done.16, ...), custom_call_target="tpu_custom_call" | custom-call | flops 21872640 | bytes 21872640 | tf_op jit(solution)/shard_map/pallas_call | solution.py:371
  483.9 9.3 %collective-permute-done.47.xg = bf16[384,768]{1,0:T(8,128)(2,1)S(1)} collective-permute-done((bf16[384,768]{1,0:T(8,128)(2,1)S(1)}, bf16[384,768]{1,0:T(8,128)(2,1)S(1)}, u32[]{:S(2)}, u32[]{:S(2)}) %collective-permute-start.47) | collective-permute-done | bytes 589856 | tf_op jit(solution)/shard_map/ppermute | solution.py:739
  494.0 3.2 shard_map.262
  (200 shorter events, 64.9 us)
Async XLA Ops:
  0.6 23.4 %copy-start = (s32[1024,1]{0,1:T(1,128)S(1)}, s32[1024,1]{0,1:T(1,128)}, u32[]{:S(2)}) copy-start(s32[1024,1]{0,1:T(1,128)} %param.16) | copy-start | bytes 12292
  0.7 3.7 collective-permute-start
  4.3 71.6 %copy-start.30 = (f32[1,768]{1,0:T(1,128)}, f32[1,768]{1,0:T(1,128)S(1)}, u32[]{:S(2)}) copy-start(f32[1,768]{1,0:T(1,128)S(1)} %get-tuple-element.499.g.refs_7_) | copy-start | bytes 9220
  23.9 3.8 collective-permute-start.1
  43.5 8.4 %collective-permute-start.2 = (bf16[1024,768]{1,0:T(8,128)(2,1)}, bf16[1024,768]{1,0:T(8,128)(2,1)S(1)}, u32[]{:S(2)}, u32[]{:S(2)}) collective-permute-start(bf16[1024,768]{1,0:T(8,128)(2,1)} %get-tuple-element.254.refs_1_), channel_id=1, source_target_pairs={{0,16},{16,0},{1,17},{17,1},{2,18},{18,2},{3,19},{19,3},{4,20},{20... | collective-permute-start | bytes 4718600 | tf_op jit(solution)/shard_map/ppermute | solution.py:647
  43.7 42.5 %all-to-all-start.1 = ((bf16[16,64,768]{2,1,0:T(8,128)(2,1)}), bf16[16,64,768]{2,1,0:T(8,128)(2,1)}, u32[]{:S(2)}, u32[]{:S(2)}) async-start(bf16[16,64,768]{2,1,0:T(8,128)(2,1)} %bitcast.10), calls=%async_computation.1 | async-start | bytes 3145728 | tf_op jit(solution)/shard_map/all_to_all | solution.py:889
  72.3 3.7 collective-permute-start.4
  86.2 41.7 %all-to-all-start = ((bf16[16,64,768]{2,1,0:T(8,128)(2,1)}), bf16[16,64,768]{2,1,0:T(8,128)(2,1)S(1)}, u32[]{:S(2)}, u32[]{:S(2)}) async-start(bf16[16,64,768]{2,1,0:T(8,128)(2,1)} %bitcast.8), calls=%async_computation | async-start | bytes 3145728 | tf_op jit(solution)/shard_map/all_to_all | solution.py:889
  94.5 33.5 %collective-permute-start.6 = (bf16[1024,768]{1,0:T(8,128)(2,1)}, bf16[1024,768]{1,0:T(8,128)(2,1)}, u32[]{:S(2)}, u32[]{:S(2)}) collective-permute-start(bf16[1024,768]{1,0:T(8,128)(2,1)} %bitcast.11.go), channel_id=1, source_target_pairs={{0,16},{16,0},{1,17},{17,1},{2,18},{18,2},{3,19},{19,3},{4,20},{20... | collective-permute-start | bytes 4718600 | tf_op jit(solution)/shard_map/ppermute | solution.py:647
  127.9 3.4 collective-permute-start.5
  166.6 3.7 collective-permute-start.7
  173.2 41.6 %all-to-all-start.2 = ((bf16[16,64,768]{2,1,0:T(8,128)(2,1)}), bf16[16,64,768]{2,1,0:T(8,128)(2,1)S(1)}, u32[]{:S(2)}, u32[]{:S(2)}) async-start(bf16[16,64,768]{2,1,0:T(8,128)(2,1)} %bitcast.12), calls=%async_computation.2 | async-start | bytes 3145728 | tf_op jit(solution)/shard_map/all_to_all | solution.py:889
  180.5 44.4 %collective-permute-start.3 = (bf16[512,768]{1,0:T(8,128)(2,1)}, bf16[512,768]{1,0:T(8,128)(2,1)}, u32[]{:S(2)}, u32[]{:S(2)}) collective-permute-start(bf16[512,768]{1,0:T(8,128)(2,1)} %refs_0_.3), channel_id=1, source_target_pairs={{0,16},{16,0},{1,17},{17,1},{2,18},{18,2},{3,19},{19,3},{4,20},{20... | collective-permute-start | bytes 2359304 | tf_op jit(solution)/shard_map/ppermute | solution.py:647
  180.6 19.9 %collective-permute-start.8 = (bf16[1024,768]{1,0:T(8,128)(2,1)}, bf16[1024,768]{1,0:T(8,128)(2,1)S(1)}, u32[]{:S(2)}, u32[]{:S(2)}) collective-permute-start(bf16[1024,768]{1,0:T(8,128)(2,1)} %get-tuple-element.268), channel_id=1, source_target_pairs={{0,16},{16,0},{1,17},{17,1},{2,18},{18,2},{3,19},{19,3},{4,20},{20... | collective-permute-start | bytes 4718600 | tf_op jit(solution)/shard_map/ppermute | solution.py:647
  181.0 9.7 %copy-start.45 = (bf16[2048,768]{1,0:T(8,128)(2,1)S(1)}, bf16[2048,768]{1,0:T(8,128)(2,1)}, u32[]{:S(2)}) copy-start(bf16[2048,768]{1,0:T(8,128)(2,1)} %get-tuple-element.263) | copy-start | bytes 9437188
  190.8 9.6 %copy-start.4 = (bf16[1024,768]{1,0:T(8,128)(2,1)S(1)}, bf16[1024,768]{1,0:T(8,128)(2,1)}, u32[]{:S(2)}) copy-start(bf16[1024,768]{1,0:T(8,128)(2,1)} %get-tuple-element.267.a) | copy-start | bytes 4718596
  216.8 8.0 %collective-permute-start.9 = (bf16[512,768]{1,0:T(8,128)(2,1)}, bf16[512,768]{1,0:T(8,128)(2,1)}, u32[]{:S(2)}, u32[]{:S(2)}) collective-permute-start(bf16[512,768]{1,0:T(8,128)(2,1)} %shard_map.245.refs_2_), channel_id=1, source_target_pairs={{0,16},{16,0},{1,17},{17,1},{2,18},{18,2},{3,19},{19,3},{4,20},{20... | collective-permute-start | bytes 2359304 | tf_op jit(solution)/shard_map/ppermute | solution.py:647
  216.8 43.9 %all-to-all-start.3 = ((bf16[16,64,768]{2,1,0:T(8,128)(2,1)}), bf16[16,64,768]{2,1,0:T(8,128)(2,1)S(1)}, u32[]{:S(2)}, u32[]{:S(2)}) async-start(bf16[16,64,768]{2,1,0:T(8,128)(2,1)} %bitcast.17), calls=%async_computation.3 | async-start | bytes 3145728 | tf_op jit(solution)/shard_map/all_to_all | solution.py:889
  252.3 8.3 %collective-permute-start.10 = (bf16[1024,768]{1,0:T(8,128)(2,1)}, bf16[1024,768]{1,0:T(8,128)(2,1)}, u32[]{:S(2)}, u32[]{:S(2)}) collective-permute-start(bf16[1024,768]{1,0:T(8,128)(2,1)} %get-tuple-element.279.dna), channel_id=1, source_target_pairs={{0,16},{16,0},{1,17},{17,1},{2,18},{18,2},{3,19},{19,3},{4,20},{20... | collective-permute-start | bytes 4718600 | tf_op jit(solution)/shard_map/ppermute | solution.py:647
  273.7 6.3 %collective-permute-start.11 = (bf16[1024,768]{1,0:T(8,128)(2,1)}, bf16[1024,768]{1,0:T(8,128)(2,1)}, u32[]{:S(2)}, u32[]{:S(2)}) collective-permute-start(bf16[1024,768]{1,0:T(8,128)(2,1)} %get-tuple-element.300.refs_1_), channel_id=1, source_target_pairs={{0,16},{16,0},{1,17},{17,1},{2,18},{18,2},{3,19},{19,3},{4,20},{20... | collective-permute-start | bytes 4718600 | tf_op jit(solution)/shard_map/ppermute | solution.py:647
  285.0 35.5 %collective-permute-start.12 = (bf16[768,768]{1,0:T(8,128)(2,1)}, bf16[768,768]{1,0:T(8,128)(2,1)S(1)}, u32[]{:S(2)}, u32[]{:S(2)}) collective-permute-start(bf16[768,768]{1,0:T(8,128)(2,1)} %fusion.8), channel_id=1, source_target_pairs={{0,1},{1,0},{2,3},{3,2},{4,5},{5,4},{6,7},{7,6},{8,9},{9,8},{10,11... | collective-permute-start | bytes 3538952 | tf_op jit(solution)/shard_map/ppermute | solution.py:739
  287.0 34.6 %collective-permute-start.13 = (bf16[768,768]{1,0:T(8,128)(2,1)S(1)}, bf16[768,768]{1,0:T(8,128)(2,1)S(1)}, u32[]{:S(2)}, u32[]{:S(2)}) collective-permute-start(bf16[768,768]{1,0:T(8,128)(2,1)S(1)} %fusion.11), channel_id=1, source_target_pairs={{0,2},{1,3},{2,0},{3,1},{4,6},{5,7},{6,4},{7,5},{8,10},{9,11},{10,... | collective-permute-start | bytes 3538952 | tf_op jit(solution)/shard_map/ppermute | solution.py:739
  288.4 29.9 %collective-permute-start.14 = (bf16[384,768]{1,0:T(8,128)(2,1)}, bf16[384,768]{1,0:T(8,128)(2,1)S(1)}, u32[]{:S(2)}, u32[]{:S(2)}) collective-permute-start(bf16[384,768]{1,0:T(8,128)(2,1)} %convolution_convert_fusion.7), channel_id=1, source_target_pairs={{0,4},{1,5},{2,6},{3,7},{4,0},{5,1},{6,2},{7,3},{8,12},{9,13},{10,... | collective-permute-start | bytes 1769480 | tf_op jit(solution)/shard_map/ppermute | solution.py:739
  291.2 28.6 %collective-permute-start.15 = (bf16[384,768]{1,0:T(8,128)(2,1)}, bf16[384,768]{1,0:T(8,128)(2,1)S(1)}, u32[]{:S(2)}, u32[]{:S(2)}) collective-permute-start(bf16[384,768]{1,0:T(8,128)(2,1)} %get-tuple-element.291), channel_id=1, source_target_pairs={{0,8},{1,9},{2,10},{3,11},{4,12},{5,13},{6,14},{7,15},{8,0},{9,1},... | collective-permute-start | bytes 1769480 | tf_op jit(solution)/shard_map/ppermute | solution.py:739
  322.6 30.9 %collective-permute-start.20 = (bf16[1024,768]{1,0:T(8,128)(2,1)}, bf16[1024,768]{1,0:T(8,128)(2,1)}, u32[]{:S(2)}, u32[]{:S(2)}) collective-permute-start(bf16[1024,768]{1,0:T(8,128)(2,1)} %get-tuple-element.355.dna), channel_id=1, source_target_pairs={{0,16},{16,0},{1,17},{17,1},{2,18},{18,2},{3,19},{19,3},{4,20},{20... | collective-permute-start | bytes 4718600 | tf_op jit(solution)/shard_map/ppermute | solution.py:647
  332.0 6.2 %copy-start.37 = (bf16[1024,768]{1,0:T(8,128)(2,1)S(1)}, bf16[1024,768]{1,0:T(8,128)(2,1)}, u32[]{:S(2)}) copy-start(bf16[1024,768]{1,0:T(8,128)(2,1)} %get-tuple-element.333) | copy-start | bytes 4718596
  332.0 6.2 %copy-start.44 = (bf16[1024,384]{1,0:T(8,128)(2,1)S(1)}, bf16[1024,384]{1,0:T(8,128)(2,1)}, u32[]{:S(2)}) copy-start(bf16[1024,384]{1,0:T(8,128)(2,1)} %get-tuple-element.335) | copy-start | bytes 2359300
  333.7 18.7 %collective-permute-start.16 = (bf16[384,768]{1,0:T(8,128)(2,1)S(1)}, bf16[384,768]{1,0:T(8,128)(2,1)S(1)}, u32[]{:S(2)}, u32[]{:S(2)}) collective-permute-start(bf16[384,768]{1,0:T(8,128)(2,1)S(1)} %get-tuple-element.329), channel_id=1, source_target_pairs={{0,1},{1,0},{2,3},{3,2},{4,5},{5,4},{6,7},{7,6},{8,9},{9,8},{10,11... | collective-permute-start | bytes 1769480 | tf_op jit(solution)/shard_map/ppermute | solution.py:739
  334.6 17.8 %collective-permute-start.17 = (bf16[384,768]{1,0:T(8,128)(2,1)S(1)}, bf16[384,768]{1,0:T(8,128)(2,1)S(1)}, u32[]{:S(2)}, u32[]{:S(2)}) collective-permute-start(bf16[384,768]{1,0:T(8,128)(2,1)S(1)} %get-tuple-element.330), channel_id=1, source_target_pairs={{0,2},{1,3},{2,0},{3,1},{4,6},{5,7},{6,4},{7,5},{8,10},{9,11},{10,... | collective-permute-start | bytes 1769480 | tf_op jit(solution)/shard_map/ppermute | solution.py:739
  334.6 14.3 %collective-permute-start.18 = (bf16[192,768]{1,0:T(8,128)(2,1)S(1)}, bf16[192,768]{1,0:T(8,128)(2,1)S(1)}, u32[]{:S(2)}, u32[]{:S(2)}) collective-permute-start(bf16[192,768]{1,0:T(8,128)(2,1)S(1)} %get-tuple-element.331), channel_id=1, source_target_pairs={{0,4},{1,5},{2,6},{3,7},{4,0},{5,1},{6,2},{7,3},{8,12},{9,13},{10,... | collective-permute-start | bytes 884744 | tf_op jit(solution)/shard_map/ppermute | solution.py:739
  336.5 15.8 %collective-permute-start.19 = (bf16[192,768]{1,0:T(8,128)(2,1)S(1)}, bf16[192,768]{1,0:T(8,128)(2,1)S(1)}, u32[]{:S(2)}, u32[]{:S(2)}) collective-permute-start(bf16[192,768]{1,0:T(8,128)(2,1)S(1)} %get-tuple-element.332), channel_id=1, source_target_pairs={{0,8},{1,9},{2,10},{3,11},{4,12},{5,13},{6,14},{7,15},{8,0},{9,1},... | collective-permute-start | bytes 884744 | tf_op jit(solution)/shard_map/ppermute | solution.py:739
  352.4 5.8 %copy-start.7 = (bf16[1024,768]{1,0:T(8,128)(2,1)S(1)}, bf16[1024,768]{1,0:T(8,128)(2,1)}, u32[]{:S(2)}) copy-start(bf16[1024,768]{1,0:T(8,128)(2,1)} %get-tuple-element.355.dna) | copy-start | bytes 4718596
  353.5 16.4 %collective-permute-start.21 = (bf16[480,768]{1,0:T(8,128)(2,1)S(1)}, bf16[480,768]{1,0:T(8,128)(2,1)S(1)}, u32[]{:S(2)}, u32[]{:S(2)}) collective-permute-start(bf16[480,768]{1,0:T(8,128)(2,1)S(1)} %get-tuple-element.350), channel_id=1, source_target_pairs={{0,1},{1,0},{2,3},{3,2},{4,5},{5,4},{6,7},{7,6},{8,9},{9,8},{10,11... | collective-permute-start | bytes 2211848 | tf_op jit(solution)/shard_map/ppermute | solution.py:739
  354.4 15.6 %collective-permute-start.22 = (bf16[480,768]{1,0:T(8,128)(2,1)S(1)}, bf16[480,768]{1,0:T(8,128)(2,1)S(1)}, u32[]{:S(2)}, u32[]{:S(2)}) collective-permute-start(bf16[480,768]{1,0:T(8,128)(2,1)S(1)} %get-tuple-element.351), channel_id=1, source_target_pairs={{0,2},{1,3},{2,0},{3,1},{4,6},{5,7},{6,4},{7,5},{8,10},{9,11},{10,... | collective-permute-start | bytes 2211848 | tf_op jit(solution)/shard_map/ppermute | solution.py:739
  355.2 11.8 %collective-permute-start.23 = (bf16[192,768]{1,0:T(8,128)(2,1)S(1)}, bf16[192,768]{1,0:T(8,128)(2,1)S(1)}, u32[]{:S(2)}, u32[]{:S(2)}) collective-permute-start(bf16[192,768]{1,0:T(8,128)(2,1)S(1)} %get-tuple-element.352), channel_id=1, source_target_pairs={{0,4},{1,5},{2,6},{3,7},{4,0},{5,1},{6,2},{7,3},{8,12},{9,13},{10,... | collective-permute-start | bytes 884744 | tf_op jit(solution)/shard_map/ppermute | solution.py:739
  355.5 14.4 %collective-permute-start.24 = (bf16[192,768]{1,0:T(8,128)(2,1)S(1)}, bf16[192,768]{1,0:T(8,128)(2,1)S(1)}, u32[]{:S(2)}, u32[]{:S(2)}) collective-permute-start(bf16[192,768]{1,0:T(8,128)(2,1)S(1)} %get-tuple-element.353), channel_id=1, source_target_pairs={{0,8},{1,9},{2,10},{3,11},{4,12},{5,13},{6,14},{7,15},{8,0},{9,1},... | collective-permute-start | bytes 884744 | tf_op jit(solution)/shard_map/ppermute | solution.py:739
  371.1 11.3 %collective-permute-start.25 = (bf16[240,768]{1,0:T(8,128)(2,1)S(1)}, bf16[240,768]{1,0:T(8,128)(2,1)S(1)}, u32[]{:S(2)}, u32[]{:S(2)}) collective-permute-start(bf16[240,768]{1,0:T(8,128)(2,1)S(1)} %get-tuple-element.374), channel_id=1, source_target_pairs={{0,1},{1,0},{2,3},{3,2},{4,5},{5,4},{6,7},{7,6},{8,9},{9,8},{10,11... | collective-permute-start | bytes 1105928 | tf_op jit(solution)/shard_map/ppermute | solution.py:739
  372.0 10.4 %collective-permute-start.26 = (bf16[240,768]{1,0:T(8,128)(2,1)S(1)}, bf16[240,768]{1,0:T(8,128)(2,1)S(1)}, u32[]{:S(2)}, u32[]{:S(2)}) collective-permute-start(bf16[240,768]{1,0:T(8,128)(2,1)S(1)} %get-tuple-element.375), channel_id=1, source_target_pairs={{0,2},{1,3},{2,0},{3,1},{4,6},{5,7},{6,4},{7,5},{8,10},{9,11},{10,... | collective-permute-start | bytes 1105928 | tf_op jit(solution)/shard_map/ppermute | solution.py:739
  373.3 5.6 %collective-permute-start.27 = (bf16[96,768]{1,0:T(8,128)(2,1)S(1)}, bf16[96,768]{1,0:T(8,128)(2,1)S(1)}, u32[]{:S(2)}, u32[]{:S(2)}) collective-permute-start(bf16[96,768]{1,0:T(8,128)(2,1)S(1)} %get-tuple-element.376), channel_id=1, source_target_pairs={{0,4},{1,5},{2,6},{3,7},{4,0},{5,1},{6,2},{7,3},{8,12},{9,13},{10,... | collective-permute-start | bytes 442376 | tf_op jit(solution)/shard_map/ppermute | solution.py:739
  374.7 7.7 %collective-permute-start.28 = (bf16[96,768]{1,0:T(8,128)(2,1)S(1)}, bf16[96,768]{1,0:T(8,128)(2,1)S(1)}, u32[]{:S(2)}, u32[]{:S(2)}) collective-permute-start(bf16[96,768]{1,0:T(8,128)(2,1)S(1)} %get-tuple-element.377), channel_id=1, source_target_pairs={{0,8},{1,9},{2,10},{3,11},{4,12},{5,13},{6,14},{7,15},{8,0},{9,1},... | collective-permute-start | bytes 442376 | tf_op jit(solution)/shard_map/ppermute | solution.py:739
  383.3 10.9 %collective-permute-start.31 = (bf16[192,768]{1,0:T(8,128)(2,1)S(1)}, bf16[192,768]{1,0:T(8,128)(2,1)S(1)}, u32[]{:S(2)}, u32[]{:S(2)}) collective-permute-start(bf16[192,768]{1,0:T(8,128)(2,1)S(1)} %get-tuple-element.402.refs_2_), channel_id=1, source_target_pairs={{0,4},{1,5},{2,6},{3,7},{4,0},{5,1},{6,2},{7,3},{8,12},{9,13},{10,... | collective-permute-start | bytes 884744 | tf_op jit(solution)/shard_map/ppermute | solution.py:739
  383.3 12.6 %collective-permute-start.32 = (bf16[192,768]{1,0:T(8,128)(2,1)S(1)}, bf16[192,768]{1,0:T(8,128)(2,1)S(1)}, u32[]{:S(2)}, u32[]{:S(2)}) collective-permute-start(bf16[192,768]{1,0:T(8,128)(2,1)S(1)} %get-tuple-element.400.refs_0_), channel_id=1, source_target_pairs={{0,8},{1,9},{2,10},{3,11},{4,12},{5,13},{6,14},{7,15},{8,0},{9,1},... | collective-permute-start | bytes 884744 | tf_op jit(solution)/shard_map/ppermute | solution.py:739
  385.6 5.6 %collective-permute-start.29 = (bf16[64,768]{1,0:T(8,128)(2,1)S(1)}, bf16[64,768]{1,0:T(8,128)(2,1)S(1)}, u32[]{:S(2)}, u32[]{:S(2)}) collective-permute-start(bf16[64,768]{1,0:T(8,128)(2,1)S(1)} %get-tuple-element.406.refs_6_), channel_id=1, source_target_pairs={{0,1},{1,0},{2,3},{3,2},{4,5},{5,4},{6,7},{7,6},{8,9},{9,8},{10,11... | collective-permute-start | bytes 294920 | tf_op jit(solution)/shard_map/ppermute | solution.py:739
  386.8 4.4 collective-permute-start.30
  396.7 14.0 %collective-permute-start.35 = (bf16[240,768]{1,0:T(8,128)(2,1)S(1)}, bf16[240,768]{1,0:T(8,128)(2,1)S(1)}, u32[]{:S(2)}, u32[]{:S(2)}) collective-permute-start(bf16[240,768]{1,0:T(8,128)(2,1)S(1)} %get-tuple-element.417.refs_0_), channel_id=1, source_target_pairs={{0,4},{1,5},{2,6},{3,7},{4,0},{5,1},{6,2},{7,3},{8,12},{9,13},{10,... | collective-permute-start | bytes 1105928 | tf_op jit(solution)/shard_map/ppermute | solution.py:739
  396.8 15.5 %collective-permute-start.36 = (bf16[240,768]{1,0:T(8,128)(2,1)S(1)}, bf16[240,768]{1,0:T(8,128)(2,1)S(1)}, u32[]{:S(2)}, u32[]{:S(2)}) collective-permute-start(bf16[240,768]{1,0:T(8,128)(2,1)S(1)} %get-tuple-element.419.refs_2_), channel_id=1, source_target_pairs={{0,8},{1,9},{2,10},{3,11},{4,12},{5,13},{6,14},{7,15},{8,0},{9,1},... | collective-permute-start | bytes 1105928 | tf_op jit(solution)/shard_map/ppermute | solution.py:739
  398.4 6.7 %collective-permute-start.34 = (bf16[112,768]{1,0:T(8,128)(2,1)S(1)}, bf16[112,768]{1,0:T(8,128)(2,1)S(1)}, u32[]{:S(2)}, u32[]{:S(2)}) collective-permute-start(bf16[112,768]{1,0:T(8,128)(2,1)S(1)} %get-tuple-element.423.refs_6_), channel_id=1, source_target_pairs={{0,2},{1,3},{2,0},{3,1},{4,6},{5,7},{6,4},{7,5},{8,10},{9,11},{10,... | collective-permute-start | bytes 516104 | tf_op jit(solution)/shard_map/ppermute | solution.py:739
  399.9 5.1 %collective-permute-start.33 = (bf16[96,768]{1,0:T(8,128)(2,1)S(1)}, bf16[96,768]{1,0:T(8,128)(2,1)S(1)}, u32[]{:S(2)}, u32[]{:S(2)}) collective-permute-start(bf16[96,768]{1,0:T(8,128)(2,1)S(1)} %get-tuple-element.421.refs_4_), channel_id=1, source_target_pairs={{0,1},{1,0},{2,3},{3,2},{4,5},{5,4},{6,7},{7,6},{8,9},{9,8},{10,11... | collective-permute-start | bytes 442376 | tf_op jit(solution)/shard_map/ppermute | solution.py:739
  412.9 18.4 %collective-permute-start.37 = (bf16[384,768]{1,0:T(8,128)(2,1)S(1)}, bf16[384,768]{1,0:T(8,128)(2,1)S(1)}, u32[]{:S(2)}, u32[]{:S(2)}) collective-permute-start(bf16[384,768]{1,0:T(8,128)(2,1)S(1)} %get-tuple-element.436.refs_2_), channel_id=1, source_target_pairs={{0,1},{1,0},{2,3},{3,2},{4,5},{5,4},{6,7},{7,6},{8,9},{9,8},{10,11... | collective-permute-start | bytes 1769480 | tf_op jit(solution)/shard_map/ppermute | solution.py:739
  414.9 16.5 %collective-permute-start.38 = (bf16[384,768]{1,0:T(8,128)(2,1)S(1)}, bf16[384,768]{1,0:T(8,128)(2,1)S(1)}, u32[]{:S(2)}, u32[]{:S(2)}) collective-permute-start(bf16[384,768]{1,0:T(8,128)(2,1)S(1)} %get-tuple-element.434.refs_0_), channel_id=1, source_target_pairs={{0,2},{1,3},{2,0},{3,1},{4,6},{5,7},{6,4},{7,5},{8,10},{9,11},{10,... | collective-permute-start | bytes 1769480 | tf_op jit(solution)/shard_map/ppermute | solution.py:739
  415.9 15.5 %collective-permute-start.39 = (bf16[256,768]{1,0:T(8,128)(2,1)S(1)}, bf16[256,768]{1,0:T(8,128)(2,1)S(1)}, u32[]{:S(2)}, u32[]{:S(2)}) collective-permute-start(bf16[256,768]{1,0:T(8,128)(2,1)S(1)} %get-tuple-element.440.refs_6_), channel_id=1, source_target_pairs={{0,4},{1,5},{2,6},{3,7},{4,0},{5,1},{6,2},{7,3},{8,12},{9,13},{10,... | collective-permute-start | bytes 1179656 | tf_op jit(solution)/shard_map/ppermute | solution.py:739
  415.9 15.5 %collective-permute-start.40 = (bf16[240,768]{1,0:T(8,128)(2,1)S(1)}, bf16[240,768]{1,0:T(8,128)(2,1)S(1)}, u32[]{:S(2)}, u32[]{:S(2)}) collective-permute-start(bf16[240,768]{1,0:T(8,128)(2,1)S(1)} %get-tuple-element.438.refs_4_), channel_id=1, source_target_pairs={{0,8},{1,9},{2,10},{3,11},{4,12},{5,13},{6,14},{7,15},{8,0},{9,1},... | collective-permute-start | bytes 1105928 | tf_op jit(solution)/shard_map/ppermute | solution.py:739
  432.2 36.9 %copy-start.16 = (bf16[768,768]{1,0:T(8,128)(2,1)}, bf16[768,768]{1,0:T(8,128)(2,1)S(1)}, u32[]{:S(2)}) copy-start(bf16[768,768]{1,0:T(8,128)(2,1)S(1)} %get-tuple-element.460.yp) | copy-start | bytes 3538948
  432.2 33.7 %collective-permute-start.41 = (bf16[768,768]{1,0:T(8,128)(2,1)S(1)}, bf16[768,768]{1,0:T(8,128)(2,1)S(1)}, u32[]{:S(2)}, u32[]{:S(2)}) collective-permute-start(bf16[768,768]{1,0:T(8,128)(2,1)S(1)} %get-tuple-element.458.xp), channel_id=1, source_target_pairs={{0,1},{1,0},{2,3},{3,2},{4,5},{5,4},{6,7},{7,6},{8,9},{9,8},{10,11... | collective-permute-start | bytes 3538952 | tf_op jit(solution)/shard_map/ppermute | solution.py:739
  433.9 32.0 %collective-permute-start.42 = (bf16[768,768]{1,0:T(8,128)(2,1)S(1)}, bf16[768,768]{1,0:T(8,128)(2,1)S(1)}, u32[]{:S(2)}, u32[]{:S(2)}) collective-permute-start(bf16[768,768]{1,0:T(8,128)(2,1)S(1)} %get-tuple-element.460.yp), channel_id=1, source_target_pairs={{0,2},{1,3},{2,0},{3,1},{4,6},{5,7},{6,4},{7,5},{8,10},{9,11},{10,... | collective-permute-start | bytes 3538952 | tf_op jit(solution)/shard_map/ppermute | solution.py:739
  434.2 31.7 %collective-permute-start.44 = (bf16[496,768]{1,0:T(8,128)(2,1)S(1)}, bf16[496,768]{1,0:T(8,128)(2,1)S(1)}, u32[]{:S(2)}, u32[]{:S(2)}) collective-permute-start(bf16[496,768]{1,0:T(8,128)(2,1)S(1)} %get-tuple-element.464.refs_2_.bp), channel_id=1, source_target_pairs={{0,8},{1,9},{2,10},{3,11},{4,12},{5,13},{6,14},{7,15},{8,0},{9,1},... | collective-permute-start | bytes 2285576 | tf_op jit(solution)/shard_map/ppermute | solution.py:739
  434.9 28.4 %collective-permute-start.43 = (bf16[480,768]{1,0:T(8,128)(2,1)S(1)}, bf16[480,768]{1,0:T(8,128)(2,1)S(1)}, u32[]{:S(2)}, u32[]{:S(2)}) collective-permute-start(bf16[480,768]{1,0:T(8,128)(2,1)S(1)} %get-tuple-element.462.refs_0_.ap), channel_id=1, source_target_pairs={{0,4},{1,5},{2,6},{3,7},{4,0},{5,1},{6,2},{7,3},{8,12},{9,13},{10,... | collective-permute-start | bytes 2211848 | tf_op jit(solution)/shard_map/ppermute | solution.py:739
  466.5 11.3 %collective-permute-start.45 = (bf16[192,768]{1,0:T(8,128)(2,1)S(1)}, bf16[192,768]{1,0:T(8,128)(2,1)S(1)}, u32[]{:S(2)}, u32[]{:S(2)}) collective-permute-start(bf16[192,768]{1,0:T(8,128)(2,1)S(1)} %get-tuple-element.472.refs_2_), channel_id=1, source_target_pairs={{0,1},{1,0},{2,3},{3,2},{4,5},{5,4},{6,7},{7,6},{8,9},{9,8},{10,11... | collective-permute-start | bytes 884744 | tf_op jit(solution)/shard_map/ppermute | solution.py:739
  468.0 9.8 %collective-permute-start.46 = (bf16[192,768]{1,0:T(8,128)(2,1)S(1)}, bf16[192,768]{1,0:T(8,128)(2,1)S(1)}, u32[]{:S(2)}, u32[]{:S(2)}) collective-permute-start(bf16[192,768]{1,0:T(8,128)(2,1)S(1)} %get-tuple-element.470.refs_0_), channel_id=1, source_target_pairs={{0,2},{1,3},{2,0},{3,1},{4,6},{5,7},{6,4},{7,5},{8,10},{9,11},{10,... | collective-permute-start | bytes 884744 | tf_op jit(solution)/shard_map/ppermute | solution.py:739
  469.0 11.8 %copy-start.3 = (bf16[1024,768]{1,0:T(8,128)(2,1)S(1)}, bf16[1024,768]{1,0:T(8,128)(2,1)}, u32[]{:S(2)}) copy-start(bf16[1024,768]{1,0:T(8,128)(2,1)} %get-tuple-element.255.xr.refs_4_.xn) | copy-start | bytes 4718596
  478.4 14.8 %collective-permute-start.47 = (bf16[384,768]{1,0:T(8,128)(2,1)S(1)}, bf16[384,768]{1,0:T(8,128)(2,1)S(1)}, u32[]{:S(2)}, u32[]{:S(2)}) collective-permute-start(bf16[384,768]{1,0:T(8,128)(2,1)S(1)} %get-tuple-element.476.xp), channel_id=1, source_target_pairs={{0,1},{1,0},{2,3},{3,2},{4,5},{5,4},{6,7},{7,6},{8,9},{9,8},{10,11... | collective-permute-start | bytes 1769480 | tf_op jit(solution)/shard_map/ppermute | solution.py:739
  479.6 14.4 %collective-permute-start.48 = (bf16[384,768]{1,0:T(8,128)(2,1)S(1)}, bf16[384,768]{1,0:T(8,128)(2,1)S(1)}, u32[]{:S(2)}, u32[]{:S(2)}) collective-permute-start(bf16[384,768]{1,0:T(8,128)(2,1)S(1)} %get-tuple-element.478.yp), channel_id=1, source_target_pairs={{0,2},{1,3},{2,0},{3,1},{4,6},{5,7},{6,4},{7,5},{8,10},{9,11},{10,... | collective-permute-start | bytes 1769480 | tf_op jit(solution)/shard_map/ppermute | solution.py:739
  480.8 1.2 collective-permute-start.49
  480.8 16.4 %copy-start.1 = (s32[1024,1]{0,1:T(1,128)S(1)}, s32[1024,1]{0,1:T(1,128)}, u32[]{:S(2)}) copy-start(s32[1024,1]{0,1:T(1,128)} %param.16) | copy-start | bytes 12292
  (40 other events, 100.7 us)

commit v5 on v4

--- a/solution.py
+++ b/solution.py
@@ -133,6 +133,27 @@
             p_out[...] = total.astype(BF)
 
 
+def probs_kernel(blocks, qr, kf, lser, segc, segr, p_out):
+    i = pl.program_id(0)
+    pairs = kf.shape[2] // 128
+    for b in range(blocks):
+
+        @pl.when(i == b)
+        def _(b=b):
+            keys = BLK * (b + 1)
+            bias = mask_bias(segc[...], segr[...], b, keys)
+            lse = lser[...]
+            for pr in range(pairs):
+                cols = slice(pr * 128, pr * 128 + 128)
+                qp = qr[0, :, cols]
+                kp = kf[0, 0:keys, cols]
+                for hh in range(2):
+                    h = pr * 2 + hh
+                    qh = jnp.where(half_lane(hh), qp, jnp.zeros_like(qp))
+                    p = jnp.exp(mm_nt(qh, kp) + bias - lse[:, h : h + 1])
+                    p_out[h, :, 0:keys] = p.astype(BF)
+
+
 def attn_bwd_kernel(blocks, split, h_ref, *refs):
     if split:
         dro, drp, dno, dnp_ = refs[:4]
@@ -145,8 +166,8 @@
     else:
         xn = refs[3][...].astype(F32)
         rest = refs[4:]
-    gn, qr, kf, vf, orf, lser, wqkv, wo, segc, segr = rest[:10]
-    da_out, dqk_out, dv_out, dn_out, dg_out, dks, dvs = rest[10:]
+    gn, qr, kf, vf, orf, pr_in, wqkv, wo = rest[:8]
+    da_out, dqk_out, dv_out, dn_out, dg_out, dks, dvs = rest[8:]
     i = pl.program_id(0)
     blk = blocks - 1 - i
     if split:
@@ -175,8 +196,6 @@
         def _(b=b):
             keys = BLK * (b + 1)
             here = slice(b * BLK, b * BLK + BLK)
-            bias = mask_bias(segc[...], segr[...], b, keys)
-            lse = lser[...]
             for pr in range(pairs):
                 cols = slice(pr * 128, pr * 128 + 128)
                 qp = qr[0, :, cols]
@@ -191,12 +210,12 @@
                     doh = jnp.where(hm, dop, jnp.zeros_like(dop))
                     delta = jnp.sum(jnp.where(hm, prod, 0.0), axis=-1, keepdims=True)
                     h = pr * 2 + hh
-                    p = jnp.exp(mm_nt(qh, kp) + bias - lse[:, h : h + 1])
+                    p = pr_in[h, :, 0:keys]
                     dp = mm_nt(doh, vp)
-                    ds = (p * (dp - delta)).astype(BF)
+                    ds = (p.astype(F32) * (dp - delta)).astype(BF)
                     dqs.append(mm(ds, kp))
                     dks[0:keys, cols] += mm_tn(ds, qh)
-                    dvs[0:keys, cols] += mm_tn(p.astype(BF), doh)
+                    dvs[0:keys, cols] += mm_tn(p, doh)
                 dq = jnp.where(half_lane(0), dqs[0], dqs[1]) * 0.125
                 dqk_out[:, cols] = dq.astype(BF)
             dqk_out[:, pairs * 128 :] = dks[here, :].astype(BF)
@@ -412,9 +431,31 @@
     )
 
 
-def attention_backward(h, inputs, split, gn, saved, wqkv, wo, segc, segr):
-    qkv, o, lse = saved
-    length, d = segc.shape[0], wqkv.shape[1]
+def attention_probs(qkv, lse, segc, segr):
+    length, c = qkv.shape[1:]
+    heads = c // HEAD_DIM
+    return call(
+        functools.partial(probs_kernel, length // BLK),
+        (length // BLK,),
+        [
+            pl.BlockSpec((1, BLK, c), lambda i, *a: (0, i, 0)),
+            pl.BlockSpec((1, length, c), lambda i, *a: (1, 0, 0), pipeline_mode=pl.Buffered(1)),
+            rows_spec(128),
+            pl.BlockSpec((BLK, 1), lambda i, *a: (i, 0)),
+            fixed((1, length)),
+        ],
+        [pl.BlockSpec((heads, BLK, length), lambda i, *a: (0, i, 0))],
+        [shape((heads, length, length), BF)],
+        [],
+        4 * length * length * c,
+        2 * heads * length * length,
+        (qkv, qkv, lse, segc, segr),
+    )[0]
+
+
+def attention_backward(h, inputs, split, gn, saved, wqkv, wo):
+    qkv, o, probs = saved
+    length, d = o.shape[0], wqkv.shape[1]
     c = wqkv.shape[2]
     blocks = length // BLK
     back = lambda i: blocks - 1 - i
@@ -431,11 +472,9 @@
         part(1),
         part(2),
         rows_spec(c, back),
-        rows_spec(128, back),
+        pl.BlockSpec((c // HEAD_DIM, BLK, length), lambda i, *a: (0, back(i), 0)),
         fixed((3, d, c)),
         fixed((c, d)),
-        pl.BlockSpec((BLK, 1), lambda i, *a: (back(i), 0)),
-        fixed((1, length)),
     ]
     outs = [
         (rows_spec(d, back), shape((length, d), BF)),
@@ -455,7 +494,7 @@
         scratch,
         flops * 2,
         length * d * 20,
-        (*inputs, gn, qkv, qkv, qkv, o, lse, wqkv, wo, segc, segr),
+        (*inputs, gn, qkv, qkv, qkv, o, probs, wqkv, wo),
         prefetch=h,
     )
 
@@ -709,6 +748,45 @@
             at, lo, n = outs[0]
             put((at, lo, n // 2), pick(bits[place], g, p))
             put((at, lo + n // 2, n // 2), pick(bits[place], p, g))
+
+
+def first_fold_kernel(places, bits, *refs):
+    outs = refs[4 * len(places) :]
+    for j, place in enumerate(places):
+        kl, kh, gl, gh = refs[4 * j : 4 * j + 4]
+        lo, hi = total_of(kl[...], gl[...]), total_of(kh[...], gh[...])
+        outs[2 * j][...] = pick(bits[place], lo, hi)
+        outs[2 * j + 1][...] = pick(bits[place], hi, lo)
+
+
+def first_fold(bits, parts):
+    args, ins, outs, out_specs, places = [], [], [], [], []
+    for p in parts:
+        keep, got = p.kept[0], p.got[0]
+        n, width = keep.shape
+        low = pl.BlockSpec((n // 8, width), lambda i, *a: (i, 0))
+        high = pl.BlockSpec((n // 8, width), lambda i, *a: (i + 4, 0))
+        args += [keep, keep, got, got]
+        ins += [low, high, low, high]
+        outs += [shape((n // 2, width), BF)] * 2
+        out_specs += [low, low]
+        places.append(PLACE[p.order[p.phase]])
+    moved = sum(a.size * 2 for a in args)
+    made = call(
+        functools.partial(first_fold_kernel, tuple(places)),
+        (4,),
+        ins,
+        out_specs,
+        outs,
+        [],
+        moved,
+        moved,
+        args,
+        prefetch=bits,
+    )
+    for j, p in enumerate(parts):
+        rows = outs[2 * j].shape[0]
+        p.sent, p.kept = (made[2 * j], 0, rows), (made[2 * j + 1], 0, rows)
 
 
 class Part:
@@ -909,7 +987,9 @@
     )
     p3r = swap(p3)
     x2, sent = route_step(h, first, p3, p3r, gain[3], slot_row, slots)
-    m_own = travel(sent)
+    probs2 = attention_probs(qkv2, lse2, segc, segr)
+    probs1 = attention_probs(qkv1, lse1, segc, segr)
+    m_own, probs1, probs2 = lax.optimization_barrier((travel(sent), probs1, probs2))
     m_peer = swap(m_own)
     yo, yp, dmo, dmp, m_all, dy_all, ae_all, due_all, dc = expert_step(
         m_own, m_peer, grad_own, grad_peer, centroids, expert_up, expert_down
@@ -932,11 +1012,9 @@
         (cotangent, cot_peer, dm_own, dm_peer, first, p3, p3r),
         True,
         gain[3],
-        (qkv2, o2, lse2),
+        (qkv2, o2, probs2),
         qkv_two,
         out_two,
-        segc,
-        segr,
     )
     dn2r = swap(dn2)
     f = up_one.shape[1]
@@ -960,7 +1038,7 @@
 
     def last_attention(dr, dna, dnb):
         return attention_backward(
-            h, (dr, dna, dnb, x1), False, gain[1], (qkv1, o1, lse1), qkv_one, out_one, segc, segr
+            h, (dr, dna, dnb, x1), False, gain[1], (qkv1, o1, probs1), qkv_one, out_one
         )
 
     if steps is None:
@@ -1038,7 +1116,7 @@
         dn1r = swap(dn1)
         big[0].kept = (up_keep, 0, up_keep.shape[0])
         big[1].kept = (down_keep, 0, down_keep.shape[0])
-        fold(bits, big)
+        first_fold(bits, big)
 
         def narrow_grads(n, dqk, dv, o, da):
             return (

time: 507 us -> 499 us (0.984)
  Pallas kernels: 193 us -> 207 us
  local copies, waits for them, and re-layouts: 27.8 us -> 15.6 us
  waiting for transfers between devices: 154 us -> 143 us
    pallas_call x26 -> x28, Pallas kernels: 193 us -> 207 us  [call(): pl.pallas_call(kernel, grid_spec=spec, out_shape=outs, compiler_params=pa...]
    all_to_all x4, waiting for transfers between devices: 49.6 us -> 35.4 us  [travel(): return lax.all_to_all(box, 'dp', 0, 0, tiled=True).reshape(slots, d)]
    unnamed x101 -> x91, local copies, waits for them, and re-layouts: 22.7 us -> 10.5 us
  transfers between devices with their start and end apart: 54 -> 54, of which waited for: 26 -> 28; matrix products, arithmetic and copies ran while one was open for 9% -> 9% of each run, Pallas kernels for 20% -> 24%
where the time goes in v5:
time: 499 us; the launch traced here: 490 us
  Pallas kernels  207 us (41%)
  waiting for transfers between devices  143 us (29%)
  starting transfers between devices  78.9 us (16%)
  matrix products  40.9 us (8%)
  local copies, waits for them, and re-layouts  15.6 us (3%)
    pallas_call x28, Pallas kernels, call(): pl.pallas_call(kernel, grid_spec=spec, out_shape=outs, compiler_params=pa...  207 us
    ppermute x36, waiting for transfers between devices, advance(): lax.ppermute(v, 'dp', [(i, i ^ s) for i in range(16)])  96.7 us
    ppermute x36, starting transfers between devices, advance(): lax.ppermute(v, 'dp', [(i, i ^ s) for i in range(16)])  44.7 us
    dot_general x14, matrix products, mm_tn(): lax.dot_general(a, b, (((0,), (0,)), ((), ())), preferred_element_type=F32)  40.7 us
    all_to_all x4, waiting for transfers between devices, travel(): return lax.all_to_all(box, 'dp', 0, 0, tiled=True).reshape(slots, d)  35.4 us
    all_to_all x4, starting transfers between devices, travel(): return lax.all_to_all(box, 'dp', 0, 0, tiled=True).reshape(slots, d)  32.2 us
    ppermute x14, waiting for transfers between devices, swap(): return lax.ppermute(v, 'head', SWAP)  10.8 us
    unnamed x91, local copies, waits for them, and re-layouts  10.5 us
  transfers between devices with their start and end apart: 54, of which 28 were waited for; matrix products, arithmetic and copies ran while one was open for 9% of the time, Pallas kernels for 24%

profile of v5, /device:TPU:0, one launch (start us, length us, event | category | flops | bytes accessed | tf_op | source)
XLA Modules:
  0.0 489.9 jit_solution(10403841312868786220)
XLA Ops:
  1.2 1.7 copy.30.refs_5_.refs_6_.segc
  5.2 18.7 %shard_map.237 = (bf16[1024,768]{1,0:T(8,128)(2,1)}, bf16[3,1024,384]{2,1,0:T(8,128)(2,1)}, bf16[1024,384]{1,0:T(8,128)(2,1)}, f32[1024,128]{1,0:T(8,128)}, bf16[1024,768]{1,0:T(8,128)(2,1)}) custom-call(s32[1]{0:T(128)} %bitcast.h_ref, bf16[512,768]{1,0:T(8,128)(2,1)} %xo.1, bf16[512,768]{1,0:T(8,128)(2,1)} %copy-done.12, ...), custom_call_target="tpu_custom_call" | custom-call | flops 8053063680 | bytes 15728640 | tf_op jit(solution)/shard_map/pallas_call | solution.py:390
  25.0 2.6 shard_map.238
  27.7 15.7 %shard_map.239 = (bf16[1024,768]{1,0:T(8,128)(2,1)}, bf16[1024,768]{1,0:T(8,128)(2,1)}, bf16[1024,1536]{1,0:T(8,128)(2,1)}, bf16[1024,1536]{1,0:T(8,128)(2,1)}, bf16[1024,768]{1,0:T(8,128)(2,1)}) custom-call(s32[1]{0:T(128)} %bitcast.h_ref, bf16[512,768]{1,0:T(8,128)(2,1)} %xo.1, bf16[512,768]{1,0:T(8,128)(2,1)} %copy-done.12, ...), custom_call_target="tpu_custom_call" | custom-call | flops 4831838208 | bytes 20447232 | tf_op jit(solution)/shard_map/pallas_call | solution.py:390
  43.7 8.2 %all-to-all-start.1 = ((bf16[16,64,768]{2,1,0:T(8,128)(2,1)}), bf16[16,64,768]{2,1,0:T(8,128)(2,1)}, u32[]{:S(2)}, u32[]{:S(2)}) async-start(bf16[16,64,768]{2,1,0:T(8,128)(2,1)} %bitcast.10), calls=%async_computation.1 | async-start | bytes 3145728 | tf_op jit(solution)/shard_map/all_to_all | solution.py:967
  53.0 19.3 %shard_map.240 = (bf16[1024,768]{1,0:T(8,128)(2,1)}, bf16[1024,768]{1,0:T(8,128)(2,1)}, bf16[3,1024,384]{2,1,0:T(8,128)(2,1)}, bf16[1024,384]{1,0:T(8,128)(2,1)}...) custom-call(s32[1]{0:T(128)} %bitcast.h_ref, bf16[1024,768]{1,0:T(8,128)(2,1)} %get-tuple-element.259.refs_0_.refs_3_, ...), custom_call_target="tpu_custom_call" | custom-call | flops 8053063680 | bytes 15728640 | tf_op jit(solution)/shard_map/pallas_call | solution.py:390
  72.4 3.6 collective-permute-done.4.pb.refs_6_
  78.8 2.8 shard_map.241
  82.8 3.4 all-to-all-done.1
  86.2 8.3 %all-to-all-start = ((bf16[16,64,768]{2,1,0:T(8,128)(2,1)}), bf16[16,64,768]{2,1,0:T(8,128)(2,1)S(1)}, u32[]{:S(2)}, u32[]{:S(2)}) async-start(bf16[16,64,768]{2,1,0:T(8,128)(2,1)} %bitcast.8), calls=%async_computation | async-start | bytes 3145728 | tf_op jit(solution)/shard_map/all_to_all | solution.py:967
  94.4 8.2 %shard_map.242.refs_9_ = bf16[6,1024,1024]{2,1,0:T(8,128)(2,1)} custom-call(bf16[3,1024,384]{2,1,0:T(8,128)(2,1)} %get-tuple-element.266.qr.kf.refs_5_.refs_6_.refs_7_, bf16[3,1024,384]{2,1,0:T(8,128)(2,1)} %get-tuple-element.266.qr.kf.refs_5_.refs_6_.refs_7_, f32[1024,128]{1,0:T(8,128)} %get-tuple-element.267.lser, s32[1024,1]{1,0:T(8,128)} %copy.30.refs_5_.refs_6_.segc, ...), custom_call_target="tpu_custom_call" | custom-call | flops 1610612736 | bytes 12582912 | tf_op jit(solution)/shard_map/pallas_call | solution.py:390
  102.6 8.1 %shard_map.243.refs_12_ = bf16[6,1024,1024]{2,1,0:T(8,128)(2,1)} custom-call(bf16[3,1024,384]{2,1,0:T(8,128)(2,1)} %get-tuple-element.268.qr.kf.refs_8_.refs_9_.refs_10_, bf16[3,1024,384]{2,1,0:T(8,128)(2,1)} %get-tuple-element.268.qr.kf.refs_8_.refs_9_.refs_10_, f32[1024,128]{1,0:T(8,128)} %get-tuple-element.269.lser, s32[1024,1]{1,0:T(8,128)} %copy.30.refs_5_.refs_6_.segc, ...), custom_call_target="tpu_custom_call" | custom-call | flops 1610612736 | bytes 12582912 | tf_op jit(solution)/shard_map/pallas_call | solution.py:390
  110.8 17.2 %all-to-all-done = bf16[16,64,768]{2,1,0:T(8,128)(2,1)S(1)} async-done(((bf16[16,64,768]{2,1,0:T(8,128)(2,1)}), bf16[16,64,768]{2,1,0:T(8,128)(2,1)S(1)}, u32[]{:S(2)}, u32[]{:S(2)}) %all-to-all-start) | async-done | bytes 1572896 | tf_op jit(solution)/shard_map/all_to_all | solution.py:967
  127.9 3.4 collective-permute-done.5.mp
  132.5 34.1 %shard_map.244 = (bf16[1024,768]{1,0:T(8,128)(2,1)}, bf16[1024,768]{1,0:T(8,128)(2,1)}, bf16[1024,768]{1,0:T(8,128)(2,1)}, bf16[1024,768]{1,0:T(8,128)(2,1)}, bf...) custom-call(bf16[1024,768]{1,0:T(8,128)(2,1)} %bitcast.46, ...), custom_call_target="tpu_custom_call" | custom-call | flops 19327352832 | bytes 31457280 | tf_op jit(solution)/shard_map/pallas_call | solution.py:390
  166.8 3.5 collective-permute-done.7.b
  173.2 7.7 %all-to-all-start.2 = ((bf16[16,64,768]{2,1,0:T(8,128)(2,1)}), bf16[16,64,768]{2,1,0:T(8,128)(2,1)S(1)}, u32[]{:S(2)}, u32[]{:S(2)}) async-start(bf16[16,64,768]{2,1,0:T(8,128)(2,1)} %bitcast.12), calls=%async_computation.2 | async-start | bytes 3145728 | tf_op jit(solution)/shard_map/all_to_all | solution.py:967
  181.5 9.7 %convolution_bitcast_fusion = f32[1,1536,768]{2,1,0:T(8,128)} fusion(bf16[2048,1536]{1,0:T(8,128)(2,1)} %get-tuple-element.276, bf16[2048,768]{1,0:T(8,128)(2,1)} %get-tuple-element.277), kind=kOutput, calls=%fused_computation | convolution fusion | flops 4831838208 | bytes 14155776 | tf_op jit(solution)/shard_map/dot_general | solution.py:30
  191.3 9.6 %convolution_bitcast_fusion.1 = f32[1,768,1536]{2,1,0:T(8,128)} fusion(bf16[2048,768]{1,0:T(8,128)(2,1)S(1)} %copy-done.40, bf16[2048,1536]{1,0:T(8,128)(2,1)} %get-tuple-element.275), kind=kOutput, calls=%fused_computation.1 | convolution fusion | flops 4831838208 | bytes 14155776 | tf_op jit(solution)/shard_map/dot_general | solution.py:30
  202.4 12.8 %all-to-all-done.2 = bf16[16,64,768]{2,1,0:T(8,128)(2,1)S(1)} async-done(((bf16[16,64,768]{2,1,0:T(8,128)(2,1)}), bf16[16,64,768]{2,1,0:T(8,128)(2,1)S(1)}, u32[]{:S(2)}, u32[]{:S(2)}) %all-to-all-start.2) | async-done | bytes 1572896 | tf_op jit(solution)/shard_map/all_to_all | solution.py:967
  215.2 2.1 shard_map.247.refs_2_
  217.2 8.0 %all-to-all-start.3 = ((bf16[16,64,768]{2,1,0:T(8,128)(2,1)}), bf16[16,64,768]{2,1,0:T(8,128)(2,1)S(1)}, u32[]{:S(2)}, u32[]{:S(2)}) async-start(bf16[16,64,768]{2,1,0:T(8,128)(2,1)} %bitcast.17), calls=%async_computation.3 | async-start | bytes 3145728 | tf_op jit(solution)/shard_map/all_to_all | solution.py:967
  225.3 23.9 %shard_map.248 = (bf16[1024,768]{1,0:T(8,128)(2,1)}, bf16[1024,768]{1,0:T(8,128)(2,1)}, bf16[1024,384]{1,0:T(8,128)(2,1)}, bf16[1024,768]{1,0:T(8,128)(2,1)}, f32[8,768]{1,0:T(8,128)}) custom-call(s32[1]{0:T(128)} %bitcast.h_ref, bf16[512,768]{1,0:T(8,128)(2,1)} %refs_0_.3, bf16[512,768]{1,0:T(8,128)(2,1)} %collective-permute-done.3.refs_1_, ...), custom_call_target="tpu_custom_call" | custom-call | flops 12884901888 | bytes 15728640 | tf_op jit(solution)/shard_map/pallas_call | solution.py:390
  249.5 2.8 convolution_convert_fusion.5
  252.3 1.7 convolution_convert_fusion.6.refs_8_.refs_9_
  255.6 1.9 broadcast_select_fusion.2
  257.5 2.0 all-to-all-done.3
  259.5 13.0 %shard_map.249 = (bf16[1024,768]{1,0:T(8,128)(2,1)}, bf16[1024,1536]{1,0:T(8,128)(2,1)}, bf16[1024,768]{1,0:T(8,128)(2,1)}, f32[8,768]{1,0:T(8,128)}) custom-call(bf16[1024,768]{1,0:T(8,128)(2,1)} %get-tuple-element.288.drr, bf16[1024,768]{1,0:T(8,128)(2,1)} %get-tuple-element.289.dna, bf16[1024,768]{1,0:T(8,128)(2,1)} %collective-permute-done.10.dnb, ...), custom_call_target="tpu_custom_call" | custom-call | flops 4831838208 | bytes 20447232 | tf_op jit(solution)/shard_map/pallas_call | solution.py:390
  272.7 3.5 fusion.11
  278.5 2.5 fusion.17.refs_4_.refs_5_
  281.0 2.5 fusion.14.refs_0_.refs_1_
  284.6 2.6 collective-permute-start.13
  287.3 4.1 collective-permute-start.14
  292.2 23.0 %shard_map.250 = (bf16[1024,768]{1,0:T(8,128)(2,1)}, bf16[1024,768]{1,0:T(8,128)(2,1)}, bf16[1024,384]{1,0:T(8,128)(2,1)}, bf16[1024,768]{1,0:T(8,128)(2,1)}, f32[8,768]{1,0:T(8,128)}) custom-call(s32[1]{0:T(128)} %bitcast.h_ref, bf16[1024,768]{1,0:T(8,128)(2,1)} %get-tuple-element.309.refs_0_, bf16[1024,768]{1,0:T(8,128)(2,1)} %get-tuple-element.310.refs_1_, ...), custom_call_target="tpu_custom_call" | custom-call | flops 12884901888 | bytes 15728640 | tf_op jit(solution)/shard_map/pallas_call | solution.py:390
  315.8 4.1 collective-permute-done.15.refs_14_.refs_15_
  320.5 6.5 %shard_map.251 = (bf16[384,768]{1,0:T(8,128)(2,1)}, bf16[384,768]{1,0:T(8,128)(2,1)}, bf16[384,768]{1,0:T(8,128)(2,1)}, bf16[384,768]{1,0:T(8,128)(2,1)}, bf16[1...) custom-call(s32[4]{0:T(128)} %pad_add_fusion.bits, ...), custom_call_target="tpu_custom_call" | custom-call | flops 14155776 | bytes 14155776 | tf_op jit(solution)/shard_map/pallas_call | solution.py:390
  328.9 2.7 collective-permute-start.19
  335.8 7.5 %collective-permute-done.18.refs_7_ = bf16[192,768]{1,0:T(8,128)(2,1)S(1)} collective-permute-done((bf16[192,768]{1,0:T(8,128)(2,1)}, bf16[192,768]{1,0:T(8,128)(2,1)S(1)}, u32[]{:S(2)}, u32[]{:S(2)}) %collective-permute-start.18) | collective-permute-done | bytes 294944 | tf_op jit(solution)/shard_map/ppermute | solution.py:817
  347.1 1.7 collective-permute-start.22
  348.8 2.0 collective-permute-start.24
  350.8 5.0 %shard_map.253 = (f32[512,768]{1,0:T(8,128)}, f32[8,768]{1,0:T(8,128)S(1)}) custom-call(s32[1]{0:T(128)} %bitcast.h_ref, bf16[1024,768]{1,0:T(8,128)(2,1)S(1)} %copy-done.6, bf16[1024,768]{1,0:T(8,128)(2,1)S(1)} %copy-done.7, bf16[1024,768]{1,0:T(8,128)(2,1)} %collective-permute-done.20.dnb, bf16[512,768]{1,0:T(8,128)(2,1)S(1)} %copy-done.11, ...), custom_call_target="tpu_custom_call" | custom-call | flops 31457280 | bytes 11010048 | tf_op jit(solution)/shard_map/pallas_call | solution.py:390
  355.8 5.9 %collective-permute-done.23.refs_1_ = bf16[192,768]{1,0:T(8,128)(2,1)S(1)} collective-permute-done((bf16[192,768]{1,0:T(8,128)(2,1)S(1)}, bf16[192,768]{1,0:T(8,128)(2,1)S(1)}, u32[]{:S(2)}, u32[]{:S(2)}) %collective-permute-start.23) | collective-permute-done | bytes 294944 | tf_op jit(solution)/shard_map/ppermute | solution.py:817
  361.7 1.8 collective-permute-done.24.refs_2_
  366.3 1.7 collective-permute-start.26
  368.1 1.9 collective-permute-start.28
  370.5 2.1 shard_map.255
  372.6 2.5 collective-permute-done.27.refs_2_
  377.1 2.1 collective-permute-start.32
  381.1 3.6 collective-permute-done.30.refs_5_
  384.7 3.5 collective-permute-done.31.refs_3_
  390.3 1.6 collective-permute-start.36
  391.9 1.8 collective-permute-start.34
  394.8 4.1 collective-permute-done.33.refs_5_
  398.9 4.9 collective-permute-done.35.refs_1_
  403.8 2.0 collective-permute-done.36.refs_3_
  407.2 1.9 collective-permute-start.38
  409.1 1.9 collective-permute-start.40
  411.0 12.9 %collective-permute-done.40.refs_5_ = bf16[240,768]{1,0:T(8,128)(2,1)S(1)} collective-permute-done((bf16[240,768]{1,0:T(8,128)(2,1)S(1)}, bf16[240,768]{1,0:T(8,128)(2,1)S(1)}, u32[]{:S(2)}, u32[]{:S(2)}) %collective-permute-start.40) | collective-permute-done | bytes 368672 | tf_op jit(solution)/shard_map/ppermute | solution.py:817
  427.3 2.0 collective-permute-start.43
  429.3 27.1 %collective-permute-done.43.refs_1_.ag = bf16[480,768]{1,0:T(8,128)(2,1)S(1)} collective-permute-done((bf16[480,768]{1,0:T(8,128)(2,1)S(1)}, bf16[480,768]{1,0:T(8,128)(2,1)S(1)}, u32[]{:S(2)}, u32[]{:S(2)}) %collective-permute-start.43) | collective-permute-done | bytes 737312 | tf_op jit(solution)/shard_map/ppermute | solution.py:817
  456.4 2.6 collective-permute-done.44.refs_3_.bg
  461.7 8.7 %shard_map.262 = (f32[768,1536]{1,0:T(8,128)}, f32[1536,768]{1,0:T(8,128)}, f32[3,768,384]{2,1,0:T(8,128)}, f32[384,768]{1,0:T(8,128)}) custom-call(s32[4]{0:T(128)S(1)} %copy-done.18, bf16[768,768]{1,0:T(8,128)(2,1)S(1)} %get-tuple-element.470.xp, bf16[768,768]{1,0:T(8,128)(2,1)} %copy-done.26, bf16[768,768]{1,0:T(8,128)(2,1)} %copy-done.10, ...), custom_call_target="tpu_custom_call" | custom-call | flops 21872640 | bytes 21872640 | tf_op jit(solution)/shard_map/pallas_call | solution.py:390
  477.0 8.5 %collective-permute-done.47.xg = bf16[384,768]{1,0:T(8,128)(2,1)S(1)} collective-permute-done((bf16[384,768]{1,0:T(8,128)(2,1)S(1)}, bf16[384,768]{1,0:T(8,128)(2,1)S(1)}, u32[]{:S(2)}, u32[]{:S(2)}) %collective-permute-start.47) | collective-permute-done | bytes 589856 | tf_op jit(solution)/shard_map/ppermute | solution.py:817
  486.2 3.2 shard_map.264
  (192 shorter events, 58.2 us)
Async XLA Ops:
  0.6 23.4 %copy-start = (s32[1024,1]{0,1:T(1,128)S(1)}, s32[1024,1]{0,1:T(1,128)}, u32[]{:S(2)}) copy-start(s32[1024,1]{0,1:T(1,128)} %param.16) | copy-start | bytes 12292
  0.7 3.7 collective-permute-start
  4.3 71.7 %copy-start.23 = (f32[1,768]{1,0:T(1,128)}, f32[1,768]{1,0:T(1,128)S(1)}, u32[]{:S(2)}) copy-start(f32[1,768]{1,0:T(1,128)S(1)} %get-tuple-element.511.g.refs_7_) | copy-start | bytes 9220
  23.9 3.8 collective-permute-start.1
  43.4 8.4 %collective-permute-start.2 = (bf16[1024,768]{1,0:T(8,128)(2,1)}, bf16[1024,768]{1,0:T(8,128)(2,1)S(1)}, u32[]{:S(2)}, u32[]{:S(2)}) collective-permute-start(bf16[1024,768]{1,0:T(8,128)(2,1)} %get-tuple-element.260.refs_1_), channel_id=1, source_target_pairs={{0,16},{16,0},{1,17},{17,1},{2,18},{18,2},{3,19},{19,3},{4,20},{20... | collective-permute-start | bytes 4718600 | tf_op jit(solution)/shard_map/ppermute | solution.py:686
  43.7 42.5 %all-to-all-start.1 = ((bf16[16,64,768]{2,1,0:T(8,128)(2,1)}), bf16[16,64,768]{2,1,0:T(8,128)(2,1)}, u32[]{:S(2)}, u32[]{:S(2)}) async-start(bf16[16,64,768]{2,1,0:T(8,128)(2,1)} %bitcast.10), calls=%async_computation.1 | async-start | bytes 3145728 | tf_op jit(solution)/shard_map/all_to_all | solution.py:967
  72.3 3.7 collective-permute-start.4
  86.2 41.7 %all-to-all-start = ((bf16[16,64,768]{2,1,0:T(8,128)(2,1)}), bf16[16,64,768]{2,1,0:T(8,128)(2,1)S(1)}, u32[]{:S(2)}, u32[]{:S(2)}) async-start(bf16[16,64,768]{2,1,0:T(8,128)(2,1)} %bitcast.8), calls=%async_computation | async-start | bytes 3145728 | tf_op jit(solution)/shard_map/all_to_all | solution.py:967
  110.8 17.2 %collective-permute-start.6 = (bf16[1024,768]{1,0:T(8,128)(2,1)}, bf16[1024,768]{1,0:T(8,128)(2,1)}, u32[]{:S(2)}, u32[]{:S(2)}) collective-permute-start(bf16[1024,768]{1,0:T(8,128)(2,1)} %bitcast.11.go), channel_id=1, source_target_pairs={{0,16},{16,0},{1,17},{17,1},{2,18},{18,2},{3,19},{19,3},{4,20},{20... | collective-permute-start | bytes 4718600 | tf_op jit(solution)/shard_map/ppermute | solution.py:686
  127.9 3.4 collective-permute-start.5
  166.6 3.7 collective-permute-start.7
  173.2 41.9 %all-to-all-start.2 = ((bf16[16,64,768]{2,1,0:T(8,128)(2,1)}), bf16[16,64,768]{2,1,0:T(8,128)(2,1)S(1)}, u32[]{:S(2)}, u32[]{:S(2)}) async-start(bf16[16,64,768]{2,1,0:T(8,128)(2,1)} %bitcast.12), calls=%async_computation.2 | async-start | bytes 3145728 | tf_op jit(solution)/shard_map/all_to_all | solution.py:967
  180.9 44.3 %collective-permute-start.3 = (bf16[512,768]{1,0:T(8,128)(2,1)}, bf16[512,768]{1,0:T(8,128)(2,1)}, u32[]{:S(2)}, u32[]{:S(2)}) collective-permute-start(bf16[512,768]{1,0:T(8,128)(2,1)} %refs_0_.3), channel_id=1, source_target_pairs={{0,16},{16,0},{1,17},{17,1},{2,18},{18,2},{3,19},{19,3},{4,20},{20... | collective-permute-start | bytes 2359304 | tf_op jit(solution)/shard_map/ppermute | solution.py:686
  181.0 19.9 %collective-permute-start.8 = (bf16[1024,768]{1,0:T(8,128)(2,1)}, bf16[1024,768]{1,0:T(8,128)(2,1)S(1)}, u32[]{:S(2)}, u32[]{:S(2)}) collective-permute-start(bf16[1024,768]{1,0:T(8,128)(2,1)} %get-tuple-element.279), channel_id=1, source_target_pairs={{0,16},{16,0},{1,17},{17,1},{2,18},{18,2},{3,19},{19,3},{4,20},{20... | collective-permute-start | bytes 4718600 | tf_op jit(solution)/shard_map/ppermute | solution.py:686
  217.2 8.0 %collective-permute-start.9 = (bf16[512,768]{1,0:T(8,128)(2,1)}, bf16[512,768]{1,0:T(8,128)(2,1)}, u32[]{:S(2)}, u32[]{:S(2)}) collective-permute-start(bf16[512,768]{1,0:T(8,128)(2,1)} %shard_map.247.refs_2_), channel_id=1, source_target_pairs={{0,16},{16,0},{1,17},{17,1},{2,18},{18,2},{3,19},{19,3},{4,20},{20... | collective-permute-start | bytes 2359304 | tf_op jit(solution)/shard_map/ppermute | solution.py:686
  217.2 42.3 %all-to-all-start.3 = ((bf16[16,64,768]{2,1,0:T(8,128)(2,1)}), bf16[16,64,768]{2,1,0:T(8,128)(2,1)S(1)}, u32[]{:S(2)}, u32[]{:S(2)}) async-start(bf16[16,64,768]{2,1,0:T(8,128)(2,1)} %bitcast.17), calls=%async_computation.3 | async-start | bytes 3145728 | tf_op jit(solution)/shard_map/all_to_all | solution.py:967
  249.2 8.3 %collective-permute-start.10 = (bf16[1024,768]{1,0:T(8,128)(2,1)}, bf16[1024,768]{1,0:T(8,128)(2,1)}, u32[]{:S(2)}, u32[]{:S(2)}) collective-permute-start(bf16[1024,768]{1,0:T(8,128)(2,1)} %get-tuple-element.289.dna), channel_id=1, source_target_pairs={{0,16},{16,0},{1,17},{17,1},{2,18},{18,2},{3,19},{19,3},{4,20},{20... | collective-permute-start | bytes 4718600 | tf_op jit(solution)/shard_map/ppermute | solution.py:686
  272.6 5.1 %collective-permute-start.11 = (bf16[1024,768]{1,0:T(8,128)(2,1)}, bf16[1024,768]{1,0:T(8,128)(2,1)}, u32[]{:S(2)}, u32[]{:S(2)}) collective-permute-start(bf16[1024,768]{1,0:T(8,128)(2,1)} %get-tuple-element.310.refs_1_), channel_id=1, source_target_pairs={{0,16},{16,0},{1,17},{17,1},{2,18},{18,2},{3,19},{19,3},{4,20},{20... | collective-permute-start | bytes 4718600 | tf_op jit(solution)/shard_map/ppermute | solution.py:686
  281.0 10.4 %copy-start.31 = (bf16[384,768]{1,0:T(8,128)(2,1)S(1)}, bf16[384,768]{1,0:T(8,128)(2,1)}, u32[]{:S(2)}) copy-start(bf16[384,768]{1,0:T(8,128)(2,1)} %get-tuple-element.301) | copy-start | bytes 1769476
  283.5 36.4 %collective-permute-start.12 = (bf16[768,768]{1,0:T(8,128)(2,1)S(1)}, bf16[768,768]{1,0:T(8,128)(2,1)}, u32[]{:S(2)}, u32[]{:S(2)}) collective-permute-start(bf16[768,768]{1,0:T(8,128)(2,1)S(1)} %fusion.8), channel_id=1, source_target_pairs={{0,1},{1,0},{2,3},{3,2},{4,5},{5,4},{6,7},{7,6},{8,9},{9,8},{10,11... | collective-permute-start | bytes 3538952 | tf_op jit(solution)/shard_map/ppermute | solution.py:817
  284.6 35.3 %collective-permute-start.13 = (bf16[768,768]{1,0:T(8,128)(2,1)S(1)}, bf16[768,768]{1,0:T(8,128)(2,1)}, u32[]{:S(2)}, u32[]{:S(2)}) collective-permute-start(bf16[768,768]{1,0:T(8,128)(2,1)S(1)} %fusion.11), channel_id=1, source_target_pairs={{0,2},{1,3},{2,0},{3,1},{4,6},{5,7},{6,4},{7,5},{8,10},{9,11},{10,... | collective-permute-start | bytes 3538952 | tf_op jit(solution)/shard_map/ppermute | solution.py:817
  287.3 28.5 %collective-permute-start.14 = (bf16[384,768]{1,0:T(8,128)(2,1)S(1)}, bf16[384,768]{1,0:T(8,128)(2,1)}, u32[]{:S(2)}, u32[]{:S(2)}) collective-permute-start(bf16[384,768]{1,0:T(8,128)(2,1)S(1)} %copy-done.30), channel_id=1, source_target_pairs={{0,4},{1,5},{2,6},{3,7},{4,0},{5,1},{6,2},{7,3},{8,12},{9,13},{10,... | collective-permute-start | bytes 1769480 | tf_op jit(solution)/shard_map/ppermute | solution.py:817
  291.4 28.5 %collective-permute-start.15 = (bf16[384,768]{1,0:T(8,128)(2,1)S(1)}, bf16[384,768]{1,0:T(8,128)(2,1)}, u32[]{:S(2)}, u32[]{:S(2)}) collective-permute-start(bf16[384,768]{1,0:T(8,128)(2,1)S(1)} %copy-done.31), channel_id=1, source_target_pairs={{0,8},{1,9},{2,10},{3,11},{4,12},{5,13},{6,14},{7,15},{8,0},{9,1},... | collective-permute-start | bytes 1769480 | tf_op jit(solution)/shard_map/ppermute | solution.py:817
  319.9 26.3 %collective-permute-start.20 = (bf16[1024,768]{1,0:T(8,128)(2,1)}, bf16[1024,768]{1,0:T(8,128)(2,1)}, u32[]{:S(2)}, u32[]{:S(2)}) collective-permute-start(bf16[1024,768]{1,0:T(8,128)(2,1)} %get-tuple-element.367.dna), channel_id=1, source_target_pairs={{0,16},{16,0},{1,17},{17,1},{2,18},{18,2},{3,19},{19,3},{4,20},{20... | collective-permute-start | bytes 4718600 | tf_op jit(solution)/shard_map/ppermute | solution.py:686
  320.5 11.1 %copy-start.32 = (bf16[1024,768]{1,0:T(8,128)(2,1)S(1)}, bf16[1024,768]{1,0:T(8,128)(2,1)}, u32[]{:S(2)}) copy-start(bf16[1024,768]{1,0:T(8,128)(2,1)} %get-tuple-element.342) | copy-start | bytes 4718596
  320.5 11.1 %copy-start.39 = (bf16[1024,384]{1,0:T(8,128)(2,1)S(1)}, bf16[1024,384]{1,0:T(8,128)(2,1)}, u32[]{:S(2)}) copy-start(bf16[1024,384]{1,0:T(8,128)(2,1)} %get-tuple-element.344) | copy-start | bytes 2359300
  327.0 17.9 %collective-permute-start.16 = (bf16[384,768]{1,0:T(8,128)(2,1)}, bf16[384,768]{1,0:T(8,128)(2,1)S(1)}, u32[]{:S(2)}, u32[]{:S(2)}) collective-permute-start(bf16[384,768]{1,0:T(8,128)(2,1)} %get-tuple-element.338), channel_id=1, source_target_pairs={{0,1},{1,0},{2,3},{3,2},{4,5},{5,4},{6,7},{7,6},{8,9},{9,8},{10,11... | collective-permute-start | bytes 1769480 | tf_op jit(solution)/shard_map/ppermute | solution.py:817
  327.9 17.0 %collective-permute-start.17 = (bf16[384,768]{1,0:T(8,128)(2,1)}, bf16[384,768]{1,0:T(8,128)(2,1)S(1)}, u32[]{:S(2)}, u32[]{:S(2)}) collective-permute-start(bf16[384,768]{1,0:T(8,128)(2,1)} %get-tuple-element.339), channel_id=1, source_target_pairs={{0,2},{1,3},{2,0},{3,1},{4,6},{5,7},{6,4},{7,5},{8,10},{9,11},{10,... | collective-permute-start | bytes 1769480 | tf_op jit(solution)/shard_map/ppermute | solution.py:817
  327.9 15.4 %collective-permute-start.18 = (bf16[192,768]{1,0:T(8,128)(2,1)}, bf16[192,768]{1,0:T(8,128)(2,1)S(1)}, u32[]{:S(2)}, u32[]{:S(2)}) collective-permute-start(bf16[192,768]{1,0:T(8,128)(2,1)} %get-tuple-element.340), channel_id=1, source_target_pairs={{0,4},{1,5},{2,6},{3,7},{4,0},{5,1},{6,2},{7,3},{8,12},{9,13},{10,... | collective-permute-start | bytes 884744 | tf_op jit(solution)/shard_map/ppermute | solution.py:817
  328.9 16.1 %collective-permute-start.19 = (bf16[192,768]{1,0:T(8,128)(2,1)}, bf16[192,768]{1,0:T(8,128)(2,1)S(1)}, u32[]{:S(2)}, u32[]{:S(2)}) collective-permute-start(bf16[192,768]{1,0:T(8,128)(2,1)} %get-tuple-element.341), channel_id=1, source_target_pairs={{0,8},{1,9},{2,10},{3,11},{4,12},{5,13},{6,14},{7,15},{8,0},{9,1},... | collective-permute-start | bytes 884744 | tf_op jit(solution)/shard_map/ppermute | solution.py:817
  334.9 10.0 %copy-start.14 = (bf16[384,768]{1,0:T(8,128)(2,1)S(1)}, bf16[384,768]{1,0:T(8,128)(2,1)}, u32[]{:S(2)}) copy-start(bf16[384,768]{1,0:T(8,128)(2,1)} %get-tuple-element.329.refs_0_) | copy-start | bytes 1769476
  334.9 10.0 %copy-start.15 = (bf16[384,768]{1,0:T(8,128)(2,1)S(1)}, bf16[384,768]{1,0:T(8,128)(2,1)}, u32[]{:S(2)}) copy-start(bf16[384,768]{1,0:T(8,128)(2,1)} %get-tuple-element.348.refs_2_) | copy-start | bytes 1769476
  346.2 17.3 %collective-permute-start.21 = (bf16[480,768]{1,0:T(8,128)(2,1)S(1)}, bf16[480,768]{1,0:T(8,128)(2,1)S(1)}, u32[]{:S(2)}, u32[]{:S(2)}) collective-permute-start(bf16[480,768]{1,0:T(8,128)(2,1)S(1)} %get-tuple-element.362), channel_id=1, source_target_pairs={{0,1},{1,0},{2,3},{3,2},{4,5},{5,4},{6,7},{7,6},{8,9},{9,8},{10,11... | collective-permute-start | bytes 2211848 | tf_op jit(solution)/shard_map/ppermute | solution.py:817
  347.1 17.1 %collective-permute-start.22 = (bf16[480,768]{1,0:T(8,128)(2,1)S(1)}, bf16[480,768]{1,0:T(8,128)(2,1)S(1)}, u32[]{:S(2)}, u32[]{:S(2)}) collective-permute-start(bf16[480,768]{1,0:T(8,128)(2,1)S(1)} %get-tuple-element.363), channel_id=1, source_target_pairs={{0,2},{1,3},{2,0},{3,1},{4,6},{5,7},{6,4},{7,5},{8,10},{9,11},{10,... | collective-permute-start | bytes 2211848 | tf_op jit(solution)/shard_map/ppermute | solution.py:817
  348.8 12.9 %collective-permute-start.23 = (bf16[192,768]{1,0:T(8,128)(2,1)S(1)}, bf16[192,768]{1,0:T(8,128)(2,1)S(1)}, u32[]{:S(2)}, u32[]{:S(2)}) collective-permute-start(bf16[192,768]{1,0:T(8,128)(2,1)S(1)} %get-tuple-element.364), channel_id=1, source_target_pairs={{0,4},{1,5},{2,6},{3,7},{4,0},{5,1},{6,2},{7,3},{8,12},{9,13},{10,... | collective-permute-start | bytes 884744 | tf_op jit(solution)/shard_map/ppermute | solution.py:817
  348.8 14.7 %collective-permute-start.24 = (bf16[192,768]{1,0:T(8,128)(2,1)S(1)}, bf16[192,768]{1,0:T(8,128)(2,1)S(1)}, u32[]{:S(2)}, u32[]{:S(2)}) collective-permute-start(bf16[192,768]{1,0:T(8,128)(2,1)S(1)} %get-tuple-element.365), channel_id=1, source_target_pairs={{0,8},{1,9},{2,10},{3,11},{4,12},{5,13},{6,14},{7,15},{8,0},{9,1},... | collective-permute-start | bytes 884744 | tf_op jit(solution)/shard_map/ppermute | solution.py:817
  365.4 10.4 %collective-permute-start.25 = (bf16[240,768]{1,0:T(8,128)(2,1)S(1)}, bf16[240,768]{1,0:T(8,128)(2,1)S(1)}, u32[]{:S(2)}, u32[]{:S(2)}) collective-permute-start(bf16[240,768]{1,0:T(8,128)(2,1)S(1)} %get-tuple-element.386), channel_id=1, source_target_pairs={{0,1},{1,0},{2,3},{3,2},{4,5},{5,4},{6,7},{7,6},{8,9},{9,8},{10,11... | collective-permute-start | bytes 1105928 | tf_op jit(solution)/shard_map/ppermute | solution.py:817
  366.3 9.5 %collective-permute-start.26 = (bf16[240,768]{1,0:T(8,128)(2,1)S(1)}, bf16[240,768]{1,0:T(8,128)(2,1)S(1)}, u32[]{:S(2)}, u32[]{:S(2)}) collective-permute-start(bf16[240,768]{1,0:T(8,128)(2,1)S(1)} %get-tuple-element.387), channel_id=1, source_target_pairs={{0,2},{1,3},{2,0},{3,1},{4,6},{5,7},{6,4},{7,5},{8,10},{9,11},{10,... | collective-permute-start | bytes 1105928 | tf_op jit(solution)/shard_map/ppermute | solution.py:817
  368.1 7.1 %collective-permute-start.27 = (bf16[96,768]{1,0:T(8,128)(2,1)S(1)}, bf16[96,768]{1,0:T(8,128)(2,1)S(1)}, u32[]{:S(2)}, u32[]{:S(2)}) collective-permute-start(bf16[96,768]{1,0:T(8,128)(2,1)S(1)} %get-tuple-element.388), channel_id=1, source_target_pairs={{0,4},{1,5},{2,6},{3,7},{4,0},{5,1},{6,2},{7,3},{8,12},{9,13},{10,... | collective-permute-start | bytes 442376 | tf_op jit(solution)/shard_map/ppermute | solution.py:817
  368.1 7.7 %collective-permute-start.28 = (bf16[96,768]{1,0:T(8,128)(2,1)S(1)}, bf16[96,768]{1,0:T(8,128)(2,1)S(1)}, u32[]{:S(2)}, u32[]{:S(2)}) collective-permute-start(bf16[96,768]{1,0:T(8,128)(2,1)S(1)} %get-tuple-element.389), channel_id=1, source_target_pairs={{0,8},{1,9},{2,10},{3,11},{4,12},{5,13},{6,14},{7,15},{8,0},{9,1},... | collective-permute-start | bytes 442376 | tf_op jit(solution)/shard_map/ppermute | solution.py:817
  376.6 11.6 %collective-permute-start.31 = (bf16[192,768]{1,0:T(8,128)(2,1)S(1)}, bf16[192,768]{1,0:T(8,128)(2,1)S(1)}, u32[]{:S(2)}, u32[]{:S(2)}) collective-permute-start(bf16[192,768]{1,0:T(8,128)(2,1)S(1)} %get-tuple-element.414.refs_2_), channel_id=1, source_target_pairs={{0,4},{1,5},{2,6},{3,7},{4,0},{5,1},{6,2},{7,3},{8,12},{9,13},{10,... | collective-permute-start | bytes 884744 | tf_op jit(solution)/shard_map/ppermute | solution.py:817
  377.1 12.4 %collective-permute-start.32 = (bf16[192,768]{1,0:T(8,128)(2,1)S(1)}, bf16[192,768]{1,0:T(8,128)(2,1)S(1)}, u32[]{:S(2)}, u32[]{:S(2)}) collective-permute-start(bf16[192,768]{1,0:T(8,128)(2,1)S(1)} %get-tuple-element.412.refs_0_), channel_id=1, source_target_pairs={{0,8},{1,9},{2,10},{3,11},{4,12},{5,13},{6,14},{7,15},{8,0},{9,1},... | collective-permute-start | bytes 884744 | tf_op jit(solution)/shard_map/ppermute | solution.py:817
  379.2 5.6 %collective-permute-start.29 = (bf16[64,768]{1,0:T(8,128)(2,1)S(1)}, bf16[64,768]{1,0:T(8,128)(2,1)S(1)}, u32[]{:S(2)}, u32[]{:S(2)}) collective-permute-start(bf16[64,768]{1,0:T(8,128)(2,1)S(1)} %get-tuple-element.418.refs_6_), channel_id=1, source_target_pairs={{0,1},{1,0},{2,3},{3,2},{4,5},{5,4},{6,7},{7,6},{8,9},{9,8},{10,11... | collective-permute-start | bytes 294920 | tf_op jit(solution)/shard_map/ppermute | solution.py:817
  380.4 4.4 collective-permute-start.30
  390.2 13.6 %collective-permute-start.35 = (bf16[240,768]{1,0:T(8,128)(2,1)S(1)}, bf16[240,768]{1,0:T(8,128)(2,1)S(1)}, u32[]{:S(2)}, u32[]{:S(2)}) collective-permute-start(bf16[240,768]{1,0:T(8,128)(2,1)S(1)} %get-tuple-element.429.refs_0_), channel_id=1, source_target_pairs={{0,4},{1,5},{2,6},{3,7},{4,0},{5,1},{6,2},{7,3},{8,12},{9,13},{10,... | collective-permute-start | bytes 1105928 | tf_op jit(solution)/shard_map/ppermute | solution.py:817
  390.3 15.5 %collective-permute-start.36 = (bf16[240,768]{1,0:T(8,128)(2,1)S(1)}, bf16[240,768]{1,0:T(8,128)(2,1)S(1)}, u32[]{:S(2)}, u32[]{:S(2)}) collective-permute-start(bf16[240,768]{1,0:T(8,128)(2,1)S(1)} %get-tuple-element.431.refs_2_), channel_id=1, source_target_pairs={{0,8},{1,9},{2,10},{3,11},{4,12},{5,13},{6,14},{7,15},{8,0},{9,1},... | collective-permute-start | bytes 1105928 | tf_op jit(solution)/shard_map/ppermute | solution.py:817
  391.9 7.0 %collective-permute-start.34 = (bf16[112,768]{1,0:T(8,128)(2,1)S(1)}, bf16[112,768]{1,0:T(8,128)(2,1)S(1)}, u32[]{:S(2)}, u32[]{:S(2)}) collective-permute-start(bf16[112,768]{1,0:T(8,128)(2,1)S(1)} %get-tuple-element.435.refs_6_), channel_id=1, source_target_pairs={{0,2},{1,3},{2,0},{3,1},{4,6},{5,7},{6,4},{7,5},{8,10},{9,11},{10,... | collective-permute-start | bytes 516104 | tf_op jit(solution)/shard_map/ppermute | solution.py:817
  393.7 5.1 %collective-permute-start.33 = (bf16[96,768]{1,0:T(8,128)(2,1)S(1)}, bf16[96,768]{1,0:T(8,128)(2,1)S(1)}, u32[]{:S(2)}, u32[]{:S(2)}) collective-permute-start(bf16[96,768]{1,0:T(8,128)(2,1)S(1)} %get-tuple-element.433.refs_4_), channel_id=1, source_target_pairs={{0,1},{1,0},{2,3},{3,2},{4,5},{5,4},{6,7},{7,6},{8,9},{9,8},{10,11... | collective-permute-start | bytes 442376 | tf_op jit(solution)/shard_map/ppermute | solution.py:817
  406.5 17.4 %collective-permute-start.37 = (bf16[384,768]{1,0:T(8,128)(2,1)S(1)}, bf16[384,768]{1,0:T(8,128)(2,1)S(1)}, u32[]{:S(2)}, u32[]{:S(2)}) collective-permute-start(bf16[384,768]{1,0:T(8,128)(2,1)S(1)} %get-tuple-element.448.refs_2_), channel_id=1, source_target_pairs={{0,1},{1,0},{2,3},{3,2},{4,5},{5,4},{6,7},{7,6},{8,9},{9,8},{10,11... | collective-permute-start | bytes 1769480 | tf_op jit(solution)/shard_map/ppermute | solution.py:817
  407.2 16.7 %collective-permute-start.38 = (bf16[384,768]{1,0:T(8,128)(2,1)S(1)}, bf16[384,768]{1,0:T(8,128)(2,1)S(1)}, u32[]{:S(2)}, u32[]{:S(2)}) collective-permute-start(bf16[384,768]{1,0:T(8,128)(2,1)S(1)} %get-tuple-element.446.refs_0_), channel_id=1, source_target_pairs={{0,2},{1,3},{2,0},{3,1},{4,6},{5,7},{6,4},{7,5},{8,10},{9,11},{10,... | collective-permute-start | bytes 1769480 | tf_op jit(solution)/shard_map/ppermute | solution.py:817
  409.1 14.8 %collective-permute-start.39 = (bf16[256,768]{1,0:T(8,128)(2,1)S(1)}, bf16[256,768]{1,0:T(8,128)(2,1)S(1)}, u32[]{:S(2)}, u32[]{:S(2)}) collective-permute-start(bf16[256,768]{1,0:T(8,128)(2,1)S(1)} %get-tuple-element.452.refs_6_), channel_id=1, source_target_pairs={{0,4},{1,5},{2,6},{3,7},{4,0},{5,1},{6,2},{7,3},{8,12},{9,13},{10,... | collective-permute-start | bytes 1179656 | tf_op jit(solution)/shard_map/ppermute | solution.py:817
  409.1 14.8 %collective-permute-start.40 = (bf16[240,768]{1,0:T(8,128)(2,1)S(1)}, bf16[240,768]{1,0:T(8,128)(2,1)S(1)}, u32[]{:S(2)}, u32[]{:S(2)}) collective-permute-start(bf16[240,768]{1,0:T(8,128)(2,1)S(1)} %get-tuple-element.450.refs_4_), channel_id=1, source_target_pairs={{0,8},{1,9},{2,10},{3,11},{4,12},{5,13},{6,14},{7,15},{8,0},{9,1},... | collective-permute-start | bytes 1105928 | tf_op jit(solution)/shard_map/ppermute | solution.py:817
  424.7 37.0 %copy-start.10 = (bf16[768,768]{1,0:T(8,128)(2,1)}, bf16[768,768]{1,0:T(8,128)(2,1)S(1)}, u32[]{:S(2)}) copy-start(bf16[768,768]{1,0:T(8,128)(2,1)S(1)} %get-tuple-element.472.yp) | copy-start | bytes 3538948
  424.7 34.3 %collective-permute-start.41 = (bf16[768,768]{1,0:T(8,128)(2,1)S(1)}, bf16[768,768]{1,0:T(8,128)(2,1)S(1)}, u32[]{:S(2)}, u32[]{:S(2)}) collective-permute-start(bf16[768,768]{1,0:T(8,128)(2,1)S(1)} %get-tuple-element.470.xp), channel_id=1, source_target_pairs={{0,1},{1,0},{2,3},{3,2},{4,5},{5,4},{6,7},{7,6},{8,9},{9,8},{10,11... | collective-permute-start | bytes 3538952 | tf_op jit(solution)/shard_map/ppermute | solution.py:817
  425.9 33.1 %collective-permute-start.42 = (bf16[768,768]{1,0:T(8,128)(2,1)S(1)}, bf16[768,768]{1,0:T(8,128)(2,1)S(1)}, u32[]{:S(2)}, u32[]{:S(2)}) collective-permute-start(bf16[768,768]{1,0:T(8,128)(2,1)S(1)} %get-tuple-element.472.yp), channel_id=1, source_target_pairs={{0,2},{1,3},{2,0},{3,1},{4,6},{5,7},{6,4},{7,5},{8,10},{9,11},{10,... | collective-permute-start | bytes 3538952 | tf_op jit(solution)/shard_map/ppermute | solution.py:817
  426.7 32.3 %collective-permute-start.44 = (bf16[496,768]{1,0:T(8,128)(2,1)S(1)}, bf16[496,768]{1,0:T(8,128)(2,1)S(1)}, u32[]{:S(2)}, u32[]{:S(2)}) collective-permute-start(bf16[496,768]{1,0:T(8,128)(2,1)S(1)} %get-tuple-element.476.refs_2_.bp), channel_id=1, source_target_pairs={{0,8},{1,9},{2,10},{3,11},{4,12},{5,13},{6,14},{7,15},{8,0},{9,1},... | collective-permute-start | bytes 2285576 | tf_op jit(solution)/shard_map/ppermute | solution.py:817
  427.3 29.1 %collective-permute-start.43 = (bf16[480,768]{1,0:T(8,128)(2,1)S(1)}, bf16[480,768]{1,0:T(8,128)(2,1)S(1)}, u32[]{:S(2)}, u32[]{:S(2)}) collective-permute-start(bf16[480,768]{1,0:T(8,128)(2,1)S(1)} %get-tuple-element.474.refs_0_.ap), channel_id=1, source_target_pairs={{0,4},{1,5},{2,6},{3,7},{4,0},{5,1},{6,2},{7,3},{8,12},{9,13},{10,... | collective-permute-start | bytes 2211848 | tf_op jit(solution)/shard_map/ppermute | solution.py:817
  459.6 10.9 %collective-permute-start.45 = (bf16[192,768]{1,0:T(8,128)(2,1)S(1)}, bf16[192,768]{1,0:T(8,128)(2,1)S(1)}, u32[]{:S(2)}, u32[]{:S(2)}) collective-permute-start(bf16[192,768]{1,0:T(8,128)(2,1)S(1)} %get-tuple-element.484.refs_2_), channel_id=1, source_target_pairs={{0,1},{1,0},{2,3},{3,2},{4,5},{5,4},{6,7},{7,6},{8,9},{9,8},{10,11... | collective-permute-start | bytes 884744 | tf_op jit(solution)/shard_map/ppermute | solution.py:817
  460.3 10.2 %collective-permute-start.46 = (bf16[192,768]{1,0:T(8,128)(2,1)S(1)}, bf16[192,768]{1,0:T(8,128)(2,1)S(1)}, u32[]{:S(2)}, u32[]{:S(2)}) collective-permute-start(bf16[192,768]{1,0:T(8,128)(2,1)S(1)} %get-tuple-element.482.refs_0_), channel_id=1, source_target_pairs={{0,2},{1,3},{2,0},{3,1},{4,6},{5,7},{6,4},{7,5},{8,10},{9,11},{10,... | collective-permute-start | bytes 884744 | tf_op jit(solution)/shard_map/ppermute | solution.py:817
  461.7 12.2 %copy-start.3 = (bf16[1024,768]{1,0:T(8,128)(2,1)S(1)}, bf16[1024,768]{1,0:T(8,128)(2,1)}, u32[]{:S(2)}) copy-start(bf16[1024,768]{1,0:T(8,128)(2,1)} %get-tuple-element.261.xr.refs_4_.xn) | copy-start | bytes 4718596
  471.1 14.4 %collective-permute-start.47 = (bf16[384,768]{1,0:T(8,128)(2,1)S(1)}, bf16[384,768]{1,0:T(8,128)(2,1)S(1)}, u32[]{:S(2)}, u32[]{:S(2)}) collective-permute-start(bf16[384,768]{1,0:T(8,128)(2,1)S(1)} %get-tuple-element.488.xp), channel_id=1, source_target_pairs={{0,1},{1,0},{2,3},{3,2},{4,5},{5,4},{6,7},{7,6},{8,9},{9,8},{10,11... | collective-permute-start | bytes 1769480 | tf_op jit(solution)/shard_map/ppermute | solution.py:817
  471.8 14.4 %collective-permute-start.48 = (bf16[384,768]{1,0:T(8,128)(2,1)S(1)}, bf16[384,768]{1,0:T(8,128)(2,1)S(1)}, u32[]{:S(2)}, u32[]{:S(2)}) collective-permute-start(bf16[384,768]{1,0:T(8,128)(2,1)S(1)} %get-tuple-element.490.yp), channel_id=1, source_target_pairs={{0,2},{1,3},{2,0},{3,1},{4,6},{5,7},{6,4},{7,5},{8,10},{9,11},{10,... | collective-permute-start | bytes 1769480 | tf_op jit(solution)/shard_map/ppermute | solution.py:817
  473.9 1.2 collective-permute-start.49
  473.9 15.5 %copy-start.1 = (s32[1024,1]{0,1:T(1,128)S(1)}, s32[1024,1]{0,1:T(1,128)}, u32[]{:S(2)}) copy-start(s32[1024,1]{0,1:T(1,128)} %param.16) | copy-start | bytes 12292
  (35 other events, 147.6 us)

commit v6 on v5

--- a/solution.py
+++ b/solution.py
@@ -1100,9 +1100,7 @@
             return gather_y(y), stacked
 
         def heavy(dr, dna, dnb, n, g, a, b):
-            kept = grad(n, columns(g, bits[0])), grad(columns(a, bits[1]), b)
-            kept, dr, dna, dnb = lax.optimization_barrier((kept, dr, dna, dnb))
-            return last_attention(dr, dna, dnb), *kept
+            return last_attention(dr, dna, dnb), n, g, a, b
 
         orders = [halving(o) for o in ((1, 2, 4, 8), (2, 1, 8, 4), (4, 8, 1, 2), (8, 4, 2, 1))]
         big = [
@@ -1111,7 +1109,9 @@
             Part(orders[2], qk_send, qk_keep),
             Part(orders[3], vo_send, vo_keep),
         ]
-        last, up_keep, down_keep = advance(bits, big, heavy, (df, dnd, dndr, n2, du, act, df))
+        last, n2, du, act, df = advance(bits, big, heavy, (df, dnd, dndr, n2, du, act, df))
+        up_keep = grad(n2, columns(du, bits[0]))
+        down_keep = grad(columns(act, bits[1]), df)
         da1, dqk1, dv1, dn1, dg1 = last
         dn1r = swap(dn1)
         big[0].kept = (up_keep, 0, up_keep.shape[0])

time: 499 us -> 501 us (level)
    unnamed x91 -> x97, local copies, waits for them, and re-layouts: 10.5 us -> 10.4 us
  transfers between devices with their start and end apart: 54 -> 54, of which waited for: 28 -> 28; matrix products, arithmetic and copies ran while one was open for 9% -> 11% of each run, Pallas kernels for 24% -> 23%
where the time goes in v6:
time: 501 us; the launch traced here: 492 us
  Pallas kernels  206 us (41%)
  waiting for transfers between devices  142 us (28%)
  starting transfers between devices  78.7 us (16%)
  matrix products  45.2 us (9%)
  local copies, waits for them, and re-layouts  15.5 us (3%)
    pallas_call x28, Pallas kernels, call(): pl.pallas_call(kernel, grid_spec=spec, out_shape=outs, compiler_params=pa...  206 us
    ppermute x36, waiting for transfers between devices, advance(): lax.ppermute(v, 'dp', [(i, i ^ s) for i in range(16)])  96.1 us
    dot_general x14, matrix products, mm_tn(): lax.dot_general(a, b, (((0,), (0,)), ((), ())), preferred_element_type=F32)  44.9 us
    ppermute x36, starting transfers between devices, advance(): lax.ppermute(v, 'dp', [(i, i ^ s) for i in range(16)])  44.5 us
    all_to_all x4, waiting for transfers between devices, travel(): return lax.all_to_all(box, 'dp', 0, 0, tiled=True).reshape(slots, d)  35.2 us
    all_to_all x4, starting transfers between devices, travel(): return lax.all_to_all(box, 'dp', 0, 0, tiled=True).reshape(slots, d)  32.2 us
    ppermute x14, waiting for transfers between devices, swap(): return lax.ppermute(v, 'head', SWAP)  10.8 us
    unnamed x97, local copies, waits for them, and re-layouts  10.4 us
  transfers between devices with their start and end apart: 54, of which 28 were waited for; matrix products, arithmetic and copies ran while one was open for 11% of the time, Pallas kernels for 23%

profile of v6, /device:TPU:0, one launch (start us, length us, event | category | flops | bytes accessed | tf_op | source)
XLA Modules:
  0.0 492.2 jit_solution(17018285402426309181)
XLA Ops:
  1.2 1.7 copy.30.refs_5_.refs_6_.segc
  5.2 18.7 %shard_map.237 = (bf16[1024,768]{1,0:T(8,128)(2,1)}, bf16[3,1024,384]{2,1,0:T(8,128)(2,1)}, bf16[1024,384]{1,0:T(8,128)(2,1)}, f32[1024,128]{1,0:T(8,128)}, bf16[1024,768]{1,0:T(8,128)(2,1)}) custom-call(s32[1]{0:T(128)} %bitcast.h_ref, bf16[512,768]{1,0:T(8,128)(2,1)} %xo.1, bf16[512,768]{1,0:T(8,128)(2,1)} %copy-done.12, ...), custom_call_target="tpu_custom_call" | custom-call | flops 8053063680 | bytes 15728640 | tf_op jit(solution)/shard_map/pallas_call | solution.py:390
  25.1 2.6 shard_map.238
  27.7 15.7 %shard_map.239 = (bf16[1024,768]{1,0:T(8,128)(2,1)}, bf16[1024,768]{1,0:T(8,128)(2,1)}, bf16[1024,1536]{1,0:T(8,128)(2,1)}, bf16[1024,1536]{1,0:T(8,128)(2,1)}, bf16[1024,768]{1,0:T(8,128)(2,1)}) custom-call(s32[1]{0:T(128)} %bitcast.h_ref, bf16[512,768]{1,0:T(8,128)(2,1)} %xo.1, bf16[512,768]{1,0:T(8,128)(2,1)} %copy-done.12, ...), custom_call_target="tpu_custom_call" | custom-call | flops 4831838208 | bytes 20447232 | tf_op jit(solution)/shard_map/pallas_call | solution.py:390
  43.7 8.2 %all-to-all-start.1 = ((bf16[16,64,768]{2,1,0:T(8,128)(2,1)}), bf16[16,64,768]{2,1,0:T(8,128)(2,1)}, u32[]{:S(2)}, u32[]{:S(2)}) async-start(bf16[16,64,768]{2,1,0:T(8,128)(2,1)} %bitcast.10), calls=%async_computation.1 | async-start | bytes 3145728 | tf_op jit(solution)/shard_map/all_to_all | solution.py:967
  53.0 19.3 %shard_map.240 = (bf16[1024,768]{1,0:T(8,128)(2,1)}, bf16[1024,768]{1,0:T(8,128)(2,1)}, bf16[3,1024,384]{2,1,0:T(8,128)(2,1)}, bf16[1024,384]{1,0:T(8,128)(2,1)}...) custom-call(s32[1]{0:T(128)} %bitcast.h_ref, bf16[1024,768]{1,0:T(8,128)(2,1)} %get-tuple-element.256.refs_0_.refs_3_, ...), custom_call_target="tpu_custom_call" | custom-call | flops 8053063680 | bytes 15728640 | tf_op jit(solution)/shard_map/pallas_call | solution.py:390
  72.4 3.6 collective-permute-done.4.pb.refs_6_
  78.8 2.8 shard_map.241
  82.8 3.4 all-to-all-done.1
  86.2 8.3 %all-to-all-start = ((bf16[16,64,768]{2,1,0:T(8,128)(2,1)}), bf16[16,64,768]{2,1,0:T(8,128)(2,1)S(1)}, u32[]{:S(2)}, u32[]{:S(2)}) async-start(bf16[16,64,768]{2,1,0:T(8,128)(2,1)} %bitcast.8), calls=%async_computation | async-start | bytes 3145728 | tf_op jit(solution)/shard_map/all_to_all | solution.py:967
  94.4 8.2 %shard_map.242.refs_9_ = bf16[6,1024,1024]{2,1,0:T(8,128)(2,1)} custom-call(bf16[3,1024,384]{2,1,0:T(8,128)(2,1)} %get-tuple-element.263.qr.kf.refs_5_.refs_6_.refs_7_, bf16[3,1024,384]{2,1,0:T(8,128)(2,1)} %get-tuple-element.263.qr.kf.refs_5_.refs_6_.refs_7_, f32[1024,128]{1,0:T(8,128)} %get-tuple-element.264.lser, s32[1024,1]{1,0:T(8,128)} %copy.30.refs_5_.refs_6_.segc, ...), custom_call_target="tpu_custom_call" | custom-call | flops 1610612736 | bytes 12582912 | tf_op jit(solution)/shard_map/pallas_call | solution.py:390
  102.6 8.2 %shard_map.243.refs_12_ = bf16[6,1024,1024]{2,1,0:T(8,128)(2,1)} custom-call(bf16[3,1024,384]{2,1,0:T(8,128)(2,1)} %get-tuple-element.265.qr.kf.refs_8_.refs_9_.refs_10_, bf16[3,1024,384]{2,1,0:T(8,128)(2,1)} %get-tuple-element.265.qr.kf.refs_8_.refs_9_.refs_10_, f32[1024,128]{1,0:T(8,128)} %get-tuple-element.266.lser, s32[1024,1]{1,0:T(8,128)} %copy.30.refs_5_.refs_6_.segc, ...), custom_call_target="tpu_custom_call" | custom-call | flops 1610612736 | bytes 12582912 | tf_op jit(solution)/shard_map/pallas_call | solution.py:390
  110.8 17.1 %all-to-all-done = bf16[16,64,768]{2,1,0:T(8,128)(2,1)S(1)} async-done(((bf16[16,64,768]{2,1,0:T(8,128)(2,1)}), bf16[16,64,768]{2,1,0:T(8,128)(2,1)S(1)}, u32[]{:S(2)}, u32[]{:S(2)}) %all-to-all-start) | async-done | bytes 1572896 | tf_op jit(solution)/shard_map/all_to_all | solution.py:967
  127.9 3.4 collective-permute-done.5.mp
  132.5 34.1 %shard_map.244 = (bf16[1024,768]{1,0:T(8,128)(2,1)}, bf16[1024,768]{1,0:T(8,128)(2,1)}, bf16[1024,768]{1,0:T(8,128)(2,1)}, bf16[1024,768]{1,0:T(8,128)(2,1)}, bf...) custom-call(bf16[1024,768]{1,0:T(8,128)(2,1)} %bitcast.46, ...), custom_call_target="tpu_custom_call" | custom-call | flops 19327352832 | bytes 31457280 | tf_op jit(solution)/shard_map/pallas_call | solution.py:390
  166.8 3.5 collective-permute-done.7.b
  173.2 7.7 %all-to-all-start.2 = ((bf16[16,64,768]{2,1,0:T(8,128)(2,1)}), bf16[16,64,768]{2,1,0:T(8,128)(2,1)S(1)}, u32[]{:S(2)}, u32[]{:S(2)}) async-start(bf16[16,64,768]{2,1,0:T(8,128)(2,1)} %bitcast.12), calls=%async_computation.2 | async-start | bytes 3145728 | tf_op jit(solution)/shard_map/all_to_all | solution.py:967
  181.5 9.7 %convolution_bitcast_fusion = f32[1,1536,768]{2,1,0:T(8,128)} fusion(bf16[2048,1536]{1,0:T(8,128)(2,1)} %get-tuple-element.273, bf16[2048,768]{1,0:T(8,128)(2,1)} %get-tuple-element.274), kind=kOutput, calls=%fused_computation | convolution fusion | flops 4831838208 | bytes 14155776 | tf_op jit(solution)/shard_map/dot_general | solution.py:30
  191.3 9.6 %convolution_bitcast_fusion.1 = f32[1,768,1536]{2,1,0:T(8,128)} fusion(bf16[2048,768]{1,0:T(8,128)(2,1)S(1)} %copy-done.43, bf16[2048,1536]{1,0:T(8,128)(2,1)} %get-tuple-element.272), kind=kOutput, calls=%fused_computation.1 | convolution fusion | flops 4831838208 | bytes 14155776 | tf_op jit(solution)/shard_map/dot_general | solution.py:30
  202.4 12.8 %all-to-all-done.2 = bf16[16,64,768]{2,1,0:T(8,128)(2,1)S(1)} async-done(((bf16[16,64,768]{2,1,0:T(8,128)(2,1)}), bf16[16,64,768]{2,1,0:T(8,128)(2,1)S(1)}, u32[]{:S(2)}, u32[]{:S(2)}) %all-to-all-start.2) | async-done | bytes 1572896 | tf_op jit(solution)/shard_map/all_to_all | solution.py:967
  215.2 2.1 shard_map.247.refs_2_
  217.2 8.0 %all-to-all-start.3 = ((bf16[16,64,768]{2,1,0:T(8,128)(2,1)}), bf16[16,64,768]{2,1,0:T(8,128)(2,1)S(1)}, u32[]{:S(2)}, u32[]{:S(2)}) async-start(bf16[16,64,768]{2,1,0:T(8,128)(2,1)} %bitcast.17), calls=%async_computation.3 | async-start | bytes 3145728 | tf_op jit(solution)/shard_map/all_to_all | solution.py:967
  225.3 23.9 %shard_map.248 = (bf16[1024,768]{1,0:T(8,128)(2,1)}, bf16[1024,768]{1,0:T(8,128)(2,1)}, bf16[1024,384]{1,0:T(8,128)(2,1)}, bf16[1024,768]{1,0:T(8,128)(2,1)}, f32[8,768]{1,0:T(8,128)}) custom-call(s32[1]{0:T(128)} %bitcast.h_ref, bf16[512,768]{1,0:T(8,128)(2,1)} %refs_0_.3, bf16[512,768]{1,0:T(8,128)(2,1)} %collective-permute-done.3.refs_1_, ...), custom_call_target="tpu_custom_call" | custom-call | flops 12884901888 | bytes 15728640 | tf_op jit(solution)/shard_map/pallas_call | solution.py:390
  249.5 2.8 convolution_convert_fusion.5
  252.3 1.6 convolution_convert_fusion.6.refs_8_.refs_9_
  254.0 1.6 convolution_convert_fusion.7
  255.6 2.0 broadcast_select_fusion.2
  257.6 1.9 all-to-all-done.3
  259.5 13.1 %shard_map.249 = (bf16[1024,768]{1,0:T(8,128)(2,1)}, bf16[1024,1536]{1,0:T(8,128)(2,1)}, bf16[1024,768]{1,0:T(8,128)(2,1)}, f32[8,768]{1,0:T(8,128)}) custom-call(bf16[1024,768]{1,0:T(8,128)(2,1)} %get-tuple-element.285.drr, bf16[1024,768]{1,0:T(8,128)(2,1)} %get-tuple-element.286.dna, bf16[1024,768]{1,0:T(8,128)(2,1)} %collective-permute-done.10.dnb, ...), custom_call_target="tpu_custom_call" | custom-call | flops 4831838208 | bytes 20447232 | tf_op jit(solution)/shard_map/pallas_call | solution.py:390
  273.3 4.5 fusion.11
  277.8 2.5 fusion.8
  281.4 2.7 collective-permute-start.13
  284.1 4.1 collective-permute-start.14
  289.0 23.3 %shard_map.250 = (bf16[1024,768]{1,0:T(8,128)(2,1)}, bf16[1024,768]{1,0:T(8,128)(2,1)}, bf16[1024,384]{1,0:T(8,128)(2,1)}, bf16[1024,768]{1,0:T(8,128)(2,1)}, f32[8,768]{1,0:T(8,128)}) custom-call(s32[1]{0:T(128)} %bitcast.h_ref, bf16[1024,768]{1,0:T(8,128)(2,1)} %get-tuple-element.317.refs_0_, bf16[1024,768]{1,0:T(8,128)(2,1)} %get-tuple-element.300.refs_1_, ...), custom_call_target="tpu_custom_call" | custom-call | flops 12884901888 | bytes 15728640 | tf_op jit(solution)/shard_map/pallas_call | solution.py:390
  312.3 4.5 collective-permute-done.15.refs_14_.refs_15_
  317.6 4.6 fusion.17.refs_4_.refs_5_
  322.2 2.5 fusion.14.refs_0_.refs_1_
  324.7 6.3 %shard_map.251 = (bf16[384,768]{1,0:T(8,128)(2,1)}, bf16[384,768]{1,0:T(8,128)(2,1)}, bf16[384,768]{1,0:T(8,128)(2,1)}, bf16[384,768]{1,0:T(8,128)(2,1)}, bf16[1...) custom-call(s32[4]{0:T(128)} %pad_add_fusion.bits, ...), custom_call_target="tpu_custom_call" | custom-call | flops 14155776 | bytes 14155776 | tf_op jit(solution)/shard_map/pallas_call | solution.py:390
  332.7 2.8 collective-permute-start.19
  339.7 7.4 %collective-permute-done.18.refs_7_ = bf16[192,768]{1,0:T(8,128)(2,1)S(1)} collective-permute-done((bf16[192,768]{1,0:T(8,128)(2,1)}, bf16[192,768]{1,0:T(8,128)(2,1)S(1)}, u32[]{:S(2)}, u32[]{:S(2)}) %collective-permute-start.18) | collective-permute-done | bytes 294944 | tf_op jit(solution)/shard_map/ppermute | solution.py:817
  350.8 1.7 collective-permute-start.22
  352.6 2.0 collective-permute-start.24
  354.6 3.6 shard_map.253
  358.2 7.0 %collective-permute-done.23.refs_1_ = bf16[192,768]{1,0:T(8,128)(2,1)S(1)} collective-permute-done((bf16[192,768]{1,0:T(8,128)(2,1)S(1)}, bf16[192,768]{1,0:T(8,128)(2,1)S(1)}, u32[]{:S(2)}, u32[]{:S(2)}) %collective-permute-start.23) | collective-permute-done | bytes 294944 | tf_op jit(solution)/shard_map/ppermute | solution.py:817
  365.2 1.8 collective-permute-done.24.refs_2_
  369.4 1.7 collective-permute-start.26
  373.3 2.4 shard_map.255
  375.7 2.5 collective-permute-done.27.refs_2_
  380.2 2.5 collective-permute-start.32
  384.3 4.0 collective-permute-done.30.refs_5_
  388.3 2.9 collective-permute-done.31.refs_3_
  393.3 2.1 collective-permute-start.36
  397.9 3.9 collective-permute-done.33.refs_5_
  401.8 5.1 %collective-permute-done.35.refs_1_ = bf16[240,768]{1,0:T(8,128)(2,1)S(1)} collective-permute-done((bf16[240,768]{1,0:T(8,128)(2,1)S(1)}, bf16[240,768]{1,0:T(8,128)(2,1)S(1)}, u32[]{:S(2)}, u32[]{:S(2)}) %collective-permute-start.35) | collective-permute-done | bytes 368672 | tf_op jit(solution)/shard_map/ppermute | solution.py:817
  406.9 1.9 collective-permute-done.36.refs_3_
  410.8 1.8 collective-permute-start.38
  412.6 1.9 collective-permute-start.40
  414.5 12.4 %collective-permute-done.40.refs_5_ = bf16[240,768]{1,0:T(8,128)(2,1)S(1)} collective-permute-done((bf16[240,768]{1,0:T(8,128)(2,1)S(1)}, bf16[240,768]{1,0:T(8,128)(2,1)S(1)}, u32[]{:S(2)}, u32[]{:S(2)}) %collective-permute-start.40) | collective-permute-done | bytes 368672 | tf_op jit(solution)/shard_map/ppermute | solution.py:817
  430.5 1.7 collective-permute-start.43
  432.2 26.5 %collective-permute-done.43.refs_1_.ag = bf16[480,768]{1,0:T(8,128)(2,1)S(1)} collective-permute-done((bf16[480,768]{1,0:T(8,128)(2,1)S(1)}, bf16[480,768]{1,0:T(8,128)(2,1)S(1)}, u32[]{:S(2)}, u32[]{:S(2)}) %collective-permute-start.43) | collective-permute-done | bytes 737312 | tf_op jit(solution)/shard_map/ppermute | solution.py:817
  458.7 2.7 collective-permute-done.44.refs_3_.bg
  464.0 8.7 %shard_map.262 = (f32[768,1536]{1,0:T(8,128)}, f32[1536,768]{1,0:T(8,128)}, f32[3,768,384]{2,1,0:T(8,128)}, f32[384,768]{1,0:T(8,128)}) custom-call(s32[4]{0:T(128)S(1)} %copy-done.18, bf16[768,768]{1,0:T(8,128)(2,1)S(1)} %get-tuple-element.464.xp, bf16[768,768]{1,0:T(8,128)(2,1)} %copy-done.30, bf16[768,768]{1,0:T(8,128)(2,1)} %copy-done.10, ...), custom_call_target="tpu_custom_call" | custom-call | flops 21872640 | bytes 21872640 | tf_op jit(solution)/shard_map/pallas_call | solution.py:390
  479.5 8.5 %collective-permute-done.47.xg = bf16[384,768]{1,0:T(8,128)(2,1)S(1)} collective-permute-done((bf16[384,768]{1,0:T(8,128)(2,1)S(1)}, bf16[384,768]{1,0:T(8,128)(2,1)S(1)}, u32[]{:S(2)}, u32[]{:S(2)}) %collective-permute-start.47) | collective-permute-done | bytes 589856 | tf_op jit(solution)/shard_map/ppermute | solution.py:817
  488.5 3.2 shard_map.264
  (198 shorter events, 57.1 us)
Async XLA Ops:
  0.6 23.4 %copy-start = (s32[1024,1]{0,1:T(1,128)S(1)}, s32[1024,1]{0,1:T(1,128)}, u32[]{:S(2)}) copy-start(s32[1024,1]{0,1:T(1,128)} %param.16) | copy-start | bytes 12292
  0.7 3.7 collective-permute-start
  4.3 71.7 %copy-start.23 = (f32[1,768]{1,0:T(1,128)}, f32[1,768]{1,0:T(1,128)S(1)}, u32[]{:S(2)}) copy-start(f32[1,768]{1,0:T(1,128)S(1)} %get-tuple-element.505.g.refs_7_) | copy-start | bytes 9220
  23.9 3.8 collective-permute-start.1
  43.4 8.4 %collective-permute-start.2 = (bf16[1024,768]{1,0:T(8,128)(2,1)}, bf16[1024,768]{1,0:T(8,128)(2,1)S(1)}, u32[]{:S(2)}, u32[]{:S(2)}) collective-permute-start(bf16[1024,768]{1,0:T(8,128)(2,1)} %get-tuple-element.257.refs_1_), channel_id=1, source_target_pairs={{0,16},{16,0},{1,17},{17,1},{2,18},{18,2},{3,19},{19,3},{4,20},{20... | collective-permute-start | bytes 4718600 | tf_op jit(solution)/shard_map/ppermute | solution.py:686
  43.7 42.5 %all-to-all-start.1 = ((bf16[16,64,768]{2,1,0:T(8,128)(2,1)}), bf16[16,64,768]{2,1,0:T(8,128)(2,1)}, u32[]{:S(2)}, u32[]{:S(2)}) async-start(bf16[16,64,768]{2,1,0:T(8,128)(2,1)} %bitcast.10), calls=%async_computation.1 | async-start | bytes 3145728 | tf_op jit(solution)/shard_map/all_to_all | solution.py:967
  72.3 3.7 collective-permute-start.4
  86.2 41.7 %all-to-all-start = ((bf16[16,64,768]{2,1,0:T(8,128)(2,1)}), bf16[16,64,768]{2,1,0:T(8,128)(2,1)S(1)}, u32[]{:S(2)}, u32[]{:S(2)}) async-start(bf16[16,64,768]{2,1,0:T(8,128)(2,1)} %bitcast.8), calls=%async_computation | async-start | bytes 3145728 | tf_op jit(solution)/shard_map/all_to_all | solution.py:967
  110.8 17.1 %collective-permute-start.6 = (bf16[1024,768]{1,0:T(8,128)(2,1)}, bf16[1024,768]{1,0:T(8,128)(2,1)}, u32[]{:S(2)}, u32[]{:S(2)}) collective-permute-start(bf16[1024,768]{1,0:T(8,128)(2,1)} %bitcast.11.go), channel_id=1, source_target_pairs={{0,16},{16,0},{1,17},{17,1},{2,18},{18,2},{3,19},{19,3},{4,20},{20... | collective-permute-start | bytes 4718600 | tf_op jit(solution)/shard_map/ppermute | solution.py:686
  127.9 3.4 collective-permute-start.5
  166.6 3.7 collective-permute-start.7
  173.2 41.9 %all-to-all-start.2 = ((bf16[16,64,768]{2,1,0:T(8,128)(2,1)}), bf16[16,64,768]{2,1,0:T(8,128)(2,1)S(1)}, u32[]{:S(2)}, u32[]{:S(2)}) async-start(bf16[16,64,768]{2,1,0:T(8,128)(2,1)} %bitcast.12), calls=%async_computation.2 | async-start | bytes 3145728 | tf_op jit(solution)/shard_map/all_to_all | solution.py:967
  180.9 44.3 %collective-permute-start.3 = (bf16[512,768]{1,0:T(8,128)(2,1)}, bf16[512,768]{1,0:T(8,128)(2,1)}, u32[]{:S(2)}, u32[]{:S(2)}) collective-permute-start(bf16[512,768]{1,0:T(8,128)(2,1)} %refs_0_.3), channel_id=1, source_target_pairs={{0,16},{16,0},{1,17},{17,1},{2,18},{18,2},{3,19},{19,3},{4,20},{20... | collective-permute-start | bytes 2359304 | tf_op jit(solution)/shard_map/ppermute | solution.py:686
  181.0 19.9 %collective-permute-start.8 = (bf16[1024,768]{1,0:T(8,128)(2,1)}, bf16[1024,768]{1,0:T(8,128)(2,1)S(1)}, u32[]{:S(2)}, u32[]{:S(2)}) collective-permute-start(bf16[1024,768]{1,0:T(8,128)(2,1)} %get-tuple-element.276), channel_id=1, source_target_pairs={{0,16},{16,0},{1,17},{17,1},{2,18},{18,2},{3,19},{19,3},{4,20},{20... | collective-permute-start | bytes 4718600 | tf_op jit(solution)/shard_map/ppermute | solution.py:686
  217.2 8.0 %collective-permute-start.9 = (bf16[512,768]{1,0:T(8,128)(2,1)}, bf16[512,768]{1,0:T(8,128)(2,1)}, u32[]{:S(2)}, u32[]{:S(2)}) collective-permute-start(bf16[512,768]{1,0:T(8,128)(2,1)} %shard_map.247.refs_2_), channel_id=1, source_target_pairs={{0,16},{16,0},{1,17},{17,1},{2,18},{18,2},{3,19},{19,3},{4,20},{20... | collective-permute-start | bytes 2359304 | tf_op jit(solution)/shard_map/ppermute | solution.py:686
  217.2 42.3 %all-to-all-start.3 = ((bf16[16,64,768]{2,1,0:T(8,128)(2,1)}), bf16[16,64,768]{2,1,0:T(8,128)(2,1)S(1)}, u32[]{:S(2)}, u32[]{:S(2)}) async-start(bf16[16,64,768]{2,1,0:T(8,128)(2,1)} %bitcast.17), calls=%async_computation.3 | async-start | bytes 3145728 | tf_op jit(solution)/shard_map/all_to_all | solution.py:967
  249.2 8.4 %collective-permute-start.10 = (bf16[1024,768]{1,0:T(8,128)(2,1)}, bf16[1024,768]{1,0:T(8,128)(2,1)}, u32[]{:S(2)}, u32[]{:S(2)}) collective-permute-start(bf16[1024,768]{1,0:T(8,128)(2,1)} %get-tuple-element.286.dna), channel_id=1, source_target_pairs={{0,16},{16,0},{1,17},{17,1},{2,18},{18,2},{3,19},{19,3},{4,20},{20... | collective-permute-start | bytes 4718600 | tf_op jit(solution)/shard_map/ppermute | solution.py:686
  272.6 7.7 %collective-permute-start.11 = (bf16[1024,768]{1,0:T(8,128)(2,1)}, bf16[1024,768]{1,0:T(8,128)(2,1)}, u32[]{:S(2)}, u32[]{:S(2)}) collective-permute-start(bf16[1024,768]{1,0:T(8,128)(2,1)} %get-tuple-element.300.refs_1_), channel_id=1, source_target_pairs={{0,16},{16,0},{1,17},{17,1},{2,18},{18,2},{3,19},{19,3},{4,20},{20... | collective-permute-start | bytes 4718600 | tf_op jit(solution)/shard_map/ppermute | solution.py:686
  280.3 36.6 %collective-permute-start.12 = (bf16[768,768]{1,0:T(8,128)(2,1)}, bf16[768,768]{1,0:T(8,128)(2,1)S(1)}, u32[]{:S(2)}, u32[]{:S(2)}) collective-permute-start(bf16[768,768]{1,0:T(8,128)(2,1)} %fusion.8), channel_id=1, source_target_pairs={{0,1},{1,0},{2,3},{3,2},{4,5},{5,4},{6,7},{7,6},{8,9},{9,8},{10,11... | collective-permute-start | bytes 3538952 | tf_op jit(solution)/shard_map/ppermute | solution.py:817
  281.4 35.4 %collective-permute-start.13 = (bf16[768,768]{1,0:T(8,128)(2,1)}, bf16[768,768]{1,0:T(8,128)(2,1)S(1)}, u32[]{:S(2)}, u32[]{:S(2)}) collective-permute-start(bf16[768,768]{1,0:T(8,128)(2,1)} %fusion.11), channel_id=1, source_target_pairs={{0,2},{1,3},{2,0},{3,1},{4,6},{5,7},{6,4},{7,5},{8,10},{9,11},{10,... | collective-permute-start | bytes 3538952 | tf_op jit(solution)/shard_map/ppermute | solution.py:817
  284.1 28.2 %collective-permute-start.14 = (bf16[384,768]{1,0:T(8,128)(2,1)S(1)}, bf16[384,768]{1,0:T(8,128)(2,1)S(1)}, u32[]{:S(2)}, u32[]{:S(2)}) collective-permute-start(bf16[384,768]{1,0:T(8,128)(2,1)S(1)} %copy-done.34), channel_id=1, source_target_pairs={{0,4},{1,5},{2,6},{3,7},{4,0},{5,1},{6,2},{7,3},{8,12},{9,13},{10,... | collective-permute-start | bytes 1769480 | tf_op jit(solution)/shard_map/ppermute | solution.py:817
  288.2 28.6 %collective-permute-start.15 = (bf16[384,768]{1,0:T(8,128)(2,1)}, bf16[384,768]{1,0:T(8,128)(2,1)S(1)}, u32[]{:S(2)}, u32[]{:S(2)}) collective-permute-start(bf16[384,768]{1,0:T(8,128)(2,1)} %get-tuple-element.298), channel_id=1, source_target_pairs={{0,8},{1,9},{2,10},{3,11},{4,12},{5,13},{6,14},{7,15},{8,0},{9,1},... | collective-permute-start | bytes 1769480 | tf_op jit(solution)/shard_map/ppermute | solution.py:817
  312.3 9.9 %copy-start.27 = (bf16[384,768]{1,0:T(8,128)(2,1)}, bf16[384,768]{1,0:T(8,128)(2,1)S(1)}, u32[]{:S(2)}) copy-start(bf16[384,768]{1,0:T(8,128)(2,1)S(1)} %collective-permute-done.14.refs_10_.refs_11_) | copy-start | bytes 1769476
  317.6 32.3 %collective-permute-start.20 = (bf16[1024,768]{1,0:T(8,128)(2,1)}, bf16[1024,768]{1,0:T(8,128)(2,1)S(1)}, u32[]{:S(2)}, u32[]{:S(2)}) collective-permute-start(bf16[1024,768]{1,0:T(8,128)(2,1)} %get-tuple-element.361.dna), channel_id=1, source_target_pairs={{0,16},{16,0},{1,17},{17,1},{2,18},{18,2},{3,19},{19,3},{4,20},{20... | collective-permute-start | bytes 4718600 | tf_op jit(solution)/shard_map/ppermute | solution.py:686
  324.7 10.8 %copy-start.35 = (bf16[1024,768]{1,0:T(8,128)(2,1)S(1)}, bf16[1024,768]{1,0:T(8,128)(2,1)}, u32[]{:S(2)}) copy-start(bf16[1024,768]{1,0:T(8,128)(2,1)} %get-tuple-element.336) | copy-start | bytes 4718596
  324.7 10.8 %copy-start.42 = (bf16[1024,384]{1,0:T(8,128)(2,1)S(1)}, bf16[1024,384]{1,0:T(8,128)(2,1)}, u32[]{:S(2)}) copy-start(bf16[1024,384]{1,0:T(8,128)(2,1)} %get-tuple-element.338) | copy-start | bytes 2359300
  331.0 17.6 %collective-permute-start.16 = (bf16[384,768]{1,0:T(8,128)(2,1)}, bf16[384,768]{1,0:T(8,128)(2,1)S(1)}, u32[]{:S(2)}, u32[]{:S(2)}) collective-permute-start(bf16[384,768]{1,0:T(8,128)(2,1)} %get-tuple-element.332), channel_id=1, source_target_pairs={{0,1},{1,0},{2,3},{3,2},{4,5},{5,4},{6,7},{7,6},{8,9},{9,8},{10,11... | collective-permute-start | bytes 1769480 | tf_op jit(solution)/shard_map/ppermute | solution.py:817
  331.9 16.8 %collective-permute-start.17 = (bf16[384,768]{1,0:T(8,128)(2,1)}, bf16[384,768]{1,0:T(8,128)(2,1)S(1)}, u32[]{:S(2)}, u32[]{:S(2)}) collective-permute-start(bf16[384,768]{1,0:T(8,128)(2,1)} %get-tuple-element.333), channel_id=1, source_target_pairs={{0,2},{1,3},{2,0},{3,1},{4,6},{5,7},{6,4},{7,5},{8,10},{9,11},{10,... | collective-permute-start | bytes 1769480 | tf_op jit(solution)/shard_map/ppermute | solution.py:817
  332.1 14.9 %collective-permute-start.18 = (bf16[192,768]{1,0:T(8,128)(2,1)}, bf16[192,768]{1,0:T(8,128)(2,1)S(1)}, u32[]{:S(2)}, u32[]{:S(2)}) collective-permute-start(bf16[192,768]{1,0:T(8,128)(2,1)} %get-tuple-element.334), channel_id=1, source_target_pairs={{0,4},{1,5},{2,6},{3,7},{4,0},{5,1},{6,2},{7,3},{8,12},{9,13},{10,... | collective-permute-start | bytes 884744 | tf_op jit(solution)/shard_map/ppermute | solution.py:817
  332.7 16.0 %collective-permute-start.19 = (bf16[192,768]{1,0:T(8,128)(2,1)}, bf16[192,768]{1,0:T(8,128)(2,1)S(1)}, u32[]{:S(2)}, u32[]{:S(2)}) collective-permute-start(bf16[192,768]{1,0:T(8,128)(2,1)} %get-tuple-element.335), channel_id=1, source_target_pairs={{0,8},{1,9},{2,10},{3,11},{4,12},{5,13},{6,14},{7,15},{8,0},{9,1},... | collective-permute-start | bytes 884744 | tf_op jit(solution)/shard_map/ppermute | solution.py:817
  338.8 9.8 %copy-start.14 = (bf16[384,768]{1,0:T(8,128)(2,1)S(1)}, bf16[384,768]{1,0:T(8,128)(2,1)}, u32[]{:S(2)}) copy-start(bf16[384,768]{1,0:T(8,128)(2,1)} %get-tuple-element.323.refs_0_) | copy-start | bytes 1769476
  338.8 9.8 %copy-start.15 = (bf16[384,768]{1,0:T(8,128)(2,1)S(1)}, bf16[384,768]{1,0:T(8,128)(2,1)}, u32[]{:S(2)}) copy-start(bf16[384,768]{1,0:T(8,128)(2,1)} %get-tuple-element.342.refs_2_) | copy-start | bytes 1769476
  349.9 17.1 %collective-permute-start.21 = (bf16[480,768]{1,0:T(8,128)(2,1)S(1)}, bf16[480,768]{1,0:T(8,128)(2,1)S(1)}, u32[]{:S(2)}, u32[]{:S(2)}) collective-permute-start(bf16[480,768]{1,0:T(8,128)(2,1)S(1)} %get-tuple-element.356), channel_id=1, source_target_pairs={{0,1},{1,0},{2,3},{3,2},{4,5},{5,4},{6,7},{7,6},{8,9},{9,8},{10,11... | collective-permute-start | bytes 2211848 | tf_op jit(solution)/shard_map/ppermute | solution.py:817
  350.8 16.9 %collective-permute-start.22 = (bf16[480,768]{1,0:T(8,128)(2,1)S(1)}, bf16[480,768]{1,0:T(8,128)(2,1)S(1)}, u32[]{:S(2)}, u32[]{:S(2)}) collective-permute-start(bf16[480,768]{1,0:T(8,128)(2,1)S(1)} %get-tuple-element.357), channel_id=1, source_target_pairs={{0,2},{1,3},{2,0},{3,1},{4,6},{5,7},{6,4},{7,5},{8,10},{9,11},{10,... | collective-permute-start | bytes 2211848 | tf_op jit(solution)/shard_map/ppermute | solution.py:817
  352.6 12.7 %collective-permute-start.23 = (bf16[192,768]{1,0:T(8,128)(2,1)S(1)}, bf16[192,768]{1,0:T(8,128)(2,1)S(1)}, u32[]{:S(2)}, u32[]{:S(2)}) collective-permute-start(bf16[192,768]{1,0:T(8,128)(2,1)S(1)} %get-tuple-element.358), channel_id=1, source_target_pairs={{0,4},{1,5},{2,6},{3,7},{4,0},{5,1},{6,2},{7,3},{8,12},{9,13},{10,... | collective-permute-start | bytes 884744 | tf_op jit(solution)/shard_map/ppermute | solution.py:817
  352.6 14.5 %collective-permute-start.24 = (bf16[192,768]{1,0:T(8,128)(2,1)S(1)}, bf16[192,768]{1,0:T(8,128)(2,1)S(1)}, u32[]{:S(2)}, u32[]{:S(2)}) collective-permute-start(bf16[192,768]{1,0:T(8,128)(2,1)S(1)} %get-tuple-element.359), channel_id=1, source_target_pairs={{0,8},{1,9},{2,10},{3,11},{4,12},{5,13},{6,14},{7,15},{8,0},{9,1},... | collective-permute-start | bytes 884744 | tf_op jit(solution)/shard_map/ppermute | solution.py:817
  369.0 9.9 %collective-permute-start.25 = (bf16[240,768]{1,0:T(8,128)(2,1)S(1)}, bf16[240,768]{1,0:T(8,128)(2,1)S(1)}, u32[]{:S(2)}, u32[]{:S(2)}) collective-permute-start(bf16[240,768]{1,0:T(8,128)(2,1)S(1)} %get-tuple-element.380), channel_id=1, source_target_pairs={{0,1},{1,0},{2,3},{3,2},{4,5},{5,4},{6,7},{7,6},{8,9},{9,8},{10,11... | collective-permute-start | bytes 1105928 | tf_op jit(solution)/shard_map/ppermute | solution.py:817
  369.4 9.5 %collective-permute-start.26 = (bf16[240,768]{1,0:T(8,128)(2,1)S(1)}, bf16[240,768]{1,0:T(8,128)(2,1)S(1)}, u32[]{:S(2)}, u32[]{:S(2)}) collective-permute-start(bf16[240,768]{1,0:T(8,128)(2,1)S(1)} %get-tuple-element.381), channel_id=1, source_target_pairs={{0,2},{1,3},{2,0},{3,1},{4,6},{5,7},{6,4},{7,5},{8,10},{9,11},{10,... | collective-permute-start | bytes 1105928 | tf_op jit(solution)/shard_map/ppermute | solution.py:817
  371.1 7.1 %collective-permute-start.27 = (bf16[96,768]{1,0:T(8,128)(2,1)S(1)}, bf16[96,768]{1,0:T(8,128)(2,1)S(1)}, u32[]{:S(2)}, u32[]{:S(2)}) collective-permute-start(bf16[96,768]{1,0:T(8,128)(2,1)S(1)} %get-tuple-element.382), channel_id=1, source_target_pairs={{0,4},{1,5},{2,6},{3,7},{4,0},{5,1},{6,2},{7,3},{8,12},{9,13},{10,... | collective-permute-start | bytes 442376 | tf_op jit(solution)/shard_map/ppermute | solution.py:817
  371.1 7.7 %collective-permute-start.28 = (bf16[96,768]{1,0:T(8,128)(2,1)S(1)}, bf16[96,768]{1,0:T(8,128)(2,1)S(1)}, u32[]{:S(2)}, u32[]{:S(2)}) collective-permute-start(bf16[96,768]{1,0:T(8,128)(2,1)S(1)} %get-tuple-element.383), channel_id=1, source_target_pairs={{0,8},{1,9},{2,10},{3,11},{4,12},{5,13},{6,14},{7,15},{8,0},{9,1},... | collective-permute-start | bytes 442376 | tf_op jit(solution)/shard_map/ppermute | solution.py:817
  379.7 11.5 %collective-permute-start.31 = (bf16[192,768]{1,0:T(8,128)(2,1)S(1)}, bf16[192,768]{1,0:T(8,128)(2,1)S(1)}, u32[]{:S(2)}, u32[]{:S(2)}) collective-permute-start(bf16[192,768]{1,0:T(8,128)(2,1)S(1)} %get-tuple-element.408.refs_2_), channel_id=1, source_target_pairs={{0,4},{1,5},{2,6},{3,7},{4,0},{5,1},{6,2},{7,3},{8,12},{9,13},{10,... | collective-permute-start | bytes 884744 | tf_op jit(solution)/shard_map/ppermute | solution.py:817
  380.2 12.3 %collective-permute-start.32 = (bf16[192,768]{1,0:T(8,128)(2,1)S(1)}, bf16[192,768]{1,0:T(8,128)(2,1)S(1)}, u32[]{:S(2)}, u32[]{:S(2)}) collective-permute-start(bf16[192,768]{1,0:T(8,128)(2,1)S(1)} %get-tuple-element.406.refs_0_), channel_id=1, source_target_pairs={{0,8},{1,9},{2,10},{3,11},{4,12},{5,13},{6,14},{7,15},{8,0},{9,1},... | collective-permute-start | bytes 884744 | tf_op jit(solution)/shard_map/ppermute | solution.py:817
  382.7 5.6 %collective-permute-start.29 = (bf16[64,768]{1,0:T(8,128)(2,1)S(1)}, bf16[64,768]{1,0:T(8,128)(2,1)S(1)}, u32[]{:S(2)}, u32[]{:S(2)}) collective-permute-start(bf16[64,768]{1,0:T(8,128)(2,1)S(1)} %get-tuple-element.412.refs_6_), channel_id=1, source_target_pairs={{0,1},{1,0},{2,3},{3,2},{4,5},{5,4},{6,7},{7,6},{8,9},{9,8},{10,11... | collective-permute-start | bytes 294920 | tf_op jit(solution)/shard_map/ppermute | solution.py:817
  384.0 4.4 collective-permute-start.30
  393.2 13.7 %collective-permute-start.35 = (bf16[240,768]{1,0:T(8,128)(2,1)S(1)}, bf16[240,768]{1,0:T(8,128)(2,1)S(1)}, u32[]{:S(2)}, u32[]{:S(2)}) collective-permute-start(bf16[240,768]{1,0:T(8,128)(2,1)S(1)} %get-tuple-element.423.refs_0_), channel_id=1, source_target_pairs={{0,4},{1,5},{2,6},{3,7},{4,0},{5,1},{6,2},{7,3},{8,12},{9,13},{10,... | collective-permute-start | bytes 1105928 | tf_op jit(solution)/shard_map/ppermute | solution.py:817
  393.3 15.5 %collective-permute-start.36 = (bf16[240,768]{1,0:T(8,128)(2,1)S(1)}, bf16[240,768]{1,0:T(8,128)(2,1)S(1)}, u32[]{:S(2)}, u32[]{:S(2)}) collective-permute-start(bf16[240,768]{1,0:T(8,128)(2,1)S(1)} %get-tuple-element.425.refs_2_), channel_id=1, source_target_pairs={{0,8},{1,9},{2,10},{3,11},{4,12},{5,13},{6,14},{7,15},{8,0},{9,1},... | collective-permute-start | bytes 1105928 | tf_op jit(solution)/shard_map/ppermute | solution.py:817
  395.4 6.4 %collective-permute-start.34 = (bf16[112,768]{1,0:T(8,128)(2,1)S(1)}, bf16[112,768]{1,0:T(8,128)(2,1)S(1)}, u32[]{:S(2)}, u32[]{:S(2)}) collective-permute-start(bf16[112,768]{1,0:T(8,128)(2,1)S(1)} %get-tuple-element.429.refs_6_), channel_id=1, source_target_pairs={{0,2},{1,3},{2,0},{3,1},{4,6},{5,7},{6,4},{7,5},{8,10},{9,11},{10,... | collective-permute-start | bytes 516104 | tf_op jit(solution)/shard_map/ppermute | solution.py:817
  396.6 5.1 %collective-permute-start.33 = (bf16[96,768]{1,0:T(8,128)(2,1)S(1)}, bf16[96,768]{1,0:T(8,128)(2,1)S(1)}, u32[]{:S(2)}, u32[]{:S(2)}) collective-permute-start(bf16[96,768]{1,0:T(8,128)(2,1)S(1)} %get-tuple-element.427.refs_4_), channel_id=1, source_target_pairs={{0,1},{1,0},{2,3},{3,2},{4,5},{5,4},{6,7},{7,6},{8,9},{9,8},{10,11... | collective-permute-start | bytes 442376 | tf_op jit(solution)/shard_map/ppermute | solution.py:817
  409.5 17.4 %collective-permute-start.37 = (bf16[384,768]{1,0:T(8,128)(2,1)S(1)}, bf16[384,768]{1,0:T(8,128)(2,1)S(1)}, u32[]{:S(2)}, u32[]{:S(2)}) collective-permute-start(bf16[384,768]{1,0:T(8,128)(2,1)S(1)} %get-tuple-element.442.refs_2_), channel_id=1, source_target_pairs={{0,1},{1,0},{2,3},{3,2},{4,5},{5,4},{6,7},{7,6},{8,9},{9,8},{10,11... | collective-permute-start | bytes 1769480 | tf_op jit(solution)/shard_map/ppermute | solution.py:817
  410.8 16.1 %collective-permute-start.38 = (bf16[384,768]{1,0:T(8,128)(2,1)S(1)}, bf16[384,768]{1,0:T(8,128)(2,1)S(1)}, u32[]{:S(2)}, u32[]{:S(2)}) collective-permute-start(bf16[384,768]{1,0:T(8,128)(2,1)S(1)} %get-tuple-element.440.refs_0_), channel_id=1, source_target_pairs={{0,2},{1,3},{2,0},{3,1},{4,6},{5,7},{6,4},{7,5},{8,10},{9,11},{10,... | collective-permute-start | bytes 1769480 | tf_op jit(solution)/shard_map/ppermute | solution.py:817
  412.6 14.3 %collective-permute-start.39 = (bf16[256,768]{1,0:T(8,128)(2,1)S(1)}, bf16[256,768]{1,0:T(8,128)(2,1)S(1)}, u32[]{:S(2)}, u32[]{:S(2)}) collective-permute-start(bf16[256,768]{1,0:T(8,128)(2,1)S(1)} %get-tuple-element.446.refs_6_), channel_id=1, source_target_pairs={{0,4},{1,5},{2,6},{3,7},{4,0},{5,1},{6,2},{7,3},{8,12},{9,13},{10,... | collective-permute-start | bytes 1179656 | tf_op jit(solution)/shard_map/ppermute | solution.py:817
  412.6 14.3 %collective-permute-start.40 = (bf16[240,768]{1,0:T(8,128)(2,1)S(1)}, bf16[240,768]{1,0:T(8,128)(2,1)S(1)}, u32[]{:S(2)}, u32[]{:S(2)}) collective-permute-start(bf16[240,768]{1,0:T(8,128)(2,1)S(1)} %get-tuple-element.444.refs_4_), channel_id=1, source_target_pairs={{0,8},{1,9},{2,10},{3,11},{4,12},{5,13},{6,14},{7,15},{8,0},{9,1},... | collective-permute-start | bytes 1105928 | tf_op jit(solution)/shard_map/ppermute | solution.py:817
  427.7 36.3 %copy-start.10 = (bf16[768,768]{1,0:T(8,128)(2,1)}, bf16[768,768]{1,0:T(8,128)(2,1)S(1)}, u32[]{:S(2)}) copy-start(bf16[768,768]{1,0:T(8,128)(2,1)S(1)} %get-tuple-element.466.yp) | copy-start | bytes 3538948
  427.7 33.7 %collective-permute-start.41 = (bf16[768,768]{1,0:T(8,128)(2,1)S(1)}, bf16[768,768]{1,0:T(8,128)(2,1)S(1)}, u32[]{:S(2)}, u32[]{:S(2)}) collective-permute-start(bf16[768,768]{1,0:T(8,128)(2,1)S(1)} %get-tuple-element.464.xp), channel_id=1, source_target_pairs={{0,1},{1,0},{2,3},{3,2},{4,5},{5,4},{6,7},{7,6},{8,9},{9,8},{10,11... | collective-permute-start | bytes 3538952 | tf_op jit(solution)/shard_map/ppermute | solution.py:817
  428.1 33.3 %collective-permute-start.42 = (bf16[768,768]{1,0:T(8,128)(2,1)S(1)}, bf16[768,768]{1,0:T(8,128)(2,1)S(1)}, u32[]{:S(2)}, u32[]{:S(2)}) collective-permute-start(bf16[768,768]{1,0:T(8,128)(2,1)S(1)} %get-tuple-element.466.yp), channel_id=1, source_target_pairs={{0,2},{1,3},{2,0},{3,1},{4,6},{5,7},{6,4},{7,5},{8,10},{9,11},{10,... | collective-permute-start | bytes 3538952 | tf_op jit(solution)/shard_map/ppermute | solution.py:817
  429.6 31.8 %collective-permute-start.44 = (bf16[496,768]{1,0:T(8,128)(2,1)S(1)}, bf16[496,768]{1,0:T(8,128)(2,1)S(1)}, u32[]{:S(2)}, u32[]{:S(2)}) collective-permute-start(bf16[496,768]{1,0:T(8,128)(2,1)S(1)} %get-tuple-element.470.refs_2_.bp), channel_id=1, source_target_pairs={{0,8},{1,9},{2,10},{3,11},{4,12},{5,13},{6,14},{7,15},{8,0},{9,1},... | collective-permute-start | bytes 2285576 | tf_op jit(solution)/shard_map/ppermute | solution.py:817
  430.5 28.3 %collective-permute-start.43 = (bf16[480,768]{1,0:T(8,128)(2,1)S(1)}, bf16[480,768]{1,0:T(8,128)(2,1)S(1)}, u32[]{:S(2)}, u32[]{:S(2)}) collective-permute-start(bf16[480,768]{1,0:T(8,128)(2,1)S(1)} %get-tuple-element.468.refs_0_.ap), channel_id=1, source_target_pairs={{0,4},{1,5},{2,6},{3,7},{4,0},{5,1},{6,2},{7,3},{8,12},{9,13},{10,... | collective-permute-start | bytes 2211848 | tf_op jit(solution)/shard_map/ppermute | solution.py:817
  462.1 10.7 %collective-permute-start.45 = (bf16[192,768]{1,0:T(8,128)(2,1)S(1)}, bf16[192,768]{1,0:T(8,128)(2,1)S(1)}, u32[]{:S(2)}, u32[]{:S(2)}) collective-permute-start(bf16[192,768]{1,0:T(8,128)(2,1)S(1)} %get-tuple-element.478.refs_2_), channel_id=1, source_target_pairs={{0,1},{1,0},{2,3},{3,2},{4,5},{5,4},{6,7},{7,6},{8,9},{9,8},{10,11... | collective-permute-start | bytes 884744 | tf_op jit(solution)/shard_map/ppermute | solution.py:817
  462.7 10.1 %collective-permute-start.46 = (bf16[192,768]{1,0:T(8,128)(2,1)S(1)}, bf16[192,768]{1,0:T(8,128)(2,1)S(1)}, u32[]{:S(2)}, u32[]{:S(2)}) collective-permute-start(bf16[192,768]{1,0:T(8,128)(2,1)S(1)} %get-tuple-element.476.refs_0_), channel_id=1, source_target_pairs={{0,2},{1,3},{2,0},{3,1},{4,6},{5,7},{6,4},{7,5},{8,10},{9,11},{10,... | collective-permute-start | bytes 884744 | tf_op jit(solution)/shard_map/ppermute | solution.py:817
  464.0 12.4 %copy-start.3 = (bf16[1024,768]{1,0:T(8,128)(2,1)S(1)}, bf16[1024,768]{1,0:T(8,128)(2,1)}, u32[]{:S(2)}) copy-start(bf16[1024,768]{1,0:T(8,128)(2,1)} %get-tuple-element.258.xr.refs_4_.xn) | copy-start | bytes 4718596
  473.4 14.5 %collective-permute-start.47 = (bf16[384,768]{1,0:T(8,128)(2,1)S(1)}, bf16[384,768]{1,0:T(8,128)(2,1)S(1)}, u32[]{:S(2)}, u32[]{:S(2)}) collective-permute-start(bf16[384,768]{1,0:T(8,128)(2,1)S(1)} %get-tuple-element.482.xp), channel_id=1, source_target_pairs={{0,1},{1,0},{2,3},{3,2},{4,5},{5,4},{6,7},{7,6},{8,9},{9,8},{10,11... | collective-permute-start | bytes 1769480 | tf_op jit(solution)/shard_map/ppermute | solution.py:817
  474.8 13.8 %collective-permute-start.48 = (bf16[384,768]{1,0:T(8,128)(2,1)S(1)}, bf16[384,768]{1,0:T(8,128)(2,1)S(1)}, u32[]{:S(2)}, u32[]{:S(2)}) collective-permute-start(bf16[384,768]{1,0:T(8,128)(2,1)S(1)} %get-tuple-element.484.yp), channel_id=1, source_target_pairs={{0,2},{1,3},{2,0},{3,1},{4,6},{5,7},{6,4},{7,5},{8,10},{9,11},{10,... | collective-permute-start | bytes 1769480 | tf_op jit(solution)/shard_map/ppermute | solution.py:817
  476.4 1.2 collective-permute-start.49
  476.4 15.3 %copy-start.1 = (s32[1024,1]{0,1:T(1,128)S(1)}, s32[1024,1]{0,1:T(1,128)}, u32[]{:S(2)}) copy-start(s32[1024,1]{0,1:T(1,128)} %param.16) | copy-start | bytes 12292
  (38 other events, 163.2 us)
